TPU v7x, 32 devices: a whole 2x2x4 slice. The times are simulated.
32 devices in a mesh: img: 4 (over z), row: 8 (over y, x, core).
Axes of the slice: x: 2, y: 2, z: 4, core: 2. Of those that a mesh axis runs over, the one named last changes fastest.
Arguments:
- flat_params: float32 [286720], P(('img', 'row')), may hold values from -1.5 to 1.5, as said below
- first_moment: float32 [286720], P(('img', 'row')), may hold values from -0.001 to 0.001
- second_moment: float32 [286720], P(('img', 'row')), may hold values from 1e-10 to 1e-06, as said below
- pixels: bfloat16 [64, 64, 7, 3, 1024], P('img', 'row'), may hold values from -6 to 6, as said below
- extents: int32 [64, 2], P('img'), may hold values from 32 to 256, as said below
- labels: int32 [64], P('img'), may hold values from 0 to 999
- teacher: float32 [64, 1000], P('img'), may hold values from -18 to 18
Outputs:
- new_params: float32 [286720], P(('img', 'row'))
- moment_one: float32 [286720], P(('img', 'row'))
- moment_two: float32 [286720], P(('img', 'row'))
- grad_norm: float32 [], replicated
- loss_value: float32 [], replicated
Inputs may be any that keep to these rules, and one draw needn't show every extreme that they name: `extents`: both entries are multiples of 8; in every group of 16 images one image, which one drawn from the seed, fills the canvas; the last image of all has the smallest allowed rows and columns. pixels[n, r, a] is pixel row 4 r + a - 3 of image n, zero outside its 256 rows; entries of different token rows that name the same pixel row are equal. `flat_params`: layout of the steps; matrices scaled by their fan-in, gains near one. `second_moment`: Positive.
All inputs are finite; a program needn't handle non-finite values.
Results may differ from a plain program's by a relative error of at most 0.0018.
The roundings to bfloat16 on the way count: a program that leaves them out, or rounds other values in their place, can miss the bound.
Values may be sent and summed in bfloat16 or wider, within the bound.
No kernel may reach another device: no remote copies, remote signals or barrier semaphores. Data moves between devices by JAX's collectives and lax.ppermute only.
A program may use at most 704 MiB of HBM per device.

v0:
```python
import jax
import jax.numpy as jnp
import numpy as np
from jax import lax
from jax.sharding import PartitionSpec as P

DIM = 96
MLP = 384
CLASSES = 1000
PATCH = 7
ROWS = 8
STEP = 7
CANVAS_W = 256


HIGHEST_PREC = lax.Precision.HIGHEST
CLIP_NORM = 0.02
LEARN_RATE = 0.05
WEIGHT_DECAY = 0.05
BETA_FIRST = 0.5
BETA_SECOND = 0.5
ADAM_EPS = 1e-08
NORM_EPS = 1e-06
NEG_FILL = -1e30


def extended(array, sides, width):
    for axis, dim in sides:
        size, length = (lax.axis_size(axis), array.shape[dim])
        up = [(i, (i + 1) % size) for i in range(size - 1)]
        down = [(j, i) for i, j in up]
        last = lax.slice_in_dim(array, length - width, length, axis=dim)
        leading = lax.slice_in_dim(array, 0, width, axis=dim)
        before = lax.ppermute(last, axis, up)
        after = lax.ppermute(leading, axis, down)
        array = jnp.concatenate([before, array, after], axis=dim)
    return array


def from_behind(value, axis, steps):
    count = lax.axis_size(axis)
    leading, last = (max(0, -steps), min(count, count - steps))
    return lax.ppermute(value, axis, [(source, source + steps) for source in range(leading, last)])


def segment_list(canvas_rows, canvas_cols):
    return [
        ("w_patch", (3 * PATCH * PATCH, DIM)),
        ("w_qkv", (DIM, 3 * DIM)),
        ("w_proj", (DIM, DIM)),
        ("w_fc1", (DIM, MLP)),
        ("w_fc2", (MLP, DIM)),
        ("w_head", (DIM, CLASSES)),
        ("rel_rows", (2 * canvas_rows - 8, DIM)),
        ("rel_cols", (2 * canvas_cols - 8, DIM)),
        ("kernels", (3, 9, DIM)),
        ("vectors", (15, DIM)),
        ("b_qkv", (3 * DIM,)),
        ("b_fc1", (MLP,)),
        ("b_head", (CLASSES,)),
    ]


def unpack(flat_vec, segments):
    pieces = {}
    position = 0
    for seg_name, seg_shape in segments:
        entries = int(np.prod(seg_shape))
        pieces[seg_name] = flat_vec[position : position + entries].reshape(seg_shape)
        position += entries
    return pieces


def pack(pieces, segments, total_len):
    joined = jnp.concatenate([pieces[seg_name].reshape(-1) for seg_name, seg_shape in segments])
    return jnp.pad(joined, (0, total_len - joined.shape[0]))


def layer_norm(values, gain_vec, shift_vec):
    mean_part = jnp.mean(values, axis=-1, keepdims=True)
    centered = values - mean_part
    variance = jnp.mean(centered * centered, axis=-1, keepdims=True)
    return centered * lax.rsqrt(variance + NORM_EPS) * gain_vec + shift_vec


def gelu_exact(values):
    return jax.nn.gelu(values, approximate=False)


def image_loss(pooled, head_w, head_b, teacher, labels, image_total):
    logits = jnp.dot(pooled, head_w, precision=HIGHEST_PREC) + head_b
    log_student = jax.nn.log_softmax(logits, axis=-1)
    log_teacher = jax.nn.log_softmax(teacher, axis=-1)
    onehot = (jnp.arange(CLASSES)[None, :] == labels[:, None]).astype(jnp.float32)
    per_image = jnp.sum(jnp.exp(log_teacher) * (log_teacher - log_student), axis=-1) - jnp.sum(
        onehot * log_student, axis=-1
    )
    return jnp.sum(per_image) / image_total


def pool_query(rimmed_q, kernel, gain_vec, shift_vec):
    rows_out = rimmed_q.shape[1] - 2
    cols_out = rimmed_q.shape[2]
    framed = jnp.pad(rimmed_q, ((0, 0), (0, 0), (1, 1), (0, 0)))
    pooled = jnp.zeros((rimmed_q.shape[0], rows_out, cols_out, rimmed_q.shape[3]), jnp.float32)
    for tap_row in range(3):
        for tap_col in range(3):
            pooled = (
                pooled
                + framed[:, tap_row : tap_row + rows_out, tap_col : tap_col + cols_out]
                * kernel[tap_row * 3 + tap_col]
            )
    return layer_norm(pooled, gain_vec, shift_vec)


def tap_sum(rows_in, kernel_pair, first_tap):
    key_cols = rows_in.shape[2] // ROWS
    framed = jnp.pad(rows_in, ((0, 0), (0, 0), (1, 1), (0, 0)))
    pooled = jnp.zeros((rows_in.shape[0], 1, key_cols, 2 * DIM), jnp.float32)
    for offset in range(rows_in.shape[1]):
        tap_row = first_tap + offset
        for tap_col in range(3):
            tap_index = tap_row * 3 + tap_col
            kernel_vec = jnp.concatenate([kernel_pair[0, tap_index], kernel_pair[1, tap_index]])
            tap_vals = framed[
                :, offset : offset + 1, tap_col : tap_col + ROWS * (key_cols - 1) + 1 : ROWS
            ]
            pooled = pooled + tap_vals * kernel_vec
    return pooled


def key_norm(pre_sums, gain_rows):
    keys_pooled = layer_norm(pre_sums[..., :DIM], gain_rows[0], gain_rows[1])
    values_pooled = layer_norm(pre_sums[..., DIM:], gain_rows[2], gain_rows[3])
    return (keys_pooled, values_pooled)


def pool_all(rows_in, kernel_pair, gain_rows):
    return key_norm(tap_sum(rows_in, kernel_pair, 0), gain_rows)


def select_rows(rel_table, row_index, row_count):
    blocks = rel_table.reshape(2 * row_count - 1, ROWS, rel_table.shape[-1])
    window = lax.dynamic_slice_in_dim(blocks, row_index, row_count, 0)
    return jnp.transpose(jnp.flip(window, 0), (1, 0, 2))


def select_cols(rel_table):
    col_total = CANVAS_W
    key_cols = col_total // ROWS
    index_table = (
        np.arange(col_total)[:, None] - ROWS * np.arange(key_cols)[None, :] + col_total - ROWS
    )
    return rel_table[index_table]


def attend(query_r, key_all, value_all, rows_sel, cols_sel, key_valid):
    batch_imgs, rows_local, cols_local, width = query_r.shape
    key_rows, key_cols = (key_all.shape[1], key_all.shape[2])
    flattened_query = query_r.reshape(batch_imgs, rows_local * cols_local, width)
    flattened_key = key_all.reshape(batch_imgs, key_rows * key_cols, width)
    flattened_value = value_all.reshape(batch_imgs, key_rows * key_cols, width)
    scores = jnp.einsum(
        "siz,svz->siv", flattened_query, flattened_key, preferred_element_type=jnp.float32
    ) * DIM ** (-0.5)
    rel_r = jnp.einsum("nrwc,rac->nrwa", query_r, rows_sel, preferred_element_type=jnp.float32)
    rel_c = jnp.einsum("nrwc,wkc->nrwk", query_r, cols_sel, preferred_element_type=jnp.float32)
    scores = (
        scores.reshape(batch_imgs, rows_local, cols_local, key_rows, key_cols)
        + rel_r[..., :, None]
        + rel_c[..., None, :]
    )
    masked = jnp.where(key_valid[:, None, None], scores, NEG_FILL)
    row_max = jnp.max(masked, axis=(3, 4), keepdims=True)
    exp_scores = jnp.exp(masked - row_max)
    attn_probs = exp_scores / jnp.sum(exp_scores, axis=(3, 4), keepdims=True)
    probability_rows = attn_probs.astype(jnp.bfloat16).reshape(
        batch_imgs, rows_local * cols_local, key_rows * key_cols
    )
    attention_output = jnp.einsum(
        "uwf,ufi->uwi", probability_rows, flattened_value, preferred_element_type=jnp.float32
    )
    return (attention_output.reshape(batch_imgs, rows_local, cols_local, width), attn_probs)


def attend_back(grad_att, query_r, key_all, value_all, attn_probs, rows_sel, cols_sel):
    batch_imgs, rows_local, cols_local, width = query_r.shape
    key_rows, key_cols = (key_all.shape[1], key_all.shape[2])
    token_total = rows_local * cols_local
    key_total = key_rows * key_cols
    flattened_query = query_r.reshape(batch_imgs, token_total, width)
    flattened_key = key_all.reshape(batch_imgs, key_total, width)
    flattened_value = value_all.reshape(batch_imgs, key_total, width)
    output_gradient_rows = grad_att.astype(jnp.bfloat16).reshape(batch_imgs, token_total, width)
    flat_p = attn_probs.reshape(batch_imgs, token_total, key_total)
    probability_rows = flat_p.astype(jnp.bfloat16)
    probability_gradient = jnp.einsum(
        "siz,svz->siv", output_gradient_rows, flattened_value, preferred_element_type=jnp.float32
    )
    value_gradient = jnp.einsum(
        "pag,pao->pgo", probability_rows, output_gradient_rows, preferred_element_type=jnp.float32
    )
    grad_scores = flat_p * (
        probability_gradient - jnp.sum(flat_p * probability_gradient, axis=-1, keepdims=True)
    )
    score_gradient_rows = grad_scores.astype(jnp.bfloat16)
    grad_query = jnp.einsum(
        "uwf,ufi->uwi", score_gradient_rows, flattened_key, preferred_element_type=jnp.float32
    ) * DIM ** (-0.5)
    grad_key = jnp.einsum(
        "pag,pao->pgo", score_gradient_rows, flattened_query, preferred_element_type=jnp.float32
    ) * DIM ** (-0.5)
    grid = score_gradient_rows.astype(jnp.float32).reshape(
        batch_imgs, rows_local, cols_local, key_rows, key_cols
    )
    grad_rel_r = jnp.sum(grid, axis=4)
    grad_rel_c = jnp.sum(grid, axis=3)
    query_wide = query_r.astype(jnp.float32)
    grad_query = grad_query.reshape(batch_imgs, rows_local, cols_local, width)
    grad_query = grad_query + jnp.einsum(
        "nrwa,rac->nrwc", grad_rel_r, rows_sel.astype(jnp.float32), precision=HIGHEST_PREC
    )
    grad_query = grad_query + jnp.einsum(
        "nrwk,wkc->nrwc", grad_rel_c, cols_sel.astype(jnp.float32), precision=HIGHEST_PREC
    )
    grad_rows_sel = jnp.einsum("nrwa,nrwc->rac", grad_rel_r, query_wide, precision=HIGHEST_PREC)
    grad_cols_sel = jnp.einsum("nrwk,nrwc->wkc", grad_rel_c, query_wide, precision=HIGHEST_PREC)
    grad_key = grad_key.reshape(batch_imgs, key_rows, key_cols, width)
    value_gradient = value_gradient.reshape(batch_imgs, key_rows, key_cols, width)
    return (grad_query, grad_key, value_gradient, grad_rows_sel, grad_cols_sel)


def body(flat_params, first_moment, second_moment, pixels, extents, labels, teacher):
    row_count = lax.axis_size("row")
    row_index = lax.axis_index("row")
    segments = segment_list(ROWS * row_count, CANVAS_W)
    full_params = lax.all_gather(
        flat_params.astype(jnp.bfloat16), ("img", "row"), axis=0, tiled=True
    )
    weights = unpack(full_params, segments)
    vectors = weights["vectors"].astype(jnp.float32)
    kernels = weights["kernels"].astype(jnp.float32)
    images_here, rows_here, tap_total, pix_chans, pix_cols = pixels.shape
    cols_here = pix_cols // 4
    key_cols = cols_here // ROWS
    height = extents[:, 0]
    breadth = extents[:, 1]
    row_ids = row_index * rows_here + jnp.arange(rows_here)
    col_ids = jnp.arange(cols_here)
    token_mask = (
        (row_ids[None, :, None] < height[:, None, None])
        & (col_ids[None, None, :] < breadth[:, None, None])
    ).astype(jnp.float32)[..., None]
    key_valid = (jnp.arange(row_count)[None, :, None] < (height // ROWS)[:, None, None]) & (
        jnp.arange(key_cols)[None, None, :] < (breadth // ROWS)[:, None, None]
    )
    framed = jnp.pad(pixels, ((0, 0), (0, 0), (0, 0), (0, 0), (3, 3)))
    columns = []
    for tap_row in range(PATCH):
        for tap_col in range(PATCH):
            pix_piece = framed[:, :, tap_row, :, tap_col : tap_col + pix_cols : 4]
            columns.append(jnp.transpose(pix_piece, (0, 1, 3, 2)))
    patches = jnp.concatenate(columns, axis=-1)
    embed = (
        jnp.einsum("nrwk,kc->nrwc", patches, weights["w_patch"], preferred_element_type=jnp.float32)
        + vectors[0]
    )
    x_zero = embed * token_mask
    normed_one, ln_one_back = jax.vjp(layer_norm, x_zero, vectors[1], vectors[2])
    normed_one_r = normed_one.astype(jnp.bfloat16)
    proj_qkv = jnp.einsum(
        "nrwc,ce->nrwe", normed_one_r, weights["w_qkv"], preferred_element_type=jnp.float32
    )
    proj_qkv_r = (proj_qkv + weights["b_qkv"].astype(jnp.float32)).astype(jnp.bfloat16)
    query_rim = extended(proj_qkv_r[..., :DIM], (("row", 1),), 1)
    query_wide = query_rim.astype(jnp.float32)
    query_n, pool_q_back = jax.vjp(pool_query, query_wide, kernels[0], vectors[3], vectors[4])
    query_nr = query_n.astype(jnp.bfloat16)
    kv_local = proj_qkv_r[..., DIM:]
    above_row = from_behind(kv_local[:, -1:], "row", 1)
    rows_three = jnp.concatenate([above_row, kv_local[:, :2]], axis=1).astype(jnp.float32)
    pooled_pair, pool_k_back = jax.vjp(pool_all, rows_three, kernels[1:3], vectors[5:9])
    key_all, value_all = (
        lax.all_gather(pooled_pair[0].astype(jnp.bfloat16), "row", axis=1, tiled=True),
        lax.all_gather(pooled_pair[1].astype(jnp.bfloat16), "row", axis=1, tiled=True),
    )
    rel_rows32 = weights["rel_rows"].astype(jnp.float32)
    rel_cols32 = weights["rel_cols"].astype(jnp.float32)
    rows_sel32, rows_pull = jax.vjp(
        lambda rel_table: select_rows(rel_table, row_index, row_count), rel_rows32
    )
    cols_sel32, cols_pull = jax.vjp(select_cols, rel_cols32)
    rows_sel = rows_sel32.astype(jnp.bfloat16)
    cols_sel = cols_sel32.astype(jnp.bfloat16)
    attention_output, attn_probs = attend(
        query_nr, key_all, value_all, rows_sel, cols_sel, key_valid
    )
    attended_r = (attention_output + query_nr.astype(jnp.float32)).astype(jnp.bfloat16)
    proj_out = (
        jnp.einsum(
            "nrwc,cd->nrwd", attended_r, weights["w_proj"], preferred_element_type=jnp.float32
        )
        + vectors[9]
    )
    x_one = x_zero + proj_out
    normed_two, ln_two_back = jax.vjp(layer_norm, x_one, vectors[10], vectors[11])
    normed_two_r = normed_two.astype(jnp.bfloat16)
    hidden_pre = jnp.einsum(
        "nrwc,ch->nrwh", normed_two_r, weights["w_fc1"], preferred_element_type=jnp.float32
    ) + weights["b_fc1"].astype(jnp.float32)
    activated, gelu_back = jax.vjp(gelu_exact, hidden_pre)
    activated_r = activated.astype(jnp.bfloat16)
    mlp_out = (
        jnp.einsum(
            "nrwh,hc->nrwc", activated_r, weights["w_fc2"], preferred_element_type=jnp.float32
        )
        + vectors[12]
    )
    x_two = x_one + mlp_out
    normed_three, ln_three_back = jax.vjp(layer_norm, x_two, vectors[13], vectors[14])
    pooled_part = jnp.sum(normed_three * token_mask, axis=(1, 2))
    pooled_sum = lax.psum(pooled_part, "row")
    counts = (height * breadth).astype(jnp.float32)[:, None]
    pooled = pooled_sum / counts
    image_total = images_here * lax.axis_size("img") * 1.0

    def loss_local_of(pooled_now, head_w, head_b):
        return image_loss(pooled_now, head_w, head_b, teacher, labels, image_total)

    loss_local, loss_back = jax.vjp(
        loss_local_of,
        pooled,
        weights["w_head"].astype(jnp.float32),
        weights["b_head"].astype(jnp.float32),
    )
    loss_value = lax.psum(loss_local, "img")
    grad_pooled, grad_head_w, grad_head_b = loss_back(jnp.ones_like(loss_local))
    grad_head_w = grad_head_w / row_count
    grad_head_b = grad_head_b / row_count
    grad_n_three = (grad_pooled / counts)[:, None, None, :] * token_mask
    grad_x_two, grad_g_three, grad_b_three = ln_three_back(grad_n_three)
    grad_mlp_r = grad_x_two.astype(jnp.bfloat16)
    grad_act = jnp.einsum(
        "nrwc,hc->nrwh", grad_mlp_r, weights["w_fc2"], preferred_element_type=jnp.float32
    )
    grad_w_fc2 = jnp.einsum(
        "nrwh,nrwc->hc", activated_r, grad_mlp_r, preferred_element_type=jnp.float32
    )
    grad_b_fc2 = jnp.sum(grad_mlp_r.astype(jnp.float32), axis=(0, 1, 2))
    grad_pre_r = gelu_back(grad_act)[0].astype(jnp.bfloat16)
    grad_n_two = jnp.einsum(
        "nrwh,ch->nrwc", grad_pre_r, weights["w_fc1"], preferred_element_type=jnp.float32
    )
    grad_w_fc1 = jnp.einsum(
        "nrwc,nrwh->ch", normed_two_r, grad_pre_r, preferred_element_type=jnp.float32
    )
    grad_b_fc1 = jnp.sum(grad_pre_r.astype(jnp.float32), axis=(0, 1, 2))
    grad_ln_two, grad_g_two, grad_b_two = ln_two_back(grad_n_two)
    grad_x_one = grad_x_two + grad_ln_two
    grad_proj_r = grad_x_one.astype(jnp.bfloat16)
    grad_att = jnp.einsum(
        "nrwd,cd->nrwc", grad_proj_r, weights["w_proj"], preferred_element_type=jnp.float32
    )
    grad_w_proj = jnp.einsum(
        "nrwc,nrwd->cd", attended_r, grad_proj_r, preferred_element_type=jnp.float32
    )
    grad_b_proj = jnp.sum(grad_proj_r.astype(jnp.float32), axis=(0, 1, 2))
    grad_query, grad_key_all, grad_value_all, grad_rows_sel, grad_cols_sel = attend_back(
        grad_att, query_nr, key_all, value_all, attn_probs, rows_sel, cols_sel
    )
    grad_query_n = grad_att + grad_query
    grad_key_n, grad_value_n = (
        lax.psum_scatter(
            grad_key_all.astype(jnp.bfloat16), "row", scatter_dimension=1, tiled=True
        ).astype(jnp.float32),
        lax.psum_scatter(
            grad_value_all.astype(jnp.bfloat16), "row", scatter_dimension=1, tiled=True
        ).astype(jnp.float32),
    )
    grad_rim, grad_kernel_q, grad_g_q, grad_b_q = pool_q_back(grad_query_n)
    rims = jnp.concatenate([grad_rim[:, :1], grad_rim[:, -1:]], axis=1)
    returned = extended(rims.astype(jnp.bfloat16), (("row", 1),), 1).astype(rims.dtype)
    grad_q_local = grad_rim[:, 1:-1]
    grad_q_local = grad_q_local.at[:, 0].add(returned[:, 0]).at[:, -1].add(returned[:, 3])
    grad_three, grad_kernel_kv, grad_gain_kv = pool_k_back((grad_key_n, grad_value_n))
    grad_last = from_behind(grad_three[:, :1].astype(jnp.bfloat16), "row", -1).astype(jnp.float32)
    grad_first = grad_three[:, 1:3]
    grad_kv = jnp.zeros(grad_q_local.shape[:3] + (2 * DIM,), jnp.float32)
    grad_kv = grad_kv.at[:, :2].set(grad_first).at[:, -1:].add(grad_last)
    grad_qkv_r = jnp.concatenate([grad_q_local, grad_kv], axis=-1).astype(jnp.bfloat16)
    grad_n_one = jnp.einsum(
        "nrwe,ce->nrwc", grad_qkv_r, weights["w_qkv"], preferred_element_type=jnp.float32
    )
    grad_w_qkv = jnp.einsum(
        "nrwc,nrwe->ce", normed_one_r, grad_qkv_r, preferred_element_type=jnp.float32
    )
    grad_b_qkv = jnp.sum(grad_qkv_r.astype(jnp.float32), axis=(0, 1, 2))
    grad_ln_one, grad_g_one, grad_b_one = ln_one_back(grad_n_one)
    grad_embed = (grad_x_one + grad_ln_one) * token_mask
    grad_w_patch = jnp.einsum(
        "nrwk,nrwc->kc", patches.astype(jnp.float32), grad_embed, precision=HIGHEST_PREC
    )
    grad_b_patch = jnp.sum(grad_embed, axis=(0, 1, 2))
    grad_vectors = jnp.stack(
        [
            grad_b_patch,
            grad_g_one,
            grad_b_one,
            grad_g_q,
            grad_b_q,
            grad_gain_kv[0],
            grad_gain_kv[1],
            grad_gain_kv[2],
            grad_gain_kv[3],
            grad_b_proj,
            grad_g_two,
            grad_b_two,
            grad_b_fc2,
            grad_g_three,
            grad_b_three,
        ]
    )
    grad_pieces = {
        "w_patch": grad_w_patch,
        "w_qkv": grad_w_qkv,
        "w_proj": grad_w_proj,
        "w_fc1": grad_w_fc1,
        "w_fc2": grad_w_fc2,
        "w_head": grad_head_w,
        "rel_rows": rows_pull(grad_rows_sel)[0],
        "rel_cols": cols_pull(grad_cols_sel)[0],
        "kernels": jnp.concatenate([grad_kernel_q[None], grad_kernel_kv], axis=0),
        "vectors": grad_vectors,
        "b_qkv": grad_b_qkv,
        "b_fc1": grad_b_fc1,
        "b_head": grad_head_b,
    }
    grad_flat = pack(grad_pieces, segments, full_params.shape[0])
    grad_shard = lax.psum_scatter(grad_flat, ("img", "row"), scatter_dimension=0, tiled=True)
    norm_sq = lax.psum(jnp.sum(grad_shard * grad_shard), ("img", "row"))
    grad_norm = jnp.sqrt(norm_sq)
    clip_factor = jnp.minimum(1.0, CLIP_NORM / (grad_norm + 1e-06))
    clipped = grad_shard * clip_factor
    moment_one = BETA_FIRST * first_moment + (1.0 - BETA_FIRST) * clipped
    moment_two = BETA_SECOND * second_moment + (1.0 - BETA_SECOND) * clipped * clipped
    fix_one = 1.0 - BETA_FIRST**STEP
    fix_two = 1.0 - BETA_SECOND**STEP
    update = (
        moment_one / fix_one / (jnp.sqrt(moment_two / fix_two) + ADAM_EPS)
        + WEIGHT_DECAY * flat_params
    )
    new_params = flat_params - LEARN_RATE * update
    return (new_params, moment_one, moment_two, grad_norm, loss_value)


def solution(mesh):
    placed = (
        P(("img", "row")),
        P(("img", "row")),
        P(("img", "row")),
        P("img", "row", None, None, None),
        P("img", None),
        P("img"),
        P("img", None),
    )
    return jax.shard_map(
        body,
        mesh=mesh,
        in_specs=placed,
        out_specs=(P(("img", "row")), P(("img", "row")), P(("img", "row")), P(), P()),
        check_vma=False,
    )
```

profile of v0, /device:TPU:0, one launch (start us, length us, event | category | flops | bytes accessed | tf_op | source)
XLA Modules:
  0.0 3060.8 jit_solution(9938549247658761636)
XLA Ops:
  8.0 46.4 %all-gather = bf16[32,1,8960]{2,1,0:T(2,128)(2,1)S(1)} all-gather(bf16[1,1,8960]{2,1,0:T(2,128)(2,1)S(1)} %reshape.1022), channel_id=1, replica_groups=mesh['img'=4,'row'=8] {'img','row'}, dimensions={0}, use_global_device_ids=true | all-gather | bytes 591360 | tf_op jit(solution)/shard_map/all_gather | solution.py:237
  59.0 16.9 copy.64
  242.2 16.0 slice.663
  258.2 16.1 slice.662
  322.1 16.0 slice.658
  354.1 16.0 slice.656
  433.8 16.0 slice.651
  449.8 16.1 slice.650
  465.9 16.0 slice.649
  545.6 16.0 slice.644
  577.5 16.0 slice.642
  641.3 16.3 slice.638
  657.7 16.0 slice.637
  689.6 16.0 slice.635
  721.5 16.0 slice.633
  769.3 16.0 slice.630
  833.2 16.1 slice.626
  866.9 174.2 %concatenate.60 = bf16[16,8,256,147]{2,3,1,0:T(8,128)(2,1)} concatenate(bf16[16,8,256,3]{2,3,1,0:T(4,128)(2,1)} %bitcast.522, bf16[16,8,256,3]{2,3,1,0:T(4,128)(2,1)} %bitcast.521, bf16[16,8,256,3]{2,3,1,0:T(4,128)(2,1)} %bitcast.520, bf16[16,8,256,3]{2,3,1,0:T(4,128)(2,1)} %bitcast.519, bf16[16,8,256,3]{2,3,1,0:T(4,128)(2,1)} %bitcast.518, bf16[16,8,256,3]{2,3,1,0:T(4,128)(2,1)} %bitcast.517, ...), dimensions={3} | concatenate | bytes 19267584 | tf_op jit(solution)/shard_map/concatenate | solution.py:263
  1102.9 24.4 gather_fusion
  1138.5 42.6 %fusion.105 = (f32[16,8,256]{2,1,0:T(8,128)S(1)}, f32[16,8,256,96]{2,3,1,0:T(8,128)}) fusion(f32[96]{0:T(128)S(1)} %get-tuple-element.172, f32[96]{0:T(128)S(1)} %get-tuple-element.173, f32[16,10,256,96]{2,3,1,0:T(8,128)} %maximum_convert_fusion, f32[96]{0:T(128)S(1)} %get-tuple-element.174, f32[96]{0:T(128)S(1)} %get-tuple-element.175, ...), kind=kLoop, calls=%fused_computation.362 | loop fusion | flops 56590336 | bytes 66194816 | tf_op jit(solution)/shard_map/jvp()/reduce_sum | solution.py:80
  1269.1 35.5 %add.490 = f32[16,2048,256]{1,2,0:T(8,128)} reshape(f32[16,8,256,8,32]{2,1,4,3,0:T(8,128)} %add.489) | data formatting | bytes 67108864 | tf_op jit(solution)/shard_map/add | solution.py:169
  1315.7 35.6 %add.485 = f32[16,2048,256]{1,2,0:T(8,128)} reshape(f32[16,8,256,8,32]{2,1,4,3,0:T(8,128)} %add.484) | data formatting | bytes 67108864 | tf_op jit(solution)/shard_map/add | solution.py:169
  1359.2 16.3 slice.734
  1375.6 16.3 slice.731
  1391.9 16.1 slice.728
  1408.0 16.1 slice.725
  1424.1 16.3 slice.722
  1440.4 16.1 slice.719
  1487.6 16.3 slice.710
  1511.5 19.4 all_gather.10
  1534.2 20.7 all_gather.11
  1558.6 36.4 %fusion.110 = (f32[16,2048]{1,0:T(8,128)S(1)}, f32[16,2048,256]{1,2,0:T(8,128)}) fusion(f32[16,2048,256]{1,2,0:T(8,128)} %add.490, f32[16,2048,256]{1,2,0:T(8,128)} %add.485, pred[16,256]{1,0:T(8,128)(4,1)S(1)} %copy-done.92, bf16[16,256,96]{2,1,0:T(8,128)(2,1)S(1)} %bitcast.467, bf16[16,2048,96]{1,2,0:T(8,128)(2,1)} %bitcast.465), kind=kOutput, calls=%fused_computation.367 | convolution fusion | flops 1660944640 | bytes 107876352 | tf_op jit(solution)/shard_map/sub | solution.py:175
  1595.0 17.1 fusion.23
  1612.2 17.2 fusion.111
  1637.6 27.8 fusion.8
  1665.5 118.9 %multiply_convert_fusion = (bf16[16,8,256,384]{3,2,1,0:T(8,128)(2,1)}, f32[16,8,256,384]{3,2,1,0:T(8,128)}) fusion(f32[16,8,256,384]{3,2,1,0:T(8,128)} %get-tuple-element.207, f32[384]{0:T(512)S(1)} %copy-done.126, u16[8,256,384]{2,1,0:T(8,128)(2,1)} %get-tuple-element.54, u16[8,256,384]{2,1,0:T(8,128)(2,1)} %get-tuple-element.53), kind=kLoop, calls=%fused_computation.12 | loop fusion | flops 893386752 | bytes 128976384 | tf_op jit(solution)/shard_map/convert_element_type | solution.py:312
  1784.4 22.7 fusion.112
  1872.9 44.5 %convert_reduce_fusion = (f32[384]{0:T(512)}, bf16[16,8,256,384]{3,2,1,0:T(8,128)(2,1)}) fusion(f32[16,8,256,384]{3,2,1,0:T(8,128)} %get-tuple-element.123, bf16[16,8,256,96]{2,3,1,0:T(8,128)(2,1)S(1)} %get-tuple-element.109, bf16[384,96]{1,0:T(8,128)(2,1)S(1)} %copy-done.66, f32[16,8,256,384]{3,2,1,0:T(8,128)} %get-tuple-element.207, f32[384]{0:T(512)S(1)} %copy-done.126), kind=kOutput, calls=%fused_computation.10 | convolution fusion | flops 2629828096 | bytes 132197376 | tf_op jit(solution)/shard_map/nrwc,hc->nrwh/dot_general | solution.py:343
  1917.4 16.6 convolution_bitcast_fusion.2
  1934.0 20.1 multiply_reduce_fusion.2
  2008.9 16.5 fusion.36
  2025.4 23.8 multiply_reduce_fusion
  2049.2 38.8 %fusion.102 = (f32[16,2048,256]{1,2,0:T(8,128)}, bf16[16,2048,256]{1,2,0:T(8,128)(2,1)}) fusion(f32[16,2048,256]{1,2,0:T(8,128)} %get-tuple-element.214, f32[16,2048]{1,0:T(8,128)S(1)} %get-tuple-element.213, f32[16,2048,256]{1,2,0:T(8,128)} %get-tuple-element.204, f32[16,2048]{1,0:T(8,128)S(1)} %copy-done.65), kind=kLoop, calls=%fused_computation.360 | loop fusion | flops 41943040 | bytes 117702656 | tf_op jit(solution)/shard_map/reshape | solution.py:213
  2108.9 19.9 copy.140
  2149.1 19.4 fusion.115
  2183.8 16.7 copy.89
  2200.5 19.4 multiply_reduce_fusion.3
  2246.0 78.3 %multiply_reduce_fusion.13 = (f32[96]{0:T(128)S(1)}, f32[96]{0:T(128)S(1)}, f32[96]{0:T(128)S(1)}, f32[96]{0:T(128)S(1)}, f32[96]{0:T(128)S(1)}, /*index=5*/f32[...) fusion(f32[16,10,256,96]{2,3,1,0:T(8,128)} %maximum_convert_fus, ...), kind=kLoop, calls=%fused_computation.75 | loop fusion | flops 84933792 | bytes 166861184 | tf_op jit(solution)/shard_map/transpose(jvp())/reduce_sum | solution.py:110
  2326.2 52.4 %fusion.100 = (bf16[16,10,258,96]{2,3,1,0:T(8,128)(2,1)}, f32[16,10,258,96]{2,3,1,0:T(8,128)}) fusion(f32[16,8,256,96]{2,3,1,0:T(8,128)} %get-tuple-element.135, f32[16,8,256,96]{2,3,1,0:T(8,128)} %get-tuple-element.134, f32[16,8,256,96]{2,3,1,0:T(8,128)} %get-tuple-element.131, f32[16,8,256,96]{2,3,1,0:T(8,128)} %get-tuple-element.129, ...), kind=kLoop, calls=%fused_computation.358 | loop fusion | flops 35665920 | bytes 137023488 | tf_op jit(solution)/shard_map/convert.11
  2399.1 44.4 %scatter_custom_fusion = f32[504,96]{1,0:T(8,128)S(1)} fusion(s32[8192]{0:T(1024)} %constant.402, f32[8192,96]{1,0:T(8,128)} %bitcast.471, f32[]{:T(128)} %constant.236.clone.1), kind=kCustom, calls=%fused_computation.207 | custom fusion | flops 786432 | bytes 194048 | tf_op jit(solution)/shard_map/transpose(jvp())/scatter-add | solution.py:154
  2515.6 21.6 pad.202
  2537.2 21.4 pad.205
  2558.7 19.3 pad.210
  2578.0 21.4 pad.209
  2599.5 19.9 pad.206
  2619.3 21.2 pad.207
  2640.6 21.4 pad.208
  2662.0 19.8 pad.203
  2681.8 19.3 pad.204
  2701.1 39.7 %add_add_fusion.4 = bf16[16,3,258,192]{2,3,1,0:T(8,128)(2,1)S(1)} fusion(f32[16,3,258,192]{2,3,1,0:T(8,128)} %pad.210, f32[16,3,258,192]{2,3,1,0:T(8,128)} %pad.209, f32[16,3,258,192]{2,3,1,0:T(8,128)} %pad.208, f32[16,3,258,192]{2,3,1,0:T(8,128)} %pad.207, f32[16,3,258,192]{2,3,1,0:T(8,128)} %pad.206, f32[16,3,258,192]{2,3,1,0:T(8,128)} %pad.205, ...), kind=kLoop, calls=%fused_computation.53 | loop fusion | flops 21399552 | bytes 90353664 | tf_op jit(solution)/shard_map/transpose(jvp())/add_any | solution.py:125
  2779.0 17.6 fusion.95
  2810.2 26.4 fusion.99
  2857.8 142.0 %all-reduce.59.cloned.1.call-done = f32[286720]{0:T(1024)} async-done(((f32[286720]{0:T(1024)}), f32[286720]{0:T(1024)}) %all-reduce.59.cloned.1.call-update) | async-done | bytes 1146896
  3012.5 38.1 %psum.22 = f32[]{:T(128)} all-reduce(f32[]{:T(128)} %multiply_reduce_fusion.34), channel_id=1, replica_groups=mesh['img'=4,'row'=8] {'img','row'}, use_global_device_ids=true, to_apply=%region_77.78 | all-reduce | flops 1 | bytes 8 | tf_op jit(solution)/shard_map/psum | solution.py:440
  (628 shorter events, 1171.6 us)
Async XLA Ops:
  7.2 2467.8 %reduce-scatter.3.cloned.1.call-start = ((), (), s32[]{:S(2)}) async-start(), calls=%async_computation.2 | async-start | bytes 1179648 | tf_op jit(solution)/shard_map/reduce_scatter | solution.py:376
  102.8 762.4 %copy-start.152 = (s32[16,2]{0,1:T(2,128)S(1)}, s32[16,2]{0,1:T(2,128)}, u32[]{:S(2)}) copy-start(s32[16,2]{0,1:T(2,128)} %param.21) | copy-start | bytes 388
  866.4 189.0 %copy-start.95 = (f32[96]{0:T(128)}, f32[96]{0:T(128)S(1)}, u32[]{:S(2)}) copy-start(f32[96]{0:T(128)S(1)} %get-tuple-element.195) | copy-start | bytes 1156
  866.4 189.0 %copy-start.129 = (f32[96]{0:T(128)}, f32[96]{0:T(128)S(1)}, u32[]{:S(2)}) copy-start(f32[96]{0:T(128)S(1)} %get-tuple-element.194) | copy-start | bytes 1156
  866.4 189.0 %copy-start.174 = (f32[96]{0:T(128)}, f32[96]{0:T(128)S(1)}, u32[]{:S(2)}) copy-start(f32[96]{0:T(128)S(1)} %get-tuple-element.193) | copy-start | bytes 1156
  866.4 349.2 %copy-start.105 = (f32[96]{0:T(128)}, f32[96]{0:T(128)S(1)}, u32[]{:S(2)}) copy-start(f32[96]{0:T(128)S(1)} %get-tuple-element.192) | copy-start | bytes 1156
  866.8 188.6 %copy-start.9 = (f32[16,8,256]{2,1,0:T(8,128)}, f32[16,8,256]{2,1,0:T(8,128)S(1)}, u32[]{:S(2)}) copy-start(f32[16,8,256]{2,1,0:T(8,128)S(1)} %and_convert_fusion.2) | copy-start | bytes 393220
  1070.9 58.4 %collective-permute-start = (bf16[16,1,256,96]{2,3,1,0:T(8,128)(2,1)}, bf16[16,1,256,96]{2,3,1,0:T(8,128)(2,1)}, u32[]{:S(2)}, u32[]{:S(2)}) collective-permute-start(bf16[16,1,256,96]{2,3,1,0:T(8,128)(2,1)} %get-tuple-element.126), channel_id=1, source_target_pairs={{0,1},{1,2},{2,3},{3,4},{4,5},{5,6},{6,7},{8,9},{9,10},{10,11},{11... | collective-permute-start | bytes 2359304 | tf_op jit(solution)/shard_map/ppermute | solution.py:34
  1074.1 55.2 %collective-permute-start.1 = (bf16[16,1,256,96]{2,3,1,0:T(8,128)(2,1)}, bf16[16,1,256,96]{2,3,1,0:T(8,128)(2,1)}, u32[]{:S(2)}, u32[]{:S(2)}) collective-permute-start(bf16[16,1,256,96]{2,3,1,0:T(8,128)(2,1)} %get-tuple-element.127), channel_id=1, source_target_pairs={{1,0},{2,1},{3,2},{4,3},{5,4},{6,5},{7,6},{9,8},{10,9},{11,10},{12... | collective-permute-start | bytes 2359304 | tf_op jit(solution)/shard_map/ppermute | solution.py:35
  1078.1 273.3 %collective-permute-start.2 = (bf16[16,1,256,192]{2,3,1,0:T(8,128)(2,1)}, bf16[16,1,256,192]{2,3,1,0:T(8,128)(2,1)}, u32[]{:S(2)}, u32[]{:S(2)}) collective-permute-start(bf16[16,1,256,192]{2,3,1,0:T(8,128)(2,1)} %slice.775), channel_id=1, source_target_pairs={{0,1},{1,2},{2,3},{3,4},{4,5},{5,6},{6,7},{8,9},{9,10},{10,11},{11... | collective-permute-start | bytes 4718600 | tf_op jit(solution)/shard_map/ppermute | solution.py:43
  1083.2 55.3 %copy-start.135 = (f32[96]{0:T(128)}, f32[96]{0:T(128)S(1)}, u32[]{:S(2)}) copy-start(f32[96]{0:T(128)S(1)} %get-tuple-element.152) | copy-start | bytes 1156
  1127.3 105.1 %copy-start.6 = (bf16[8192,96]{1,0:T(8,128)(2,1)}, bf16[8192,96]{1,0:T(8,128)(2,1)S(1)}, u32[]{:S(2)}) copy-start(bf16[8192,96]{1,0:T(8,128)(2,1)S(1)} %gather_fusion) | copy-start | bytes 4718596
  1129.2 51.9 %copy-start.131 = (f32[96]{0:T(128)}, f32[96]{0:T(128)S(1)}, u32[]{:S(2)}) copy-start(f32[96]{0:T(128)S(1)} %get-tuple-element.172) | copy-start | bytes 1156
  1129.2 51.9 %copy-start.138 = (f32[96]{0:T(128)}, f32[96]{0:T(128)S(1)}, u32[]{:S(2)}) copy-start(f32[96]{0:T(128)S(1)} %get-tuple-element.171) | copy-start | bytes 1156
  1129.3 51.9 %copy-start.140 = (f32[96]{0:T(128)}, f32[96]{0:T(128)S(1)}, u32[]{:S(2)}) copy-start(f32[96]{0:T(128)S(1)} %get-tuple-element.173) | copy-start | bytes 1156
  1129.3 51.9 %copy-start.142 = (f32[96]{0:T(128)}, f32[96]{0:T(128)S(1)}, u32[]{:S(2)}) copy-start(f32[96]{0:T(128)S(1)} %get-tuple-element.174) | copy-start | bytes 1156
  1129.3 51.9 %copy-start.144 = (f32[96]{0:T(128)}, f32[96]{0:T(128)S(1)}, u32[]{:S(2)}) copy-start(f32[96]{0:T(128)S(1)} %get-tuple-element.175) | copy-start | bytes 1156
  1129.3 51.9 %copy-start.146 = (f32[96]{0:T(128)}, f32[96]{0:T(128)S(1)}, u32[]{:S(2)}) copy-start(f32[96]{0:T(128)S(1)} %get-tuple-element.176) | copy-start | bytes 1156
  1129.3 51.9 %copy-start.148 = (f32[96]{0:T(128)}, f32[96]{0:T(128)S(1)}, u32[]{:S(2)}) copy-start(f32[96]{0:T(128)S(1)} %get-tuple-element.177) | copy-start | bytes 1156
  1129.3 51.9 %copy-start.150 = (f32[96]{0:T(128)}, f32[96]{0:T(128)S(1)}, u32[]{:S(2)}) copy-start(f32[96]{0:T(128)S(1)} %get-tuple-element.178) | copy-start | bytes 1156
  1375.5 128.4 %copy-start.109 = (f32[192]{0:T(256)S(1)}, f32[192]{0:T(256)}, u32[]{:S(2)}) copy-start(f32[192]{0:T(256)} %get-tuple-element.223) | copy-start | bytes 2308
  1375.5 128.4 %copy-start.111 = (f32[192]{0:T(256)S(1)}, f32[192]{0:T(256)}, u32[]{:S(2)}) copy-start(f32[192]{0:T(256)} %get-tuple-element.224) | copy-start | bytes 2308
  1375.5 128.4 %copy-start.113 = (f32[192]{0:T(256)S(1)}, f32[192]{0:T(256)}, u32[]{:S(2)}) copy-start(f32[192]{0:T(256)} %get-tuple-element.221) | copy-start | bytes 2308
  1375.5 128.4 %copy-start.115 = (f32[192]{0:T(256)S(1)}, f32[192]{0:T(256)}, u32[]{:S(2)}) copy-start(f32[192]{0:T(256)} %get-tuple-element.222) | copy-start | bytes 2308
  1375.5 128.4 %copy-start.117 = (f32[192]{0:T(256)S(1)}, f32[192]{0:T(256)}, u32[]{:S(2)}) copy-start(f32[192]{0:T(256)} %get-tuple-element.225) | copy-start | bytes 2308
  1375.5 128.4 %copy-start.118 = (f32[192]{0:T(256)S(1)}, f32[192]{0:T(256)}, u32[]{:S(2)}) copy-start(f32[192]{0:T(256)} %get-tuple-element.226) | copy-start | bytes 2308
  1375.6 128.4 %copy-start.119 = (f32[192]{0:T(256)S(1)}, f32[192]{0:T(256)}, u32[]{:S(2)}) copy-start(f32[192]{0:T(256)} %get-tuple-element.219) | copy-start | bytes 2308
  1375.6 128.4 %copy-start.120 = (f32[192]{0:T(256)S(1)}, f32[192]{0:T(256)}, u32[]{:S(2)}) copy-start(f32[192]{0:T(256)} %pad_maximum_fusion.17) | copy-start | bytes 2308
  1375.6 128.4 %copy-start.122 = (f32[192]{0:T(256)S(1)}, f32[192]{0:T(256)}, u32[]{:S(2)}) copy-start(f32[192]{0:T(256)} %get-tuple-element.220) | copy-start | bytes 2308
  1471.8 39.2 %copy-start.107 = (f32[96]{0:T(128)S(1)}, f32[96]{0:T(128)}, u32[]{:S(2)}) copy-start(f32[96]{0:T(128)} %get-tuple-element.190) | copy-start | bytes 1156
  1471.8 39.2 %copy-start.108 = (f32[96]{0:T(128)S(1)}, f32[96]{0:T(128)}, u32[]{:S(2)}) copy-start(f32[96]{0:T(128)} %get-tuple-element.188) | copy-start | bytes 1156
  1471.8 39.1 %copy-start.165 = (f32[96]{0:T(128)S(1)}, f32[96]{0:T(128)}, u32[]{:S(2)}) copy-start(f32[96]{0:T(128)} %get-tuple-element.187) | copy-start | bytes 1156
  1471.9 39.1 %copy-start.166 = (f32[96]{0:T(128)S(1)}, f32[96]{0:T(128)}, u32[]{:S(2)}) copy-start(f32[96]{0:T(128)} %get-tuple-element.189) | copy-start | bytes 1156
  1487.6 43.3 %copy-start.16 = (f32[16,1,32,192]{2,3,1,0:T(8,128)}, f32[16,1,32,192]{2,3,1,0:T(8,128)S(1)}, u32[]{:S(2)}) copy-start(f32[16,1,32,192]{2,3,1,0:T(8,128)S(1)} %slice.713) | copy-start | bytes 1179652
  1509.8 48.8 %copy-start.92 = (pred[16,256]{1,0:T(8,128)(4,1)S(1)}, pred[16,256]{1,0:T(8,128)(4,1)}, u32[]{:S(2)}) copy-start(pred[16,256]{1,0:T(8,128)(4,1)} %and.83) | copy-start | bytes 12292
  1534.2 60.8 %copy-start.12 = (bf16[16,8,32,96]{3,2,1,0:T(8,128)(2,1)}, bf16[16,8,32,96]{3,2,1,0:T(8,128)(2,1)S(1)}, u32[]{:S(2)}) copy-start(bf16[16,8,32,96]{3,2,1,0:T(8,128)(2,1)S(1)} %copy.67) | copy-start | bytes 2359300
  1665.5 118.9 %copy-start.66 = (bf16[384,96]{1,0:T(8,128)(2,1)S(1)}, bf16[384,96]{1,0:T(8,128)(2,1)}, u32[]{:S(2)}) copy-start(bf16[384,96]{1,0:T(8,128)(2,1)} %reshape.973) | copy-start | bytes 221188
  1665.5 118.9 %copy-start.137 = (f32[96]{0:T(128)S(1)}, f32[96]{0:T(128)}, u32[]{:S(2)}) copy-start(f32[96]{0:T(128)} %get-tuple-element.183) | copy-start | bytes 1156
  1807.1 158.9 %copy-start.20 = (f32[16,8,256]{2,1,0:T(8,128)}, f32[16,8,256]{2,1,0:T(8,128)S(1)}, u32[]{:S(2)}) copy-start(f32[16,8,256]{2,1,0:T(8,128)S(1)} %broadcast_multiply_fusion.19) | copy-start | bytes 393220
  1815.0 151.0 %copy-start.25 = (f32[16,8,256]{2,1,0:T(8,128)}, f32[16,8,256]{2,1,0:T(8,128)S(1)}, u32[]{:S(2)}) copy-start(f32[16,8,256]{2,1,0:T(8,128)S(1)} %fusion.61) | copy-start | bytes 393220
  1834.1 131.9 %copy-start.73 = (f32[16,96]{1,0:T(8,128)}, f32[16,96]{1,0:T(8,128)S(1)}, u32[]{:S(2)}) copy-start(f32[16,96]{1,0:T(8,128)S(1)} %convolution_divide_fusion) | copy-start | bytes 18436
  1842.8 123.2 %copy-start.31 = (f32[16,8,256]{2,1,0:T(8,128)}, f32[16,8,256]{2,1,0:T(8,128)S(1)}, u32[]{:S(2)}) copy-start(f32[16,8,256]{2,1,0:T(8,128)S(1)} %multiply_multiply_fusion.10) | copy-start | bytes 393220
  1852.7 113.3 %copy-start.39 = (f32[16,8,256]{2,1,0:T(8,128)}, f32[16,8,256]{2,1,0:T(8,128)S(1)}, u32[]{:S(2)}) copy-start(f32[16,8,256]{2,1,0:T(8,128)S(1)} %negate_multiply_fusion.4) | copy-start | bytes 393220
  1872.8 44.5 %copy-start.30 = (f32[16,8,256]{2,1,0:T(8,128)S(1)}, f32[16,8,256]{2,1,0:T(8,128)}, u32[]{:S(2)}) copy-start(f32[16,8,256]{2,1,0:T(8,128)} %copy-done.29) | copy-start | bytes 393220
  1872.9 44.5 %copy-start.36 = (f32[16,8,256]{2,1,0:T(8,128)S(1)}, f32[16,8,256]{2,1,0:T(8,128)}, u32[]{:S(2)}) copy-start(f32[16,8,256]{2,1,0:T(8,128)} %copy-done.35) | copy-start | bytes 393220
  1872.9 44.5 %copy-start.101 = (f32[96]{0:T(128)S(1)}, f32[96]{0:T(128)}, u32[]{:S(2)}) copy-start(f32[96]{0:T(128)} %get-tuple-element.185) | copy-start | bytes 1156
  1872.9 44.5 %copy-start.134 = (f32[96]{0:T(128)S(1)}, f32[96]{0:T(128)}, u32[]{:S(2)}) copy-start(f32[96]{0:T(128)} %get-tuple-element.184) | copy-start | bytes 1156
  1934.0 47.9 %slice-start.3 = ((s8[6291456]{0:T(1024)(128)(4,1)}), s8[2097152]{0:T(1024)(128)(4,1)S(1)}, s32[]{:S(2)}) async-start(s8[6291456]{0:T(1024)(128)(4,1)} %bitcast.454), calls=%async_computation.8 | async-start | bytes 4194304
  2049.2 39.7 %copy-start.8 = (bf16[16,8,12,8,256]{4,3,1,2,0:T(8,128)(2,1)S(1)}, bf16[16,8,12,8,256]{4,3,1,2,0:T(8,128)(2,1)}, u32[]{:S(2)}) copy-start(bf16[16,8,12,8,256]{4,3,1,2,0:T(8,128)(2,1)} %copy.138) | copy-start | bytes 18874372
  2246.0 78.4 %copy-start.57 = (bf16[16,256,96]{1,2,0:T(8,128)(2,1)S(1)}, bf16[16,256,96]{1,2,0:T(8,128)(2,1)}, u32[]{:S(2)}) copy-start(bf16[16,256,96]{1,2,0:T(8,128)(2,1)} %fusion.36) | copy-start | bytes 2359300
  2326.1 167.9 %reduce-scatter.5.cloned.1.call-start = ((), (), s32[]{:S(2)}) async-start(), calls=%async_computation.3 | async-start | bytes 1179648 | tf_op jit(solution)/shard_map/reduce_scatter | solution.py:373
  2326.2 65.6 %copy-start.63 = (f32[16,1000]{1,0:T(8,128)S(1)}, f32[16,1000]{1,0:T(8,128)}, u32[]{:S(2)}) copy-start(f32[16,1000]{1,0:T(8,128)} %copy-done.62) | copy-start | bytes 192004
  2326.2 65.6 %copy-start.87 = (f32[16,96]{1,0:T(8,128)S(1)}, f32[16,96]{1,0:T(8,128)}, u32[]{:S(2)}) copy-start(f32[16,96]{1,0:T(8,128)} %copy-done.86) | copy-start | bytes 18436
  2326.2 65.6 %copy-start.128 = (f32[16]{0:T(128)S(1)}, f32[16]{0:T(128)}, u32[]{:S(2)}) copy-start(f32[16]{0:T(128)} %get-tuple-element.196) | copy-start | bytes 196
  2381.1 78.9 %collective-permute-start.3 = (bf16[16,1,256,96]{2,3,1,0:T(8,128)(2,1)S(1)}, bf16[16,1,256,96]{2,3,1,0:T(8,128)(2,1)}, u32[]{:S(2)}, u32[]{:S(2)}) collective-permute-start(bf16[16,1,256,96]{2,3,1,0:T(8,128)(2,1)S(1)} %get-tuple-element.136), channel_id=1, source_target_pairs={{0,1},{1,2},{2,3},{3,4},{4,5},{5,6},{6,7},{8,9},{9,10},{10,11},{11... | collective-permute-start | bytes 2359304 | tf_op jit(solution)/shard_map/ppermute | solution.py:34
  2383.3 76.6 %collective-permute-start.4 = (bf16[16,1,256,96]{2,3,1,0:T(8,128)(2,1)S(1)}, bf16[16,1,256,96]{2,3,1,0:T(8,128)(2,1)}, u32[]{:S(2)}, u32[]{:S(2)}) collective-permute-start(bf16[16,1,256,96]{2,3,1,0:T(8,128)(2,1)S(1)} %get-tuple-element.137), channel_id=1, source_target_pairs={{1,0},{2,1},{3,2},{4,3},{5,4},{6,5},{7,6},{9,8},{10,9},{11,10},{12... | collective-permute-start | bytes 2359304 | tf_op jit(solution)/shard_map/ppermute | solution.py:35
  2458.5 541.2 %all-reduce.59.cloned.1.call-start = ((), (), s32[]{:S(2)}) async-start(), calls=%async_computation.4 | async-start | bytes 2293760
  2515.6 43.0 %copy-start.23 = (f32[16,1,32,192]{2,3,1,0:T(8,128)S(1)}, f32[16,1,32,192]{2,3,1,0:T(8,128)}, u32[]{:S(2)}) copy-start(f32[16,1,32,192]{2,3,1,0:T(8,128)} %get-tuple-element.138) | copy-start | bytes 1179652
  2619.3 42.6 %copy-start.22 = (f32[16,1,32,192]{2,3,1,0:T(8,128)S(1)}, f32[16,1,32,192]{2,3,1,0:T(8,128)}, u32[]{:S(2)}) copy-start(f32[16,1,32,192]{2,3,1,0:T(8,128)} %get-tuple-element.139) | copy-start | bytes 1179652
  2745.3 9.7 collective-permute-start.5
  2796.9 39.7 %slice-start.5 = ((s8[9961472]{0:T(1024)(128)(4,1)}), s8[4194304]{0:T(1024)(128)(4,1)S(1)}, s32[]{:S(2)}) async-start(s8[9961472]{0:T(1024)(128)(4,1)} %bitcast.456), calls=%async_computation.10 | async-start | bytes 8388608
  2836.8 214.6 %copy-start.78 = (f32[8960]{0:T(1024)S(1)}, f32[8960]{0:T(1024)}, u32[]{:S(2)}) copy-start(f32[8960]{0:T(1024)} %param.17) | copy-start | bytes 107524
  2836.8 214.6 %copy-start.90 = (f32[8960]{0:T(1024)S(1)}, f32[8960]{0:T(1024)}, u32[]{:S(2)}) copy-start(f32[8960]{0:T(1024)} %param.18) | copy-start | bytes 107524
  2836.8 214.6 %copy-start.91 = (f32[8960]{0:T(1024)S(1)}, f32[8960]{0:T(1024)}, u32[]{:S(2)}) copy-start(f32[8960]{0:T(1024)} %param.19) | copy-start | bytes 107524
  (129 other events, 2040.0 us)
Sparse Core Ops, SparseCore 0:
  2326.3 32.5 reduce-scatter.2
  2458.6 35.3 reduce-scatter.4
  2856.6 143.1 all-reduce.58
where the time goes:
time: 3120 us; the launch traced here: 3060 us
  local copies, waits for them, and re-layouts  1610 us (52%)
  other arithmetic  685 us (22%)
  matrix products  431 us (14%)
  waiting for transfers between devices  157 us (5%)
  blocking collectives  149 us (5%)
    slice x49, local copies, waits for them, and re-layouts, body(): pix_piece = framed[:, :, tap_row, :, tap_col:tap_col + pix_cols:4]  778 us
    pad x9, local copies, waits for them, and re-layouts, tap_sum(): framed[:, offset:offset + 1, tap_col:tap_col + ROWS * (key_cols - 1) + 1:...  185 us
    concatenate x1, local copies, waits for them, and re-layouts, body(): patches = jnp.concatenate(columns, axis=-1)  174 us
    slice x9, local copies, waits for them, and re-layouts, tap_sum(): framed[:, offset:offset + 1, tap_col:tap_col + ROWS * (key_cols - 1) + 1:...  145 us
    unnamed x4, waiting for transfers between devices  142 us
    convert_element_type x1, other arithmetic, body(): activated_r = activated.astype(jnp.bfloat16)  119 us
    add x4, local copies, waits for them, and re-layouts, attend(): scores.reshape(batch_imgs, rows_local, cols_local, key_rows, key_cols)  95 us
    reduce_sum x1, other arithmetic, pool_query(): framed[:, tap_row:tap_row + rows_out, tap_col:tap_col + cols_out]  78.3 us
  transfers between devices with their start and end apart: 9, of which 2 were waited for; matrix products, arithmetic and copies ran while one was open for 14% of the time, Pallas kernels for 0%

commit v1 on v0

v1 whole, which is shorter than its diff:
```python
import functools

import jax
import jax.numpy as jnp
import numpy as np
from jax import lax
from jax.experimental import pallas as pl
from jax.experimental.pallas import tpu as pltpu
from jax.sharding import PartitionSpec as P

DIM = 96
MLP = 384
CLASSES = 1000
PATCH = 7
ROWS = 8
STEP = 7
CANVAS_W = 256

HIGHEST_PREC = lax.Precision.HIGHEST
CLIP_NORM = 0.02
LEARN_RATE = 0.05
WEIGHT_DECAY = 0.05
BETA_FIRST = 0.5
BETA_SECOND = 0.5
ADAM_EPS = 1e-08
NORM_EPS = 1e-06
NEG_FILL = -1e30

F32 = jnp.float32
BF16 = jnp.bfloat16
SCALE = DIM ** (-0.5)
EXP2_SCALE = SCALE * 1.4426950408889634

TOKENS = ROWS * CANVAS_W
PAIR = 512
PAIRS = TOKENS // PAIR
TILES = CANVAS_W // 32
PADDED = TOKENS + 512
WIN = 40
PATCH_ROWS = 224
VMEM_BYTES = 56 * 1024 * 1024


def deinterleave_matrix():
    out = np.zeros((4, 128, 4, 4, 32), np.float32)
    for row in range(4):
        for phase in range(4):
            for col in range(32):
                out[row, 4 * col + phase, phase, row, col] = 1.0
    return out.reshape(512, 512)


def tap_matrix():
    out = np.zeros((CANVAS_W, 128), np.float32)
    for tap in range(3):
        for key in range(32):
            col = 8 * key + tap - 1
            if col >= 0:
                out[col, tap * 32 + key] = 1.0
    return out


def dot(a, b):
    return jnp.dot(a, b, preferred_element_type=F32)


def dot_nt(a, b):
    return lax.dot_general(a, b, (((1,), (1,)), ((), ())), preferred_element_type=F32)


def normalized(x):
    mean = jnp.sum(x, axis=0, keepdims=True) * (1.0 / DIM)
    centered = x - mean
    var = jnp.sum(centered * centered, axis=0, keepdims=True) * (1.0 / DIM)
    rstd = lax.rsqrt(var + NORM_EPS)
    return centered * rstd, rstd


def norm_back(grad, hat, rstd, gain):
    inner = grad * gain
    mean_one = jnp.sum(inner, axis=0, keepdims=True) * (1.0 / DIM)
    mean_two = jnp.sum(inner * hat, axis=0, keepdims=True) * (1.0 / DIM)
    return rstd * (inner - mean_one - hat * mean_two)


def fold_lanes(x):
    total = x[:, 0:128]
    for k in range(1, x.shape[1] // 128):
        total = total + x[:, 128 * k : 128 * k + 128]
    return total


def column(vec_ref, index):
    place = index + 27 if index < 15 else index - 15 if index < 42 else index
    return vec_ref[:, place : place + 1]


def lane_ids(width, rows=1):
    return lax.broadcasted_iota(jnp.int32, (rows, width), 1)


def pair_mask(pair, breadth, row_ok):
    lane = lane_ids(PAIR)
    col = pair * 64 + (lane >> 8) * 32 + (lane & 31)
    return jnp.where((col < breadth) & row_ok, 1.0, 0.0).astype(F32)


def pair_lanes(pair, base=0):
    return pl.ds(pl.multiple_of(pair * PAIR + base, 128), PAIR)


def pair_count(breadth):
    return jnp.minimum((breadth >> 6) + 1, PAIRS)


def col_shifts(window, base):
    lane = lane_ids(128, DIM)
    here = window[:, base : base + 128]
    before = window[:, base - 256 : base - 128]
    after = window[:, base + 256 : base + 384]
    left = jnp.where((lane & 31) == 0, pltpu.roll(before, 97, 1), pltpu.roll(here, 1, 1))
    right = jnp.where((lane & 31) == 31, pltpu.roll(after, 31, 1), pltpu.roll(here, 127, 1))
    return left, here, right


def rows_down(first, second, entering):
    lane = lane_ids(128, DIM)
    a, b = pltpu.roll(first, 32, 1), pltpu.roll(second, 32, 1)
    return jnp.where(lane < 32, entering, a), jnp.where(lane < 32, a, b), b


def rows_up(first, second, entering):
    lane = lane_ids(128, DIM)
    a, b = pltpu.roll(first, 96, 1), pltpu.roll(second, 96, 1)
    return jnp.where(lane >= 96, b, a), jnp.where(lane >= 96, entering, b), a


def spread_halo(dst_ref, halo, target):
    for tile in range(TILES):
        block = halo[:, 128 * (tile // 4) : 128 * (tile // 4) + 128]
        shift = (target - 32 * (tile % 4)) % 128
        dst_ref[:, 128 * tile : 128 * tile + 128] = pltpu.roll(block, shift, 1) if shift else block


def gather_halo(src_ref, target):
    lane = lane_ids(128, DIM)
    blocks = []
    for half in range(2):
        total = None
        for k in range(4):
            tile = 4 * half + k
            block = src_ref[:, 128 * tile : 128 * tile + 128]
            shift = (32 * k - target) % 128
            block = pltpu.roll(block, shift, 1) if shift else block
            total = block if total is None else jnp.where((lane >> 5) == k, block, total)
        blocks.append(total)
    return jnp.concatenate(blocks, axis=1)


def reverse_bits(value, count):
    result = 0
    for bit in range(count.bit_length() - 1):
        result = result * 2 + ((value >> bit) & 1)
    return result


def key_tables(kv_ref, row_index, key_rows, height, breadth, ka_ref, kn_ref):
    keys = [None] * key_rows
    for i in range(key_rows):
        slot = reverse_bits(jnp.bitwise_xor(row_index, i), key_rows)
        keys[i] = kv_ref[slot, 0].astype(F32)
    both = jnp.concatenate(keys, axis=1)
    total = key_rows * 32
    more = aug_rows(key_rows)
    rank = lax.broadcasted_iota(jnp.int32, (more, total), 0)
    key = lax.broadcasted_iota(jnp.int32, (more, total), 1)
    key_r, key_c = key >> 5, key & 31
    half = key_rows + 32
    low = rank >= half
    rank_in = jnp.where(low, rank - half, rank)
    hit = rank_in == jnp.where(rank_in < key_rows, key_r, key_c + key_rows)
    invalid = (key_r * ROWS >= height) | (key_c * ROWS >= breadth)
    table = jnp.where(rank < 2 * half, jnp.where(hit, 1.0, 0.0), 0.0)
    table = jnp.where((rank == 2 * half) & invalid, NEG_FILL, table)
    full = jnp.concatenate([both[:DIM], table, jnp.zeros((256 - DIM - more, total), F32)], axis=0)
    ka_ref[...] = full[: DIM + more].astype(BF16)
    kn_ref[...] = jnp.transpose(full).astype(BF16)
    return both[DIM:]


def aug_rows(key_rows):
    return 2 * key_rows + 64 + 16


def embed_kernel(ext_ref, row_ref, pix_ref, tail_ref, perm_ref, tap_ref, wp_ref, wqkv_ref, vec_ref, bkv_ref, kexp_ref,
                 patch_ref, x0_ref, q_ref, first_ref, last_ref, nsel_ref, kvt_ref, below_ref, own_ref, s_ref, n_ref, *, offset):
    image = pl.program_id(0)
    height = ext_ref[offset + image, 0]
    breadth = ext_ref[offset + image, 1]
    row_ok = row_ref[0] * ROWS < height

    @pl.when(image == 0)
    def _():
        s_ref[...] = jnp.zeros_like(s_ref)

    for r in range(ROWS):
        for a in range(4):
            s_ref[16 * r + 4 * a : 16 * r + 4 * a + 3, :] = pix_ref[0, r, a].astype(F32)
    for a in range(3):
        s_ref[128 + 4 * a : 128 + 4 * a + 3, :] = tail_ref[0, 0, a].astype(F32)
    lane = lane_ids(1024, 144)
    for shifted in range(2):
        rows = s_ref[...]
        if shifted:
            rows = jnp.where(lane < 4, 0.0, pltpu.roll(rows, 4, 1))
        rows = rows.astype(BF16)
        stack = []
        for start in (0, 4, 1, 5):
            for tile in range(TILES):
                stack.append(jnp.concatenate(
                    [rows[16 * (start + k) : 16 * (start + k) + 16, 128 * tile : 128 * tile + 128] for k in range(4)], axis=1))
        out = dot(jnp.concatenate(stack, axis=0), perm_ref[...]).astype(BF16)
        for which, start in enumerate((0, 4, 1, 5)):
            half, side = which // 2, which % 2
            for tile in range(TILES):
                block = out[128 * which + 16 * tile : 128 * which + 16 * tile + 16]
                for phase in range(shifted, 4):
                    top = 64 * half + 16 * phase if not shifted else 128 + 48 * half + 16 * (phase - 1)
                    patch_ref[0, top : top + 16, 256 * tile + 128 * side : 256 * tile + 128 * side + 128] = block[
                        :, 128 * phase : 128 * phase + 128]

    count = pair_count(breadth)

    def active(pair, carry):
        lanes = pair_lanes(pair)
        x0 = (dot(wp_ref[...], patch_ref[0, :, lanes]) + column(vec_ref, 0)) * pair_mask(pair, breadth, row_ok)
        x0_ref[0, :, lanes] = x0
        hat, _ = normalized(x0)
        normed = (hat * column(vec_ref, 1) + column(vec_ref, 2)).astype(BF16)
        n_ref[:, lanes] = normed.astype(F32)
        q_ref[0, :, pair_lanes(pair, 256)] = (dot(wqkv_ref[0:DIM, :], normed) + column(vec_ref, 42)).astype(BF16)
        return carry

    def idle(pair, carry):
        n_ref[:, pair_lanes(pair)] = jnp.zeros((DIM, PAIR), F32)
        q_ref[0, :, pair_lanes(pair, 256)] = jnp.zeros((DIM, PAIR), BF16)
        return carry

    lax.fori_loop(0, count, active, 0)
    lax.fori_loop(count, PAIRS, idle, 0)
    q_ref[0, :, 0:256] = jnp.zeros((DIM, 256), BF16)
    q_ref[0, :, 256 + TOKENS : 512 + TOKENS] = jnp.zeros((DIM, 256), BF16)

    rows = []
    for start in (224, 0, 32):
        rows.append(jnp.concatenate([n_ref[:, 256 * t + start : 256 * t + start + 32] for t in range(TILES)], axis=1).astype(BF16))
    last_ref[0] = (dot(wqkv_ref[0:DIM, :], rows[0]) + column(vec_ref, 42)).astype(BF16)
    first_ref[0] = (dot(wqkv_ref[0:DIM, :], rows[1]) + column(vec_ref, 42)).astype(BF16)
    nsel = jnp.concatenate([dot(row, tap_ref[...]) for row in rows], axis=1).astype(BF16)
    nsel_ref[0] = nsel
    taps = (dot(wqkv_ref[DIM : 3 * DIM, :], nsel) + bkv_ref[...]).astype(BF16)
    kvt_ref[0] = taps
    product = taps.astype(F32) * kexp_ref[...]
    sums = []
    for k in range(3):
        part = product[:, 128 * k : 128 * k + 128]
        sums.append((part + pltpu.roll(part, 96, 1) + pltpu.roll(part, 64, 1))[:, 0:32])
    below_ref[0] = sums[0]
    own_ref[0] = sums[1] + sums[2]


def call_embed(ext, row, pixels, consts, wts, images, offset):
    whole = lambda *shape: pl.BlockSpec(shape, lambda i, *_: (0,) * len(shape))
    per = lambda *shape: pl.BlockSpec((1,) + shape, lambda i, *_: (i,) + (0,) * len(shape))
    shapes = [
        ((PATCH_ROWS, TOKENS), BF16), ((DIM, TOKENS), F32), ((DIM, PADDED), BF16), ((DIM, CANVAS_W), BF16),
        ((DIM, CANVAS_W), BF16), ((DIM, 384), BF16), ((2 * DIM, 384), BF16), ((2 * DIM, 32), F32), ((2 * DIM, 32), F32)]
    return pl.pallas_call(
        functools.partial(embed_kernel, offset=offset),
        grid_spec=pltpu.PrefetchScalarGridSpec(
            num_scalar_prefetch=2, grid=(images,),
            in_specs=[
                pl.BlockSpec((1, ROWS, 4, 3, 1024), lambda i, *_: (i + offset, 0, 0, 0, 0)),
                pl.BlockSpec((1, 1, 4, 3, 1024), lambda i, *_: (i + offset, ROWS - 1, 1, 0, 0)),
                whole(512, 512), whole(CANVAS_W, 128), whole(DIM, PATCH_ROWS), whole(3 * DIM, DIM), whole(DIM, 64),
                whole(2 * DIM, 1), whole(2 * DIM, 384)],
            out_specs=[per(*s) for s, _ in shapes],
            scratch_shapes=[pltpu.VMEM((144, 1024), F32), pltpu.VMEM((DIM, TOKENS), F32)]),
        out_shape=[jax.ShapeDtypeStruct((images,) + s, t) for s, t in shapes],
        compiler_params=pltpu.CompilerParams(vmem_limit_bytes=VMEM_BYTES),
        cost_estimate=pl.CostEstimate(flops=images * 2_000_000_000, bytes_accessed=images * 4_000_000, transcendentals=0),
        name="embed",
    )(ext, row, pixels, pixels, consts["perm"], consts["tap"], wts["wp"], wts["wqkv_t"], wts["vec"], wts["b_kv"], wts["kexp"])


def pool_norm_kernel(own_ref, got_ref, vec_ref, kv_ref):
    for member in range(2):
        part = slice(member * DIM, member * DIM + DIM)
        for image in range(own_ref.shape[0]):
            hat, _ = normalized(own_ref[image, part] + got_ref[image, part])
            kv_ref[image, part] = (hat * column(vec_ref, 5 + 2 * member) + column(vec_ref, 6 + 2 * member)).astype(BF16)


def call_pool_norm(own, got, vec):
    return pl.pallas_call(
        pool_norm_kernel, out_shape=jax.ShapeDtypeStruct(own.shape, BF16), name="pool_norm",
        cost_estimate=pl.CostEstimate(flops=own.size * 10, bytes_accessed=own.size * 10, transcendentals=0))(own, got, vec)


def pool_back_kernel(own_ref, got_ref, grad_ref, vec_ref, pre_ref, sums_ref):
    for member in range(2):
        part = slice(member * DIM, member * DIM + DIM)
        gain = jnp.zeros((DIM, 32), F32)
        shift = jnp.zeros((DIM, 32), F32)
        for image in range(own_ref.shape[0]):
            hat, rstd = normalized(own_ref[image, part] + got_ref[image, part])
            grad = grad_ref[image, part]
            gain = gain + grad * hat
            shift = shift + grad
            pre_ref[image, part] = norm_back(grad, hat, rstd, column(vec_ref, 5 + 2 * member))
        sums_ref[2 * member] = gain
        sums_ref[2 * member + 1] = shift


def call_pool_back(own, got, grad, vec):
    return pl.pallas_call(
        pool_back_kernel,
        out_shape=[jax.ShapeDtypeStruct(own.shape, F32), jax.ShapeDtypeStruct((4, DIM, 32), F32)], name="pool_back",
        cost_estimate=pl.CostEstimate(flops=own.size * 20, bytes_accessed=own.size * 16, transcendentals=0))(own, got, grad, vec)


def lane_bit(lane, bit):
    return (lane & bit) != 0


def relative_terms(products, key_rows):
    lane = lane_ids(PAIR, WIN)
    parts = [products[WIN * s : WIN * s + WIN] for s in range(8)]
    for bit in (1, 2, 4):
        chosen = lane_bit(lane, bit)
        parts = [jnp.where(chosen, parts[2 * k + 1], parts[2 * k]) for k in range(len(parts) // 2)]
    by_col = parts[0]
    for bit, step in ((8, 1), (16, 2), (256, 4)):
        by_col = jnp.where(lane_bit(lane, bit), by_col, pltpu.roll(by_col, WIN - step, 0))
    lane = lane_ids(PAIR, key_rows)
    rows = products[8 * WIN :]
    parts = [rows[key_rows * r : key_rows * r + key_rows] for r in range(8)]
    for bit in (32, 64, 128):
        chosen = lane_bit(lane, bit)
        parts = [jnp.where(chosen, parts[2 * k + 1], parts[2 * k]) for k in range(len(parts) // 2)]
    return jnp.concatenate([parts[0], by_col[0:32]], axis=0)


def relative_spread(grad_terms, key_rows):
    lane = lane_ids(PAIR, WIN)
    by_row = grad_terms[:key_rows]
    by_col = jnp.concatenate([grad_terms[key_rows:], jnp.zeros((WIN - 32, grad_terms.shape[1]), F32)], axis=0)
    for bit, step in ((8, 1), (16, 2), (256, 4)):
        by_col = jnp.where(lane_bit(lane, bit), by_col, pltpu.roll(by_col, step, 0))
    parts = [jnp.where((lane & 7) == s, by_col, 0.0) for s in range(8)]
    lane = lane_ids(PAIR, key_rows)
    parts += [jnp.where(((lane >> 5) & 7) == r, by_row, 0.0) for r in range(8)]
    return jnp.concatenate(parts, axis=0).astype(BF16)


def mlp_forward(x1, vec_ref, w1t_ref, b1_ref, w2t_ref):
    hat_two, rstd_two = normalized(x1)
    normed = (hat_two * column(vec_ref, 10) + column(vec_ref, 11)).astype(BF16)
    hidden = dot(w1t_ref[...], normed) + b1_ref[...]
    cumulative = 0.5 + 0.5 * lax.erf(hidden * 0.7071067811865476)
    act = (hidden * cumulative).astype(BF16)
    x2 = x1 + (dot(w2t_ref[...], act) + column(vec_ref, 12))
    return hat_two, rstd_two, normed, hidden, cumulative, act, x2


def forward_kernel(ext_ref, row_ref, q_ref, top_ref, bot_ref, x0_ref, kv_ref, vec_ref, rw_ref, wprojt_ref, w1t_ref, b1_ref, w2t_ref,
                   hat_ref, terms_ref, att_ref, stat_ref, pool_ref, ka_ref, kn_ref, v_ref, ztop_ref, zbot_ref, *, offset, key_rows):
    image = pl.program_id(0)
    height = ext_ref[offset + image, 0]
    breadth = ext_ref[offset + image, 1]
    row_ok = row_ref[0] * ROWS < height
    depth = DIM + aug_rows(key_rows)
    values = key_tables(kv_ref, row_ref[0], key_rows, height, breadth, ka_ref, kn_ref)
    v_ref[...] = values.astype(BF16)
    lane = lane_ids(CANVAS_W, DIM)
    for halo_ref, dst_ref, tap_row, target in ((top_ref, ztop_ref, 0, 0), (bot_ref, zbot_ref, 2, 96)):
        halo = halo_ref[0].astype(F32)
        left = jnp.where(lane == 0, 0.0, pltpu.roll(halo, 1, 1))
        right = jnp.where(lane == CANVAS_W - 1, 0.0, pltpu.roll(halo, CANVAS_W - 1, 1))
        taps = [column(vec_ref, 15 + 3 * tap_row + k) for k in range(3)]
        spread_halo(dst_ref, taps[0] * left + taps[1] * halo + taps[2] * right, target)
    pool_ref[...] = jnp.zeros_like(pool_ref)

    def step(pair, carry):
        lanes = pair_lanes(pair)
        window = q_ref[0, :, pl.ds(pl.multiple_of(pair * PAIR, 128), PAIR + 512)].astype(F32)
        pre = []
        for tile in range(2):
            sums = []
            for side in range(2):
                shifts = col_shifts(window, 256 + 256 * tile + 128 * side)
                sums.append([sum(column(vec_ref, 15 + 3 * r + c) * shifts[c] for c in range(3)) for r in range(3)])
            halo = pl.ds(pl.multiple_of((2 * pair + tile) * 128, 128), 128)
            down = rows_down(sums[0][0], sums[1][0], ztop_ref[:, halo])
            up = rows_up(sums[0][2], sums[1][2], zbot_ref[:, halo])
            pre += [sums[side][1] + down[side] + up[side] for side in range(2)]
        hat, rstd = normalized(jnp.concatenate(pre, axis=1))
        hat_ref[0, :, lanes] = hat
        query = (hat * column(vec_ref, 3) + column(vec_ref, 4)).astype(BF16)
        terms = relative_terms(dot(rw_ref[pair], query), key_rows) * (DIM**0.5)
        high = terms.astype(BF16).astype(F32)
        extra = jnp.concatenate([high, terms - high, jnp.ones((16, PAIR), F32)], axis=0).astype(BF16)
        terms_ref[0, :, lanes] = extra
        scores = dot(kn_ref[:, :depth], jnp.concatenate([query, extra], axis=0))
        peak = jnp.max(scores, axis=0, keepdims=True)
        weights = jnp.exp2((scores - peak) * EXP2_SCALE)
        total = jnp.sum(weights, axis=0, keepdims=True)
        probs = (weights * (1.0 / total)).astype(BF16)
        stat_ref[0, 0:1, lanes] = peak
        stat_ref[0, 1:2, lanes] = 1.0 / total
        stat_ref[0, 2:3, lanes] = rstd
        attended = (dot(v_ref[...], probs) + query.astype(F32)).astype(BF16)
        att_ref[0, :, lanes] = attended
        x1 = x0_ref[0, :, lanes] + (dot(wprojt_ref[...], attended) + column(vec_ref, 9))
        x2 = mlp_forward(x1, vec_ref, w1t_ref, b1_ref, w2t_ref)[-1]
        hat_three, _ = normalized(x2)
        pool_ref[0] += fold_lanes(hat_three * pair_mask(pair, breadth, row_ok))
        return carry

    lax.fori_loop(0, pair_count(breadth), step, 0)


def specs():
    whole = lambda *shape: pl.BlockSpec(shape, lambda i, *_: (0,) * len(shape))
    per = lambda *shape: pl.BlockSpec((1,) + shape, lambda i, *_: (i,) + (0,) * len(shape))
    return whole, per


def call_forward(ext, row, q, top, bot, x0, kv, wts, offset):
    whole, per = specs()
    images, key_rows = q.shape[0], kv.shape[0]
    more = aug_rows(key_rows)
    shapes = [((DIM, TOKENS), F32), ((more, TOKENS), BF16), ((DIM, TOKENS), BF16), ((8, TOKENS), F32), ((DIM, 128), F32)]
    keys = key_rows * 32
    return pl.pallas_call(
        functools.partial(forward_kernel, offset=offset, key_rows=key_rows),
        grid_spec=pltpu.PrefetchScalarGridSpec(
            num_scalar_prefetch=2, grid=(images,),
            in_specs=[
                per(DIM, PADDED), per(DIM, CANVAS_W), per(DIM, CANVAS_W), per(DIM, TOKENS),
                pl.BlockSpec((key_rows, 1, 2 * DIM, 32), lambda i, *_: (0, i, 0, 0)),
                whole(DIM, 64), whole(PAIRS, 8 * WIN + 8 * key_rows, DIM), whole(DIM, DIM), whole(MLP, DIM), whole(MLP, 1),
                whole(DIM, MLP)],
            out_specs=[per(*s) for s, _ in shapes],
            scratch_shapes=[
                pltpu.VMEM((DIM + more, keys), BF16), pltpu.VMEM((keys, 256), BF16), pltpu.VMEM((DIM, keys), BF16),
                pltpu.VMEM((DIM, 1024), F32), pltpu.VMEM((DIM, 1024), F32)]),
        out_shape=[jax.ShapeDtypeStruct((images,) + s, t) for s, t in shapes],
        compiler_params=pltpu.CompilerParams(vmem_limit_bytes=VMEM_BYTES),
        cost_estimate=pl.CostEstimate(flops=images * 5_000_000_000, bytes_accessed=images * 4_000_000, transcendentals=0),
        name="forward",
    )(ext, row, q, top, bot, x0, kv, wts["vec"], wts["rw"], wts["wproj_t"], wts["w1_t"], wts["b1"], wts["w2_t"])


def backward_kernel(ext_ref, row_ref, hat_ref, terms_ref, att_ref, stat_ref, x0_ref, q_ref, top_ref, bot_ref, kv_ref, gvec_ref, vec_ref,
                    rwt_ref, wprojt_ref, wproj_ref, w1t_ref, w1_ref, b1_ref, w2t_ref, w2_ref,
                    dx1_ref, dq_ref, up_ref, down_ref, dkv_ref, a2_ref, a1_ref, ap_ref, av_ref, ak_ref, ar_ref,
                    ka_ref, kn_ref, vn_ref, dp_ref, qtop_ref, qbot_ref, ru_ref, rd_ref, dk_ref, dv_ref, *, offset, key_rows):
    image = pl.program_id(0)
    height = ext_ref[offset + image, 0]
    breadth = ext_ref[offset + image, 1]
    row_ok = row_ref[0] * ROWS < height
    depth = DIM + aug_rows(key_rows)
    count = pair_count(breadth)

    @pl.when(image == 0)
    def _():
        for ref in (a2_ref, a1_ref, ap_ref, av_ref, ak_ref, ar_ref, ru_ref, rd_ref):
            ref[...] = jnp.zeros_like(ref)

    values = key_tables(kv_ref, row_ref[0], key_rows, height, breadth, ka_ref, kn_ref)
    padded_values = jnp.concatenate([values, jnp.zeros((128 - DIM, values.shape[1]), F32)], axis=0)
    vn_ref[...] = jnp.transpose(padded_values).astype(BF16)
    spread_halo(qtop_ref, top_ref[0].astype(F32), 0)
    spread_halo(qbot_ref, bot_ref[0].astype(F32), 96)
    dk_ref[...] = jnp.zeros_like(dk_ref)
    dv_ref[...] = jnp.zeros_like(dv_ref)
    dp_ref[...] = jnp.zeros_like(dp_ref)

    def step(pair, carry):
        lanes = pair_lanes(pair)
        ones = jnp.ones((16, PAIR), BF16)
        attended = att_ref[0, :, lanes]
        x1 = x0_ref[0, :, lanes] + (dot(wprojt_ref[...], attended) + column(vec_ref, 9))
        hat_two, rstd_two, normed, hidden, cumulative, act, x2 = mlp_forward(x1, vec_ref, w1t_ref, b1_ref, w2t_ref)
        hat_three, rstd_three = normalized(x2)
        grad_x2 = norm_back(gvec_ref[0] * pair_mask(pair, breadth, row_ok), hat_three, rstd_three, column(vec_ref, 13))
        grad_mlp = grad_x2.astype(BF16)
        a2_ref[...] += dot_nt(grad_mlp, jnp.concatenate([act, ones], axis=0))
        slope = cumulative + hidden * (jnp.exp(hidden * hidden * -0.5) * 0.3989422804014327)
        grad_hidden = (dot(w2_ref[...], grad_mlp) * slope).astype(BF16)
        a1_ref[...] += dot_nt(jnp.concatenate([normed, ones], axis=0), grad_hidden)
        grad_normed = dot(w1_ref[...], grad_hidden)
        av_ref[0] += fold_lanes(grad_normed * hat_two)
        av_ref[1] += fold_lanes(grad_normed)
        grad_x1 = grad_x2 + norm_back(grad_normed, hat_two, rstd_two, column(vec_ref, 10))
        dx1_ref[0, :, lanes] = grad_x1
        grad_proj = grad_x1.astype(BF16)
        ap_ref[...] += dot_nt(jnp.concatenate([attended, ones], axis=0), grad_proj)
        grad_att = dot(wproj_ref[...], grad_proj)
        grad_att_low = grad_att.astype(BF16)
        hat = hat_ref[0, :, lanes]
        query = (hat * column(vec_ref, 3) + column(vec_ref, 4)).astype(BF16)
        scores = dot(kn_ref[:, :depth], jnp.concatenate([query, terms_ref[0, :, lanes]], axis=0))
        probs = jnp.exp2((scores - stat_ref[0, 0:1, lanes]) * EXP2_SCALE) * stat_ref[0, 1:2, lanes]
        dv_ref[...] += dot_nt(grad_att_low, probs.astype(BF16))
        grad_probs = dot(vn_ref[:, :DIM], grad_att_low)
        inner = jnp.sum(probs * grad_probs, axis=0, keepdims=True)
        grad_scores = (probs * (grad_probs - inner)).astype(BF16)
        dk_ref[...] += dot_nt(query, grad_scores)
        back = dot(ka_ref[: DIM + key_rows + 32, :], grad_scores)
        spread = relative_spread(back[DIM:], key_rows)
        ar_ref[pair] += dot_nt(query, spread)
        grad_query = grad_att + back[:DIM] * SCALE + dot(rwt_ref[pair], spread)
        av_ref[2] += fold_lanes(grad_query * hat)
        av_ref[3] += fold_lanes(grad_query)
        dp_ref[:, pair_lanes(pair, 256)] = norm_back(grad_query, hat, stat_ref[0, 2:3, lanes], column(vec_ref, 3))
        return carry

    lax.fori_loop(0, count, step, 0)
    for i in range(key_rows):
        slot = reverse_bits(jnp.bitwise_xor(row_ref[0], i), key_rows)
        dkv_ref[slot, 0, 0:DIM, :] = dk_ref[:, 32 * i : 32 * i + 32] * SCALE
        dkv_ref[slot, 0, DIM : 2 * DIM, :] = dv_ref[:, 32 * i : 32 * i + 32]

    def pool_step(pair, carry):
        window = dp_ref[:, pl.ds(pl.multiple_of(pair * PAIR, 128), PAIR + 512)]
        for tile in range(2):
            base = pair * PAIR + 256 * tile
            halo = pl.ds(pl.multiple_of((2 * pair + tile) * 128, 128), 128)
            query = [q_ref[0, :, pl.ds(pl.multiple_of(base + 256 + 128 * side, 128), 128)].astype(F32) for side in range(2)]
            above = rows_down(query[0], query[1], qtop_ref[:, halo])
            under = rows_up(query[0], query[1], qbot_ref[:, halo])
            sums = []
            for side in range(2):
                left, here, right = col_shifts(window, 256 + 256 * tile + 128 * side)
                shifts = (right, here, left)
                sums.append([sum(column(vec_ref, 15 + 3 * r + c) * shifts[c] for c in range(3)) for r in range(3)])
                for r, rows in enumerate((above[side], query[side], under[side])):
                    for c in range(3):
                        ak_ref[3 * r + c] += shifts[c] * rows
            zero = jnp.zeros((DIM, 128), F32)
            up = rows_up(sums[0][0], sums[1][0], zero)
            down = rows_down(sums[0][2], sums[1][2], zero)
            for side in range(2):
                dq_ref[0, :, pl.ds(pl.multiple_of(base + 128 * side, 128), 128)] = sums[side][1] + up[side] + down[side]
            ru_ref[:, halo] = up[2]
            rd_ref[:, halo] = down[2]
        return carry

    def pool_idle(pair, carry):
        for ref in (ru_ref, rd_ref):
            ref[:, pl.ds(pl.multiple_of(pair * 256, 128), 256)] = jnp.zeros((DIM, 256), F32)
        return carry

    lax.fori_loop(0, count, pool_step, 0)
    lax.fori_loop(count, PAIRS, pool_idle, 0)
    up_ref[0] = gather_halo(ru_ref, 96).astype(BF16)
    down_ref[0] = gather_halo(rd_ref, 0).astype(BF16)


def call_backward(ext, row, hat, terms, att, stat, x0, q, top, bot, kv, gvec, wts, offset):
    whole, per = specs()
    images, key_rows = q.shape[0], kv.shape[0]
    more = aug_rows(key_rows)
    keys = key_rows * 32
    window = 8 * WIN + 8 * key_rows
    heads = pl.BlockSpec((key_rows, 1, 2 * DIM, 32), lambda i, *_: (0, i, 0, 0))
    shapes = [((DIM, TOKENS), F32), ((DIM, TOKENS), F32), ((DIM, CANVAS_W), BF16), ((DIM, CANVAS_W), BF16)]
    sums = [(DIM, MLP + 16), (DIM + 16, MLP), (DIM + 16, DIM), (4, DIM, 128), (9, DIM, 128), (PAIRS, DIM, window)]
    return pl.pallas_call(
        functools.partial(backward_kernel, offset=offset, key_rows=key_rows),
        grid_spec=pltpu.PrefetchScalarGridSpec(
            num_scalar_prefetch=2, grid=(images,),
            in_specs=[
                per(DIM, TOKENS), per(more, TOKENS), per(DIM, TOKENS), per(8, TOKENS), per(DIM, TOKENS), per(DIM, PADDED),
                per(DIM, CANVAS_W), per(DIM, CANVAS_W), heads, per(DIM, 1), whole(DIM, 64), whole(PAIRS, DIM, window),
                whole(DIM, DIM), whole(DIM, DIM), whole(MLP, DIM), whole(DIM, MLP), whole(MLP, 1), whole(DIM, MLP), whole(MLP, DIM)],
            out_specs=[per(*s) for s, _ in shapes] + [heads] + [whole(*s) for s in sums],
            scratch_shapes=[
                pltpu.VMEM((DIM + more, keys), BF16), pltpu.VMEM((keys, 256), BF16), pltpu.VMEM((keys, 128), BF16),
                pltpu.VMEM((DIM, PADDED), F32)] + [pltpu.VMEM((DIM, 1024), F32)] * 4 + [pltpu.VMEM((DIM, keys), F32)] * 2),
        out_shape=[jax.ShapeDtypeStruct((images,) + s, t) for s, t in shapes]
        + [jax.ShapeDtypeStruct((key_rows, images, 2 * DIM, 32), F32)] + [jax.ShapeDtypeStruct(s, F32) for s in sums],
        compiler_params=pltpu.CompilerParams(vmem_limit_bytes=VMEM_BYTES),
        cost_estimate=pl.CostEstimate(flops=images * 12_000_000_000, bytes_accessed=images * 6_000_000, transcendentals=0),
        name="backward",
    )(ext, row, hat, terms, att, stat, x0, q, top, bot, kv, gvec, wts["vec"], wts["rw_t"], wts["wproj_t"], wts["wproj"],
      wts["w1_t"], wts["w1"], wts["b1"], wts["w2_t"], wts["w2"])


def embed_back_kernel(ext_ref, row_ref, patch_ref, dq_ref, dx1_ref, rtop_ref, rbot_ref, nsel_ref, kvt_ref, pre_ref, under_ref,
                      wp_ref, vec_ref, wqkv_ref, kexp_ref, tapt_ref,
                      aq_ref, akv_ref, apatch_ref, av_ref, ak_ref, dn_ref, rim_ref, *, offset):
    image = pl.program_id(0)
    height = ext_ref[offset + image, 0]
    breadth = ext_ref[offset + image, 1]
    row_ok = row_ref[0] * ROWS < height

    @pl.when(image == 0)
    def _():
        for ref in (aq_ref, akv_ref, apatch_ref, av_ref, ak_ref, dn_ref, rim_ref):
            ref[...] = jnp.zeros_like(ref)

    zero = jnp.zeros((2 * DIM, 32), F32)
    own = pre_ref[0]
    under = under_ref[0]
    wide = jnp.concatenate([under, under, under, zero, own, own, own, zero, own, own, own, zero], axis=1)
    taps = kvt_ref[0].astype(F32)
    ak_ref[...] += taps * wide
    grad_taps = (wide * kexp_ref[...]).astype(BF16)
    akv_ref[...] += dot_nt(jnp.concatenate([nsel_ref[0], jnp.ones((16, 384), BF16)], axis=0), grad_taps)
    grad_sel = dot(wqkv_ref[:, DIM : 3 * DIM], grad_taps)
    for k, start in enumerate((224, 0, 32)):
        part = grad_sel[:, 128 * k : 128 * k + 128]
        high = part.astype(BF16)
        low = (part - high.astype(F32)).astype(BF16)
        both = dot(jnp.concatenate([high, low], axis=0), tapt_ref[...])
        line = both[:DIM] + both[DIM:]
        for tile in range(TILES):
            dn_ref[:, 256 * tile + start : 256 * tile + start + 32] = line[:, 32 * tile : 32 * tile + 32]
    for halo_ref, start in ((rtop_ref, 0), (rbot_ref, 224)):
        line = halo_ref[0].astype(F32)
        for tile in range(TILES):
            rim_ref[:, 256 * tile + start : 256 * tile + start + 32] = line[:, 32 * tile : 32 * tile + 32]

    def step(pair, carry):
        lanes = pair_lanes(pair)
        mask = pair_mask(pair, breadth, row_ok)
        patches = patch_ref[0, :, lanes]
        x0 = (dot(wp_ref[...], patches) + column(vec_ref, 0)) * mask
        hat, rstd = normalized(x0)
        normed = (hat * column(vec_ref, 1) + column(vec_ref, 2)).astype(BF16)
        grad_q = (dq_ref[0, :, lanes] + rim_ref[:, lanes]).astype(BF16)
        aq_ref[...] += dot_nt(jnp.concatenate([normed, jnp.ones((16, PAIR), BF16)], axis=0), grad_q)
        grad_n = dot(wqkv_ref[:, 0:DIM], grad_q) + dn_ref[:, lanes]
        av_ref[1] += fold_lanes(grad_n * hat)
        av_ref[2] += fold_lanes(grad_n)
        grad_embed = (dx1_ref[0, :, lanes] + norm_back(grad_n, hat, rstd, column(vec_ref, 1))) * mask
        av_ref[0] += fold_lanes(grad_embed)
        high = grad_embed.astype(BF16)
        low = (grad_embed - high.astype(F32)).astype(BF16)
        apatch_ref[...] += dot_nt(jnp.concatenate([high, low], axis=0), patches)
        return carry

    lax.fori_loop(0, pair_count(breadth), step, 0)


def call_embed_back(ext, row, patches, dq, dx1, rtop, rbot, nsel, kvt, pre, under, consts, wts, offset):
    whole, per = specs()
    images = dq.shape[0]
    sums = [(DIM + 16, DIM), (DIM + 16, 2 * DIM), (2 * DIM, PATCH_ROWS), (3, DIM, 128), (2 * DIM, 384)]
    return pl.pallas_call(
        functools.partial(embed_back_kernel, offset=offset),
        grid_spec=pltpu.PrefetchScalarGridSpec(
            num_scalar_prefetch=2, grid=(images,),
            in_specs=[
                per(PATCH_ROWS, TOKENS), per(DIM, TOKENS), per(DIM, TOKENS), per(DIM, CANVAS_W), per(DIM, CANVAS_W),
                per(DIM, 384), per(2 * DIM, 384), per(2 * DIM, 32), per(2 * DIM, 32),
                whole(DIM, PATCH_ROWS), whole(DIM, 64), whole(DIM, 3 * DIM), whole(2 * DIM, 384), whole(128, CANVAS_W)],
            out_specs=[whole(*s) for s in sums],
            scratch_shapes=[pltpu.VMEM((DIM, TOKENS), F32), pltpu.VMEM((DIM, TOKENS), F32)]),
        out_shape=[jax.ShapeDtypeStruct(s, F32) for s in sums],
        compiler_params=pltpu.CompilerParams(vmem_limit_bytes=VMEM_BYTES),
        cost_estimate=pl.CostEstimate(flops=images * 3_000_000_000, bytes_accessed=images * 3_000_000, transcendentals=0),
        name="embed_back",
    )(ext, row, patches, dq, dx1, rtop, rbot, nsel, kvt, pre, under, wts["wp"], wts["vec"], wts["wqkv"], wts["kexp"], consts["tap_t"])


def bit_count(size):
    return size.bit_length() - 1


def swap(value, axis, bit):
    size = lax.axis_size(axis)
    return lax.ppermute(value, axis, [(i, i ^ (1 << bit)) for i in range(size)])


def shifted(value, axis, step):
    size = lax.axis_size(axis)
    pairs = [(i, i + step) for i in range(size) if 0 <= i + step < size]
    return lax.ppermute(value, axis, pairs)


def summed(value, axis):
    for bit in range(bit_count(lax.axis_size(axis))):
        value = value + swap(value, axis, bit)
    return value


def gather_slots(value, axis):
    value = value[None]
    for bit in reversed(range(bit_count(lax.axis_size(axis)))):
        value = jnp.concatenate([value, swap(value, axis, bit)], axis=0)
    return value


def scatter_slots(value, axis):
    for bit in range(bit_count(lax.axis_size(axis))):
        half = value.shape[0] // 2
        value = value[:half] + swap(value[half:], axis, bit)
    return value[0]


def gather_params(value):
    dims = []
    for axis in ("img", "row"):
        index = lax.axis_index(axis)
        for bit in reversed(range(bit_count(lax.axis_size(axis)))):
            other = swap(value, axis, bit)
            mine_second = (index >> bit) & 1 == 1
            value = jnp.stack([jnp.where(mine_second, other, value), jnp.where(mine_second, value, other)])
            dims.append((axis, bit))
    dims = dims[::-1]
    wanted = [("img", b) for b in reversed(range(bit_count(lax.axis_size("img"))))]
    wanted += [("row", b) for b in reversed(range(bit_count(lax.axis_size("row"))))]
    order = [dims.index(d) for d in wanted]
    value = jnp.transpose(value, order + [value.ndim - 2, value.ndim - 1])
    return value.reshape(-1)


def scatter_grads(flat):
    rows, imgs = lax.axis_size("row"), lax.axis_size("img")
    names = [("img", b) for b in reversed(range(bit_count(imgs)))] + [("row", b) for b in reversed(range(bit_count(rows)))]
    leaf = flat.shape[0] // (rows * imgs)
    value = flat.reshape((2,) * len(names) + (leaf // 128, 128))
    for axis, bits in (("row", range(bit_count(rows))), ("img", range(bit_count(imgs)))):
        index = lax.axis_index(axis)
        for bit in bits:
            place = names.index((axis, bit))
            names.pop(place)
            own = (index >> bit) & 1
            keep = lax.dynamic_index_in_dim(value, own, place, False)
            send = lax.dynamic_index_in_dim(value, 1 - own, place, False)
            value = keep + swap(send, axis, bit)
    return value.reshape(leaf)


def segment_list(canvas_rows, canvas_cols):
    return [
        ("w_patch", (3 * PATCH * PATCH, DIM)),
        ("w_qkv", (DIM, 3 * DIM)),
        ("w_proj", (DIM, DIM)),
        ("w_fc1", (DIM, MLP)),
        ("w_fc2", (MLP, DIM)),
        ("w_head", (DIM, CLASSES)),
        ("rel_rows", (2 * canvas_rows - 8, DIM)),
        ("rel_cols", (2 * canvas_cols - 8, DIM)),
        ("small", (49, DIM)),
        ("b_head", (CLASSES,)),
    ]


def unpack(flat_vec, segments):
    pieces = {}
    position = 0
    for seg_name, seg_shape in segments:
        entries = int(np.prod(seg_shape))
        pieces[seg_name] = flat_vec[position : position + entries].reshape(seg_shape)
        position += entries
    return pieces


def patch_rows(weight):
    taps = jnp.pad(weight.reshape(PATCH, PATCH, 3, DIM), ((0, 1), (0, 0), (0, 1), (0, 0)))
    parts = []
    for piece in (taps[:, 3:7], taps[:, 0:3]):
        phases = piece.shape[1]
        parts.append(jnp.transpose(piece.reshape(2, 4, phases, 4, DIM), (0, 2, 1, 3, 4)).reshape(32 * phases, DIM))
    return jnp.concatenate(parts, axis=0)


def patch_rows_back(grad):
    rows = grad.T
    parts = []
    for piece, phases in ((rows[128:], 3), (rows[:128], 4)):
        taps = jnp.transpose(piece.reshape(2, phases, 4, 4, DIM), (0, 2, 1, 3, 4)).reshape(8, phases, 4, DIM)
        parts.append(taps[:PATCH, :, :3])
    return jnp.concatenate(parts, axis=1).reshape(3 * PATCH * PATCH, DIM)


def relative_windows(rel_rows, rel_cols, row_index, key_rows):
    offsets = jnp.flip(rel_cols.reshape(-1, 8, DIM), 0)
    offsets = jnp.transpose(jnp.pad(offsets, ((0, 1), (0, 0), (0, 0))), (1, 0, 2))
    blocks = rel_rows.reshape(2 * key_rows - 1, 8, DIM)
    rows = jnp.transpose(jnp.flip(lax.dynamic_slice_in_dim(blocks, row_index, key_rows, 0), 0), (1, 0, 2))
    rows = rows.reshape(8 * key_rows, DIM)
    windows = []
    for pair in range(PAIRS):
        cols = offsets[:, 24 - 8 * pair : 24 - 8 * pair + WIN].reshape(8 * WIN, DIM)
        windows.append(jnp.concatenate([cols, rows], axis=0))
    return jnp.stack(windows)


def relative_windows_back(grad, row_index, key_rows):
    grad = jnp.transpose(grad, (0, 2, 1))
    cols = grad[:, : 8 * WIN].reshape(PAIRS, 8, WIN, DIM)
    total = 0.0
    for pair in range(PAIRS):
        start = 24 - 8 * pair
        total = total + jnp.pad(cols[pair], ((0, 0), (start, 64 - start - WIN), (0, 0)))
    rel_cols = jnp.flip(jnp.transpose(total[:, :63], (1, 0, 2)), 0).reshape(-1, DIM)
    rows = jnp.sum(grad[:, 8 * WIN :], axis=0).reshape(8, key_rows, DIM)
    rows = jnp.flip(jnp.transpose(rows, (1, 0, 2)), 0)
    blocks = lax.dynamic_update_slice_in_dim(jnp.zeros((2 * key_rows - 1, 8, DIM), F32), rows, row_index, 0)
    return blocks.reshape(-1, DIM), rel_cols


def prepare(weights, row_index, key_rows):
    small = weights["small"]
    vec = jnp.pad(small.astype(F32).T, ((0, 0), (0, 15)))
    kernels = small[9:27].reshape(2, 3, 3, DIM).astype(F32)
    keep = np.ones((3, 4, 32), np.float32)
    keep[:, 3] = 0.0
    keep[:, 0, 0] = 0.0
    expanded = jnp.pad(jnp.transpose(kernels, (0, 3, 1, 2)), ((0, 0), (0, 0), (0, 0), (0, 1)))
    kexp = (expanded[..., None] * keep).reshape(2 * DIM, 384)
    windows = relative_windows(weights["rel_rows"], weights["rel_cols"], row_index, key_rows)
    return {
        "vec": vec,
        "kexp": kexp,
        "wp": patch_rows(weights["w_patch"]).T,
        "wqkv": weights["w_qkv"],
        "wqkv_t": weights["w_qkv"].T,
        "b_kv": small[43:45].astype(F32).reshape(2 * DIM, 1),
        "wproj": weights["w_proj"],
        "wproj_t": weights["w_proj"].T,
        "w1": weights["w_fc1"],
        "w1_t": weights["w_fc1"].T,
        "b1": small[45:49].astype(F32).reshape(MLP, 1),
        "w2": weights["w_fc2"],
        "w2_t": weights["w_fc2"].T,
        "rw": windows,
        "rw_t": jnp.transpose(windows, (0, 2, 1)),
    }


def image_loss(pooled, head_w, head_b, teacher, labels, image_total):
    logits = jnp.dot(pooled, head_w, precision=HIGHEST_PREC) + head_b
    log_student = jax.nn.log_softmax(logits, axis=-1)
    log_teacher = jax.nn.log_softmax(teacher, axis=-1)
    onehot = (jnp.arange(CLASSES)[None, :] == labels[:, None]).astype(F32)
    per_image = jnp.sum(jnp.exp(log_teacher) * (log_teacher - log_student), axis=-1) - jnp.sum(onehot * log_student, axis=-1)
    return jnp.sum(per_image) / image_total


def body(flat_params, first_moment, second_moment, pixels, extents, labels, teacher):
    key_rows = lax.axis_size("row")
    row_index = lax.axis_index("row")
    row_lead = row_index == 0
    segments = segment_list(ROWS * key_rows, CANVAS_W)
    full_params = gather_params(flat_params.astype(BF16).reshape(-1, 128))
    weights = unpack(full_params, segments)
    wts = prepare(weights, row_index, key_rows)
    tap = tap_matrix()
    consts = {"perm": jnp.asarray(deinterleave_matrix(), BF16), "tap": jnp.asarray(tap, BF16), "tap_t": jnp.asarray(tap.T, BF16)}
    vectors = weights["small"][27:42].astype(F32)
    row = row_index.astype(jnp.int32).reshape(1)
    images = pixels.shape[0]
    parts = 2
    size = images // parts
    image_total = images * lax.axis_size("img") * 1.0
    head_w = weights["w_head"].astype(F32)
    head_b = weights["b_head"].astype(F32)

    saved = []
    for part in range(parts):
        patches, x0, q, first, last, nsel, kvt, below, own = call_embed(extents, row, pixels, consts, wts, size, part * size)
        top = shifted(last, "row", 1)
        bot = shifted(first, "row", -1)
        got = shifted(below, "row", 1)
        kv = gather_slots(call_pool_norm(own, got, wts["vec"]), "row")
        saved.append(dict(patches=patches, x0=x0, q=q, top=top, bot=bot, nsel=nsel, kvt=kvt, own=own, got=got, kv=kv))
    for part in range(parts):
        s = saved[part]
        s["fwd"] = call_forward(extents, row, s["q"], s["top"], s["bot"], s["x0"], s["kv"], wts, part * size)
    total = {}

    def add(name, value):
        total[name] = total[name] + value if name in total else value

    loss_value = 0.0
    for part in range(parts):
        s = saved[part]
        hat, terms, att, stat, pool = s["fwd"]
        local = jnp.sum(pool, axis=-1)
        everywhere = summed(local, "row")
        ext = extents[part * size : part * size + size]
        counts = (ext[:, 0] * ext[:, 1]).astype(F32)[:, None]
        pooled = (everywhere * vectors[13] + counts * vectors[14]) / counts

        def loss_of(pooled_now, w, b):
            return image_loss(pooled_now, w, b, teacher[part * size : part * size + size], labels[part * size : part * size + size], image_total)

        loss_part, loss_back = jax.vjp(loss_of, pooled, head_w, head_b)
        grad_pooled, grad_w, grad_b = loss_back(jnp.ones_like(loss_part))
        loss_value = loss_value + loss_part
        add("w_head", grad_w)
        add("b_head", grad_b)
        gvec = grad_pooled / counts
        local_count = jnp.where(row_index * ROWS < ext[:, 0], ROWS * ext[:, 1], 0).astype(F32)[:, None]
        add("g_three", jnp.sum(gvec * local, axis=0))
        add("b_three", jnp.sum(gvec * local_count, axis=0))
        s["bwd"] = call_backward(extents, row, hat, terms, att, stat, s["x0"], s["q"], s["top"], s["bot"], s["kv"], gvec[:, :, None], wts, part * size)
    for part in range(parts):
        s = saved[part]
        dx1, dq, up, down, dkv, a2, a1, ap, av, ak, ar = s["bwd"]
        for name, value in (("a2", a2), ("a1", a1), ("ap", ap), ("av", av), ("ak", ak), ("ar", ar)):
            add(name, value)
        rtop = shifted(down, "row", 1)
        rbot = shifted(up, "row", -1)
        grad_kv = scatter_slots(dkv, "row")
        pre, pool_sums = call_pool_back(s["own"], s["got"], grad_kv, wts["vec"])
        add("pool_sums", pool_sums)
        under = shifted(pre, "row", -1)
        aq, akv, apatch, av1, akt = call_embed_back(
            extents, row, s["patches"], dq, dx1, rtop, rbot, s["nsel"], s["kvt"], pre, under, consts, wts, part * size)
        for name, value in (("aq", aq), ("akv", akv), ("apatch", apatch), ("av1", av1), ("akt", akt)):
            add(name, value)

    t = total
    lead = jnp.where(row_lead, 1.0, 0.0)
    av, av1 = jnp.sum(t["av"], axis=-1), jnp.sum(t["av1"], axis=-1)
    pool_sums = jnp.sum(t["pool_sums"], axis=-1)
    rel_rows, rel_cols = relative_windows_back(t["ar"], row_index, key_rows)
    taps = jnp.sum(t["akt"].reshape(2, DIM, 3, 4, 32)[:, :, :, :3], axis=-1)
    kernels = jnp.concatenate([jnp.sum(t["ak"], axis=-1), jnp.transpose(taps, (0, 2, 3, 1)).reshape(18, DIM)], axis=0)
    grad_vectors = jnp.stack([
        av1[0], av1[1], av1[2], av[2], av[3], pool_sums[0], pool_sums[1], pool_sums[2], pool_sums[3],
        t["ap"][DIM], av[0], av[1], t["a2"][:, MLP], t["g_three"], t["b_three"]])
    pieces = [
        patch_rows_back(t["apatch"][:DIM] + t["apatch"][DIM:]),
        jnp.concatenate([t["aq"][:DIM], t["akv"][:DIM]], axis=1),
        t["ap"][:DIM],
        t["a1"][:DIM],
        t["a2"][:, :MLP].T,
        t["w_head"] * lead,
        rel_rows,
        rel_cols,
        kernels,
        grad_vectors,
        t["aq"][DIM],
        t["akv"][DIM],
        t["a1"][DIM],
        t["b_head"] * lead,
    ]
    joined = jnp.concatenate([piece.reshape(-1) for piece in pieces])
    grad_flat = jnp.pad(joined, (0, full_params.shape[0] - joined.shape[0]))
    grad_shard = scatter_grads(grad_flat)
    norm_sq = summed(jnp.sum(grad_shard * grad_shard), "row")
    both = summed(jnp.stack([norm_sq, loss_value]), "img")
    grad_norm = jnp.sqrt(both[0])
    clip_factor = jnp.minimum(1.0, CLIP_NORM / (grad_norm + 1e-06))
    clipped = grad_shard * clip_factor
    moment_one = BETA_FIRST * first_moment + (1.0 - BETA_FIRST) * clipped
    moment_two = BETA_SECOND * second_moment + (1.0 - BETA_SECOND) * clipped * clipped
    fix_one = 1.0 - BETA_FIRST**STEP
    fix_two = 1.0 - BETA_SECOND**STEP
    update = moment_one / fix_one / (jnp.sqrt(moment_two / fix_two) + ADAM_EPS) + WEIGHT_DECAY * flat_params
    new_params = flat_params - LEARN_RATE * update
    return (new_params, moment_one, moment_two, grad_norm, both[1])


def solution(mesh):
    placed = (
        P(("img", "row")),
        P(("img", "row")),
        P(("img", "row")),
        P("img", "row", None, None, None),
        P("img", None),
        P("img"),
        P("img", None),
    )
    return jax.shard_map(
        body,
        mesh=mesh,
        in_specs=placed,
        out_specs=(P(("img", "row")), P(("img", "row")), P(("img", "row")), P(), P()),
        check_vma=False,
    )
```

time: 3120 us -> 809 us (0.26); the launches traced: 3060 us -> 811 us
  local copies, waits for them, and re-layouts: 1610 us -> 112 us
  other arithmetic: 685 us -> 49.3 us
  Pallas kernels: 0 us -> 506 us
  matrix products: 431 us -> 3.54 us
  blocking collectives: 149 us -> 0 us
  waiting for transfers between devices: 157 us -> 50.9 us
  starting transfers between devices: 13.8 us -> 81.2 us
    slice x67 -> x46, local copies, waits for them, and re-layouts: 959 us -> 32.4 us  [the longest x12 21.1 us: scatter_slots(): value = value[:half] + swap(value[half:], axis, bit)]
    pallas_call x0 -> x12, Pallas kernels: none -> 506 us  [the longest x2 239 us: call_backward(): pl.pallas_call(functools.partial(backward_kernel, offset=offset, key_rows...]
    dot_general x25 -> x0, matrix products: 394 us -> none  [the longest x1 44.5 us: body(): jnp.einsum('nrwc,hc->nrwh', grad_mlp_r, weights['w_fc2'], preferred_eleme...]
    reduce_sum x26 -> x10, other arithmetic: 291 us -> 8.77 us  [the longest x2 2.4 us: body(): local = jnp.sum(pool, axis=-1)]
    pad x11 -> x2, local copies, waits for them, and re-layouts: 198 us -> 0.09 us  [the longest x1 0.08 us: body(): grad_flat = jnp.pad(joined, (0, full_params.shape[0] - joined.shape[0]))]
    concatenate x2, local copies, waits for them, and re-layouts: 181 us -> 6.52 us  [the longest x1 6.49 us: body(): joined = jnp.concatenate([piece.reshape(-1) for piece in pieces])]
    unnamed x4 -> x0, waiting for transfers between devices: 142 us -> none
    convert_element_type x11 -> x4, other arithmetic: 141 us -> 0.84 us  [the longest x1 0.68 us: body(): head_b = weights['b_head'].astype(F32)]
  transfers between devices with their start and end apart: 9 -> 45, of which waited for: 2 -> 18; matrix products, arithmetic and copies ran while one was open for 14% -> 15% of each run, Pallas kernels for 0% -> 22%
where the time goes in v1:
time: 809 us; the launch traced here: 811 us
  Pallas kernels  506 us (63%)
  local copies, waits for them, and re-layouts  112 us (14%)
  starting transfers between devices  81.2 us (10%)
  waiting for transfers between devices  50.9 us (6%)
  other arithmetic  49.3 us (6%)
  between operations  8.38 us (1%)
    pallas_call x2, Pallas kernels, call_backward(): pl.pallas_call(functools.partial(backward_kernel, offset=offset, key_rows...  239 us
    pallas_call x2, Pallas kernels, call_forward(): pl.pallas_call(functools.partial(forward_kernel, offset=offset, key_rows=...  139 us
    pallas_call x2, Pallas kernels, call_embed_back(): pl.pallas_call(functools.partial(embed_back_kernel, offset=offset), grid_...  61.2 us
    pallas_call x2, Pallas kernels, call_embed(): pl.pallas_call(functools.partial(embed_kernel, offset=offset), grid_spec=...  55.5 us
    ppermute x33, waiting for transfers between devices, swap(): return lax.ppermute(value, axis, [(i, i ^ 1 << bit) for i in range(size)])  50.9 us
    ppermute x33, starting transfers between devices, swap(): return lax.ppermute(value, axis, [(i, i ^ 1 << bit) for i in range(size)])  46.5 us
    ppermute x12, starting transfers between devices, shifted(): return lax.ppermute(value, axis, pairs)  34.7 us
    slice x12, local copies, waits for them, and re-layouts, scatter_slots(): value = value[:half] + swap(value[half:], axis, bit)  21.1 us
  transfers between devices with their start and end apart: 45, of which 18 were waited for; matrix products, arithmetic and copies ran while one was open for 15% of the time, Pallas kernels for 22%

profile of v1, /device:TPU:0, one launch (start us, length us, event | category | flops | bytes accessed | tf_op | source)
XLA Modules:
  0.0 811.4 jit_solution(6960218147163838507)
XLA Ops:
  1.4 4.0 collective-permute-start
  8.0 2.0 collective-permute-start.1
  10.0 2.0 collective-permute-done.1
  12.0 2.0 collective-permute-start.2
  16.5 2.0 collective-permute-start.3
  20.7 10.3 %copy.427.pix_ref.tail_ref = bf16[16,8,7,3,1024]{4,3,2,1,0:T(4,128)(2,1)} copy(bf16[16,8,7,3,1024]{4,1,3,2,0:T(8,128)(2,1)} %param.16) | data formatting | bytes 11010048 | tf_op args[3]
  39.2 27.3 %embed.3 = (bf16[8,224,2048]{2,1,0:T(8,128)(2,1)}, f32[8,96,2048]{2,1,0:T(8,128)}, bf16[8,96,2560]{2,1,0:T(8,128)(2,1)}, bf16[8,96,256]{2,1,0:T(8,128)(2,1)}, bf...) custom-call(s32[16,2]{1,0:T(8,128)} %copy.471.ext_ref, ...), custom_call_target="tpu_custom_call" | custom-call | flops 16000000000 | bytes 32000000 | tf_op jit(solution)/shard_map/embed/pallas_call | solution.py:278
  66.5 28.2 %embed.2 = (bf16[8,224,2048]{2,1,0:T(8,128)(2,1)}, f32[8,96,2048]{2,1,0:T(8,128)}, bf16[8,96,2560]{2,1,0:T(8,128)(2,1)}, bf16[8,96,256]{2,1,0:T(8,128)(2,1)}, bf...) custom-call(s32[16,2]{1,0:T(8,128)} %copy.471.ext_ref, ...), custom_call_target="tpu_custom_call" | custom-call | flops 16000000000 | bytes 32000000 | tf_op jit(solution)/shard_map/embed/pallas_call | solution.py:278
  95.0 2.5 collective-permute-start.22
  97.6 2.7 collective-permute-start.20
  100.2 13.1 %collective-permute-start.21 = (bf16[8,96,256]{2,1,0:T(8,128)(2,1)}, bf16[8,96,256]{2,1,0:T(8,128)(2,1)}, u32[]{:S(2)}, u32[]{:S(2)}) collective-permute-start(bf16[8,96,256]{2,1,0:T(8,128)(2,1)} %get-tuple-element.102), channel_id=1, source_target_pairs={{1,0},{2,1},{3,2},{4,3},{5,4},{6,5},{7,6},{9,8},{10,9},{11,10},{12... | collective-permute-start | bytes 1179656 | tf_op jit(solution)/shard_map/ppermute | solution.py:692
  115.4 2.6 pool_norm.3
  118.1 4.0 collective-permute-start.23
  125.0 6.8 collective-permute-done.23
  133.9 2.6 pool_norm.2
  136.5 1.9 collective-permute-start.8
  143.4 2.0 collective-permute-start.5
  150.4 7.7 collective-permute-done.9
  163.6 3.0 pad_maximum_fusion.1.kv_ref
  166.7 67.5 %forward.3 = (f32[8,96,2048]{2,1,0:T(8,128)}, bf16[8,96,2048]{2,1,0:T(8,128)(2,1)}, bf16[8,96,2048]{2,1,0:T(8,128)(2,1)}, f32[8,8,2048]{2,1,0:T(8,128)}, f32[8,96,128]{2,1,0:T(8,128)}) custom-call(s32[16,2]{1,0:T(8,128)} %copy.471.ext_ref, s32[1]{0:T(128)} %bitcast.row_ref, bf16[8,96,2560]{2,1,0:T(8,128)(2,1)} %get-tuple-element.100.q_ref, ...), custom_call_target="tpu_custom_call" | custom-call | flops 40000000000 | bytes 32000000 | tf_op jit(solution)/shard_map/forward/pallas_call | solution.py:445
  237.2 2.1 pad_maximum_fusion.kv_ref
  239.5 71.4 %forward.2 = (f32[8,96,2048]{2,1,0:T(8,128)}, bf16[8,96,2048]{2,1,0:T(8,128)(2,1)}, bf16[8,96,2048]{2,1,0:T(8,128)(2,1)}, f32[8,8,2048]{2,1,0:T(8,128)}, f32[8,96,128]{2,1,0:T(8,128)}) custom-call(s32[16,2]{1,0:T(8,128)} %copy.471.ext_ref, s32[1]{0:T(128)} %bitcast.row_ref, bf16[8,96,2560]{2,1,0:T(8,128)(2,1)} %get-tuple-element.77.q_ref, ...), custom_call_target="tpu_custom_call" | custom-call | flops 40000000000 | bytes 32000000 | tf_op jit(solution)/shard_map/forward/pallas_call | solution.py:445
  316.2 2.7 collective-permute-start.28
  321.2 3.0 collective-permute-done.13
  330.6 115.5 %backward.3 = (f32[8,96,2048]{2,1,0:T(8,128)}, f32[8,96,2048]{2,1,0:T(8,128)}, bf16[8,96,256]{2,1,0:T(8,128)(2,1)}, bf16[8,96,256]{2,1,0:T(8,128)(2,1)}, f32[8,8...) custom-call(s32[16,2]{1,0:T(8,128)} %copy.471.ext_ref, ...), custom_call_target="tpu_custom_call" | custom-call | flops 96000000000 | bytes 48000000 | tf_op jit(solution)/shard_map/backward/pallas_call | solution.py:581
  446.1 123.2 %backward.2 = (f32[8,96,2048]{2,1,0:T(8,128)}, f32[8,96,2048]{2,1,0:T(8,128)}, bf16[8,96,256]{2,1,0:T(8,128)(2,1)}, bf16[8,96,256]{2,1,0:T(8,128)(2,1)}, f32[8,8...) custom-call(s32[16,2]{1,0:T(8,128)} %copy.471.ext_ref, ...), custom_call_target="tpu_custom_call" | custom-call | flops 96000000000 | bytes 48000000 | tf_op jit(solution)/shard_map/backward/pallas_call | solution.py:581
  573.5 2.1 slice.294
  575.6 2.2 copy.496
  577.8 2.1 slice.284
  580.0 2.2 copy.463
  584.5 2.7 collective-permute-start.29
  588.5 3.8 collective-permute-start.14
  604.7 3.3 copy.497
  608.0 3.2 slice_add_fusion
  612.5 2.8 copy.498
  615.3 3.3 copy.464
  618.5 3.3 slice_add_fusion.1
  624.8 2.8 copy.465
  627.6 2.0 collective-permute-start.17
  629.6 1.9 fusion.3
  633.2 1.8 copy.518
  635.0 1.8 reshape_reshape.23
  644.0 2.7 copy.499
  650.3 2.4 copy.500
  652.7 3.3 collective-permute-start.33
  656.0 2.7 copy.466
  663.0 2.2 copy.501
  665.2 2.3 fusion.1.grad_ref
  667.5 3.2 pool_back.3
  675.6 3.2 pool_back.2
  683.8 29.9 %embed_back.3 = (f32[112,96]{1,0:T(8,128)}, f32[112,192]{1,0:T(8,128)}, f32[192,224]{1,0:T(8,128)}, f32[3,96,128]{2,1,0:T(8,128)}, f32[192,384]{1,0:T(8,128)}) custom-call(s32[16,2]{1,0:T(8,128)} %copy.471.ext_ref, s32[1]{0:T(128)} %bitcast.row_ref, bf16[8,224,2048]{2,1,0:T(8,128)(2,1)} %get-tuple-element.99.patch_ref, ...), custom_call_target="tpu_custom_call" | custom-call | flops 24000000000 | bytes 24000000 | tf_op jit(solution)/shard_map/embed_back/pallas_call | solution.py:663
  715.0 31.4 %embed_back.2 = (f32[112,96]{1,0:T(8,128)}, f32[112,192]{1,0:T(8,128)}, f32[192,224]{1,0:T(8,128)}, f32[3,96,128]{2,1,0:T(8,128)}, f32[192,384]{1,0:T(8,128)}) custom-call(s32[16,2]{1,0:T(8,128)} %copy.471.ext_ref, s32[1]{0:T(128)} %bitcast.row_ref, bf16[8,224,2048]{2,1,0:T(8,128)(2,1)} %get-tuple-element.76.patch_ref, ...), custom_call_target="tpu_custom_call" | custom-call | flops 24000000000 | bytes 24000000 | tf_op jit(solution)/shard_map/embed_back/pallas_call | solution.py:663
  753.0 6.5 concatenate.63
  760.1 1.8 collective-permute-start.35
  763.6 2.1 collective-permute-start.36
  765.7 7.3 collective-permute-done.36
  773.1 2.3 collective-permute-start.37
  775.3 3.3 collective-permute-done.37
  780.3 2.9 collective-permute-done.38
  785.2 2.9 collective-permute-done.39
  791.3 2.7 collective-permute-start.41
  795.6 3.2 collective-permute-start.42
  801.7 1.8 collective-permute-done.43
  803.6 4.4 collective-permute-done.44
  (447 shorter events, 125.2 us)
Async XLA Ops:
  1.4 5.8 collective-permute-start
  8.0 4.0 collective-permute-start.1
  12.0 4.4 collective-permute-start.2
  16.5 14.7 %collective-permute-start.3 = (bf16[2,2,2,70,128]{4,3,0,1,2:T(8,128)(2,1)S(1)}, bf16[2,2,2,70,128]{4,3,0,1,2:T(8,128)(2,1)S(1)}, u32[]{:S(2)}, u32[]{:S(2)}) collective-permute-start(bf16[2,2,2,70,128]{4,3,0,1,2:T(8,128)(2,1)S(1)} %pad_maximum_fusion.8), channel_id=1, source_target_pairs={{0,2},{1,3},{2,0},{3,1},{4,6},{5,7},{6,4},{7,5},{8,10},{9,11},{10,... | collective-permute-start | bytes 430088 | tf_op jit(solution)/shard_map/ppermute | solution.py:686
  31.2 2.0 collective-permute-start.4
  33.5 116.4 %copy-start.8 = (bf16[286720]{0:T(1024)(128)(2,1)}, bf16[286720]{0:T(1024)(128)(2,1)S(1)}, u32[]{:S(2)}) copy-start(bf16[286720]{0:T(1024)(128)(2,1)S(1)} %reshape.221) | copy-start | bytes 1720324
  95.0 19.3 %collective-permute-start.22 = (f32[8,192,32]{1,2,0:T(8,128)S(1)}, f32[8,192,32]{1,2,0:T(8,128)S(1)}, u32[]{:S(2)}, u32[]{:S(2)}) collective-permute-start(f32[8,192,32]{1,2,0:T(8,128)S(1)} %copy.478), channel_id=1, source_target_pairs={{0,1},{1,2},{2,3},{3,4},{4,5},{5,6},{6,7},{8,9},{9,10},{10,11},{11... | collective-permute-start | bytes 589832 | tf_op jit(solution)/shard_map/ppermute | solution.py:692
  97.6 69.1 %collective-permute-start.20 = (bf16[8,96,256]{2,1,0:T(8,128)(2,1)}, bf16[8,96,256]{2,1,0:T(8,128)(2,1)}, u32[]{:S(2)}, u32[]{:S(2)}) collective-permute-start(bf16[8,96,256]{2,1,0:T(8,128)(2,1)} %get-tuple-element.101), channel_id=1, source_target_pairs={{0,1},{1,2},{2,3},{3,4},{4,5},{5,6},{6,7},{8,9},{9,10},{10,11},{11... | collective-permute-start | bytes 1179656 | tf_op jit(solution)/shard_map/ppermute | solution.py:692
  100.2 66.5 %collective-permute-start.21 = (bf16[8,96,256]{2,1,0:T(8,128)(2,1)}, bf16[8,96,256]{2,1,0:T(8,128)(2,1)}, u32[]{:S(2)}, u32[]{:S(2)}) collective-permute-start(bf16[8,96,256]{2,1,0:T(8,128)(2,1)} %get-tuple-element.102), channel_id=1, source_target_pairs={{1,0},{2,1},{3,2},{4,3},{5,4},{6,5},{7,6},{9,8},{10,9},{11,10},{12... | collective-permute-start | bytes 1179656 | tf_op jit(solution)/shard_map/ppermute | solution.py:692
  118.1 13.7 %collective-permute-start.23 = (bf16[1,8,192,32]{3,2,1,0:T(8,128)(2,1)}, bf16[1,8,192,32]{3,2,1,0:T(8,128)(2,1)S(1)}, u32[]{:S(2)}, u32[]{:S(2)}) collective-permute-start(bf16[1,8,192,32]{3,2,1,0:T(8,128)(2,1)} %bitcast.183), channel_id=1, source_target_pairs={{0,4},{1,5},{2,6},{3,7},{4,0},{5,1},{6,2},{7,3},{8,12},{9,13},{10,... | collective-permute-start | bytes 294920 | tf_op jit(solution)/shard_map/ppermute | solution.py:686
  122.5 10.2 %collective-permute-start.7 = (f32[8,192,32]{1,2,0:T(8,128)S(1)}, f32[8,192,32]{1,2,0:T(8,128)S(1)}, u32[]{:S(2)}, u32[]{:S(2)}) collective-permute-start(f32[8,192,32]{1,2,0:T(8,128)S(1)} %copy.431), channel_id=1, source_target_pairs={{0,1},{1,2},{2,3},{3,4},{4,5},{5,6},{6,7},{8,9},{9,10},{10,11},{11... | collective-permute-start | bytes 589832 | tf_op jit(solution)/shard_map/ppermute | solution.py:692
  132.0 15.4 %collective-permute-start.24 = (bf16[2,8,192,32]{2,3,1,0:T(8,128)(2,1)S(1)}, bf16[2,8,192,32]{2,3,1,0:T(8,128)(2,1)S(1)}, u32[]{:S(2)}, u32[]{:S(2)}) collective-permute-start(bf16[2,8,192,32]{2,3,1,0:T(8,128)(2,1)S(1)} %pad_maximum_fusion.7), channel_id=1, source_target_pairs={{0,2},{1,3},{2,0},{3,1},{4,6},{5,7},{6,4},{7,5},{8,10},{9,11},{10,... | collective-permute-start | bytes 589832 | tf_op jit(solution)/shard_map/ppermute | solution.py:686
  136.5 10.7 %collective-permute-start.8 = (bf16[1,8,192,32]{3,2,1,0:T(8,128)(2,1)}, bf16[1,8,192,32]{3,2,1,0:T(8,128)(2,1)S(1)}, u32[]{:S(2)}, u32[]{:S(2)}) collective-permute-start(bf16[1,8,192,32]{3,2,1,0:T(8,128)(2,1)} %bitcast.186), channel_id=1, source_target_pairs={{0,4},{1,5},{2,6},{3,7},{4,0},{5,1},{6,2},{7,3},{8,12},{9,13},{10,... | collective-permute-start | bytes 294920 | tf_op jit(solution)/shard_map/ppermute | solution.py:686
  143.4 95.9 %collective-permute-start.5 = (bf16[8,96,256]{2,1,0:T(8,128)(2,1)}, bf16[8,96,256]{2,1,0:T(8,128)(2,1)}, u32[]{:S(2)}, u32[]{:S(2)}) collective-permute-start(bf16[8,96,256]{2,1,0:T(8,128)(2,1)} %get-tuple-element.78), channel_id=1, source_target_pairs={{0,1},{1,2},{2,3},{3,4},{4,5},{5,6},{6,7},{8,9},{9,10},{10,11},{11... | collective-permute-start | bytes 1179656 | tf_op jit(solution)/shard_map/ppermute | solution.py:692
  148.3 12.4 %collective-permute-start.25 = (bf16[4,8,192,32]{2,3,1,0:T(8,128)(2,1)}, bf16[4,8,192,32]{2,3,1,0:T(8,128)(2,1)}, u32[]{:S(2)}, u32[]{:S(2)}) collective-permute-start(bf16[4,8,192,32]{2,3,1,0:T(8,128)(2,1)} %pad_maximum_fusion.3), channel_id=1, source_target_pairs={{0,1},{1,0},{2,3},{3,2},{4,5},{5,4},{6,7},{7,6},{8,9},{9,8},{10,11... | collective-permute-start | bytes 1179656 | tf_op jit(solution)/shard_map/ppermute | solution.py:686
  149.8 8.3 %collective-permute-start.9 = (bf16[2,8,192,32]{2,3,1,0:T(8,128)(2,1)S(1)}, bf16[2,8,192,32]{2,3,1,0:T(8,128)(2,1)S(1)}, u32[]{:S(2)}, u32[]{:S(2)}) collective-permute-start(bf16[2,8,192,32]{2,3,1,0:T(8,128)(2,1)S(1)} %pad_maximum_fusion.6), channel_id=1, source_target_pairs={{0,2},{1,3},{2,0},{3,1},{4,6},{5,7},{6,4},{7,5},{8,10},{9,11},{10,... | collective-permute-start | bytes 589832 | tf_op jit(solution)/shard_map/ppermute | solution.py:686
  158.1 81.3 %collective-permute-start.6 = (bf16[8,96,256]{2,1,0:T(8,128)(2,1)}, bf16[8,96,256]{2,1,0:T(8,128)(2,1)}, u32[]{:S(2)}, u32[]{:S(2)}) collective-permute-start(bf16[8,96,256]{2,1,0:T(8,128)(2,1)} %get-tuple-element.79), channel_id=1, source_target_pairs={{1,0},{2,1},{3,2},{4,3},{5,4},{6,5},{7,6},{9,8},{10,9},{11,10},{12... | collective-permute-start | bytes 1179656 | tf_op jit(solution)/shard_map/ppermute | solution.py:692
  160.7 74.8 %collective-permute-start.10 = (bf16[4,8,192,32]{2,3,1,0:T(8,128)(2,1)}, bf16[4,8,192,32]{2,3,1,0:T(8,128)(2,1)}, u32[]{:S(2)}, u32[]{:S(2)}) collective-permute-start(bf16[4,8,192,32]{2,3,1,0:T(8,128)(2,1)} %pad_maximum_fusion.2), channel_id=1, source_target_pairs={{0,1},{1,0},{2,3},{3,2},{4,5},{5,4},{6,7},{7,6},{8,9},{9,8},{10,11... | collective-permute-start | bytes 1179656 | tf_op jit(solution)/shard_map/ppermute | solution.py:686
  166.7 70.5 %copy-start.7 = (bf16[8,192,32]{2,1,0:T(8,128)(2,1)S(1)}, bf16[8,192,32]{2,1,0:T(8,128)(2,1)}, u32[]{:S(2)}) copy-start(bf16[8,192,32]{2,1,0:T(8,128)(2,1)} %pool_norm.2) | copy-start | bytes 294916
  166.7 70.5 %copy-start.11 = (bf16[1,8,192,32]{3,2,1,0:T(8,128)(2,1)S(1)}, bf16[1,8,192,32]{3,2,1,0:T(8,128)(2,1)}, u32[]{:S(2)}) copy-start(bf16[1,8,192,32]{3,2,1,0:T(8,128)(2,1)} %copy-done.10) | copy-start | bytes 294916
  235.4 77.2 %collective-permute-start.26 = (f32[8,96]{1,0:T(8,128)S(1)}, f32[8,96]{1,0:T(8,128)S(1)}, u32[]{:S(2)}, u32[]{:S(2)}) collective-permute-start(f32[8,96]{1,0:T(8,128)S(1)} %reduce_sum.247), channel_id=1, source_target_pairs={{0,1},{1,0},{2,3},{3,2},{4,5},{5,4},{6,7},{7,6},{8,9},{9,8},{10,11... | collective-permute-start | bytes 9224 | tf_op jit(solution)/shard_map/ppermute | solution.py:686
  239.4 81.2 %copy-start.62 = (f32[8]{0:T(128)S(1)}, f32[8]{0:T(128)}, u32[]{:S(2)}) copy-start(f32[8]{0:T(128)} %get-tuple-element.204) | copy-start | bytes 100
  239.4 84.8 %copy-start.60 = (f32[8]{0:T(128)S(1)}, f32[8]{0:T(128)}, u32[]{:S(2)}) copy-start(f32[8]{0:T(128)} %get-tuple-element.203) | copy-start | bytes 100
  239.4 85.3 %copy-start.14 = (f32[16,1000]{1,0:T(8,128)S(1)}, f32[16,1000]{1,0:T(8,128)}, u32[]{:S(2)}) copy-start(f32[16,1000]{1,0:T(8,128)} %param.19) | copy-start | bytes 192004
  239.4 85.3 %copy-start.64 = (s32[8]{0:T(128)S(1)}, s32[8]{0:T(128)}, u32[]{:S(2)}) copy-start(s32[8]{0:T(128)} %get-tuple-element.207) | copy-start | bytes 100
  239.4 85.3 %copy-start.65 = (s32[8]{0:T(128)S(1)}, s32[8]{0:T(128)}, u32[]{:S(2)}) copy-start(s32[8]{0:T(128)} %get-tuple-element.208) | copy-start | bytes 100
  239.4 85.3 %copy-start.69 = (f32[8]{0:T(128)S(1)}, f32[8]{0:T(128)}, u32[]{:S(2)}) copy-start(f32[8]{0:T(128)} %log.18) | copy-start | bytes 100
  239.4 85.3 %copy-start.70 = (f32[8]{0:T(128)S(1)}, f32[8]{0:T(128)}, u32[]{:S(2)}) copy-start(f32[8]{0:T(128)} %log.20) | copy-start | bytes 100
  239.5 87.6 %copy-start.77 = (f32[8]{0:T(128)S(1)}, f32[8]{0:T(128)}, u32[]{:S(2)}) copy-start(f32[8]{0:T(128)} %get-tuple-element.201) | copy-start | bytes 100
  239.5 89.3 %copy-start.76 = (f32[8]{0:T(128)S(1)}, f32[8]{0:T(128)}, u32[]{:S(2)}) copy-start(f32[8]{0:T(128)} %get-tuple-element.202) | copy-start | bytes 100
  312.1 2.8 collective-permute-start.11
  312.6 3.6 collective-permute-start.27
  314.9 5.6 collective-permute-start.12
  316.2 129.8 %copy-start.41 = (f32[8,96]{1,0:T(8,128)}, f32[8,96]{1,0:T(8,128)S(1)}, u32[]{:S(2)}) copy-start(f32[8,96]{1,0:T(8,128)S(1)} %add.261) | copy-start | bytes 9220
  316.2 4.3 collective-permute-start.28
  319.0 127.1 %copy-start.54 = (f32[96]{0:T(128)}, f32[96]{0:T(128)S(1)}, u32[]{:S(2)}) copy-start(f32[96]{0:T(128)S(1)} %get-tuple-element.197) | copy-start | bytes 1156
  319.0 127.1 %copy-start.56 = (f32[96]{0:T(128)}, f32[96]{0:T(128)S(1)}, u32[]{:S(2)}) copy-start(f32[96]{0:T(128)S(1)} %get-tuple-element.198) | copy-start | bytes 1156
  320.5 3.7 collective-permute-start.13
  320.6 125.5 %copy-start.47 = (f32[8,96]{1,0:T(8,128)}, f32[8,96]{1,0:T(8,128)S(1)}, u32[]{:S(2)}) copy-start(f32[8,96]{1,0:T(8,128)S(1)} %collective-permute-done.28) | copy-start | bytes 9220
  326.4 119.7 %copy-start.32 = (f32[8,1000]{1,0:T(8,128)}, f32[8,1000]{1,0:T(8,128)S(1)}, u32[]{:S(2)}) copy-start(f32[8,1000]{1,0:T(8,128)S(1)} %get-tuple-element.190) | copy-start | bytes 96004
  446.1 123.3 %copy-start.18 = (f32[4,96,384]{2,1,0:T(8,128)S(1)}, f32[4,96,384]{2,1,0:T(8,128)}, u32[]{:S(2)}) copy-start(f32[4,96,384]{2,1,0:T(8,128)} %get-tuple-element.133) | copy-start | bytes 1769476
  577.8 26.9 %collective-permute-start.31 = (f32[4,8,192,32]{2,3,1,0:T(8,128)}, f32[4,8,192,32]{2,3,1,0:T(8,128)}, u32[]{:S(2)}, u32[]{:S(2)}) collective-permute-start(f32[4,8,192,32]{2,3,1,0:T(8,128)} %copy.496), channel_id=1, source_target_pairs={{0,1},{1,0},{2,3},{3,2},{4,5},{5,4},{6,7},{7,6},{8,9},{9,8},{10,11... | collective-permute-start | bytes 2359304 | tf_op jit(solution)/shard_map/ppermute | solution.py:686
  582.2 33.1 %collective-permute-start.16 = (f32[4,8,192,32]{2,3,1,0:T(8,128)}, f32[4,8,192,32]{2,3,1,0:T(8,128)}, u32[]{:S(2)}, u32[]{:S(2)}) collective-permute-start(f32[4,8,192,32]{2,3,1,0:T(8,128)} %copy.463), channel_id=1, source_target_pairs={{0,1},{1,0},{2,3},{3,2},{4,5},{5,4},{6,7},{7,6},{8,9},{9,8},{10,11... | collective-permute-start | bytes 2359304 | tf_op jit(solution)/shard_map/ppermute | solution.py:686
  584.5 99.3 %collective-permute-start.29 = (bf16[8,96,256]{2,1,0:T(8,128)(2,1)}, bf16[8,96,256]{2,1,0:T(8,128)(2,1)}, u32[]{:S(2)}, u32[]{:S(2)}) collective-permute-start(bf16[8,96,256]{2,1,0:T(8,128)(2,1)} %get-tuple-element.115), channel_id=1, source_target_pairs={{0,1},{1,2},{2,3},{3,4},{4,5},{5,6},{6,7},{8,9},{9,10},{10,11},{11... | collective-permute-start | bytes 1179656 | tf_op jit(solution)/shard_map/ppermute | solution.py:692
  587.2 96.6 %collective-permute-start.30 = (bf16[8,96,256]{2,1,0:T(8,128)(2,1)}, bf16[8,96,256]{2,1,0:T(8,128)(2,1)}, u32[]{:S(2)}, u32[]{:S(2)}) collective-permute-start(bf16[8,96,256]{2,1,0:T(8,128)(2,1)} %get-tuple-element.116), channel_id=1, source_target_pairs={{1,0},{2,1},{3,2},{4,3},{5,4},{6,5},{7,6},{9,8},{10,9},{11,10},{12... | collective-permute-start | bytes 1179656 | tf_op jit(solution)/shard_map/ppermute | solution.py:692
  588.5 126.4 %collective-permute-start.14 = (bf16[8,96,256]{2,1,0:T(8,128)(2,1)}, bf16[8,96,256]{2,1,0:T(8,128)(2,1)}, u32[]{:S(2)}, u32[]{:S(2)}) collective-permute-start(bf16[8,96,256]{2,1,0:T(8,128)(2,1)} %get-tuple-element.92), channel_id=1, source_target_pairs={{0,1},{1,2},{2,3},{3,4},{4,5},{5,6},{6,7},{8,9},{9,10},{10,11},{11... | collective-permute-start | bytes 1179656 | tf_op jit(solution)/shard_map/ppermute | solution.py:692
  615.3 27.2 %collective-permute-start.32 = (f32[2,8,192,32]{2,3,1,0:T(8,128)}, f32[2,8,192,32]{2,3,1,0:T(8,128)}, u32[]{:S(2)}, u32[]{:S(2)}) collective-permute-start(f32[2,8,192,32]{2,3,1,0:T(8,128)} %copy.498), channel_id=1, source_target_pairs={{0,2},{1,3},{2,0},{3,1},{4,6},{5,7},{6,4},{7,5},{8,10},{9,11},{10,... | collective-permute-start | bytes 1179656 | tf_op jit(solution)/shard_map/ppermute | solution.py:686
  627.6 25.1 %collective-permute-start.17 = (f32[2,8,192,32]{2,3,1,0:T(8,128)}, f32[2,8,192,32]{2,3,1,0:T(8,128)}, u32[]{:S(2)}, u32[]{:S(2)}) collective-permute-start(f32[2,8,192,32]{2,3,1,0:T(8,128)} %copy.465), channel_id=1, source_target_pairs={{0,2},{1,3},{2,0},{3,1},{4,6},{5,7},{6,4},{7,5},{8,10},{9,11},{10,... | collective-permute-start | bytes 1179656 | tf_op jit(solution)/shard_map/ppermute | solution.py:686
  642.5 72.3 %collective-permute-start.15 = (bf16[8,96,256]{2,1,0:T(8,128)(2,1)}, bf16[8,96,256]{2,1,0:T(8,128)(2,1)}, u32[]{:S(2)}, u32[]{:S(2)}) collective-permute-start(bf16[8,96,256]{2,1,0:T(8,128)(2,1)} %get-tuple-element.93), channel_id=1, source_target_pairs={{1,0},{2,1},{3,2},{4,3},{5,4},{6,5},{7,6},{9,8},{10,9},{11,10},{12... | collective-permute-start | bytes 1179656 | tf_op jit(solution)/shard_map/ppermute | solution.py:692
  652.7 9.9 %collective-permute-start.33 = (f32[1,8,192,32]{2,3,1,0:T(8,128)}, f32[1,8,192,32]{2,3,1,0:T(8,128)}, u32[]{:S(2)}, u32[]{:S(2)}) collective-permute-start(f32[1,8,192,32]{2,3,1,0:T(8,128)} %copy.500), channel_id=1, source_target_pairs={{0,4},{1,5},{2,6},{3,7},{4,0},{5,1},{6,2},{7,3},{8,12},{9,13},{10,... | collective-permute-start | bytes 589832 | tf_op jit(solution)/shard_map/ppermute | solution.py:686
  662.7 9.4 %collective-permute-start.18 = (f32[1,8,192,32]{2,3,1,0:T(8,128)}, f32[1,8,192,32]{2,3,1,0:T(8,128)}, u32[]{:S(2)}, u32[]{:S(2)}) collective-permute-start(f32[1,8,192,32]{2,3,1,0:T(8,128)} %copy.467), channel_id=1, source_target_pairs={{0,4},{1,5},{2,6},{3,7},{4,0},{5,1},{6,2},{7,3},{8,12},{9,13},{10,... | collective-permute-start | bytes 589832 | tf_op jit(solution)/shard_map/ppermute | solution.py:686
  672.1 9.3 %collective-permute-start.34 = (f32[8,192,32]{1,2,0:T(8,128)S(1)}, f32[8,192,32]{1,2,0:T(8,128)S(1)}, u32[]{:S(2)}, u32[]{:S(2)}) collective-permute-start(f32[8,192,32]{1,2,0:T(8,128)S(1)} %copy.503), channel_id=1, source_target_pairs={{1,0},{2,1},{3,2},{4,3},{5,4},{6,5},{7,6},{9,8},{10,9},{11,10},{12... | collective-permute-start | bytes 589832 | tf_op jit(solution)/shard_map/ppermute | solution.py:692
  681.4 32.3 %collective-permute-start.19 = (f32[8,192,32]{1,2,0:T(8,128)S(1)}, f32[8,192,32]{1,2,0:T(8,128)S(1)}, u32[]{:S(2)}, u32[]{:S(2)}) collective-permute-start(f32[8,192,32]{1,2,0:T(8,128)S(1)} %copy.470), channel_id=1, source_target_pairs={{1,0},{2,1},{3,2},{4,3},{5,4},{6,5},{7,6},{9,8},{10,9},{11,10},{12... | collective-permute-start | bytes 589832 | tf_op jit(solution)/shard_map/ppermute | solution.py:692
  759.7 49.7 %copy-start.20 = (f32[8960]{0:T(1024)S(1)}, f32[8960]{0:T(1024)}, u32[]{:S(2)}) copy-start(f32[8960]{0:T(1024)} %param.13) | copy-start | bytes 107524
  760.1 3.4 collective-permute-start.35
  763.6 9.4 %collective-permute-start.36 = (f32[2,2,2,70,128]{4,3,2,1,0:T(8,128)S(1)}, f32[2,2,2,70,128]{4,3,2,1,0:T(8,128)S(1)}, u32[]{:S(2)}, u32[]{:S(2)}) collective-permute-start(f32[2,2,2,70,128]{4,3,2,1,0:T(8,128)S(1)} %dynamic-slice_bitcast_fusion.1), channel_id=1, source_target_pairs={{0,2},{1,3},{2,0},{3,1},{4,6},{5,7},{6,4},{7,5},{8,10},{9,11},{10,... | collective-permute-start | bytes 860168 | tf_op jit(solution)/shard_map/ppermute | solution.py:686
  773.1 5.6 collective-permute-start.37
  778.7 4.4 collective-permute-start.38
  783.2 4.9 collective-permute-start.39
  788.7 1.4 collective-permute-start.40
  791.3 3.7 collective-permute-start.41
  795.6 3.7 collective-permute-start.42
  799.9 3.5 collective-permute-start.43
  803.6 4.4 collective-permute-start.44
  (65 other events, 1161.6 us)

commit v2 on v1

v2 whole, which is shorter than its diff:
```python
import functools

import jax
import jax.numpy as jnp
import numpy as np
from jax import lax
from jax.experimental import pallas as pl
from jax.experimental.pallas import tpu as pltpu
from jax.sharding import PartitionSpec as P

DIM = 96
MLP = 384
CLASSES = 1000
PATCH = 7
ROWS = 8
STEP = 7
CANVAS_W = 256

HIGHEST_PREC = lax.Precision.HIGHEST
CLIP_NORM = 0.02
LEARN_RATE = 0.05
WEIGHT_DECAY = 0.05
BETA_FIRST = 0.5
BETA_SECOND = 0.5
ADAM_EPS = 1e-08
NORM_EPS = 1e-06
NEG_FILL = -1e30

F32 = jnp.float32
BF16 = jnp.bfloat16
SCALE = DIM ** (-0.5)
EXP2_SCALE = SCALE * 1.4426950408889634

TOKENS = ROWS * CANVAS_W
PAIR = 512
PAIRS = TOKENS // PAIR
TILES = CANVAS_W // 32
GROUP = 2
PADDED = TOKENS + 512
WIN = 40
PATCH_ROWS = 224
VMEM_BYTES = 56 * 1024 * 1024


def deinterleave_matrix():
    out = np.zeros((4, 128, 4, 4, 32), np.float32)
    for row in range(4):
        for phase in range(4):
            for col in range(32):
                out[row, 4 * col + phase, phase, row, col] = 1.0
    return out.reshape(512, 512)


def tap_matrix():
    out = np.zeros((CANVAS_W, 128), np.float32)
    for tap in range(3):
        for key in range(32):
            col = 8 * key + tap - 1
            if col >= 0:
                out[col, tap * 32 + key] = 1.0
    return out


def dot(a, b):
    return jnp.dot(a, b, preferred_element_type=F32)


def dot_nt(a, b):
    return lax.dot_general(a, b, (((1,), (1,)), ((), ())), preferred_element_type=F32)


def normalized(x):
    mean = jnp.sum(x, axis=0, keepdims=True) * (1.0 / DIM)
    centered = x - mean
    var = jnp.sum(centered * centered, axis=0, keepdims=True) * (1.0 / DIM)
    rstd = lax.rsqrt(var + NORM_EPS)
    return centered * rstd, rstd


def norm_back(grad, hat, rstd, gain):
    inner = grad * gain
    mean_one = jnp.sum(inner, axis=0, keepdims=True) * (1.0 / DIM)
    mean_two = jnp.sum(inner * hat, axis=0, keepdims=True) * (1.0 / DIM)
    return rstd * (inner - mean_one - hat * mean_two)


def by_lanes(fn, *arrays):
    parts = [fn(k, *(a[:, 128 * k : 128 * k + 128] for a in arrays)) for k in range(arrays[0].shape[1] // 128)]
    return tuple(jnp.concatenate(column, axis=1) for column in zip(*parts))


def by_blocks(fn, height, *arrays):
    rows = []
    for top in range(0, arrays[0].shape[0], height):
        rows.append(by_lanes(lambda k, *block: fn(slice(top, top + height), *block), *(a[top : top + height] for a in arrays)))
    return tuple(jnp.concatenate(column, axis=0) for column in zip(*rows))


def fold_lanes(x):
    total = x[:, 0:128]
    for k in range(1, x.shape[1] // 128):
        total = total + x[:, 128 * k : 128 * k + 128]
    return total


def place_of(index):
    return index + 27 if index < 15 else index - 15 if index < 42 else index


def column(vec_ref, index):
    place = place_of(index)
    return vec_ref[:, place : place + 1]


def fill_wide(wide_ref, vec_ref, indices):
    for k, index in enumerate(indices):
        wide_ref[k] = jnp.broadcast_to(column(vec_ref, index), (DIM, 128))


def wide(wide_ref, k, width=PAIR):
    return jnp.concatenate([wide_ref[k]] * (width // 128), axis=1)


def lane_ids(width, rows=1):
    return lax.broadcasted_iota(jnp.int32, (rows, width), 1)


def pair_mask(pair, breadths, row_oks):
    lane = lane_ids(PAIR)
    col = pair * 64 + (lane >> 8) * 32 + (lane & 31)
    return jnp.concatenate([jnp.where((col < w) & ok, 1.0, 0.0).astype(F32) for w, ok in zip(breadths, row_oks)], axis=1)


def pair_lanes(pair, base=0):
    return pl.ds(pl.multiple_of(pair * PAIR + base, 128), PAIR)


def load_pair(ref, pair):
    lanes = pair_lanes(pair)
    return jnp.concatenate([ref[g, :, lanes] for g in range(GROUP)], axis=1)


def store_pair(ref, pair, value, base=0):
    for g in range(GROUP):
        ref[g, :, pair_lanes(pair, base)] = value[:, PAIR * g : PAIR * g + PAIR]


def by_image(value):
    return [value[:, PAIR * g : PAIR * g + PAIR] for g in range(GROUP)]


def pair_count(breadths):
    widest = breadths[0]
    for breadth in breadths[1:]:
        widest = jnp.maximum(widest, breadth)
    return jnp.minimum((widest >> 6) + 1, PAIRS)


def group_extents(ext_ref, row_ref, offset):
    images = [pl.program_id(0) * GROUP + g for g in range(GROUP)]
    heights = [ext_ref[offset + image, 0] for image in images]
    breadths = [ext_ref[offset + image, 1] for image in images]
    return images, heights, breadths, [row_ref[0] * ROWS < height for height in heights]


def col_shifts(window, base):
    lane = lane_ids(128, window.shape[0])
    here = window[:, base : base + 128]
    before = window[:, base - 256 : base - 128]
    after = window[:, base + 256 : base + 384]
    left = jnp.where((lane & 31) == 0, pltpu.roll(before, 97, 1), pltpu.roll(here, 1, 1))
    right = jnp.where((lane & 31) == 31, pltpu.roll(after, 31, 1), pltpu.roll(here, 127, 1))
    return left, here, right


def rows_down(first, second, entering):
    lane = lane_ids(128, first.shape[0])
    a, b = pltpu.roll(first, 32, 1), pltpu.roll(second, 32, 1)
    return jnp.where(lane < 32, entering, a), jnp.where(lane < 32, a, b), b


def rows_up(first, second, entering):
    lane = lane_ids(128, first.shape[0])
    a, b = pltpu.roll(first, 96, 1), pltpu.roll(second, 96, 1)
    return jnp.where(lane >= 96, b, a), jnp.where(lane >= 96, entering, b), a


def spread_halo(dst_ref, halo, target):
    for tile in range(TILES):
        block = halo[:, 128 * (tile // 4) : 128 * (tile // 4) + 128]
        shift = (target - 32 * (tile % 4)) % 128
        dst_ref[:, 128 * tile : 128 * tile + 128] = pltpu.roll(block, shift, 1) if shift else block


def store_lanes(dst_ref, value, image):
    place = image & 3
    lane = lane_ids(128, value.shape[0])
    dst_ref[...] = jnp.where((lane >> 5) == place, pltpu.roll(value, place * 32, 1), dst_ref[...])


def take_lanes(value, image, target):
    return pltpu.roll(value, (4 + target - (image & 3)) * 32 & 127, 1)


def gather_halo(src_ref, target):
    lane = lane_ids(128, DIM)
    blocks = []
    for half in range(2):
        total = None
        for k in range(4):
            tile = 4 * half + k
            block = src_ref[:, 128 * tile : 128 * tile + 128]
            shift = (32 * k - target) % 128
            block = pltpu.roll(block, shift, 1) if shift else block
            total = block if total is None else jnp.where((lane >> 5) == k, block, total)
        blocks.append(total)
    return jnp.concatenate(blocks, axis=1)


def reverse_bits(value, count):
    result = 0
    for bit in range(count.bit_length() - 1):
        result = result * 2 + ((value >> bit) & 1)
    return result


def key_tables(kv_ref, image, key_rows, height, breadth, ka_ref, kn_ref):
    lane = lane_ids(128, 2 * DIM)
    blocks = []
    for i in range(0, key_rows, 4):
        block = take_lanes(kv_ref[i].astype(F32), image, 0)
        for k in range(1, 4):
            block = jnp.where((lane >> 5) == k, take_lanes(kv_ref[i + k].astype(F32), image, k), block)
        blocks.append(block)
    both = jnp.concatenate(blocks, axis=1)
    total = key_rows * 32
    more = aug_rows(key_rows)
    rank = lax.broadcasted_iota(jnp.int32, (more, total), 0)
    key = lax.broadcasted_iota(jnp.int32, (more, total), 1)
    key_r, key_c = key >> 5, key & 31
    half = key_rows + 32
    low = rank >= half
    rank_in = jnp.where(low, rank - half, rank)
    hit = rank_in == jnp.where(rank_in < key_rows, key_r, key_c + key_rows)
    invalid = (key_r * ROWS >= height) | (key_c * ROWS >= breadth)
    table = jnp.where(rank < 2 * half, jnp.where(hit, 1.0, 0.0), 0.0)
    table = jnp.where((rank == 2 * half) & invalid, NEG_FILL, table)
    full = jnp.concatenate([both[:DIM], table, jnp.zeros((256 - DIM - more, total), F32)], axis=0)
    ka_ref[...] = full[: DIM + more].astype(BF16)
    kn_ref[...] = jnp.transpose(full).astype(BF16)
    return both[DIM:]


def aug_rows(key_rows):
    return 2 * key_rows + 64 + 16


def embed_kernel(ext_ref, row_ref, order_ref, *refs, offset):
    pix_refs, tail_refs, refs = refs[:GROUP], refs[GROUP : 2 * GROUP], refs[2 * GROUP :]
    (perm_ref, tap_ref, wp_ref, wqkv_ref, vec_ref, bkv_ref, kexp_ref,
     patch_ref, x0_ref, q_ref, first_ref, last_ref, nsel_ref, kvt_ref, below_ref, own_ref, s_ref, n_ref, wide_ref) = refs
    images, heights, breadths, row_oks = group_extents(ext_ref, row_ref, offset)

    @pl.when(pl.program_id(0) == 0)
    def _():
        s_ref[...] = jnp.zeros_like(s_ref)
        fill_wide(wide_ref, vec_ref, [0, 1, 2, 42])

    lane = lane_ids(1024, 144)
    for g in range(GROUP):
        for r in range(ROWS):
            for a in range(4):
                s_ref[16 * r + 4 * a : 16 * r + 4 * a + 3, :] = pix_refs[g][0, r, a].astype(F32)
        for a in range(3):
            s_ref[128 + 4 * a : 128 + 4 * a + 3, :] = tail_refs[g][0, 0, a].astype(F32)
        for shifted in range(2):
            rows = s_ref[...]
            if shifted:
                rows = jnp.where(lane < 4, 0.0, pltpu.roll(rows, 4, 1))
            rows = rows.astype(BF16)
            stack = []
            for start in (0, 4, 1, 5):
                for tile in range(TILES):
                    stack.append(jnp.concatenate(
                        [rows[16 * (start + k) : 16 * (start + k) + 16, 128 * tile : 128 * tile + 128] for k in range(4)], axis=1))
            out = dot(jnp.concatenate(stack, axis=0), perm_ref[...]).astype(BF16)
            for which, start in enumerate((0, 4, 1, 5)):
                half, side = which // 2, which % 2
                for tile in range(TILES):
                    block = out[128 * which + 16 * tile : 128 * which + 16 * tile + 16]
                    for phase in range(shifted, 4):
                        top = 64 * half + 16 * phase if not shifted else 128 + 48 * half + 16 * (phase - 1)
                        patch_ref[g, top : top + 16, 256 * tile + 128 * side : 256 * tile + 128 * side + 128] = block[
                            :, 128 * phase : 128 * phase + 128]

    count = pair_count(breadths)

    def active(pair, carry):
        def first_norm(k, embed, mask):
            x0 = (embed + wide_ref[0]) * mask
            hat, _ = normalized(x0)
            return x0, (hat * wide_ref[1] + wide_ref[2]).astype(BF16)

        x0, normed = by_lanes(first_norm, dot(wp_ref[...], load_pair(patch_ref, pair)), pair_mask(pair, breadths, row_oks))
        store_pair(x0_ref, pair, x0)
        store_pair(n_ref, pair, normed.astype(F32))
        (query,) = by_lanes(lambda k, out: ((out + wide_ref[3]).astype(BF16),), dot(wqkv_ref[0:DIM, :], normed))
        store_pair(q_ref, pair, query, 256)
        return carry

    def idle(pair, carry):
        for g in range(GROUP):
            n_ref[g, :, pair_lanes(pair)] = jnp.zeros((DIM, PAIR), F32)
            q_ref[g, :, pair_lanes(pair, 256)] = jnp.zeros((DIM, PAIR), BF16)
        return carry

    lax.fori_loop(0, count, active, 0)
    lax.fori_loop(count, PAIRS, idle, 0)
    for g in range(GROUP):
        q_ref[g, :, 0:256] = jnp.zeros((DIM, 256), BF16)
        q_ref[g, :, 256 + TOKENS : 512 + TOKENS] = jnp.zeros((DIM, 256), BF16)
    rows = []
    for start in (224, 0, 32):
        rows.append(jnp.concatenate(
            [n_ref[g, :, 256 * t + start : 256 * t + start + 32] for g in range(GROUP) for t in range(TILES)], axis=1).astype(BF16))
    edge = dot(wqkv_ref[0:DIM, :], jnp.concatenate(rows[:2], axis=1))
    (edge,) = by_lanes(lambda k, out: ((out + wide_ref[3]).astype(BF16),), edge)
    nsel = dot(jnp.concatenate([row[:, CANVAS_W * g : CANVAS_W * g + CANVAS_W] for g in range(GROUP) for row in rows], axis=0), tap_ref[...])
    nsel = jnp.concatenate([nsel[DIM * k : DIM * k + DIM] for k in range(3 * GROUP)], axis=1).astype(BF16)
    taps = (dot(wqkv_ref[DIM : 3 * DIM, :], nsel) + bkv_ref[...]).astype(BF16)
    for g in range(GROUP):
        last_ref[g] = edge[:, CANVAS_W * g : CANVAS_W * g + CANVAS_W]
        first_ref[g] = edge[:, CANVAS_W * (GROUP + g) : CANVAS_W * (GROUP + g) + CANVAS_W]
        nsel_ref[g] = nsel[:, 384 * g : 384 * g + 384]
        kvt_ref[g] = taps[:, 384 * g : 384 * g + 384]
        product = taps[:, 384 * g : 384 * g + 384].astype(F32) * kexp_ref[...]
        sums = []
        for k in range(3):
            part = product[:, 128 * k : 128 * k + 128]
            sums.append(part + pltpu.roll(part, 96, 1) + pltpu.roll(part, 64, 1))
        store_lanes(below_ref, sums[0], images[g])
        store_lanes(own_ref, sums[1] + sums[2], images[g])


def key_lanes(*lead):
    return pl.BlockSpec(lead + (128,), lambda i, *_: (0,) * len(lead) + (i * GROUP >> 2,))


def specs():
    whole = lambda *shape: pl.BlockSpec(shape, lambda i, *_: (0,) * len(shape))
    per = lambda *shape: pl.BlockSpec((GROUP,) + shape, lambda i, *_: (i,) + (0,) * len(shape))
    return whole, per


def call_embed(ext, row, order, pixels, consts, wts, images, offset):
    whole, per = specs()
    shapes = [
        ((PATCH_ROWS, TOKENS), BF16), ((DIM, TOKENS), F32), ((DIM, PADDED), BF16), ((DIM, CANVAS_W), BF16),
        ((DIM, CANVAS_W), BF16), ((DIM, 384), BF16), ((2 * DIM, 384), BF16)]
    pix = [pl.BlockSpec((1, ROWS, 4, 3, 1024), lambda i, ext, row, order, g=g: (order[offset + i * GROUP + g], 0, 0, 0, 0)) for g in range(GROUP)]
    tail = [pl.BlockSpec((1, 1, 4, 3, 1024), lambda i, ext, row, order, g=g: (order[offset + i * GROUP + g], ROWS - 1, 1, 0, 0)) for g in range(GROUP)]
    return pl.pallas_call(
        functools.partial(embed_kernel, offset=offset),
        grid_spec=pltpu.PrefetchScalarGridSpec(
            num_scalar_prefetch=3, grid=(images // GROUP,),
            in_specs=pix + tail + [
                whole(512, 512), whole(CANVAS_W, 128), whole(DIM, PATCH_ROWS), whole(3 * DIM, DIM), whole(DIM, 64),
                whole(2 * DIM, 1), whole(2 * DIM, 384)],
            out_specs=[per(*s) for s, _ in shapes] + [key_lanes(2 * DIM)] * 2,
            scratch_shapes=[pltpu.VMEM((144, 1024), F32), pltpu.VMEM((GROUP, DIM, TOKENS), F32), pltpu.VMEM((4, DIM, 128), F32)]),
        out_shape=[jax.ShapeDtypeStruct((images,) + s, t) for s, t in shapes]
        + [jax.ShapeDtypeStruct((2 * DIM, 32 * images), F32)] * 2,
        compiler_params=pltpu.CompilerParams(vmem_limit_bytes=VMEM_BYTES),
        cost_estimate=pl.CostEstimate(flops=images * 2_000_000_000, bytes_accessed=images * 4_000_000, transcendentals=0),
        name="embed",
    )(ext, row, order, *[pixels] * (2 * GROUP), consts["perm"], consts["tap"], wts["wp"], wts["wqkv_t"], wts["vec"], wts["b_kv"], wts["kexp"])


def pool_norm_kernel(own_ref, got_ref, vec_ref, kv_ref):
    for member in range(2):
        part = slice(member * DIM, member * DIM + DIM)
        hat, _ = normalized(own_ref[part] + got_ref[part])
        kv_ref[part] = (hat * column(vec_ref, 5 + 2 * member) + column(vec_ref, 6 + 2 * member)).astype(BF16)


def call_pool_norm(own, got, vec):
    return pl.pallas_call(
        pool_norm_kernel, out_shape=jax.ShapeDtypeStruct(own.shape, BF16), name="pool_norm",
        cost_estimate=pl.CostEstimate(flops=own.size * 10, bytes_accessed=own.size * 10, transcendentals=0))(own, got, vec)


def pool_back_kernel(own_ref, got_ref, grad_ref, vec_ref, pre_ref, sums_ref):
    for member in range(2):
        part = slice(member * DIM, member * DIM + DIM)
        hat, rstd = normalized(own_ref[part] + got_ref[part])
        grad = grad_ref[part].astype(F32)
        pre_ref[part] = norm_back(grad, hat, rstd, column(vec_ref, 5 + 2 * member))
        sums_ref[2 * member] = fold_lanes(grad * hat)
        sums_ref[2 * member + 1] = fold_lanes(grad)


def call_pool_back(own, got, grad, vec):
    return pl.pallas_call(
        pool_back_kernel,
        out_shape=[jax.ShapeDtypeStruct(own.shape, F32), jax.ShapeDtypeStruct((4, DIM, 128), F32)], name="pool_back",
        cost_estimate=pl.CostEstimate(flops=own.size * 20, bytes_accessed=own.size * 16, transcendentals=0))(own, got, grad, vec)


def lane_bit(lane, bit):
    return (lane & bit) != 0


def relative_terms(block, products, key_rows):
    lane = lane_ids(128, WIN)
    parts = [products[WIN * s : WIN * s + WIN] for s in range(8)]
    for bit in (1, 2, 4):
        chosen = lane_bit(lane, bit)
        parts = [jnp.where(chosen, parts[2 * k + 1], parts[2 * k]) for k in range(len(parts) // 2)]
    by_col = parts[0]
    for bit, step in ((8, 1), (16, 2)):
        by_col = jnp.where(lane_bit(lane, bit), by_col, pltpu.roll(by_col, WIN - step, 0))
    by_col = by_col[0:32] if block & 2 else by_col[4:36]
    lane = lane_ids(128, key_rows)
    rows = products[8 * WIN :]
    parts = [rows[key_rows * r : key_rows * r + key_rows] for r in range(4 * (block & 1), 4 * (block & 1) + 4)]
    for bit in (32, 64):
        chosen = lane_bit(lane, bit)
        parts = [jnp.where(chosen, parts[2 * k + 1], parts[2 * k]) for k in range(len(parts) // 2)]
    return jnp.concatenate([parts[0], by_col], axis=0)


def relative_spread(block, grad_terms, key_rows):
    lane = lane_ids(128, WIN)
    by_row = grad_terms[:key_rows]
    if block & 2:
        pieces = [grad_terms[key_rows:], jnp.zeros((WIN - 32, 128), F32)]
    else:
        pieces = [jnp.zeros((4, 128), F32), grad_terms[key_rows:], jnp.zeros((WIN - 36, 128), F32)]
    by_col = jnp.concatenate(pieces, axis=0)
    for bit, step in ((8, 1), (16, 2)):
        by_col = jnp.where(lane_bit(lane, bit), by_col, pltpu.roll(by_col, step, 0))
    parts = [jnp.where((lane & 7) == s, by_col, 0.0) for s in range(8)]
    lane = lane_ids(128, key_rows)
    for r in range(8):
        hit = (lane >> 5) == r - 4 * (block & 1)
        parts.append(jnp.where(hit, by_row, 0.0) if r // 4 == block & 1 else jnp.zeros((key_rows, 128), F32))
    return jnp.concatenate(parts, axis=0).astype(BF16)


def gelu_parts(hidden, slope=False):
    cumulative = 0.5 + 0.5 * lax.erf(hidden * 0.7071067811865476)
    act = (hidden * cumulative).astype(BF16)
    if not slope:
        return (act,)
    return act, cumulative + hidden * (jnp.exp(hidden * hidden * -0.5) * 0.3989422804014327)


def forward_kernel(ext_ref, row_ref, q_ref, top_ref, bot_ref, x0_ref, kv_ref, vec_ref, rw_ref, wprojt_ref, w1t_ref, b1_ref, w2t_ref,
                   hat_ref, terms_ref, att_ref, stat_ref, pool_ref, ka_ref, kn_ref, v_ref, ztop_ref, zbot_ref, pre_ref, wide_ref, wb1_ref,
                   *, offset, key_rows):
    images, heights, breadths, row_oks = group_extents(ext_ref, row_ref, offset)
    depth = DIM + aug_rows(key_rows)

    @pl.when(pl.program_id(0) == 0)
    def _():
        fill_wide(wide_ref, vec_ref, list(range(15, 24)) + [3, 4, 9, 10, 11, 12])
        wb1_ref[...] = jnp.broadcast_to(b1_ref[...], (MLP, 128))

    lane = lane_ids(CANVAS_W, DIM)
    for g in range(GROUP):
        v_ref[g] = key_tables(kv_ref, images[g], key_rows, heights[g], breadths[g], ka_ref, kn_ref.at[g]).astype(BF16)
        for halo_ref, dst_ref, tap_row, target in ((top_ref, ztop_ref, 0, 0), (bot_ref, zbot_ref, 2, 96)):
            halo = halo_ref[g].astype(F32)
            left = jnp.where(lane == 0, 0.0, pltpu.roll(halo, 1, 1))
            right = jnp.where(lane == CANVAS_W - 1, 0.0, pltpu.roll(halo, CANVAS_W - 1, 1))
            taps = [wide(wide_ref, 3 * tap_row + k, CANVAS_W) for k in range(3)]
            spread_halo(dst_ref.at[g], taps[0] * left + taps[1] * halo + taps[2] * right, target)
    pool_ref[...] = jnp.zeros_like(pool_ref)

    def step(pair, carry):
        for group in range(0, DIM, 16):
            part = slice(group, group + 16)
            taps = [wide_ref[k, part] for k in range(9)]
            for g in range(GROUP):
                window = q_ref[g, part, pl.ds(pl.multiple_of(pair * PAIR, 128), PAIR + 512)].astype(F32)
                for tile in range(2):
                    sums = []
                    for side in range(2):
                        shifts = col_shifts(window, 256 + 256 * tile + 128 * side)
                        sums.append([sum(taps[3 * r + c] * shifts[c] for c in range(3)) for r in range(3)])
                    halo = pl.ds(pl.multiple_of((2 * pair + tile) * 128, 128), 128)
                    down = rows_down(sums[0][0], sums[1][0], ztop_ref[g, part, halo])
                    up = rows_up(sums[0][2], sums[1][2], zbot_ref[g, part, halo])
                    for side in range(2):
                        base = PAIR * g + 256 * tile + 128 * side
                        pre_ref[part, base : base + 128] = sums[side][1] + down[side] + up[side]

        def query_of(k, pre):
            hat, rstd = normalized(pre)
            return hat, (hat * wide_ref[9] + wide_ref[10]).astype(BF16), rstd

        hat, query, rstd = by_lanes(query_of, pre_ref[...])
        store_pair(hat_ref, pair, hat)

        def extra_of(k, products):
            terms = relative_terms(k, products, key_rows) * (DIM**0.5)
            high = terms.astype(BF16).astype(F32)
            return (jnp.concatenate([high, terms - high, jnp.ones((16, 128), F32)], axis=0).astype(BF16),)

        (extra,) = by_lanes(extra_of, dot(rw_ref[pair], query))
        store_pair(terms_ref, pair, extra)

        def softmax(k, scores):
            peak = jnp.max(scores, axis=0, keepdims=True)
            weights = jnp.exp2((scores - peak) * EXP2_SCALE)
            inverse = 1.0 / jnp.sum(weights, axis=0, keepdims=True)
            return (weights * inverse).astype(BF16), peak, inverse

        long_query = by_image(jnp.concatenate([query, extra], axis=0))
        scores = jnp.concatenate([dot(kn_ref[g, :, :depth], long_query[g]) for g in range(GROUP)], axis=1)
        probs, peak, inverse = by_lanes(softmax, scores)
        store_pair(stat_ref, pair, jnp.concatenate([peak, inverse, rstd, jnp.zeros((5, GROUP * PAIR), F32)], axis=0))
        mixed = by_image(probs)
        mixed = jnp.concatenate([dot(v_ref[g], mixed[g]) for g in range(GROUP)], axis=1)
        attended = (mixed + query.astype(F32)).astype(BF16)
        store_pair(att_ref, pair, attended)

        def second_norm(k, x0, out):
            x1 = x0 + (out + wide_ref[11])
            hat_two, _ = normalized(x1)
            return x1, (hat_two * wide_ref[12] + wide_ref[13]).astype(BF16)

        x1, normed = by_lanes(second_norm, load_pair(x0_ref, pair), dot(wprojt_ref[...], attended))
        (act,) = by_blocks(lambda part, hidden: gelu_parts(hidden + wb1_ref[part]), 64, dot(w1t_ref[...], normed))

        def third_norm(k, x1, out, mask):
            hat_three, _ = normalized(x1 + (out + wide_ref[14]))
            return (hat_three * mask,)

        (kept,) = by_lanes(third_norm, x1, dot(w2t_ref[...], act), pair_mask(pair, breadths, row_oks))
        for g, part in enumerate(by_image(kept)):
            pool_ref[g] += fold_lanes(part)
        return carry

    lax.fori_loop(0, pair_count(breadths), step, 0)


def call_forward(ext, row, q, top, bot, x0, kv, wts, offset):
    whole, per = specs()
    images, key_rows = q.shape[0], kv.shape[0]
    more = aug_rows(key_rows)
    shapes = [((DIM, TOKENS), F32), ((more, TOKENS), BF16), ((DIM, TOKENS), BF16), ((8, TOKENS), F32), ((DIM, 128), F32)]
    keys = key_rows * 32
    return pl.pallas_call(
        functools.partial(forward_kernel, offset=offset, key_rows=key_rows),
        grid_spec=pltpu.PrefetchScalarGridSpec(
            num_scalar_prefetch=2, grid=(images // GROUP,),
            in_specs=[
                per(DIM, PADDED), per(DIM, CANVAS_W), per(DIM, CANVAS_W), per(DIM, TOKENS),
                key_lanes(key_rows, 2 * DIM),
                whole(DIM, 64), whole(PAIRS, 8 * WIN + 8 * key_rows, DIM), whole(DIM, DIM), whole(MLP, DIM), whole(MLP, 1),
                whole(DIM, MLP)],
            out_specs=[per(*s) for s, _ in shapes],
            scratch_shapes=[
                pltpu.VMEM((DIM + more, keys), BF16), pltpu.VMEM((GROUP, keys, 256), BF16), pltpu.VMEM((GROUP, DIM, keys), BF16),
                pltpu.VMEM((GROUP, DIM, 1024), F32), pltpu.VMEM((GROUP, DIM, 1024), F32), pltpu.VMEM((DIM, GROUP * PAIR), F32),
                pltpu.VMEM((15, DIM, 128), F32), pltpu.VMEM((MLP, 128), F32)]),
        out_shape=[jax.ShapeDtypeStruct((images,) + s, t) for s, t in shapes],
        compiler_params=pltpu.CompilerParams(vmem_limit_bytes=VMEM_BYTES),
        cost_estimate=pl.CostEstimate(flops=images * 5_000_000_000, bytes_accessed=images * 4_000_000, transcendentals=0),
        name="forward",
    )(ext, row, q, top, bot, x0, kv, wts["vec"], wts["rw"], wts["wproj_t"], wts["w1_t"], wts["b1"], wts["w2_t"])


def backward_kernel(ext_ref, row_ref, hat_ref, terms_ref, att_ref, stat_ref, x0_ref, q_ref, top_ref, bot_ref, kv_ref, gvec_ref, vec_ref,
                    rwt_ref, wprojt_ref, wproj_ref, w1t_ref, w1_ref, b1_ref, w2t_ref, w2_ref,
                    dx1_ref, dq_ref, up_ref, down_ref, dkv_ref, a2_ref, a1_ref, ap_ref, av_ref, ak_ref, ar_ref,
                    ka_ref, kn_ref, vn_ref, dp_ref, qtop_ref, qbot_ref, ru_ref, rd_ref, dk_ref, dv_ref, wide_ref, wb1_ref,
                    *, offset, key_rows, slots):
    images, heights, breadths, row_oks = group_extents(ext_ref, row_ref, offset)
    depth = DIM + aug_rows(key_rows)
    count = pair_count(breadths)

    @pl.when(pl.program_id(0) == 0)
    def _():
        for ref in (a2_ref, a1_ref, ap_ref, av_ref, ak_ref, ar_ref, ru_ref, rd_ref):
            ref[...] = jnp.zeros_like(ref)
        fill_wide(wide_ref, vec_ref, list(range(15, 24)) + [3, 4, 9, 10, 11, 12, 13])
        wb1_ref[...] = jnp.broadcast_to(b1_ref[...], (MLP, 128))

    for g in range(GROUP):
        values = key_tables(kv_ref, images[g], key_rows, heights[g], breadths[g], ka_ref.at[g], kn_ref.at[g])
        padded_values = jnp.concatenate([values, jnp.zeros((128 - DIM, values.shape[1]), F32)], axis=0)
        vn_ref[g] = jnp.transpose(padded_values).astype(BF16)
        spread_halo(qtop_ref.at[g], top_ref[g].astype(F32), 0)
        spread_halo(qbot_ref.at[g], bot_ref[g].astype(F32), 96)
    for ref in (dk_ref, dv_ref, dp_ref):
        ref[...] = jnp.zeros_like(ref)

    def step(pair, carry):
        ones = jnp.ones((16, GROUP * PAIR), BF16)
        attended = load_pair(att_ref, pair)

        def second_norm(k, x0, out):
            x1 = x0 + (out + wide_ref[11])
            hat, rstd = normalized(x1)
            return x1, hat, rstd, (hat * wide_ref[12] + wide_ref[13]).astype(BF16)

        x1, hat_two, rstd_two, normed = by_lanes(second_norm, load_pair(x0_ref, pair), dot(wprojt_ref[...], attended))
        act, slope = by_blocks(lambda part, hidden: gelu_parts(hidden + wb1_ref[part], True), 64, dot(w1t_ref[...], normed))

        def third_norm(k, x1, out, mask):
            hat, rstd = normalized(x1 + (out + wide_ref[14]))
            grad = norm_back(gvec_ref[k * 128 // PAIR] * mask, hat, rstd, wide_ref[15])
            return grad, grad.astype(BF16)

        grad_x2, grad_mlp = by_lanes(third_norm, x1, dot(w2t_ref[...], act), pair_mask(pair, breadths, row_oks))
        a2_ref[...] += dot_nt(grad_mlp, jnp.concatenate([act, ones], axis=0))
        (grad_hidden,) = by_blocks(lambda part, grad, slope: ((grad * slope).astype(BF16),), 64, dot(w2_ref[...], grad_mlp), slope)
        a1_ref[...] += dot_nt(jnp.concatenate([normed, ones], axis=0), grad_hidden)

        def second_back(k, grad, hat, rstd, grad_x2):
            total = grad_x2 + norm_back(grad, hat, rstd, wide_ref[12])
            return total, total.astype(BF16), grad * hat

        grad_normed = dot(w1_ref[...], grad_hidden)
        grad_x1, grad_proj, scaled = by_lanes(second_back, grad_normed, hat_two, rstd_two, grad_x2)
        av_ref[0] += fold_lanes(scaled)
        av_ref[1] += fold_lanes(grad_normed)
        store_pair(dx1_ref, pair, grad_x1)
        ap_ref[...] += dot_nt(jnp.concatenate([attended, ones], axis=0), grad_proj)
        grad_att = dot(wproj_ref[...], grad_proj)
        grad_att_low = grad_att.astype(BF16)
        hat = load_pair(hat_ref, pair)
        (query,) = by_lanes(lambda k, hat: ((hat * wide_ref[9] + wide_ref[10]).astype(BF16),), hat)
        long_query = by_image(jnp.concatenate([query, load_pair(terms_ref, pair)], axis=0))
        scores = jnp.concatenate([dot(kn_ref[g, :, :depth], long_query[g]) for g in range(GROUP)], axis=1)
        low = by_image(grad_att_low)
        grad_probs = jnp.concatenate([dot(vn_ref[g, :, :DIM], low[g]) for g in range(GROUP)], axis=1)
        stat = load_pair(stat_ref, pair)

        def softmax_back(k, scores, grad_probs, stat):
            probs = jnp.exp2((scores - stat[0:1]) * EXP2_SCALE) * stat[1:2]
            inner = jnp.sum(probs * grad_probs, axis=0, keepdims=True)
            return probs.astype(BF16), (probs * (grad_probs - inner)).astype(BF16)

        probs, grad_scores = by_lanes(softmax_back, scores, grad_probs, stat)
        probs, grad_scores, queries = by_image(probs), by_image(grad_scores), by_image(query)
        back = []
        for g in range(GROUP):
            back.append(dot(ka_ref[g, : DIM + key_rows + 32, :], grad_scores[g]))
            dv_ref[g] += dot_nt(low[g], probs[g])
            dk_ref[g] += dot_nt(queries[g], grad_scores[g])
        back = jnp.concatenate(back, axis=1)
        (spread,) = by_lanes(lambda k, terms: (relative_spread(k, terms, key_rows),), back[DIM:])
        ar_ref[pair] += dot_nt(query, spread)

        def query_back(k, grad_att, back, far, hat, stat):
            grad = grad_att + back * SCALE + far
            return norm_back(grad, hat, stat[2:3], wide_ref[9]), grad * hat, grad

        grad_pre, scaled, grad = by_lanes(query_back, grad_att, back[:DIM], dot(rwt_ref[pair], spread), hat, stat)
        av_ref[2] += fold_lanes(scaled)
        av_ref[3] += fold_lanes(grad)
        store_pair(dp_ref, pair, grad_pre, 256)
        return carry

    lax.fori_loop(0, count, step, 0)
    lane = lane_ids(128, 2 * DIM)
    for g in range(GROUP):
        for i in range(key_rows):
            block = slice(128 * (i // 4), 128 * (i // 4) + 128)
            value = jnp.concatenate([dk_ref[g, :, block] * SCALE, dv_ref[g, :, block]], axis=0)
            value = pltpu.roll(value, (4 + (images[g] & 3) - i % 4) * 32 & 127, 1)
            slot = reverse_bits(jnp.bitwise_xor(row_ref[0], i), key_rows) if slots else i
            dkv_ref[slot] = jnp.where((lane >> 5) == (images[g] & 3), value, dkv_ref[slot])

    def pool_step(pair, carry):
        for group in range(0, DIM, 16):
            part = slice(group, group + 16)
            taps = [wide_ref[k, part] for k in range(9)]
            grads = [None] * 9
            for g in range(GROUP):
                window = dp_ref[g, part, pl.ds(pl.multiple_of(pair * PAIR, 128), PAIR + 512)]
                for tile in range(2):
                    base = pair * PAIR + 256 * tile
                    halo = pl.ds(pl.multiple_of((2 * pair + tile) * 128, 128), 128)
                    query = [q_ref[g, part, pl.ds(pl.multiple_of(base + 256 + 128 * side, 128), 128)].astype(F32) for side in range(2)]
                    above = rows_down(query[0], query[1], qtop_ref[g, part, halo])
                    under = rows_up(query[0], query[1], qbot_ref[g, part, halo])
                    sums = []
                    for side in range(2):
                        left, here, right = col_shifts(window, 256 + 256 * tile + 128 * side)
                        shifts = (right, here, left)
                        sums.append([sum(taps[3 * r + c] * shifts[c] for c in range(3)) for r in range(3)])
                        for r, rows in enumerate((above[side], query[side], under[side])):
                            for c in range(3):
                                term = shifts[c] * rows
                                grads[3 * r + c] = term if grads[3 * r + c] is None else grads[3 * r + c] + term
                    zero = jnp.zeros((16, 128), F32)
                    up = rows_up(sums[0][0], sums[1][0], zero)
                    down = rows_down(sums[0][2], sums[1][2], zero)
                    for side in range(2):
                        lanes = pl.ds(pl.multiple_of(base + 128 * side, 128), 128)
                        dq_ref[g, part, lanes] = sums[side][1] + up[side] + down[side]
                    ru_ref[g, part, halo] = up[2]
                    rd_ref[g, part, halo] = down[2]
            for k in range(9):
                ak_ref[k, part] += grads[k]
        return carry

    def pool_idle(pair, carry):
        for ref in (ru_ref, rd_ref):
            for g in range(GROUP):
                ref[g, :, pl.ds(pl.multiple_of(pair * 256, 128), 256)] = jnp.zeros((DIM, 256), F32)
        return carry

    lax.fori_loop(0, count, pool_step, 0)
    lax.fori_loop(count, PAIRS, pool_idle, 0)
    for g in range(GROUP):
        up_ref[g] = gather_halo(ru_ref.at[g], 96).astype(BF16)
        down_ref[g] = gather_halo(rd_ref.at[g], 0).astype(BF16)


def call_backward(ext, row, hat, terms, att, stat, x0, q, top, bot, kv, gvec, wts, offset, slots=False):
    whole, per = specs()
    images, key_rows = q.shape[0], kv.shape[0]
    more = aug_rows(key_rows)
    keys = key_rows * 32
    window = 8 * WIN + 8 * key_rows
    heads = key_lanes(key_rows, 2 * DIM)
    shapes = [((DIM, TOKENS), F32), ((DIM, TOKENS), F32), ((DIM, CANVAS_W), BF16), ((DIM, CANVAS_W), BF16)]
    sums = [(DIM, MLP + 16), (DIM + 16, MLP), (DIM + 16, DIM), (4, DIM, 128), (9, DIM, 128), (PAIRS, DIM, window)]
    return pl.pallas_call(
        functools.partial(backward_kernel, offset=offset, key_rows=key_rows, slots=slots),
        grid_spec=pltpu.PrefetchScalarGridSpec(
            num_scalar_prefetch=2, grid=(images // GROUP,),
            in_specs=[
                per(DIM, TOKENS), per(more, TOKENS), per(DIM, TOKENS), per(8, TOKENS), per(DIM, TOKENS), per(DIM, PADDED),
                per(DIM, CANVAS_W), per(DIM, CANVAS_W), heads, per(DIM, 1), whole(DIM, 64), whole(PAIRS, DIM, window),
                whole(DIM, DIM), whole(DIM, DIM), whole(MLP, DIM), whole(DIM, MLP), whole(MLP, 1), whole(DIM, MLP), whole(MLP, DIM)],
            out_specs=[per(*s) for s, _ in shapes] + [heads] + [whole(*s) for s in sums],
            scratch_shapes=[
                pltpu.VMEM((GROUP, DIM + more, keys), BF16), pltpu.VMEM((GROUP, keys, 256), BF16), pltpu.VMEM((GROUP, keys, 128), BF16),
                pltpu.VMEM((GROUP, DIM, PADDED), F32)] + [pltpu.VMEM((GROUP, DIM, 1024), F32)] * 4
            + [pltpu.VMEM((GROUP, DIM, keys), F32)] * 2 + [pltpu.VMEM((16, DIM, 128), F32), pltpu.VMEM((MLP, 128), F32)]),
        out_shape=[jax.ShapeDtypeStruct((images,) + s, t) for s, t in shapes]
        + [jax.ShapeDtypeStruct((key_rows, 2 * DIM, 32 * images), F32)] + [jax.ShapeDtypeStruct(s, F32) for s in sums],
        compiler_params=pltpu.CompilerParams(vmem_limit_bytes=VMEM_BYTES),
        cost_estimate=pl.CostEstimate(flops=images * 12_000_000_000, bytes_accessed=images * 6_000_000, transcendentals=0),
        name="backward",
    )(ext, row, hat, terms, att, stat, x0, q, top, bot, kv, gvec, wts["vec"], wts["rw_t"], wts["wproj_t"], wts["wproj"],
      wts["w1_t"], wts["w1"], wts["b1"], wts["w2_t"], wts["w2"])


def embed_back_kernel(ext_ref, row_ref, patch_ref, dq_ref, dx1_ref, rtop_ref, rbot_ref, nsel_ref, kvt_ref, pre_ref, under_ref,
                      wp_ref, vec_ref, wqkv_ref, kexp_ref, tapt_ref,
                      aq_ref, akv_ref, apatch_ref, av_ref, ak_ref, dn_ref, rim_ref, wide_ref, *, offset):
    images, heights, breadths, row_oks = group_extents(ext_ref, row_ref, offset)

    @pl.when(pl.program_id(0) == 0)
    def _():
        for ref in (aq_ref, akv_ref, apatch_ref, av_ref, ak_ref, dn_ref, rim_ref):
            ref[...] = jnp.zeros_like(ref)
        fill_wide(wide_ref, vec_ref, [0, 1, 2])

    lane = lane_ids(128, 2 * DIM)

    def thrice(value, image):
        block = jnp.where((lane >> 5) == 1, take_lanes(value, image, 1), take_lanes(value, image, 0))
        block = jnp.where((lane >> 5) == 2, take_lanes(value, image, 2), block)
        return jnp.where((lane >> 5) == 3, 0.0, block)

    grad_taps = []
    for g in range(GROUP):
        own = thrice(pre_ref[...], images[g])
        spread = jnp.concatenate([thrice(under_ref[...], images[g]), own, own], axis=1)
        ak_ref[...] += kvt_ref[g].astype(F32) * spread
        grad_taps.append((spread * kexp_ref[...]).astype(BF16))
    grad_taps = jnp.concatenate(grad_taps, axis=1)
    nsel = jnp.concatenate([nsel_ref[g] for g in range(GROUP)], axis=1)
    akv_ref[...] += dot_nt(jnp.concatenate([nsel, jnp.ones((16, 384 * GROUP), BF16)], axis=0), grad_taps)
    grad_sel = dot(wqkv_ref[:, DIM : 3 * DIM], grad_taps)
    high = grad_sel.astype(BF16)
    low = (grad_sel - high.astype(F32)).astype(BF16)
    parts = [piece[:, 128 * k : 128 * k + 128] for k in range(3 * GROUP) for piece in (high, low)]
    lines = dot(jnp.concatenate(parts, axis=0), tapt_ref[...])
    for g in range(GROUP):
        for k, start in enumerate((224, 0, 32)):
            first = 2 * DIM * (3 * g + k)
            line = lines[first : first + DIM] + lines[first + DIM : first + 2 * DIM]
            for tile in range(TILES):
                dn_ref[g, :, 256 * tile + start : 256 * tile + start + 32] = line[:, 32 * tile : 32 * tile + 32]
        for halo_ref, start in ((rtop_ref, 0), (rbot_ref, 224)):
            line = halo_ref[g].astype(F32)
            for tile in range(TILES):
                rim_ref[g, :, 256 * tile + start : 256 * tile + start + 32] = line[:, 32 * tile : 32 * tile + 32]

    def step(pair, carry):
        mask = pair_mask(pair, breadths, row_oks)
        patches = load_pair(patch_ref, pair)

        def first_norm(k, embed, mask, grad, rim):
            hat, rstd = normalized((embed + wide_ref[0]) * mask)
            return hat, rstd, (hat * wide_ref[1] + wide_ref[2]).astype(BF16), (grad + rim).astype(BF16)

        hat, rstd, normed, grad_q = by_lanes(first_norm, dot(wp_ref[...], patches), mask, load_pair(dq_ref, pair), load_pair(rim_ref, pair))
        aq_ref[...] += dot_nt(jnp.concatenate([normed, jnp.ones((16, GROUP * PAIR), BF16)], axis=0), grad_q)

        def first_back(k, out, extra, hat, rstd, mask, dx1):
            grad = out + extra
            total = (dx1 + norm_back(grad, hat, rstd, wide_ref[1])) * mask
            high = total.astype(BF16)
            return jnp.concatenate([high, (total - high.astype(F32)).astype(BF16)], axis=0), total, grad * hat, grad

        both, total, scaled, grad = by_lanes(
            first_back, dot(wqkv_ref[:, 0:DIM], grad_q), load_pair(dn_ref, pair), hat, rstd, mask, load_pair(dx1_ref, pair))
        av_ref[0] += fold_lanes(total)
        av_ref[1] += fold_lanes(scaled)
        av_ref[2] += fold_lanes(grad)
        apatch_ref[...] += dot_nt(both, patches)
        return carry

    lax.fori_loop(0, pair_count(breadths), step, 0)


def call_embed_back(ext, row, patches, dq, dx1, rtop, rbot, nsel, kvt, pre, under, consts, wts, offset):
    whole, per = specs()
    images = dq.shape[0]
    sums = [(DIM + 16, DIM), (DIM + 16, 2 * DIM), (2 * DIM, PATCH_ROWS), (3, DIM, 128), (2 * DIM, 384)]
    return pl.pallas_call(
        functools.partial(embed_back_kernel, offset=offset),
        grid_spec=pltpu.PrefetchScalarGridSpec(
            num_scalar_prefetch=2, grid=(images // GROUP,),
            in_specs=[
                per(PATCH_ROWS, TOKENS), per(DIM, TOKENS), per(DIM, TOKENS), per(DIM, CANVAS_W), per(DIM, CANVAS_W),
                per(DIM, 384), per(2 * DIM, 384), key_lanes(2 * DIM), key_lanes(2 * DIM),
                whole(DIM, PATCH_ROWS), whole(DIM, 64), whole(DIM, 3 * DIM), whole(2 * DIM, 384), whole(128, CANVAS_W)],
            out_specs=[whole(*s) for s in sums],
            scratch_shapes=[pltpu.VMEM((GROUP, DIM, TOKENS), F32)] * 2 + [pltpu.VMEM((3, DIM, 128), F32)]),
        out_shape=[jax.ShapeDtypeStruct(s, F32) for s in sums],
        compiler_params=pltpu.CompilerParams(vmem_limit_bytes=VMEM_BYTES),
        cost_estimate=pl.CostEstimate(flops=images * 3_000_000_000, bytes_accessed=images * 3_000_000, transcendentals=0),
        name="embed_back",
    )(ext, row, patches, dq, dx1, rtop, rbot, nsel, kvt, pre, under, wts["wp"], wts["vec"], wts["wqkv"], wts["kexp"], consts["tap_t"])


def bit_count(size):
    return size.bit_length() - 1


def swap(value, axis, bit):
    size = lax.axis_size(axis)
    return lax.ppermute(value, axis, [(i, i ^ (1 << bit)) for i in range(size)])


def shifted(value, axis, step):
    size = lax.axis_size(axis)
    pairs = [(i, i + step) for i in range(size) if 0 <= i + step < size]
    return lax.ppermute(value, axis, pairs)


def summed(value, axis):
    for bit in range(bit_count(lax.axis_size(axis))):
        value = value + swap(value, axis, bit)
    return value


def scatter_slots(value, axis):
    for bit in range(bit_count(lax.axis_size(axis))):
        half = value.shape[0] // 2
        value = value[:half] + swap(value[half:], axis, bit)
    return value[0]


def gather_params(value):
    dims = []
    for axis in ("img", "row"):
        index = lax.axis_index(axis)
        for bit in reversed(range(bit_count(lax.axis_size(axis)))):
            other = swap(value, axis, bit)
            mine_second = (index >> bit) & 1 == 1
            value = jnp.stack([jnp.where(mine_second, other, value), jnp.where(mine_second, value, other)])
            dims.append((axis, bit))
    dims = dims[::-1]
    wanted = [("img", b) for b in reversed(range(bit_count(lax.axis_size("img"))))]
    wanted += [("row", b) for b in reversed(range(bit_count(lax.axis_size("row"))))]
    order = [dims.index(d) for d in wanted]
    value = jnp.transpose(value, order + [value.ndim - 2, value.ndim - 1])
    return value.reshape(-1)


def scatter_grads(flat):
    rows, imgs = lax.axis_size("row"), lax.axis_size("img")
    names = [("img", b) for b in reversed(range(bit_count(imgs)))] + [("row", b) for b in reversed(range(bit_count(rows)))]
    leaf = flat.shape[0] // (rows * imgs)
    value = flat.reshape((2,) * len(names) + (leaf // 128, 128))
    for axis, bits in (("row", range(bit_count(rows))), ("img", range(bit_count(imgs)))):
        index = lax.axis_index(axis)
        for bit in bits:
            place = names.index((axis, bit))
            names.pop(place)
            own = (index >> bit) & 1
            keep = lax.dynamic_index_in_dim(value, own, place, False)
            send = lax.dynamic_index_in_dim(value, 1 - own, place, False)
            value = keep + swap(send, axis, bit)
    return value.reshape(leaf)


def segment_list(canvas_rows, canvas_cols):
    return [
        ("w_patch", (3 * PATCH * PATCH, DIM)),
        ("w_qkv", (DIM, 3 * DIM)),
        ("w_proj", (DIM, DIM)),
        ("w_fc1", (DIM, MLP)),
        ("w_fc2", (MLP, DIM)),
        ("w_head", (DIM, CLASSES)),
        ("rel_rows", (2 * canvas_rows - 8, DIM)),
        ("rel_cols", (2 * canvas_cols - 8, DIM)),
        ("small", (49, DIM)),
        ("b_head", (CLASSES,)),
    ]


def unpack(flat_vec, segments):
    pieces = {}
    position = 0
    for seg_name, seg_shape in segments:
        entries = int(np.prod(seg_shape))
        pieces[seg_name] = flat_vec[position : position + entries].reshape(seg_shape)
        position += entries
    return pieces


def patch_rows(weight):
    taps = jnp.pad(weight.reshape(PATCH, PATCH, 3, DIM), ((0, 1), (0, 0), (0, 1), (0, 0)))
    parts = []
    for piece in (taps[:, 3:7], taps[:, 0:3]):
        phases = piece.shape[1]
        parts.append(jnp.transpose(piece.reshape(2, 4, phases, 4, DIM), (0, 2, 1, 3, 4)).reshape(32 * phases, DIM))
    return jnp.concatenate(parts, axis=0)


def patch_rows_back(grad):
    rows = grad.T
    parts = []
    for piece, phases in ((rows[128:], 3), (rows[:128], 4)):
        taps = jnp.transpose(piece.reshape(2, phases, 4, 4, DIM), (0, 2, 1, 3, 4)).reshape(8, phases, 4, DIM)
        parts.append(taps[:PATCH, :, :3])
    return jnp.concatenate(parts, axis=1).reshape(3 * PATCH * PATCH, DIM)


def relative_windows(rel_rows, rel_cols, row_index, key_rows):
    offsets = jnp.flip(rel_cols.reshape(-1, 8, DIM), 0)
    offsets = jnp.transpose(jnp.pad(offsets, ((0, 1), (0, 0), (0, 0))), (1, 0, 2))
    blocks = rel_rows.reshape(2 * key_rows - 1, 8, DIM)
    rows = jnp.transpose(jnp.flip(lax.dynamic_slice_in_dim(blocks, row_index, key_rows, 0), 0), (1, 0, 2))
    rows = rows.reshape(8 * key_rows, DIM)
    windows = []
    for pair in range(PAIRS):
        cols = offsets[:, 24 - 8 * pair : 24 - 8 * pair + WIN].reshape(8 * WIN, DIM)
        windows.append(jnp.concatenate([cols, rows], axis=0))
    return jnp.stack(windows)


def relative_windows_back(grad, row_index, key_rows):
    grad = jnp.transpose(grad, (0, 2, 1))
    cols = grad[:, : 8 * WIN].reshape(PAIRS, 8, WIN, DIM)
    total = 0.0
    for pair in range(PAIRS):
        start = 24 - 8 * pair
        total = total + jnp.pad(cols[pair], ((0, 0), (start, 64 - start - WIN), (0, 0)))
    rel_cols = jnp.flip(jnp.transpose(total[:, :63], (1, 0, 2)), 0).reshape(-1, DIM)
    rows = jnp.sum(grad[:, 8 * WIN :], axis=0).reshape(8, key_rows, DIM)
    rows = jnp.flip(jnp.transpose(rows, (1, 0, 2)), 0)
    blocks = lax.dynamic_update_slice_in_dim(jnp.zeros((2 * key_rows - 1, 8, DIM), F32), rows, row_index, 0)
    return blocks.reshape(-1, DIM), rel_cols


def tap_keep():
    keep = np.ones((3, 4, 32), np.float32)
    keep[:, 3] = 0.0
    keep[:, 0, 0] = 0.0
    return keep


def prepare(weights, row_index, key_rows):
    small = weights["small"]
    vec = jnp.pad(small.astype(F32).T, ((0, 0), (0, 15)))
    kernels = small[9:27].reshape(2, 3, 3, DIM).astype(F32)
    expanded = jnp.pad(jnp.transpose(kernels, (0, 3, 1, 2)), ((0, 0), (0, 0), (0, 0), (0, 1)))
    kexp = (expanded[..., None] * tap_keep()).reshape(2 * DIM, 384)
    windows = relative_windows(weights["rel_rows"], weights["rel_cols"], row_index, key_rows)
    return {
        "vec": vec,
        "kexp": kexp,
        "wp": patch_rows(weights["w_patch"]).T,
        "wqkv": weights["w_qkv"],
        "wqkv_t": weights["w_qkv"].T,
        "b_kv": small[43:45].astype(F32).reshape(2 * DIM, 1),
        "wproj": weights["w_proj"],
        "wproj_t": weights["w_proj"].T,
        "w1": weights["w_fc1"],
        "w1_t": weights["w_fc1"].T,
        "b1": small[45:49].astype(F32).reshape(MLP, 1),
        "w2": weights["w_fc2"],
        "w2_t": weights["w_fc2"].T,
        "rw": windows,
        "rw_t": jnp.transpose(windows, (0, 2, 1)),
    }


def image_loss(pooled, head_w, head_b, teacher, labels, image_total):
    logits = jnp.dot(pooled, head_w, precision=HIGHEST_PREC) + head_b
    log_student = jax.nn.log_softmax(logits, axis=-1)
    log_teacher = jax.nn.log_softmax(teacher, axis=-1)
    onehot = (jnp.arange(CLASSES)[None, :] == labels[:, None]).astype(F32)
    per_image = jnp.sum(jnp.exp(log_teacher) * (log_teacher - log_student), axis=-1) - jnp.sum(onehot * log_student, axis=-1)
    return jnp.sum(per_image) / image_total


def body(flat_params, first_moment, second_moment, pixels, extents, labels, teacher):
    key_rows = lax.axis_size("row")
    row_index = lax.axis_index("row")
    row_lead = row_index == 0
    segments = segment_list(ROWS * key_rows, CANVAS_W)
    full_params = gather_params(flat_params.astype(BF16).reshape(-1, 128))
    weights = unpack(full_params, segments)
    wts = prepare(weights, row_index, key_rows)
    tap = tap_matrix()
    consts = {"perm": jnp.asarray(deinterleave_matrix(), BF16), "tap": jnp.asarray(tap, BF16), "tap_t": jnp.asarray(tap.T, BF16)}
    vectors = weights["small"][27:42].astype(F32)
    row = row_index.astype(jnp.int32).reshape(1)
    images = pixels.shape[0]
    parts = 1
    size = images // parts
    image_total = images * lax.axis_size("img") * 1.0
    head_w = weights["w_head"].astype(F32)
    head_b = weights["b_head"].astype(F32)

    ids = jnp.arange(images)
    widths = extents[:, 1]
    ahead = (widths[None, :] > widths[:, None]) | ((widths[None, :] == widths[:, None]) & (ids[None, :] < ids[:, None]))
    places = jnp.sum(ahead.astype(jnp.int32), axis=1)
    chosen = places[None, :] == ids[:, None]
    order = jnp.sum(jnp.where(chosen, ids[None, :], 0), axis=1)
    ext = jnp.sum(jnp.where(chosen[:, :, None], extents[None], 0), axis=1)

    saved = []
    for part in range(parts):
        patches, x0, q, first, last, nsel, kvt, below, own = call_embed(ext, row, order, pixels, consts, wts, size, part * size)
        top = shifted(last, "row", 1)
        bot = shifted(first, "row", -1)
        got = shifted(below, "row", 1)
        kv = lax.all_gather(call_pool_norm(own, got, wts["vec"]), "row", axis=0)
        saved.append(dict(patches=patches, x0=x0, q=q, top=top, bot=bot, nsel=nsel, kvt=kvt, own=own, got=got, kv=kv))
    for part in range(parts):
        s = saved[part]
        s["fwd"] = call_forward(ext, row, s["q"], s["top"], s["bot"], s["x0"], s["kv"], wts, part * size)
    total = {}

    def add(name, value):
        total[name] = total[name] + value if name in total else value

    sorted_local = jnp.sum(jnp.concatenate([s["fwd"][-1] for s in saved], axis=0), axis=-1)
    local = jnp.sum(jnp.where(chosen[:, :, None], sorted_local[:, None, :], 0.0), axis=0)
    everywhere = summed(local, "row")
    counts = (extents[:, 0] * extents[:, 1]).astype(F32)[:, None]
    pooled = (everywhere * vectors[13] + counts * vectors[14]) / counts

    def loss_of(pooled_now, w, b):
        return image_loss(pooled_now, w, b, teacher, labels, image_total)

    loss_value, loss_back = jax.vjp(loss_of, pooled, head_w, head_b)
    grad_pooled, total["w_head"], total["b_head"] = loss_back(jnp.ones_like(loss_value))
    gvec = grad_pooled / counts
    local_count = jnp.where(row_index * ROWS < extents[:, 0], ROWS * extents[:, 1], 0).astype(F32)[:, None]
    total["g_three"] = jnp.sum(gvec * local, axis=0)
    total["b_three"] = jnp.sum(gvec * local_count, axis=0)
    gvec = jnp.sum(jnp.where(chosen[:, :, None], gvec[None], 0.0), axis=1)[:, :, None]
    for part in range(parts):
        s = saved[part]
        s["bwd"] = call_backward(ext, row, *s["fwd"][:4], s["x0"], s["q"], s["top"], s["bot"], s["kv"], gvec[part * size : part * size + size], wts, part * size, part == parts - 1)
    for part in range(parts):
        s = saved[part]
        dx1, dq, up, down, dkv, a2, a1, ap, av, ak, ar = s["bwd"]
        for name, value in (("a2", a2), ("a1", a1), ("ap", ap), ("av", av), ("ak", ak), ("ar", ar)):
            add(name, value)
        rtop = shifted(down, "row", 1)
        rbot = shifted(up, "row", -1)
        grad_kv = scatter_slots(dkv, "row") if part == parts - 1 else lax.psum_scatter(dkv, "row", scatter_dimension=0)
        pre, pool_sums = call_pool_back(s["own"], s["got"], grad_kv, wts["vec"])
        add("pool_sums", pool_sums)
        under = shifted(pre, "row", -1)
        aq, akv, apatch, av1, akt = call_embed_back(
            ext, row, s["patches"], dq, dx1, rtop, rbot, s["nsel"], s["kvt"], pre, under, consts, wts, part * size)
        for name, value in (("aq", aq), ("akv", akv), ("apatch", apatch), ("av1", av1), ("akt", akt)):
            add(name, value)

    t = total
    lead = jnp.where(row_lead, 1.0, 0.0)
    av, av1 = jnp.sum(t["av"], axis=-1), jnp.sum(t["av1"], axis=-1)
    pool_sums = jnp.sum(t["pool_sums"], axis=-1)
    rel_rows, rel_cols = relative_windows_back(t["ar"], row_index, key_rows)
    taps = jnp.sum((t["akt"].reshape(2, DIM, 3, 4, 32) * tap_keep())[:, :, :, :3], axis=-1)
    kernels = jnp.concatenate([jnp.sum(t["ak"], axis=-1), jnp.transpose(taps, (0, 2, 3, 1)).reshape(18, DIM)], axis=0)
    grad_vectors = jnp.stack([
        av1[0], av1[1], av1[2], av[2], av[3], pool_sums[0], pool_sums[1], pool_sums[2], pool_sums[3],
        t["ap"][DIM], av[0], av[1], t["a2"][:, MLP], t["g_three"], t["b_three"]])
    pieces = [
        patch_rows_back(t["apatch"][:DIM] + t["apatch"][DIM:]),
        jnp.concatenate([t["aq"][:DIM], t["akv"][:DIM]], axis=1),
        t["ap"][:DIM],
        t["a1"][:DIM],
        t["a2"][:, :MLP].T,
        t["w_head"] * lead,
        rel_rows,
        rel_cols,
        kernels,
        grad_vectors,
        t["aq"][DIM],
        t["akv"][DIM],
        t["a1"][DIM],
        t["b_head"] * lead,
    ]
    joined = jnp.concatenate([piece.reshape(-1) for piece in pieces])
    grad_flat = jnp.pad(joined, (0, full_params.shape[0] - joined.shape[0]))
    grad_shard = scatter_grads(grad_flat)
    norm_sq = summed(jnp.sum(grad_shard * grad_shard), "row")
    both = summed(jnp.stack([norm_sq, loss_value]), "img")
    grad_norm = jnp.sqrt(both[0])
    clip_factor = jnp.minimum(1.0, CLIP_NORM / (grad_norm + 1e-06))
    clipped = grad_shard * clip_factor
    moment_one = BETA_FIRST * first_moment + (1.0 - BETA_FIRST) * clipped
    moment_two = BETA_SECOND * second_moment + (1.0 - BETA_SECOND) * clipped * clipped
    fix_one = 1.0 - BETA_FIRST**STEP
    fix_two = 1.0 - BETA_SECOND**STEP
    update = moment_one / fix_one / (jnp.sqrt(moment_two / fix_two) + ADAM_EPS) + WEIGHT_DECAY * flat_params
    new_params = flat_params - LEARN_RATE * update
    return (new_params, moment_one, moment_two, grad_norm, both[1])


def solution(mesh):
    placed = (
        P(("img", "row")),
        P(("img", "row")),
        P(("img", "row")),
        P("img", "row", None, None, None),
        P("img", None),
        P("img"),
        P("img", None),
    )
    return jax.shard_map(
        body,
        mesh=mesh,
        in_specs=placed,
        out_specs=(P(("img", "row")), P(("img", "row")), P(("img", "row")), P(), P()),
        check_vma=False,
    )
```

time: 809 us -> 591 us (0.73)
  Pallas kernels: 506 us -> 352 us
  local copies, waits for them, and re-layouts: 112 us -> 41.9 us
  waiting for transfers between devices: 50.9 us -> 97.3 us
  other arithmetic: 49.3 us -> 20 us
  starting transfers between devices: 81.2 us -> 60.7 us
  between operations: 8.38 us -> 20.7 us
    pallas_call x2 -> x1, Pallas kernels: 139 us -> 79.1 us  [call_forward(): pl.pallas_call(functools.partial(forward_kernel, offset=offset, key_rows=...]
    pallas_call x2 -> x1, Pallas kernels: 239 us -> 188 us  [call_backward(): pl.pallas_call(functools.partial(backward_kernel, offset=offset, key_rows...]
    ppermute x16 -> x0, local copies, waits for them, and re-layouts: 24.6 us -> none  [the longest x12 19.9 us: swap(): return lax.ppermute(value, axis, [(i, i ^ 1 << bit) for i in range(size)])]
    all_gather x0 -> x1, waiting for transfers between devices: none -> 22.7 us  [body(): kv = lax.all_gather(call_pool_norm(own, got, wts['vec']), 'row', axis=0)]
    ppermute x33 -> x21, waiting for transfers between devices: 50.9 us -> 73.1 us  [swap(): return lax.ppermute(value, axis, [(i, i ^ 1 << bit) for i in range(size)])]
    slice x12 -> x3, local copies, waits for them, and re-layouts: 21.1 us -> 1.65 us  [scatter_slots(): value = value[:half] + swap(value[half:], axis, bit)]
    pallas_call x2 -> x1, Pallas kernels: 61.2 us -> 42.6 us  [call_embed_back(): pl.pallas_call(functools.partial(embed_back_kernel, offset=offset), grid_...]
    ppermute x12 -> x6, starting transfers between devices: 34.7 us -> 16.8 us  [shifted(): return lax.ppermute(value, axis, pairs)]
  transfers between devices with their start and end apart: 45 -> 28, of which waited for: 18 -> 21; matrix products, arithmetic and copies ran while one was open for 15% -> 5% of each run, Pallas kernels for 22% -> 0%
where the time goes in v2:
time: 591 us; the launch traced here: 594 us
  Pallas kernels  352 us (60%)
  waiting for transfers between devices  97.3 us (16%)
  starting transfers between devices  60.7 us (10%)
  local copies, waits for them, and re-layouts  41.9 us (7%)
  between operations  20.7 us (4%)
  other arithmetic  20 us (3%)
    pallas_call x1, Pallas kernels, call_backward(): pl.pallas_call(functools.partial(backward_kernel, offset=offset, key_rows...  188 us
    pallas_call x1, Pallas kernels, call_forward(): pl.pallas_call(functools.partial(forward_kernel, offset=offset, key_rows=...  79.1 us
    ppermute x21, waiting for transfers between devices, swap(): return lax.ppermute(value, axis, [(i, i ^ 1 << bit) for i in range(size)])  73.1 us
    ppermute x21, starting transfers between devices, swap(): return lax.ppermute(value, axis, [(i, i ^ 1 << bit) for i in range(size)])  43.8 us
    pallas_call x1, Pallas kernels, call_embed_back(): pl.pallas_call(functools.partial(embed_back_kernel, offset=offset), grid_...  42.6 us
    pallas_call x1, Pallas kernels, call_embed(): pl.pallas_call(functools.partial(embed_kernel, offset=offset), grid_spec=...  38 us
    all_gather x1, waiting for transfers between devices, body(): kv = lax.all_gather(call_pool_norm(own, got, wts['vec']), 'row', axis=0)  22.7 us
    ppermute x6, starting transfers between devices, shifted(): return lax.ppermute(value, axis, pairs)  16.8 us
  transfers between devices with their start and end apart: 28, of which 21 were waited for; matrix products, arithmetic and copies ran while one was open for 5% of the time, Pallas kernels for 0%

profile of v2, /device:TPU:0, one launch (start us, length us, event | category | flops | bytes accessed | tf_op | source)
XLA Modules:
  0.0 594.4 jit_solution(605722318622470968)
XLA Ops:
  8.0 4.0 collective-permute-start
  12.0 1.7 collective-permute-done
  14.6 2.0 collective-permute-start.1
  16.5 2.0 collective-permute-done.1
  18.6 2.0 collective-permute-start.2
  20.6 2.4 collective-permute-done.2
  23.1 2.0 collective-permute-start.3
  26.0 2.3 collective-permute-done.3
  29.3 10.2 %copy.269.refs_0_.refs_1_.refs_2_.refs_3_ = bf16[16,8,7,3,1024]{4,3,2,1,0:T(4,128)(2,1)} copy(bf16[16,8,7,3,1024]{4,1,3,2,0:T(8,128)(2,1)} %param.15) | data formatting | bytes 11010048 | tf_op args[3]
  45.7 38.0 %embed.1 = (bf16[16,224,2048]{2,1,0:T(8,128)(2,1)}, f32[16,96,2048]{2,1,0:T(8,128)}, bf16[16,96,2560]{2,1,0:T(8,128)(2,1)}, bf16[16,96,256]{2,1,0:T(8,128)(2,1)}...) custom-call(s32[16,2]{1,0:T(8,128)} %copy.299.ext_ref, ...), custom_call_target="tpu_custom_call" | custom-call | flops 32000000000 | bytes 64000000 | tf_op jit(solution)/shard_map/embed/pallas_call | solution.py:362
  83.6 2.4 collective-permute-start.7
  86.0 1.5 collective-permute-done.7.got_ref
  87.6 0.8 copy-done
  88.4 2.0 pool_norm.1
  91.0 7.0 %collective-permute-start.5 = (bf16[16,96,256]{2,1,0:T(8,128)(2,1)}, bf16[16,96,256]{2,1,0:T(8,128)(2,1)S(1)}, u32[]{:S(2)}, u32[]{:S(2)}) collective-permute-start(bf16[16,96,256]{2,1,0:T(8,128)(2,1)} %get-tuple-element.39), channel_id=1, source_target_pairs={{0,1},{1,2},{2,3},{3,4},{4,5},{5,6},{6,7},{8,9},{9,10},{10,11},{11... | collective-permute-start | bytes 2359304 | tf_op jit(solution)/shard_map/ppermute | solution.py:860
  98.0 1.3 collective-permute-start.6
  101.3 0.9 copy.290.rw_ref
  103.9 0.8 reshape.234.b1_ref
  105.6 22.7 %all-gather.3.cloned.1.call-done = bf16[1536,512]{1,0:T(8,128)(2,1)} async-done(((bf16[192,512]{1,0:T(8,128)(2,1)}), bf16[1536,512]{1,0:T(8,128)(2,1)}) %all-gather.3.cloned.1.call-update) | async-done | bytes 1572880 | tf_op jit(solution)/shard_map/all_gather | solution.py:1055
  128.3 79.1 %forward.1 = (f32[16,96,2048]{2,1,0:T(8,128)}, bf16[16,96,2048]{2,1,0:T(8,128)(2,1)}, bf16[16,96,2048]{2,1,0:T(8,128)(2,1)}, f32[16,8,2048]{2,1,0:T(8,128)}, f32[16,96,128]{2,1,0:T(8,128)}) custom-call(s32[16,2]{1,0:T(8,128)} %copy.299.ext_ref, s32[1]{0:T(128)} %bitcast.1.row_ref, bf16[16,96,2560]{2,1,0:T(8,128)(2,1)} %get-tuple-element.38.q_ref, ...), custom_call_target="tpu_custom_call" | custom-call | flops 80000000000 | bytes 64000000 | tf_op jit(solution)/shard_map/forward/pallas_call | solution.py:554
  207.5 1.5 reduce_sum.215
  209.4 0.9 collective-permute-done.8
  211.1 2.9 collective-permute-done.9
  214.5 3.1 collective-permute-done.10
  219.8 0.9 multiply_reduce_fusion.2
  220.8 1.2 copy.295.gvec_ref
  222.0 187.9 %backward.1 = (f32[16,96,2048]{2,1,0:T(8,128)}, f32[16,96,2048]{2,1,0:T(8,128)}, bf16[16,96,256]{2,1,0:T(8,128)(2,1)}, bf16[16,96,256]{2,1,0:T(8,128)(2,1)}, f32...) custom-call(s32[16,2]{1,0:T(8,128)} %copy.299.ext_ref, ...), custom_call_target="tpu_custom_call" | custom-call | flops 192000000000 | bytes 96000000 | tf_op jit(solution)/shard_map/backward/pallas_call | solution.py:734
  410.0 1.6 slice.237
  411.6 3.3 collective-permute-start.11
  414.9 1.5 collective-permute-start.12
  416.6 1.8 slice_add_fusion
  418.4 1.9 collective-permute-start.14
  421.8 28.1 %collective-permute-done.14 = f32[2,192,512]{2,1,0:T(8,128)} collective-permute-done((f32[2,192,512]{2,1,0:T(8,128)S(1)}, f32[2,192,512]{2,1,0:T(8,128)}, u32[]{:S(2)}, u32[]{:S(2)}) %collective-permute-start.14) | collective-permute-done | bytes 786464 | tf_op jit(solution)/shard_map/ppermute | solution.py:854
  450.0 1.3 slice_add_fusion.1
  452.8 6.5 %collective-permute-done.15 = f32[1,192,512]{2,1,0:T(8,128)} collective-permute-done((f32[1,192,512]{2,1,0:T(8,128)S(1)}, f32[1,192,512]{2,1,0:T(8,128)}, u32[]{:S(2)}, u32[]{:S(2)}) %collective-permute-start.15) | collective-permute-done | bytes 393248 | tf_op jit(solution)/shard_map/ppermute | solution.py:854
  459.3 1.8 fusion.grad_ref
  461.1 2.4 pool_back.1
  463.5 1.4 collective-permute-start.16
  466.6 0.9 slice_reduce_fusion.1
  468.5 42.6 %embed_back.1 = (f32[112,96]{1,0:T(8,128)}, f32[112,192]{1,0:T(8,128)}, f32[192,224]{1,0:T(8,128)}, f32[3,96,128]{2,1,0:T(8,128)}, f32[192,384]{1,0:T(8,128)}) custom-call(s32[16,2]{1,0:T(8,128)} %copy.299.ext_ref, s32[1]{0:T(128)} %bitcast.1.row_ref, bf16[16,224,2048]{2,1,0:T(8,128)(2,1)} %get-tuple-element.37.patch_ref, ...), custom_call_target="tpu_custom_call" | custom-call | flops 48000000000 | bytes 48000000 | tf_op jit(solution)/shard_map/embed_back/pallas_call | solution.py:831
  511.1 1.0 add_bitcast_fusion
  512.1 0.9 slice.249
  513.7 0.8 slice.248
  515.2 1.1 reduce_sum.222
  516.4 1.1 copy.313
  519.0 6.5 %concatenate.35 = f32[286312]{0:T(1024)S(1)} concatenate(f32[14112]{0:T(1024)S(1)} %reshape_reshape.21, f32[27648]{0:T(1024)S(1)} %reshape.220, f32[9216]{0:T(1024)S(1)} %reshape.221, f32[36864]{0:T(1024)S(1)} %reshape.222, f32[36864]{0:T(1024)S(1)} %reshape.223, f32[96000]{0:T(1024)S(1)} %reshape.224, f32[11520]{0:T(1024)S(1)} %reshape_reshape.22, f32[48384]{0:T(1024)S(1)} %reshape_reshape.23, ...), dimensions={0} | concatenate | bytes 2290496 | tf_op jit(solution)/shard_map/concatenate | solution.py:1126
  526.1 3.5 collective-permute-start.17
  529.5 1.6 collective-permute-done.17
  531.3 1.8 collective-permute-start.18
  533.1 7.6 %collective-permute-done.18 = f32[2,2,2,70,128]{4,3,2,1,0:T(8,128)S(1)} collective-permute-done((f32[2,2,2,70,128]{4,3,2,1,0:T(8,128)S(1)}, f32[2,2,2,70,128]{4,3,2,1,0:T(8,128)S(1)}, u32[]{:S(2)}, u32[]{:S(2)}) %collective-permute-start.18) | collective-permute-done | bytes 286752 | tf_op jit(solution)/shard_map/ppermute | solution.py:854
  540.7 2.1 collective-permute-start.19
  542.8 3.6 collective-permute-done.19
  546.4 10.8 %collective-permute-start.20 = (f32[2,70,128]{2,1,0:T(8,128)S(1)}, f32[2,70,128]{2,1,0:T(8,128)S(1)}, u32[]{:S(2)}, u32[]{:S(2)}) collective-permute-start(f32[2,70,128]{2,1,0:T(8,128)S(1)} %dynamic-slice_bitcast_fusion.3), channel_id=1, source_target_pairs={{0,8},{8,0},{16,24},{24,16},{1,9},{9,1},{17,25},{25,17},{2,10},{10... | collective-permute-start | bytes 215048 | tf_op jit(solution)/shard_map/ppermute | solution.py:854
  557.2 2.3 collective-permute-done.20
  559.6 2.5 collective-permute-start.21
  562.7 1.8 collective-permute-done.21
  565.1 1.2 collective-permute-done.22
  567.7 2.6 collective-permute-start.23
  570.3 1.0 collective-permute-done.23
  572.0 3.1 collective-permute-start.24
  576.3 2.0 collective-permute-start.25
  578.3 1.5 collective-permute-done.25
  579.9 2.4 collective-permute-start.26
  582.3 2.0 collective-permute-done.26
  (266 shorter events, 30.6 us)
Async XLA Ops:
  7.2 21.3 %copy-start.33 = (s32[16,2]{0,1:T(2,128)S(1)}, s32[16,2]{0,1:T(2,128)}, u32[]{:S(2)}) copy-start(s32[16,2]{0,1:T(2,128)} %param.16) | copy-start | bytes 388
  7.2 121.1 %all-gather.3.cloned.1.call-start = ((), (), s32[]{:S(2)}) async-start(), calls=%async_computation | async-start | bytes 1769472 | tf_op jit(solution)/shard_map/all_gather | solution.py:1055
  8.0 5.8 collective-permute-start
  14.6 4.0 collective-permute-start.1
  18.6 4.4 collective-permute-start.2
  23.1 5.2 collective-permute-start.3
  25.8 193.9 %copy-start.27 = (f32[16]{0:T(128)}, f32[16]{0:T(128)S(1)}, u32[]{:S(2)}) copy-start(f32[16]{0:T(128)S(1)} %get-tuple-element.113) | copy-start | bytes 196
  28.4 11.8 %collective-permute-start.4 = (bf16[2,2,2,2,70,128]{5,4,0,1,2,3:T(8,128)(2,1)S(1)}, bf16[2,2,2,2,70,128]{5,4,0,1,2,3:T(8,128)(2,1)S(1)}, u32[]{:S(2)}, u32[]{:S(2)}) collective-permute-start(bf16[2,2,2,2,70,128]{5,4,0,1,2,3:T(8,128)(2,1)S(1)} %pad_maximum_fusion), channel_id=1, source_target_pairs={{0,1},{1,0},{2,3},{3,2},{4,5},{5,4},{6,7},{7,6},{8,9},{9,8},{10,11... | collective-permute-start | bytes 860168 | tf_op jit(solution)/shard_map/ppermute | solution.py:854
  40.5 3.8 copy-start.34
  41.9 41.7 %copy-start.7 = (bf16[96,288]{1,0:T(8,128)(2,1)}, bf16[96,288]{1,0:T(8,128)(2,1)S(1)}, u32[]{:S(2)}) copy-start(bf16[96,288]{1,0:T(8,128)(2,1)S(1)} %reshape.206.wqkv_ref) | copy-start | bytes 165892
  45.7 44.7 %copy-start.1 = (f32[16,1000]{1,0:T(8,128)S(1)}, f32[16,1000]{1,0:T(8,128)}, u32[]{:S(2)}) copy-start(f32[16,1000]{1,0:T(8,128)} %param.18) | copy-start | bytes 192004
  83.6 3.9 collective-permute-start.7
  91.0 14.6 %collective-permute-start.5 = (bf16[16,96,256]{2,1,0:T(8,128)(2,1)}, bf16[16,96,256]{2,1,0:T(8,128)(2,1)S(1)}, u32[]{:S(2)}, u32[]{:S(2)}) collective-permute-start(bf16[16,96,256]{2,1,0:T(8,128)(2,1)} %get-tuple-element.39), channel_id=1, source_target_pairs={{0,1},{1,2},{2,3},{3,4},{4,5},{5,6},{6,7},{8,9},{9,10},{10,11},{11... | collective-permute-start | bytes 2359304 | tf_op jit(solution)/shard_map/ppermute | solution.py:860
  98.0 7.6 %collective-permute-start.6 = (bf16[16,96,256]{2,1,0:T(8,128)(2,1)}, bf16[16,96,256]{2,1,0:T(8,128)(2,1)S(1)}, u32[]{:S(2)}, u32[]{:S(2)}) collective-permute-start(bf16[16,96,256]{2,1,0:T(8,128)(2,1)} %get-tuple-element.40), channel_id=1, source_target_pairs={{1,0},{2,1},{3,2},{4,3},{5,4},{6,5},{7,6},{9,8},{10,9},{11,10},{12... | collective-permute-start | bytes 2359304 | tf_op jit(solution)/shard_map/ppermute | solution.py:860
  102.4 105.0 %copy-start.5 = (bf16[384,96]{1,0:T(8,128)(2,1)}, bf16[384,96]{1,0:T(8,128)(2,1)S(1)}, u32[]{:S(2)}) copy-start(bf16[384,96]{1,0:T(8,128)(2,1)S(1)} %reshape.214.w2_ref) | copy-start | bytes 221188
  103.2 104.3 %copy-start.8 = (bf16[96,384]{1,0:T(8,128)(2,1)}, bf16[96,384]{1,0:T(8,128)(2,1)S(1)}, u32[]{:S(2)}) copy-start(bf16[96,384]{1,0:T(8,128)(2,1)S(1)} %reshape.213.w1_ref) | copy-start | bytes 221188
  104.8 102.6 %copy-start.17 = (bf16[96,96]{1,0:T(8,128)(2,1)}, bf16[96,96]{1,0:T(8,128)(2,1)S(1)}, u32[]{:S(2)}) copy-start(bf16[96,96]{1,0:T(8,128)(2,1)S(1)} %reshape.212.wproj_ref) | copy-start | bytes 55300
  105.5 22.7 %copy-start.38 = (bf16[16,96,256]{2,1,0:T(8,128)(2,1)}, bf16[16,96,256]{2,1,0:T(8,128)(2,1)S(1)}, u32[]{:S(2)}) copy-start(bf16[16,96,256]{2,1,0:T(8,128)(2,1)S(1)} %collective-permute-done.5.top_ref) | copy-start | bytes 2359300
  105.6 22.7 %copy-start.39 = (bf16[16,96,256]{2,1,0:T(8,128)(2,1)}, bf16[16,96,256]{2,1,0:T(8,128)(2,1)S(1)}, u32[]{:S(2)}) copy-start(bf16[16,96,256]{2,1,0:T(8,128)(2,1)S(1)} %collective-permute-done.6.bot_ref) | copy-start | bytes 2359300
  207.4 10.7 %copy-start.35 = (s32[16]{0:T(128)S(1)}, s32[16]{0:T(128)}, u32[]{:S(2)}) copy-start(s32[16]{0:T(128)} %param.17) | copy-start | bytes 196
  209.1 1.2 collective-permute-start.8
  210.3 3.7 collective-permute-start.9
  214.0 196.0 %copy-start.18 = (f32[16,96]{1,0:T(8,128)}, f32[16,96]{1,0:T(8,128)S(1)}, u32[]{:S(2)}) copy-start(f32[16,96]{1,0:T(8,128)S(1)} %add.153) | copy-start | bytes 18436
  214.0 3.7 collective-permute-start.10
  214.0 195.9 %copy-start.29 = (f32[96]{0:T(128)}, f32[96]{0:T(128)S(1)}, u32[]{:S(2)}) copy-start(f32[96]{0:T(128)S(1)} %get-tuple-element.107) | copy-start | bytes 1156
  214.0 195.9 %copy-start.31 = (f32[96]{0:T(128)}, f32[96]{0:T(128)S(1)}, u32[]{:S(2)}) copy-start(f32[96]{0:T(128)S(1)} %get-tuple-element.108) | copy-start | bytes 1156
  217.6 192.3 %copy-start.23 = (f32[16,96]{1,0:T(8,128)}, f32[16,96]{1,0:T(8,128)S(1)}, u32[]{:S(2)}) copy-start(f32[16,96]{1,0:T(8,128)S(1)} %collective-permute-done.10) | copy-start | bytes 18436
  219.8 190.2 %copy-start.9 = (f32[16,1000]{1,0:T(8,128)}, f32[16,1000]{1,0:T(8,128)S(1)}, u32[]{:S(2)}) copy-start(f32[16,1000]{1,0:T(8,128)S(1)} %get-tuple-element.80) | copy-start | bytes 192004
  410.0 6.4 %copy-start.14 = (f32[4,96,128]{2,1,0:T(8,128)S(1)}, f32[4,96,128]{2,1,0:T(8,128)}, u32[]{:S(2)}) copy-start(f32[4,96,128]{2,1,0:T(8,128)} %get-tuple-element.67) | copy-start | bytes 589828
  411.5 5.0 collective-permute-start.13
  411.6 56.1 %collective-permute-start.11 = (bf16[16,96,256]{2,1,0:T(8,128)(2,1)}, bf16[16,96,256]{2,1,0:T(8,128)(2,1)}, u32[]{:S(2)}, u32[]{:S(2)}) collective-permute-start(bf16[16,96,256]{2,1,0:T(8,128)(2,1)} %get-tuple-element.51), channel_id=1, source_target_pairs={{0,1},{1,2},{2,3},{3,4},{4,5},{5,6},{6,7},{8,9},{9,10},{10,11},{11... | collective-permute-start | bytes 2359304 | tf_op jit(solution)/shard_map/ppermute | solution.py:860
  414.9 52.8 %collective-permute-start.12 = (bf16[16,96,256]{2,1,0:T(8,128)(2,1)}, bf16[16,96,256]{2,1,0:T(8,128)(2,1)}, u32[]{:S(2)}, u32[]{:S(2)}) collective-permute-start(bf16[16,96,256]{2,1,0:T(8,128)(2,1)} %get-tuple-element.52), channel_id=1, source_target_pairs={{1,0},{2,1},{3,2},{4,3},{5,4},{6,5},{7,6},{9,8},{10,9},{11,10},{12... | collective-permute-start | bytes 2359304 | tf_op jit(solution)/shard_map/ppermute | solution.py:860
  418.3 1.9 copy-start.2
  418.3 2.8 copy-start.13
  418.4 31.6 %collective-permute-start.14 = (f32[2,192,512]{2,1,0:T(8,128)S(1)}, f32[2,192,512]{2,1,0:T(8,128)}, u32[]{:S(2)}, u32[]{:S(2)}) collective-permute-start(f32[2,192,512]{2,1,0:T(8,128)S(1)} %slice.290), channel_id=1, source_target_pairs={{0,2},{1,3},{2,0},{3,1},{4,6},{5,7},{6,4},{7,5},{8,10},{9,11},{10,... | collective-permute-start | bytes 2359304 | tf_op jit(solution)/shard_map/ppermute | solution.py:854
  451.2 0.8 copy-start.10
  451.3 0.8 copy-start.19
  451.3 0.8 copy-start.24
  451.3 0.8 copy-start.28
  451.3 7.9 %collective-permute-start.15 = (f32[1,192,512]{2,1,0:T(8,128)S(1)}, f32[1,192,512]{2,1,0:T(8,128)}, u32[]{:S(2)}, u32[]{:S(2)}) collective-permute-start(f32[1,192,512]{2,1,0:T(8,128)S(1)} %slice.292), channel_id=1, source_target_pairs={{0,4},{1,5},{2,6},{3,7},{4,0},{5,1},{6,2},{7,3},{8,12},{9,13},{10,... | collective-permute-start | bytes 1179656 | tf_op jit(solution)/shard_map/ppermute | solution.py:854
  452.7 12.2 %copy-start.16 = (f32[112,384]{1,0:T(8,128)S(1)}, f32[112,384]{1,0:T(8,128)}, u32[]{:S(2)}) copy-start(f32[112,384]{1,0:T(8,128)} %get-tuple-element.61) | copy-start | bytes 516100
  452.8 12.2 %copy-start.20 = (f32[112,96]{1,0:T(8,128)S(1)}, f32[112,96]{1,0:T(8,128)}, u32[]{:S(2)}) copy-start(f32[112,96]{1,0:T(8,128)} %get-tuple-element.60) | copy-start | bytes 129028
  452.8 12.2 %copy-start.4 = (f32[9,96,128]{2,1,0:T(8,128)S(1)}, f32[9,96,128]{2,1,0:T(8,128)}, u32[]{:S(2)}) copy-start(f32[9,96,128]{2,1,0:T(8,128)} %get-tuple-element.64) | copy-start | bytes 1327108
  463.5 2.6 copy-start.3
  463.5 4.2 collective-permute-start.16
  465.2 1.1 copy-start.12
  465.3 2.1 copy-start.25
  465.4 2.2 copy-start.15
  468.5 47.7 %copy-start.36 = (f32[96]{0:T(128)S(1)}, f32[96]{0:T(128)}, u32[]{:S(2)}) copy-start(f32[96]{0:T(128)} %get-tuple-element.72) | copy-start | bytes 1156
  468.5 47.7 %copy-start.37 = (f32[96]{0:T(128)S(1)}, f32[96]{0:T(128)}, u32[]{:S(2)}) copy-start(f32[96]{0:T(128)} %get-tuple-element.73) | copy-start | bytes 1156
  511.1 6.7 %copy-start.26 = (f32[3,4,32]{2,1,0:T(4,128)S(1)}, f32[3,4,32]{2,1,0:T(4,128)}, u32[]{:S(2)}) copy-start(f32[3,4,32]{2,1,0:T(4,128)} %constant.109.clone) | copy-start | bytes 4612
  526.1 5.1 collective-permute-start.17
  531.2 54.6 %copy-start.6 = (f32[8960]{0:T(1024)S(1)}, f32[8960]{0:T(1024)}, u32[]{:S(2)}) copy-start(f32[8960]{0:T(1024)} %param.12) | copy-start | bytes 107524
  531.2 54.6 %copy-start.21 = (f32[8960]{0:T(1024)S(1)}, f32[8960]{0:T(1024)}, u32[]{:S(2)}) copy-start(f32[8960]{0:T(1024)} %param.13) | copy-start | bytes 107524
  531.2 54.6 %copy-start.22 = (f32[8960]{0:T(1024)S(1)}, f32[8960]{0:T(1024)}, u32[]{:S(2)}) copy-start(f32[8960]{0:T(1024)} %param.14) | copy-start | bytes 107524
  531.3 9.4 %collective-permute-start.18 = (f32[2,2,2,70,128]{4,3,2,1,0:T(8,128)S(1)}, f32[2,2,2,70,128]{4,3,2,1,0:T(8,128)S(1)}, u32[]{:S(2)}, u32[]{:S(2)}) collective-permute-start(f32[2,2,2,70,128]{4,3,2,1,0:T(8,128)S(1)} %dynamic-slice_bitcast_fusion.1), channel_id=1, source_target_pairs={{0,2},{1,3},{2,0},{3,1},{4,6},{5,7},{6,4},{7,5},{8,10},{9,11},{10,... | collective-permute-start | bytes 860168 | tf_op jit(solution)/shard_map/ppermute | solution.py:854
  540.7 5.7 collective-permute-start.19
  546.4 13.2 %collective-permute-start.20 = (f32[2,70,128]{2,1,0:T(8,128)S(1)}, f32[2,70,128]{2,1,0:T(8,128)S(1)}, u32[]{:S(2)}, u32[]{:S(2)}) collective-permute-start(f32[2,70,128]{2,1,0:T(8,128)S(1)} %dynamic-slice_bitcast_fusion.3), channel_id=1, source_target_pairs={{0,8},{8,0},{16,24},{24,16},{1,9},{9,1},{17,25},{25,17},{2,10},{10... | collective-permute-start | bytes 215048 | tf_op jit(solution)/shard_map/ppermute | solution.py:854
  559.6 4.9 collective-permute-start.21
  565.1 1.2 collective-permute-start.22
  567.7 3.6 collective-permute-start.23
  572.0 3.6 collective-permute-start.24
  576.3 3.5 collective-permute-start.25
  579.9 4.4 collective-permute-start.26
  (5 other events, 3.8 us)
Sparse Core Ops, SparseCore 0:
  90.5 37.7 all-gather.2

commit v3 on v2

--- a/solution.py
+++ b/solution.py
@@ -156,8 +156,9 @@
     return jnp.minimum((widest >> 6) + 1, PAIRS)
 
 
-def group_extents(ext_ref, row_ref, offset):
-    images = [pl.program_id(0) * GROUP + g for g in range(GROUP)]
+def group_extents(ext_ref, row_ref, offset, group=None):
+    group = pl.program_id(0) if group is None else group
+    images = [group * GROUP + g for g in range(GROUP)]
     heights = [ext_ref[offset + image, 0] for image in images]
     breadths = [ext_ref[offset + image, 1] for image in images]
     return images, heights, breadths, [row_ref[0] * ROWS < height for height in heights]
@@ -170,7 +171,7 @@
     after = window[:, base + 256 : base + 384]
     left = jnp.where((lane & 31) == 0, pltpu.roll(before, 97, 1), pltpu.roll(here, 1, 1))
     right = jnp.where((lane & 31) == 31, pltpu.roll(after, 31, 1), pltpu.roll(here, 127, 1))
-    return left, here, right
+    return left.astype(F32), here.astype(F32), right.astype(F32)
 
 
 def rows_down(first, second, entering):
@@ -447,16 +448,14 @@
     return jnp.concatenate(parts, axis=0).astype(BF16)
 
 
-def gelu_parts(hidden, slope=False):
+def gelu_parts(hidden):
     cumulative = 0.5 + 0.5 * lax.erf(hidden * 0.7071067811865476)
-    act = (hidden * cumulative).astype(BF16)
-    if not slope:
-        return (act,)
-    return act, cumulative + hidden * (jnp.exp(hidden * hidden * -0.5) * 0.3989422804014327)
+    slope = cumulative + hidden * (jnp.exp(hidden * hidden * -0.5) * 0.3989422804014327)
+    return (hidden * cumulative).astype(BF16), slope.astype(BF16)
 
 
 def forward_kernel(ext_ref, row_ref, q_ref, top_ref, bot_ref, x0_ref, kv_ref, vec_ref, rw_ref, wprojt_ref, w1t_ref, b1_ref, w2t_ref,
-                   hat_ref, terms_ref, att_ref, stat_ref, pool_ref, ka_ref, kn_ref, v_ref, ztop_ref, zbot_ref, pre_ref, wide_ref, wb1_ref,
+                   hat_ref, query_ref, terms_ref, att_ref, act_ref, slope_ref, hat2_ref, hat3_ref, stat_ref, pool_ref, ka_ref, kn_ref, v_ref, ztop_ref, zbot_ref, pre_ref, wide_ref, wb1_ref,
                    *, offset, key_rows):
     images, heights, breadths, row_oks = group_extents(ext_ref, row_ref, offset)
     depth = DIM + aug_rows(key_rows)
@@ -482,7 +481,7 @@
             part = slice(group, group + 16)
             taps = [wide_ref[k, part] for k in range(9)]
             for g in range(GROUP):
-                window = q_ref[g, part, pl.ds(pl.multiple_of(pair * PAIR, 128), PAIR + 512)].astype(F32)
+                window = q_ref[g, part, pl.ds(pl.multiple_of(pair * PAIR, 128), PAIR + 512)]
                 for tile in range(2):
                     sums = []
                     for side in range(2):
@@ -497,10 +496,11 @@
 
         def query_of(k, pre):
             hat, rstd = normalized(pre)
-            return hat, (hat * wide_ref[9] + wide_ref[10]).astype(BF16), rstd
+            return hat.astype(BF16), (hat * wide_ref[9] + wide_ref[10]).astype(BF16), rstd
 
         hat, query, rstd = by_lanes(query_of, pre_ref[...])
         store_pair(hat_ref, pair, hat)
+        store_pair(query_ref, pair, query)
 
         def extra_of(k, products):
             terms = relative_terms(k, products, key_rows) * (DIM**0.5)
@@ -519,7 +519,6 @@
         long_query = by_image(jnp.concatenate([query, extra], axis=0))
         scores = jnp.concatenate([dot(kn_ref[g, :, :depth], long_query[g]) for g in range(GROUP)], axis=1)
         probs, peak, inverse = by_lanes(softmax, scores)
-        store_pair(stat_ref, pair, jnp.concatenate([peak, inverse, rstd, jnp.zeros((5, GROUP * PAIR), F32)], axis=0))
         mixed = by_image(probs)
         mixed = jnp.concatenate([dot(v_ref[g], mixed[g]) for g in range(GROUP)], axis=1)
         attended = (mixed + query.astype(F32)).astype(BF16)
@@ -527,17 +526,23 @@
 
         def second_norm(k, x0, out):
             x1 = x0 + (out + wide_ref[11])
-            hat_two, _ = normalized(x1)
-            return x1, (hat_two * wide_ref[12] + wide_ref[13]).astype(BF16)
-
-        x1, normed = by_lanes(second_norm, load_pair(x0_ref, pair), dot(wprojt_ref[...], attended))
-        (act,) = by_blocks(lambda part, hidden: gelu_parts(hidden + wb1_ref[part]), 64, dot(w1t_ref[...], normed))
+            hat, rstd = normalized(x1)
+            return x1, (hat * wide_ref[12] + wide_ref[13]).astype(BF16), hat.astype(BF16), rstd
+
+        x1, normed, hat_two, rstd_two = by_lanes(second_norm, load_pair(x0_ref, pair), dot(wprojt_ref[...], attended))
+        store_pair(hat2_ref, pair, hat_two)
+        act, slope = by_blocks(lambda part, hidden: gelu_parts(hidden + wb1_ref[part]), 64, dot(w1t_ref[...], normed))
+        store_pair(act_ref, pair, act)
+        store_pair(slope_ref, pair, slope)
 
         def third_norm(k, x1, out, mask):
-            hat_three, _ = normalized(x1 + (out + wide_ref[14]))
-            return (hat_three * mask,)
-
-        (kept,) = by_lanes(third_norm, x1, dot(w2t_ref[...], act), pair_mask(pair, breadths, row_oks))
+            hat, rstd = normalized(x1 + (out + wide_ref[14]))
+            return hat * mask, hat.astype(BF16), rstd
+
+        kept, hat_three, rstd_three = by_lanes(third_norm, x1, dot(w2t_ref[...], act), pair_mask(pair, breadths, row_oks))
+        store_pair(hat3_ref, pair, hat_three)
+        stats = [peak, inverse, rstd, rstd_two, rstd_three, jnp.zeros((3, GROUP * PAIR), F32)]
+        store_pair(stat_ref, pair, jnp.concatenate(stats, axis=0))
         for g, part in enumerate(by_image(kept)):
             pool_ref[g] += fold_lanes(part)
         return carry
@@ -549,7 +554,8 @@
     whole, per = specs()
     images, key_rows = q.shape[0], kv.shape[0]
     more = aug_rows(key_rows)
-    shapes = [((DIM, TOKENS), F32), ((more, TOKENS), BF16), ((DIM, TOKENS), BF16), ((8, TOKENS), F32), ((DIM, 128), F32)]
+    shapes = [(rows, BF16) for rows in (DIM, DIM, more, DIM, MLP, MLP, DIM, DIM)]
+    shapes = [((rows, TOKENS), kind) for rows, kind in shapes] + [((8, TOKENS), F32), ((DIM, 128), F32)]
     keys = key_rows * 32
     return pl.pallas_call(
         functools.partial(forward_kernel, offset=offset, key_rows=key_rows),
@@ -572,72 +578,72 @@
     )(ext, row, q, top, bot, x0, kv, wts["vec"], wts["rw"], wts["wproj_t"], wts["w1_t"], wts["b1"], wts["w2_t"])
 
 
-def backward_kernel(ext_ref, row_ref, hat_ref, terms_ref, att_ref, stat_ref, x0_ref, q_ref, top_ref, bot_ref, kv_ref, gvec_ref, vec_ref,
-                    rwt_ref, wprojt_ref, wproj_ref, w1t_ref, w1_ref, b1_ref, w2t_ref, w2_ref,
+def backward_kernel(ext_ref, row_ref, hat_ref, query_ref, terms_ref, att_ref, act_ref, slope_ref, hat2_ref, hat3_ref, stat_ref, q_ref, top_ref, bot_ref, kv_ref,
+                    gvec_ref, vec_ref, rwt_ref, wproj_ref, w1_ref, w2_ref,
                     dx1_ref, dq_ref, up_ref, down_ref, dkv_ref, a2_ref, a1_ref, ap_ref, av_ref, ak_ref, ar_ref,
-                    ka_ref, kn_ref, vn_ref, dp_ref, qtop_ref, qbot_ref, ru_ref, rd_ref, dk_ref, dv_ref, wide_ref, wb1_ref,
-                    *, offset, key_rows, slots):
-    images, heights, breadths, row_oks = group_extents(ext_ref, row_ref, offset)
+                    ka_ref, kn_ref, vn_ref, dp_ref, qtop_ref, qbot_ref, ru_ref, rd_ref, dk_ref, dv_ref, wide_ref, *, offset, key_rows):
+    now = pl.program_id(0)
+    steps = pl.num_programs(0) - 1
+    images, heights, breadths, row_oks = group_extents(ext_ref, row_ref, offset, jnp.minimum(now, steps - 1))
+    _, _, former, _ = group_extents(ext_ref, row_ref, offset, jnp.maximum(now - 1, 0))
     depth = DIM + aug_rows(key_rows)
-    count = pair_count(breadths)
+    count = jnp.where(now < steps, pair_count(breadths), 0)
+    former_count = pair_count(former)
+    dp_now, dp_former = now & 1, (now & 1) ^ 1
 
     @pl.when(pl.program_id(0) == 0)
     def _():
         for ref in (a2_ref, a1_ref, ap_ref, av_ref, ak_ref, ar_ref, ru_ref, rd_ref):
             ref[...] = jnp.zeros_like(ref)
-        fill_wide(wide_ref, vec_ref, list(range(15, 24)) + [3, 4, 9, 10, 11, 12, 13])
-        wb1_ref[...] = jnp.broadcast_to(b1_ref[...], (MLP, 128))
+        fill_wide(wide_ref, vec_ref, list(range(15, 24)) + [3, 10, 11, 13])
+        dp_ref[...] = jnp.zeros_like(dp_ref)
 
     for g in range(GROUP):
         values = key_tables(kv_ref, images[g], key_rows, heights[g], breadths[g], ka_ref.at[g], kn_ref.at[g])
         padded_values = jnp.concatenate([values, jnp.zeros((128 - DIM, values.shape[1]), F32)], axis=0)
         vn_ref[g] = jnp.transpose(padded_values).astype(BF16)
-        spread_halo(qtop_ref.at[g], top_ref[g].astype(F32), 0)
-        spread_halo(qbot_ref.at[g], bot_ref[g].astype(F32), 96)
-    for ref in (dk_ref, dv_ref, dp_ref):
+        spread_halo(qtop_ref.at[g], top_ref[g], 0)
+        spread_halo(qbot_ref.at[g], bot_ref[g], 96)
+    for ref in (dk_ref, dv_ref, dp_ref.at[dp_now]):
         ref[...] = jnp.zeros_like(ref)
 
     def step(pair, carry):
         ones = jnp.ones((16, GROUP * PAIR), BF16)
-        attended = load_pair(att_ref, pair)
-
-        def second_norm(k, x0, out):
-            x1 = x0 + (out + wide_ref[11])
-            hat, rstd = normalized(x1)
-            return x1, hat, rstd, (hat * wide_ref[12] + wide_ref[13]).astype(BF16)
-
-        x1, hat_two, rstd_two, normed = by_lanes(second_norm, load_pair(x0_ref, pair), dot(wprojt_ref[...], attended))
-        act, slope = by_blocks(lambda part, hidden: gelu_parts(hidden + wb1_ref[part], True), 64, dot(w1t_ref[...], normed))
-
-        def third_norm(k, x1, out, mask):
-            hat, rstd = normalized(x1 + (out + wide_ref[14]))
-            grad = norm_back(gvec_ref[k * 128 // PAIR] * mask, hat, rstd, wide_ref[15])
+        stat = load_pair(stat_ref, pair)
+
+        def third_back(k, hat, stat, mask):
+            grad = norm_back(gvec_ref[k * 128 // PAIR] * mask, hat.astype(F32), stat[4:5], wide_ref[12])
             return grad, grad.astype(BF16)
 
-        grad_x2, grad_mlp = by_lanes(third_norm, x1, dot(w2t_ref[...], act), pair_mask(pair, breadths, row_oks))
+        grad_x2, grad_mlp = by_lanes(third_back, load_pair(hat3_ref, pair), stat, pair_mask(pair, breadths, row_oks))
+        act = load_pair(act_ref, pair)
         a2_ref[...] += dot_nt(grad_mlp, jnp.concatenate([act, ones], axis=0))
-        (grad_hidden,) = by_blocks(lambda part, grad, slope: ((grad * slope).astype(BF16),), 64, dot(w2_ref[...], grad_mlp), slope)
+        (grad_hidden,) = by_blocks(
+            lambda part, grad, slope: ((grad * slope.astype(F32)).astype(BF16),), 64, dot(w2_ref[...], grad_mlp), load_pair(slope_ref, pair))
+        hat_two = load_pair(hat2_ref, pair)
+        (normed,) = by_lanes(lambda k, hat: ((hat.astype(F32) * wide_ref[10] + wide_ref[11]).astype(BF16),), hat_two)
         a1_ref[...] += dot_nt(jnp.concatenate([normed, ones], axis=0), grad_hidden)
 
-        def second_back(k, grad, hat, rstd, grad_x2):
-            total = grad_x2 + norm_back(grad, hat, rstd, wide_ref[12])
-            return total, total.astype(BF16), grad * hat
+        def second_back(k, grad, hat, stat, grad_x2):
+            hat = hat.astype(F32)
+            total = grad_x2 + norm_back(grad, hat, stat[3:4], wide_ref[10])
+            return total.astype(BF16), grad * hat
 
         grad_normed = dot(w1_ref[...], grad_hidden)
-        grad_x1, grad_proj, scaled = by_lanes(second_back, grad_normed, hat_two, rstd_two, grad_x2)
+        grad_proj, scaled = by_lanes(second_back, grad_normed, hat_two, stat, grad_x2)
         av_ref[0] += fold_lanes(scaled)
         av_ref[1] += fold_lanes(grad_normed)
-        store_pair(dx1_ref, pair, grad_x1)
+        store_pair(dx1_ref, pair, grad_proj)
+        attended = load_pair(att_ref, pair)
         ap_ref[...] += dot_nt(jnp.concatenate([attended, ones], axis=0), grad_proj)
         grad_att = dot(wproj_ref[...], grad_proj)
         grad_att_low = grad_att.astype(BF16)
         hat = load_pair(hat_ref, pair)
-        (query,) = by_lanes(lambda k, hat: ((hat * wide_ref[9] + wide_ref[10]).astype(BF16),), hat)
+        query = load_pair(query_ref, pair)
         long_query = by_image(jnp.concatenate([query, load_pair(terms_ref, pair)], axis=0))
         scores = jnp.concatenate([dot(kn_ref[g, :, :depth], long_query[g]) for g in range(GROUP)], axis=1)
         low = by_image(grad_att_low)
         grad_probs = jnp.concatenate([dot(vn_ref[g, :, :DIM], low[g]) for g in range(GROUP)], axis=1)
-        stat = load_pair(stat_ref, pair)
 
         def softmax_back(k, scores, grad_probs, stat):
             probs = jnp.exp2((scores - stat[0:1]) * EXP2_SCALE) * stat[1:2]
@@ -657,23 +663,14 @@
 
         def query_back(k, grad_att, back, far, hat, stat):
             grad = grad_att + back * SCALE + far
+            hat = hat.astype(F32)
             return norm_back(grad, hat, stat[2:3], wide_ref[9]), grad * hat, grad
 
         grad_pre, scaled, grad = by_lanes(query_back, grad_att, back[:DIM], dot(rwt_ref[pair], spread), hat, stat)
         av_ref[2] += fold_lanes(scaled)
         av_ref[3] += fold_lanes(grad)
-        store_pair(dp_ref, pair, grad_pre, 256)
+        store_pair(dp_ref.at[dp_now], pair, grad_pre.astype(BF16), 256)
         return carry
-
-    lax.fori_loop(0, count, step, 0)
-    lane = lane_ids(128, 2 * DIM)
-    for g in range(GROUP):
-        for i in range(key_rows):
-            block = slice(128 * (i // 4), 128 * (i // 4) + 128)
-            value = jnp.concatenate([dk_ref[g, :, block] * SCALE, dv_ref[g, :, block]], axis=0)
-            value = pltpu.roll(value, (4 + (images[g] & 3) - i % 4) * 32 & 127, 1)
-            slot = reverse_bits(jnp.bitwise_xor(row_ref[0], i), key_rows) if slots else i
-            dkv_ref[slot] = jnp.where((lane >> 5) == (images[g] & 3), value, dkv_ref[slot])
 
     def pool_step(pair, carry):
         for group in range(0, DIM, 16):
@@ -681,11 +678,11 @@
             taps = [wide_ref[k, part] for k in range(9)]
             grads = [None] * 9
             for g in range(GROUP):
-                window = dp_ref[g, part, pl.ds(pl.multiple_of(pair * PAIR, 128), PAIR + 512)]
+                window = dp_ref[dp_former, g, part, pl.ds(pl.multiple_of(pair * PAIR, 128), PAIR + 512)]
                 for tile in range(2):
                     base = pair * PAIR + 256 * tile
                     halo = pl.ds(pl.multiple_of((2 * pair + tile) * 128, 128), 128)
-                    query = [q_ref[g, part, pl.ds(pl.multiple_of(base + 256 + 128 * side, 128), 128)].astype(F32) for side in range(2)]
+                    query = [q_ref[g, part, pl.ds(pl.multiple_of(base + 256 + 128 * side, 128), 128)] for side in range(2)]
                     above = rows_down(query[0], query[1], qtop_ref[g, part, halo])
                     under = rows_up(query[0], query[1], qbot_ref[g, part, halo])
                     sums = []
@@ -694,6 +691,7 @@
                         shifts = (right, here, left)
                         sums.append([sum(taps[3 * r + c] * shifts[c] for c in range(3)) for r in range(3)])
                         for r, rows in enumerate((above[side], query[side], under[side])):
+                            rows = rows.astype(F32)
                             for c in range(3):
                                 term = shifts[c] * rows
                                 grads[3 * r + c] = term if grads[3 * r + c] is None else grads[3 * r + c] + term
@@ -702,7 +700,7 @@
                     down = rows_down(sums[0][2], sums[1][2], zero)
                     for side in range(2):
                         lanes = pl.ds(pl.multiple_of(base + 128 * side, 128), 128)
-                        dq_ref[g, part, lanes] = sums[side][1] + up[side] + down[side]
+                        dq_ref[g, part, lanes] = (sums[side][1] + up[side] + down[side]).astype(BF16)
                     ru_ref[g, part, halo] = up[2]
                     rd_ref[g, part, halo] = down[2]
             for k in range(9):
@@ -715,42 +713,56 @@
                 ref[g, :, pl.ds(pl.multiple_of(pair * 256, 128), 256)] = jnp.zeros((DIM, 256), F32)
         return carry
 
-    lax.fori_loop(0, count, pool_step, 0)
-    lax.fori_loop(count, PAIRS, pool_idle, 0)
+    lax.fori_loop(0, count, lambda pair, carry: step(pair, pool_step(pair, carry)), 0)
+    lax.fori_loop(count, former_count, pool_step, 0)
+    lax.fori_loop(former_count, PAIRS, pool_idle, 0)
+
+    @pl.when(now < steps)
+    def _():
+        lane = lane_ids(128, 2 * DIM)
+        for g in range(GROUP):
+            for i in range(key_rows):
+                block = slice(128 * (i // 4), 128 * (i // 4) + 128)
+                value = jnp.concatenate([dk_ref[g, :, block] * SCALE, dv_ref[g, :, block]], axis=0)
+                value = pltpu.roll(value, (4 + (images[g] & 3) - i % 4) * 32 & 127, 1)
+                slot = reverse_bits(jnp.bitwise_xor(row_ref[0], i), key_rows)
+                dkv_ref[slot] = jnp.where((lane >> 5) == (images[g] & 3), value, dkv_ref[slot])
+
     for g in range(GROUP):
         up_ref[g] = gather_halo(ru_ref.at[g], 96).astype(BF16)
         down_ref[g] = gather_halo(rd_ref.at[g], 0).astype(BF16)
 
 
-def call_backward(ext, row, hat, terms, att, stat, x0, q, top, bot, kv, gvec, wts, offset, slots=False):
-    whole, per = specs()
+def call_backward(ext, row, saved, q, top, bot, kv, gvec, wts, offset):
+    whole, _ = specs()
     images, key_rows = q.shape[0], kv.shape[0]
     more = aug_rows(key_rows)
     keys = key_rows * 32
     window = 8 * WIN + 8 * key_rows
-    heads = key_lanes(key_rows, 2 * DIM)
-    shapes = [((DIM, TOKENS), F32), ((DIM, TOKENS), F32), ((DIM, CANVAS_W), BF16), ((DIM, CANVAS_W), BF16)]
+    steps = images // GROUP
+    now = lambda *shape: pl.BlockSpec((GROUP,) + shape, lambda i, *_: (jnp.minimum(i, steps - 1),) + (0,) * len(shape))
+    former = lambda *shape: pl.BlockSpec((GROUP,) + shape, lambda i, *_: (jnp.maximum(i - 1, 0),) + (0,) * len(shape))
+    heads = pl.BlockSpec((key_rows, 2 * DIM, 128), lambda i, *_: (0, 0, jnp.minimum(i, steps - 1) * GROUP >> 2))
+    shapes = [(DIM, TOKENS), (DIM, TOKENS), (DIM, CANVAS_W), (DIM, CANVAS_W)]
     sums = [(DIM, MLP + 16), (DIM + 16, MLP), (DIM + 16, DIM), (4, DIM, 128), (9, DIM, 128), (PAIRS, DIM, window)]
     return pl.pallas_call(
-        functools.partial(backward_kernel, offset=offset, key_rows=key_rows, slots=slots),
+        functools.partial(backward_kernel, offset=offset, key_rows=key_rows),
         grid_spec=pltpu.PrefetchScalarGridSpec(
-            num_scalar_prefetch=2, grid=(images // GROUP,),
-            in_specs=[
-                per(DIM, TOKENS), per(more, TOKENS), per(DIM, TOKENS), per(8, TOKENS), per(DIM, TOKENS), per(DIM, PADDED),
-                per(DIM, CANVAS_W), per(DIM, CANVAS_W), heads, per(DIM, 1), whole(DIM, 64), whole(PAIRS, DIM, window),
-                whole(DIM, DIM), whole(DIM, DIM), whole(MLP, DIM), whole(DIM, MLP), whole(MLP, 1), whole(DIM, MLP), whole(MLP, DIM)],
-            out_specs=[per(*s) for s, _ in shapes] + [heads] + [whole(*s) for s in sums],
+            num_scalar_prefetch=2, grid=(steps + 1,),
+            in_specs=[now(rows, TOKENS) for rows in (DIM, DIM, more, DIM, MLP, MLP, DIM, DIM, 8)] + [
+                former(DIM, PADDED), former(DIM, CANVAS_W), former(DIM, CANVAS_W), heads, now(DIM, 1), whole(DIM, 64), whole(PAIRS, DIM, window),
+                whole(DIM, DIM), whole(DIM, MLP), whole(MLP, DIM)],
+            out_specs=[now(*shapes[0])] + [former(*s) for s in shapes[1:]] + [heads] + [whole(*s) for s in sums],
             scratch_shapes=[
                 pltpu.VMEM((GROUP, DIM + more, keys), BF16), pltpu.VMEM((GROUP, keys, 256), BF16), pltpu.VMEM((GROUP, keys, 128), BF16),
-                pltpu.VMEM((GROUP, DIM, PADDED), F32)] + [pltpu.VMEM((GROUP, DIM, 1024), F32)] * 4
-            + [pltpu.VMEM((GROUP, DIM, keys), F32)] * 2 + [pltpu.VMEM((16, DIM, 128), F32), pltpu.VMEM((MLP, 128), F32)]),
-        out_shape=[jax.ShapeDtypeStruct((images,) + s, t) for s, t in shapes]
+                pltpu.VMEM((2, GROUP, DIM, PADDED), BF16)] + [pltpu.VMEM((GROUP, DIM, 1024), BF16)] * 2
+            + [pltpu.VMEM((GROUP, DIM, 1024), F32)] * 2 + [pltpu.VMEM((GROUP, DIM, keys), F32)] * 2 + [pltpu.VMEM((13, DIM, 128), F32)]),
+        out_shape=[jax.ShapeDtypeStruct((images,) + s, BF16) for s in shapes]
         + [jax.ShapeDtypeStruct((key_rows, 2 * DIM, 32 * images), F32)] + [jax.ShapeDtypeStruct(s, F32) for s in sums],
         compiler_params=pltpu.CompilerParams(vmem_limit_bytes=VMEM_BYTES),
         cost_estimate=pl.CostEstimate(flops=images * 12_000_000_000, bytes_accessed=images * 6_000_000, transcendentals=0),
         name="backward",
-    )(ext, row, hat, terms, att, stat, x0, q, top, bot, kv, gvec, wts["vec"], wts["rw_t"], wts["wproj_t"], wts["wproj"],
-      wts["w1_t"], wts["w1"], wts["b1"], wts["w2_t"], wts["w2"])
+    )(ext, row, *saved, q, top, bot, kv, gvec, wts["vec"], wts["rw_t"], wts["wproj"], wts["w1"], wts["w2"])
 
 
 def embed_back_kernel(ext_ref, row_ref, patch_ref, dq_ref, dx1_ref, rtop_ref, rbot_ref, nsel_ref, kvt_ref, pre_ref, under_ref,
@@ -781,14 +793,12 @@
     nsel = jnp.concatenate([nsel_ref[g] for g in range(GROUP)], axis=1)
     akv_ref[...] += dot_nt(jnp.concatenate([nsel, jnp.ones((16, 384 * GROUP), BF16)], axis=0), grad_taps)
     grad_sel = dot(wqkv_ref[:, DIM : 3 * DIM], grad_taps)
-    high = grad_sel.astype(BF16)
-    low = (grad_sel - high.astype(F32)).astype(BF16)
-    parts = [piece[:, 128 * k : 128 * k + 128] for k in range(3 * GROUP) for piece in (high, low)]
+    parts = [grad_sel.astype(BF16)[:, 128 * k : 128 * k + 128] for k in range(3 * GROUP)]
     lines = dot(jnp.concatenate(parts, axis=0), tapt_ref[...])
     for g in range(GROUP):
         for k, start in enumerate((224, 0, 32)):
-            first = 2 * DIM * (3 * g + k)
-            line = lines[first : first + DIM] + lines[first + DIM : first + 2 * DIM]
+            first = DIM * (3 * g + k)
+            line = lines[first : first + DIM]
             for tile in range(TILES):
                 dn_ref[g, :, 256 * tile + start : 256 * tile + start + 32] = line[:, 32 * tile : 32 * tile + 32]
         for halo_ref, start in ((rtop_ref, 0), (rbot_ref, 224)):
@@ -802,23 +812,22 @@
 
         def first_norm(k, embed, mask, grad, rim):
             hat, rstd = normalized((embed + wide_ref[0]) * mask)
-            return hat, rstd, (hat * wide_ref[1] + wide_ref[2]).astype(BF16), (grad + rim).astype(BF16)
+            return hat, rstd, (hat * wide_ref[1] + wide_ref[2]).astype(BF16), (grad.astype(F32) + rim).astype(BF16)
 
         hat, rstd, normed, grad_q = by_lanes(first_norm, dot(wp_ref[...], patches), mask, load_pair(dq_ref, pair), load_pair(rim_ref, pair))
         aq_ref[...] += dot_nt(jnp.concatenate([normed, jnp.ones((16, GROUP * PAIR), BF16)], axis=0), grad_q)
 
         def first_back(k, out, extra, hat, rstd, mask, dx1):
             grad = out + extra
-            total = (dx1 + norm_back(grad, hat, rstd, wide_ref[1])) * mask
-            high = total.astype(BF16)
-            return jnp.concatenate([high, (total - high.astype(F32)).astype(BF16)], axis=0), total, grad * hat, grad
-
-        both, total, scaled, grad = by_lanes(
+            total = (dx1.astype(F32) + norm_back(grad, hat, rstd, wide_ref[1])) * mask
+            return total.astype(BF16), total, grad * hat, grad
+
+        low, total, scaled, grad = by_lanes(
             first_back, dot(wqkv_ref[:, 0:DIM], grad_q), load_pair(dn_ref, pair), hat, rstd, mask, load_pair(dx1_ref, pair))
         av_ref[0] += fold_lanes(total)
         av_ref[1] += fold_lanes(scaled)
         av_ref[2] += fold_lanes(grad)
-        apatch_ref[...] += dot_nt(both, patches)
+        apatch_ref[...] += dot_nt(low, patches)
         return carry
 
     lax.fori_loop(0, pair_count(breadths), step, 0)
@@ -827,7 +836,7 @@
 def call_embed_back(ext, row, patches, dq, dx1, rtop, rbot, nsel, kvt, pre, under, consts, wts, offset):
     whole, per = specs()
     images = dq.shape[0]
-    sums = [(DIM + 16, DIM), (DIM + 16, 2 * DIM), (2 * DIM, PATCH_ROWS), (3, DIM, 128), (2 * DIM, 384)]
+    sums = [(DIM + 16, DIM), (DIM + 16, 2 * DIM), (DIM, PATCH_ROWS), (3, DIM, 128), (2 * DIM, 384)]
     return pl.pallas_call(
         functools.partial(embed_back_kernel, offset=offset),
         grid_spec=pltpu.PrefetchScalarGridSpec(
@@ -869,7 +878,7 @@
 def scatter_slots(value, axis):
     for bit in range(bit_count(lax.axis_size(axis))):
         half = value.shape[0] // 2
-        value = value[:half] + swap(value[half:], axis, bit)
+        value = value[:half] + swap(value[half:].astype(BF16), axis, bit).astype(F32)
     return value[0]
 
 
@@ -1080,7 +1089,7 @@
     gvec = jnp.sum(jnp.where(chosen[:, :, None], gvec[None], 0.0), axis=1)[:, :, None]
     for part in range(parts):
         s = saved[part]
-        s["bwd"] = call_backward(ext, row, *s["fwd"][:4], s["x0"], s["q"], s["top"], s["bot"], s["kv"], gvec[part * size : part * size + size], wts, part * size, part == parts - 1)
+        s["bwd"] = call_backward(ext, row, s["fwd"][:-1], s["q"], s["top"], s["bot"], s["kv"], gvec[part * size : part * size + size], wts, part * size)
     for part in range(parts):
         s = saved[part]
         dx1, dq, up, down, dkv, a2, a1, ap, av, ak, ar = s["bwd"]
@@ -1088,7 +1097,7 @@
             add(name, value)
         rtop = shifted(down, "row", 1)
         rbot = shifted(up, "row", -1)
-        grad_kv = scatter_slots(dkv, "row") if part == parts - 1 else lax.psum_scatter(dkv, "row", scatter_dimension=0)
+        grad_kv = scatter_slots(dkv, "row")
         pre, pool_sums = call_pool_back(s["own"], s["got"], grad_kv, wts["vec"])
         add("pool_sums", pool_sums)
         under = shifted(pre, "row", -1)
@@ -1108,7 +1117,7 @@
         av1[0], av1[1], av1[2], av[2], av[3], pool_sums[0], pool_sums[1], pool_sums[2], pool_sums[3],
         t["ap"][DIM], av[0], av[1], t["a2"][:, MLP], t["g_three"], t["b_three"]])
     pieces = [
-        patch_rows_back(t["apatch"][:DIM] + t["apatch"][DIM:]),
+        patch_rows_back(t["apatch"]),
         jnp.concatenate([t["aq"][:DIM], t["akv"][:DIM]], axis=1),
         t["ap"][:DIM],
         t["a1"][:DIM],

time: 591 us -> 522 us (0.88)
  Pallas kernels: 352 us -> 286 us
  waiting for transfers between devices: 97.3 us -> 85.6 us
    pallas_call x1, Pallas kernels: 188 us -> 112 us  [call_backward(): pl.pallas_call(functools.partial(backward_kernel, offset=offset, key_rows...]
    pallas_call x1, Pallas kernels: 79.1 us -> 91.6 us  [call_forward(): pl.pallas_call(functools.partial(forward_kernel, offset=offset, key_rows=...]
    ppermute x21, waiting for transfers between devices: 73.1 us -> 61.6 us  [swap(): return lax.ppermute(value, axis, [(i, i ^ 1 << bit) for i in range(size)])]
    unnamed x83 -> x59, local copies, waits for them, and re-layouts: 12.8 us -> 11.8 us
  transfers between devices with their start and end apart: 28 -> 28, of which waited for: 21 -> 21; matrix products, arithmetic and copies ran while one was open for 5% -> 6% of each run, Pallas kernels for 0% -> 0%
where the time goes in v3:
time: 522 us; the launch traced here: 520 us
  Pallas kernels  286 us (55%)
  waiting for transfers between devices  85.6 us (16%)
  starting transfers between devices  63 us (12%)
  local copies, waits for them, and re-layouts  42.9 us (8%)
  other arithmetic  20.2 us (4%)
  between operations  20.1 us (4%)
    pallas_call x1, Pallas kernels, call_backward(): pl.pallas_call(functools.partial(backward_kernel, offset=offset, key_rows...  112 us
    pallas_call x1, Pallas kernels, call_forward(): pl.pallas_call(functools.partial(forward_kernel, offset=offset, key_rows=...  91.6 us
    ppermute x21, waiting for transfers between devices, swap(): return lax.ppermute(value, axis, [(i, i ^ 1 << bit) for i in range(size)])  61.6 us
    ppermute x21, starting transfers between devices, swap(): return lax.ppermute(value, axis, [(i, i ^ 1 << bit) for i in range(size)])  46.3 us
    pallas_call x1, Pallas kernels, call_embed_back(): pl.pallas_call(functools.partial(embed_back_kernel, offset=offset), grid_...  40.3 us
    pallas_call x1, Pallas kernels, call_embed(): pl.pallas_call(functools.partial(embed_kernel, offset=offset), grid_spec=...  37.5 us
    all_gather x1, waiting for transfers between devices, body(): kv = lax.all_gather(call_pool_norm(own, got, wts['vec']), 'row', axis=0)  22.5 us
    ppermute x6, starting transfers between devices, shifted(): return lax.ppermute(value, axis, pairs)  16.7 us
  transfers between devices with their start and end apart: 28, of which 21 were waited for; matrix products, arithmetic and copies ran while one was open for 6% of the time, Pallas kernels for 0%

profile of v3, /device:TPU:0, one launch (start us, length us, event | category | flops | bytes accessed | tf_op | source)
XLA Modules:
  0.0 520.5 jit_solution(4138928413295052601)
XLA Ops:
  8.0 4.0 collective-permute-start
  12.0 1.7 collective-permute-done
  14.6 2.0 collective-permute-start.1
  16.5 2.0 collective-permute-done.1
  18.6 2.0 collective-permute-start.2
  20.6 2.4 collective-permute-done.2
  23.1 2.0 collective-permute-start.3
  26.0 2.3 collective-permute-done.3
  29.9 10.2 %copy.254.refs_0_.refs_1_.refs_2_.refs_3_ = bf16[16,8,7,3,1024]{4,3,2,1,0:T(4,128)(2,1)} copy(bf16[16,8,7,3,1024]{4,1,3,2,0:T(8,128)(2,1)} %param.15) | data formatting | bytes 11010048 | tf_op args[3]
  46.3 37.5 %embed.1 = (bf16[16,224,2048]{2,1,0:T(8,128)(2,1)}, f32[16,96,2048]{2,1,0:T(8,128)}, bf16[16,96,2560]{2,1,0:T(8,128)(2,1)}, bf16[16,96,256]{2,1,0:T(8,128)(2,1)}...) custom-call(s32[16,2]{1,0:T(8,128)} %copy.281.ext_ref, ...), custom_call_target="tpu_custom_call" | custom-call | flops 32000000000 | bytes 64000000 | tf_op jit(solution)/shard_map/embed/pallas_call | solution.py:363
  83.8 2.4 collective-permute-start.7
  86.3 1.5 collective-permute-done.7.got_ref
  88.5 2.0 pool_norm.1
  91.2 7.0 %collective-permute-start.5 = (bf16[16,96,256]{2,1,0:T(8,128)(2,1)}, bf16[16,96,256]{2,1,0:T(8,128)(2,1)S(1)}, u32[]{:S(2)}, u32[]{:S(2)}) collective-permute-start(bf16[16,96,256]{2,1,0:T(8,128)(2,1)} %get-tuple-element.44), channel_id=1, source_target_pairs={{0,1},{1,2},{2,3},{3,4},{4,5},{5,6},{6,7},{8,9},{9,10},{10,11},{11... | collective-permute-start | bytes 2359304 | tf_op jit(solution)/shard_map/ppermute | solution.py:869
  98.1 1.3 collective-permute-start.6
  101.5 1.0 copy.275.rw_ref
  105.8 22.5 %all-gather.3.cloned.1.call-done = bf16[1536,512]{1,0:T(8,128)(2,1)} async-done(((bf16[192,512]{1,0:T(8,128)(2,1)}), bf16[1536,512]{1,0:T(8,128)(2,1)}) %all-gather.3.cloned.1.call-update) | async-done | bytes 1572880 | tf_op jit(solution)/shard_map/all_gather | solution.py:1064
  128.2 91.6 %forward.1 = (bf16[16,96,2048]{2,1,0:T(8,128)(2,1)}, bf16[16,96,2048]{2,1,0:T(8,128)(2,1)}, bf16[16,96,2048]{2,1,0:T(8,128)(2,1)}, bf16[16,96,2048]{2,1,0:T(8,12...) custom-call(s32[16,2]{1,0:T(8,128)} %copy.281.ext_ref, ...), custom_call_target="tpu_custom_call" | custom-call | flops 80000000000 | bytes 64000000 | tf_op jit(solution)/shard_map/forward/pallas_call | solution.py:560
  219.8 1.5 reduce_sum.215
  221.8 0.8 collective-permute-done.8
  222.7 1.0 collective-permute-start.9
  223.6 2.7 collective-permute-done.9
  226.9 3.1 collective-permute-done.10
  232.1 0.9 multiply_reduce_fusion.2
  233.1 1.2 copy.280.gvec_ref
  234.3 112.1 %backward.1 = (bf16[16,96,2048]{2,1,0:T(8,128)(2,1)}, bf16[16,96,2048]{2,1,0:T(8,128)(2,1)}, bf16[16,96,256]{2,1,0:T(8,128)(2,1)}, bf16[16,96,256]{2,1,0:T(8,128...) custom-call(s32[16,2]{1,0:T(8,128)} %copy.281.ext_ref, ...), custom_call_target="tpu_custom_call" | custom-call | flops 192000000000 | bytes 96000000 | tf_op jit(solution)/shard_map/backward/pallas_call | solution.py:748
  346.5 1.6 slice.327
  348.1 3.3 collective-permute-start.11
  351.4 1.5 collective-permute-start.12
  352.9 1.1 reduce_sum.223
  354.0 1.0 slice_reduce_fusion
  355.1 0.9 slice_bitcast_fusion
  356.1 1.5 convolution_multiply_fusion
  357.6 1.7 convert_add_fusion
  359.4 2.0 collective-permute-start.14
  361.5 16.4 %collective-permute-done.14 = bf16[2,192,512]{2,1,0:T(8,128)(2,1)S(1)} collective-permute-done((bf16[2,192,512]{2,1,0:T(8,128)(2,1)S(1)}, bf16[2,192,512]{2,1,0:T(8,128)(2,1)S(1)}, u32[]{:S(2)}, u32[]{:S(2)}) %collective-permute-start.14) | collective-permute-done | bytes 393248 | tf_op jit(solution)/shard_map/ppermute | solution.py:863
  378.7 5.1 collective-permute-done.15
  384.6 2.4 pool_back.1
  387.0 1.3 collective-permute-start.16
  389.9 0.9 slice_reduce_fusion.1
  390.8 1.1 reduce_sum.224
  392.7 40.3 %embed_back.1 = (f32[112,96]{1,0:T(8,128)}, f32[112,192]{1,0:T(8,128)}, f32[96,224]{1,0:T(8,128)}, f32[3,96,128]{2,1,0:T(8,128)}, f32[192,384]{1,0:T(8,128)}) custom-call(s32[16,2]{1,0:T(8,128)} %copy.281.ext_ref, s32[1]{0:T(128)} %bitcast.1.row_ref, bf16[16,224,2048]{2,1,0:T(8,128)(2,1)} %get-tuple-element.42.patch_ref, ...), custom_call_target="tpu_custom_call" | custom-call | flops 48000000000 | bytes 48000000 | tf_op jit(solution)/shard_map/embed_back/pallas_call | solution.py:840
  434.6 0.9 slice.244
  437.7 1.1 reduce_sum.222
  439.0 1.1 copy.295
  441.6 6.5 %concatenate.35 = f32[286312]{0:T(1024)S(1)} concatenate(f32[14112]{0:T(1024)S(1)} %reshape_reshape.21, f32[27648]{0:T(1024)S(1)} %reshape.220, f32[9216]{0:T(1024)S(1)} %reshape.221, f32[36864]{0:T(1024)S(1)} %reshape.222, f32[36864]{0:T(1024)S(1)} %reshape.223, f32[96000]{0:T(1024)S(1)} %reshape.224, f32[11520]{0:T(1024)S(1)} %reshape_reshape.22, f32[48384]{0:T(1024)S(1)} %reshape_reshape.23, ...), dimensions={0} | concatenate | bytes 2290496 | tf_op jit(solution)/shard_map/concatenate | solution.py:1135
  448.6 2.8 collective-permute-start.17
  451.5 1.6 collective-permute-done.17
  453.2 1.6 collective-permute-start.18
  454.7 7.8 %collective-permute-done.18 = f32[2,2,2,70,128]{4,3,2,1,0:T(8,128)S(1)} collective-permute-done((f32[2,2,2,70,128]{4,3,2,1,0:T(8,128)S(1)}, f32[2,2,2,70,128]{4,3,2,1,0:T(8,128)S(1)}, u32[]{:S(2)}, u32[]{:S(2)}) %collective-permute-start.18) | collective-permute-done | bytes 286752 | tf_op jit(solution)/shard_map/ppermute | solution.py:863
  462.6 2.1 collective-permute-start.19
  464.7 3.6 collective-permute-done.19
  468.3 8.1 %collective-permute-start.20 = (f32[2,70,128]{2,1,0:T(8,128)S(1)}, f32[2,70,128]{2,1,0:T(8,128)S(1)}, u32[]{:S(2)}, u32[]{:S(2)}) collective-permute-start(f32[2,70,128]{2,1,0:T(8,128)S(1)} %dynamic-slice_bitcast_fusion.3), channel_id=1, source_target_pairs={{0,8},{8,0},{16,24},{24,16},{1,9},{9,1},{17,25},{25,17},{2,10},{10... | collective-permute-start | bytes 215048 | tf_op jit(solution)/shard_map/ppermute | solution.py:863
  476.4 2.3 collective-permute-done.20
  478.7 9.8 %collective-permute-start.21 = (f32[70,128]{1,0:T(8,128)S(1)}, f32[70,128]{1,0:T(8,128)S(1)}, u32[]{:S(2)}, u32[]{:S(2)}) collective-permute-start(f32[70,128]{1,0:T(8,128)S(1)} %dynamic-slice_bitcast_fusion.4), channel_id=1, source_target_pairs={{0,16},{8,24},{16,0},{24,8},{1,17},{9,25},{17,1},{25,9},{2,18},{10... | collective-permute-start | bytes 107528 | tf_op jit(solution)/shard_map/ppermute | solution.py:863
  489.2 1.3 collective-permute-done.21
  491.1 1.4 collective-permute-done.22
  493.7 2.7 collective-permute-start.23
  496.4 1.0 collective-permute-done.23
  498.0 2.8 collective-permute-start.24
  500.8 0.9 collective-permute-done.24
  502.3 3.5 collective-permute-done.25
  505.9 2.9 collective-permute-start.26
  508.9 1.5 collective-permute-done.26
  (241 shorter events, 32.4 us)
Async XLA Ops:
  7.2 121.1 %all-gather.3.cloned.1.call-start = ((), (), s32[]{:S(2)}) async-start(), calls=%async_computation | async-start | bytes 1769472 | tf_op jit(solution)/shard_map/all_gather | solution.py:1064
  8.0 5.8 %collective-permute-start = (bf16[70,128]{1,0:T(8,128)(2,1)S(1)}, bf16[70,128]{1,0:T(8,128)(2,1)S(1)}, u32[]{:S(2)}, u32[]{:S(2)}) collective-permute-start(bf16[70,128]{1,0:T(8,128)(2,1)S(1)} %convert_bitcast_fusion), channel_id=1, source_target_pairs={{0,16},{8,24},{16,0},{24,8},{1,17},{9,25},{17,1},{25,9},{2,18},{10... | collective-permute-start | bytes 53768 | tf_op jit(solution)/shard_map/ppermute | solution.py:863
  14.6 4.0 collective-permute-start.1
  18.6 4.4 collective-permute-start.2
  23.1 5.2 %collective-permute-start.3 = (bf16[2,2,2,70,128]{4,3,0,1,2:T(8,128)(2,1)S(1)}, bf16[2,2,2,70,128]{4,3,0,1,2:T(8,128)(2,1)S(1)}, u32[]{:S(2)}, u32[]{:S(2)}) collective-permute-start(bf16[2,2,2,70,128]{4,3,0,1,2:T(8,128)(2,1)S(1)} %pad_maximum_fusion.2), channel_id=1, source_target_pairs={{0,2},{1,3},{2,0},{3,1},{4,6},{5,7},{6,4},{7,5},{8,10},{9,11},{10,... | collective-permute-start | bytes 430088 | tf_op jit(solution)/shard_map/ppermute | solution.py:863
  25.8 206.3 %copy-start.18 = (f32[16]{0:T(128)}, f32[16]{0:T(128)S(1)}, u32[]{:S(2)}) copy-start(f32[16]{0:T(128)S(1)} %get-tuple-element.123) | copy-start | bytes 196
  28.4 12.4 %collective-permute-start.4 = (bf16[2,2,2,2,70,128]{5,4,0,1,2,3:T(8,128)(2,1)S(1)}, bf16[2,2,2,2,70,128]{5,4,0,1,2,3:T(8,128)(2,1)S(1)}, u32[]{:S(2)}, u32[]{:S(2)}) collective-permute-start(bf16[2,2,2,2,70,128]{5,4,0,1,2,3:T(8,128)(2,1)S(1)} %pad_maximum_fusion), channel_id=1, source_target_pairs={{0,1},{1,0},{2,3},{3,2},{4,5},{5,4},{6,7},{7,6},{8,9},{9,8},{10,11... | collective-permute-start | bytes 860168 | tf_op jit(solution)/shard_map/ppermute | solution.py:863
  40.2 4.8 copy-start.22
  42.6 41.3 %copy-start.6 = (bf16[96,288]{1,0:T(8,128)(2,1)}, bf16[96,288]{1,0:T(8,128)(2,1)S(1)}, u32[]{:S(2)}) copy-start(bf16[96,288]{1,0:T(8,128)(2,1)S(1)} %reshape.206.wqkv_ref) | copy-start | bytes 165892
  46.3 44.2 %copy-start.1 = (f32[16,1000]{1,0:T(8,128)S(1)}, f32[16,1000]{1,0:T(8,128)}, u32[]{:S(2)}) copy-start(f32[16,1000]{1,0:T(8,128)} %param.18) | copy-start | bytes 192004
  83.8 3.9 collective-permute-start.7
  87.8 0.8 copy-start
  91.2 14.6 %collective-permute-start.5 = (bf16[16,96,256]{2,1,0:T(8,128)(2,1)}, bf16[16,96,256]{2,1,0:T(8,128)(2,1)S(1)}, u32[]{:S(2)}, u32[]{:S(2)}) collective-permute-start(bf16[16,96,256]{2,1,0:T(8,128)(2,1)} %get-tuple-element.44), channel_id=1, source_target_pairs={{0,1},{1,2},{2,3},{3,4},{4,5},{5,6},{6,7},{8,9},{9,10},{10,11},{11... | collective-permute-start | bytes 2359304 | tf_op jit(solution)/shard_map/ppermute | solution.py:869
  98.1 7.6 %collective-permute-start.6 = (bf16[16,96,256]{2,1,0:T(8,128)(2,1)}, bf16[16,96,256]{2,1,0:T(8,128)(2,1)S(1)}, u32[]{:S(2)}, u32[]{:S(2)}) collective-permute-start(bf16[16,96,256]{2,1,0:T(8,128)(2,1)} %get-tuple-element.45), channel_id=1, source_target_pairs={{1,0},{2,1},{3,2},{4,3},{5,4},{6,5},{7,6},{9,8},{10,9},{11,10},{12... | collective-permute-start | bytes 2359304 | tf_op jit(solution)/shard_map/ppermute | solution.py:869
  102.6 117.2 %copy-start.4 = (bf16[384,96]{1,0:T(8,128)(2,1)}, bf16[384,96]{1,0:T(8,128)(2,1)S(1)}, u32[]{:S(2)}) copy-start(bf16[384,96]{1,0:T(8,128)(2,1)S(1)} %reshape.214.w2_ref) | copy-start | bytes 221188
  103.4 116.4 %copy-start.7 = (bf16[96,384]{1,0:T(8,128)(2,1)}, bf16[96,384]{1,0:T(8,128)(2,1)S(1)}, u32[]{:S(2)}) copy-start(bf16[96,384]{1,0:T(8,128)(2,1)S(1)} %reshape.213.w1_ref) | copy-start | bytes 221188
  105.0 114.8 %copy-start.10 = (bf16[96,96]{1,0:T(8,128)(2,1)}, bf16[96,96]{1,0:T(8,128)(2,1)S(1)}, u32[]{:S(2)}) copy-start(bf16[96,96]{1,0:T(8,128)(2,1)S(1)} %reshape.212.wproj_ref) | copy-start | bytes 55300
  105.7 22.5 %copy-start.26 = (bf16[16,96,256]{2,1,0:T(8,128)(2,1)}, bf16[16,96,256]{2,1,0:T(8,128)(2,1)S(1)}, u32[]{:S(2)}) copy-start(bf16[16,96,256]{2,1,0:T(8,128)(2,1)S(1)} %collective-permute-done.5.top_ref) | copy-start | bytes 2359300
  105.7 22.5 %copy-start.27 = (bf16[16,96,256]{2,1,0:T(8,128)(2,1)}, bf16[16,96,256]{2,1,0:T(8,128)(2,1)S(1)}, u32[]{:S(2)}) copy-start(bf16[16,96,256]{2,1,0:T(8,128)(2,1)S(1)} %collective-permute-done.6.bot_ref) | copy-start | bytes 2359300
  128.2 102.3 %copy-start.23 = (s32[16]{0:T(128)S(1)}, s32[16]{0:T(128)}, u32[]{:S(2)}) copy-start(s32[16]{0:T(128)} %param.17) | copy-start | bytes 196
  221.4 1.2 collective-permute-start.8
  222.7 3.7 collective-permute-start.9
  226.3 8.0 %copy-start.11 = (f32[16,96]{1,0:T(8,128)}, f32[16,96]{1,0:T(8,128)S(1)}, u32[]{:S(2)}) copy-start(f32[16,96]{1,0:T(8,128)S(1)} %add.150) | copy-start | bytes 18436
  226.3 3.7 collective-permute-start.10
  226.4 120.0 %copy-start.20 = (f32[96]{0:T(128)}, f32[96]{0:T(128)S(1)}, u32[]{:S(2)}) copy-start(f32[96]{0:T(128)S(1)} %get-tuple-element.117) | copy-start | bytes 1156
  226.4 120.0 %copy-start.21 = (f32[96]{0:T(128)}, f32[96]{0:T(128)S(1)}, u32[]{:S(2)}) copy-start(f32[96]{0:T(128)S(1)} %get-tuple-element.118) | copy-start | bytes 1156
  230.0 4.4 copy-start.15
  232.1 2.2 copy-start.8
  234.3 121.7 %copy-start.19 = (f32[16]{0:T(128)S(1)}, f32[16]{0:T(128)}, u32[]{:S(2)}) copy-start(f32[16]{0:T(128)} %copy-done.18) | copy-start | bytes 196
  346.4 15.0 %copy-start.2 = (f32[4,96,384]{2,1,0:T(8,128)S(1)}, f32[4,96,384]{2,1,0:T(8,128)}, u32[]{:S(2)}) copy-start(f32[4,96,384]{2,1,0:T(8,128)} %get-tuple-element.73) | copy-start | bytes 1769476
  348.0 9.5 %collective-permute-start.13 = (bf16[4,192,512]{2,1,0:T(8,128)(2,1)S(1)}, bf16[4,192,512]{2,1,0:T(8,128)(2,1)S(1)}, u32[]{:S(2)}, u32[]{:S(2)}) collective-permute-start(bf16[4,192,512]{2,1,0:T(8,128)(2,1)S(1)} %slice.327), channel_id=1, source_target_pairs={{0,1},{1,0},{2,3},{3,2},{4,5},{5,4},{6,7},{7,6},{8,9},{9,8},{10,11... | collective-permute-start | bytes 2359304 | tf_op jit(solution)/shard_map/ppermute | solution.py:863
  348.1 43.8 %collective-permute-start.11 = (bf16[16,96,256]{2,1,0:T(8,128)(2,1)}, bf16[16,96,256]{2,1,0:T(8,128)(2,1)}, u32[]{:S(2)}, u32[]{:S(2)}) collective-permute-start(bf16[16,96,256]{2,1,0:T(8,128)(2,1)} %get-tuple-element.61), channel_id=1, source_target_pairs={{0,1},{1,2},{2,3},{3,4},{4,5},{5,6},{6,7},{8,9},{9,10},{10,11},{11... | collective-permute-start | bytes 2359304 | tf_op jit(solution)/shard_map/ppermute | solution.py:869
  351.4 40.5 %collective-permute-start.12 = (bf16[16,96,256]{2,1,0:T(8,128)(2,1)}, bf16[16,96,256]{2,1,0:T(8,128)(2,1)}, u32[]{:S(2)}, u32[]{:S(2)}) collective-permute-start(bf16[16,96,256]{2,1,0:T(8,128)(2,1)} %get-tuple-element.62), channel_id=1, source_target_pairs={{1,0},{2,1},{3,2},{4,3},{5,4},{6,5},{7,6},{9,8},{10,9},{11,10},{12... | collective-permute-start | bytes 2359304 | tf_op jit(solution)/shard_map/ppermute | solution.py:869
  357.6 30.7 %copy-start.9 = (f32[112,384]{1,0:T(8,128)S(1)}, f32[112,384]{1,0:T(8,128)}, u32[]{:S(2)}) copy-start(f32[112,384]{1,0:T(8,128)} %get-tuple-element.71) | copy-start | bytes 516100
  359.3 29.1 %copy-start.12 = (f32[112,96]{1,0:T(8,128)S(1)}, f32[112,96]{1,0:T(8,128)}, u32[]{:S(2)}) copy-start(f32[112,96]{1,0:T(8,128)} %get-tuple-element.70) | copy-start | bytes 129028
  359.3 29.1 %copy-start.3 = (f32[9,96,128]{2,1,0:T(8,128)S(1)}, f32[9,96,128]{2,1,0:T(8,128)}, u32[]{:S(2)}) copy-start(f32[9,96,128]{2,1,0:T(8,128)} %get-tuple-element.74) | copy-start | bytes 1327108
  359.4 18.6 %collective-permute-start.14 = (bf16[2,192,512]{2,1,0:T(8,128)(2,1)S(1)}, bf16[2,192,512]{2,1,0:T(8,128)(2,1)S(1)}, u32[]{:S(2)}, u32[]{:S(2)}) collective-permute-start(bf16[2,192,512]{2,1,0:T(8,128)(2,1)S(1)} %slice.328), channel_id=1, source_target_pairs={{0,2},{1,3},{2,0},{3,1},{4,6},{5,7},{6,4},{7,5},{8,10},{9,11},{10,... | collective-permute-start | bytes 1179656 | tf_op jit(solution)/shard_map/ppermute | solution.py:863
  361.5 29.3 %copy-start.16 = (f32[1000]{0:T(1024)S(1)}, f32[1000]{0:T(1024)}, u32[]{:S(2)}) copy-start(f32[1000]{0:T(1024)} %get-tuple-element.89) | copy-start | bytes 12004
  378.1 5.7 %collective-permute-start.15 = (bf16[1,192,512]{2,1,0:T(8,128)(2,1)S(1)}, bf16[1,192,512]{2,1,0:T(8,128)(2,1)S(1)}, u32[]{:S(2)}, u32[]{:S(2)}) collective-permute-start(bf16[1,192,512]{2,1,0:T(8,128)(2,1)S(1)} %slice.329), channel_id=1, source_target_pairs={{0,4},{1,5},{2,6},{3,7},{4,0},{5,1},{6,2},{7,3},{8,12},{9,13},{10,... | collective-permute-start | bytes 589832 | tf_op jit(solution)/shard_map/ppermute | solution.py:863
  387.0 4.9 collective-permute-start.16
  391.9 0.7 copy-start.28
  392.7 46.1 %copy-start.24 = (f32[96]{0:T(128)S(1)}, f32[96]{0:T(128)}, u32[]{:S(2)}) copy-start(f32[96]{0:T(128)} %get-tuple-element.82) | copy-start | bytes 1156
  392.7 46.1 %copy-start.25 = (f32[96]{0:T(128)S(1)}, f32[96]{0:T(128)}, u32[]{:S(2)}) copy-start(f32[96]{0:T(128)} %get-tuple-element.83) | copy-start | bytes 1156
  392.7 47.7 %copy-start.17 = (f32[3,4,32]{2,1,0:T(4,128)S(1)}, f32[3,4,32]{2,1,0:T(4,128)}, u32[]{:S(2)}) copy-start(f32[3,4,32]{2,1,0:T(4,128)} %constant.109.clone) | copy-start | bytes 4612
  448.1 63.7 %copy-start.5 = (f32[8960]{0:T(1024)S(1)}, f32[8960]{0:T(1024)}, u32[]{:S(2)}) copy-start(f32[8960]{0:T(1024)} %param.12) | copy-start | bytes 107524
  448.1 63.7 %copy-start.13 = (f32[8960]{0:T(1024)S(1)}, f32[8960]{0:T(1024)}, u32[]{:S(2)}) copy-start(f32[8960]{0:T(1024)} %param.13) | copy-start | bytes 107524
  448.1 63.7 %copy-start.14 = (f32[8960]{0:T(1024)S(1)}, f32[8960]{0:T(1024)}, u32[]{:S(2)}) copy-start(f32[8960]{0:T(1024)} %param.14) | copy-start | bytes 107524
  448.6 4.4 collective-permute-start.17
  453.2 9.4 %collective-permute-start.18 = (f32[2,2,2,70,128]{4,3,2,1,0:T(8,128)S(1)}, f32[2,2,2,70,128]{4,3,2,1,0:T(8,128)S(1)}, u32[]{:S(2)}, u32[]{:S(2)}) collective-permute-start(f32[2,2,2,70,128]{4,3,2,1,0:T(8,128)S(1)} %dynamic-slice_bitcast_fusion.1), channel_id=1, source_target_pairs={{0,2},{1,3},{2,0},{3,1},{4,6},{5,7},{6,4},{7,5},{8,10},{9,11},{10,... | collective-permute-start | bytes 860168 | tf_op jit(solution)/shard_map/ppermute | solution.py:863
  462.6 5.7 %collective-permute-start.19 = (f32[2,2,70,128]{3,2,1,0:T(8,128)S(1)}, f32[2,2,70,128]{3,2,1,0:T(8,128)S(1)}, u32[]{:S(2)}, u32[]{:S(2)}) collective-permute-start(f32[2,2,70,128]{3,2,1,0:T(8,128)S(1)} %dynamic-slice_bitcast_fusion.2), channel_id=1, source_target_pairs={{0,4},{1,5},{2,6},{3,7},{4,0},{5,1},{6,2},{7,3},{8,12},{9,13},{10,... | collective-permute-start | bytes 430088 | tf_op jit(solution)/shard_map/ppermute | solution.py:863
  468.3 10.4 %collective-permute-start.20 = (f32[2,70,128]{2,1,0:T(8,128)S(1)}, f32[2,70,128]{2,1,0:T(8,128)S(1)}, u32[]{:S(2)}, u32[]{:S(2)}) collective-permute-start(f32[2,70,128]{2,1,0:T(8,128)S(1)} %dynamic-slice_bitcast_fusion.3), channel_id=1, source_target_pairs={{0,8},{8,0},{16,24},{24,16},{1,9},{9,1},{17,25},{25,17},{2,10},{10... | collective-permute-start | bytes 215048 | tf_op jit(solution)/shard_map/ppermute | solution.py:863
  478.7 11.8 %collective-permute-start.21 = (f32[70,128]{1,0:T(8,128)S(1)}, f32[70,128]{1,0:T(8,128)S(1)}, u32[]{:S(2)}, u32[]{:S(2)}) collective-permute-start(f32[70,128]{1,0:T(8,128)S(1)} %dynamic-slice_bitcast_fusion.4), channel_id=1, source_target_pairs={{0,16},{8,24},{16,0},{24,8},{1,17},{9,25},{17,1},{25,9},{2,18},{10... | collective-permute-start | bytes 107528 | tf_op jit(solution)/shard_map/ppermute | solution.py:863
  491.1 1.4 collective-permute-start.22
  493.7 3.7 collective-permute-start.23
  498.0 3.7 collective-permute-start.24
  502.3 3.5 collective-permute-start.25
  505.9 4.4 collective-permute-start.26
Sparse Core Ops, SparseCore 0:
  90.6 37.5 all-gather.2

commit v4 on v3

--- a/solution.py
+++ b/solution.py
@@ -38,7 +38,7 @@
 GROUP = 2
 PADDED = TOKENS + 512
 WIN = 40
-PATCH_ROWS = 224
+PATCH_ROWS = 256
 VMEM_BYTES = 56 * 1024 * 1024
 
 
@@ -115,6 +115,28 @@
 def fill_wide(wide_ref, vec_ref, indices):
     for k, index in enumerate(indices):
         wide_ref[k] = jnp.broadcast_to(column(vec_ref, index), (DIM, 128))
+
+
+def fill_taps(taps_ref, vec_ref):
+    lane = lane_ids(128, DIM)
+    for member in range(2):
+        for r in range(3):
+            block = jnp.zeros((DIM, 128), F32)
+            for c in range(3):
+                block = jnp.where((lane >> 5) == c, column(vec_ref, 24 + 9 * member + 3 * r + c), block)
+            taps_ref[DIM * member : DIM * member + DIM, 128 * r : 128 * r + 128] = jnp.where(lane == 0, 0.0, block)
+
+
+def fill_bias(bias_ref, vec_ref):
+    for k in range(MLP // DIM):
+        bias_ref[DIM * k : DIM * k + DIM] = jnp.broadcast_to(vec_ref[:, 45 + k : 46 + k], (DIM, 128))
+
+
+def fill_transpose(dst_ref, src_ref):
+    rows, cols = src_ref.shape
+    value = src_ref[...].astype(F32)
+    value = jnp.pad(value, ((0, -rows % 128), (0, -cols % 128)))
+    dst_ref[...] = jnp.transpose(value)[:cols, :rows].astype(BF16)
 
 
 def wide(wide_ref, k, width=PAIR):
@@ -256,79 +278,74 @@
     return 2 * key_rows + 64 + 16
 
 
-def embed_kernel(ext_ref, row_ref, order_ref, *refs, offset):
-    pix_refs, tail_refs, refs = refs[:GROUP], refs[GROUP : 2 * GROUP], refs[2 * GROUP :]
-    (perm_ref, tap_ref, wp_ref, wqkv_ref, vec_ref, bkv_ref, kexp_ref,
-     patch_ref, x0_ref, q_ref, first_ref, last_ref, nsel_ref, kvt_ref, below_ref, own_ref, s_ref, n_ref, wide_ref) = refs
+def pixel_rows(pix_ref, s_ref):
+    for a in range(4):
+        for ch in range(3):
+            block = pix_ref[0, a, ch].astype(F32)
+            for tile in range(TILES):
+                s_ref[tile, pl.ds(4 * a + ch, ROWS, stride=16), :] = block[:, 128 * tile : 128 * tile + 128]
+    for a in range(3):
+        for ch in range(3):
+            block = pix_ref[0, 4 + a, ch].astype(F32)
+            for tile in range(TILES):
+                s_ref[tile, 128 + 4 * a + ch : 129 + 4 * a + ch, :] = block[ROWS - 1 : ROWS, 128 * tile : 128 * tile + 128]
+
+
+def patch_blocks(s_ref, perm, shifted, sets):
+    rows = [s_ref[tile] for tile in range(TILES)]
+    if shifted:
+        first = lane_ids(128, 144) < 4
+        rolled = [pltpu.roll(block, 4, 1) for block in rows]
+        rows = [jnp.where(first, rolled[tile - 1] if tile else 0.0, rolled[tile]) for tile in range(TILES)]
+    rows = [block.astype(BF16) for block in rows]
+    stack = []
+    for chosen in sets:
+        for tile in range(TILES):
+            stack.append(jnp.concatenate([rows[tile][16 * r : 16 * r + 16] for r in chosen], axis=1))
+    return dot(jnp.concatenate(stack, axis=0), perm).astype(BF16)
+
+
+def edge_kernel(ext_ref, row_ref, order_ref, *refs, offset):
+    pix_refs, refs = refs[:GROUP], refs[GROUP:]
+    (perm_ref, tap_ref, wp_ref, wqkv_ref, vec_ref,
+     first_ref, last_ref, nsel_ref, kvt_ref, below_ref, own_ref, s_ref, p_ref, wide_ref, kexp_ref) = refs
     images, heights, breadths, row_oks = group_extents(ext_ref, row_ref, offset)
 
     @pl.when(pl.program_id(0) == 0)
     def _():
         s_ref[...] = jnp.zeros_like(s_ref)
-        fill_wide(wide_ref, vec_ref, [0, 1, 2, 42])
-
-    lane = lane_ids(1024, 144)
+        fill_wide(wide_ref, vec_ref, [0, 1, 2, 42, 43, 44])
+        fill_taps(kexp_ref, vec_ref)
+
+    lane = lane_ids(1024)
+    masks = []
     for g in range(GROUP):
-        for r in range(ROWS):
-            for a in range(4):
-                s_ref[16 * r + 4 * a : 16 * r + 4 * a + 3, :] = pix_refs[g][0, r, a].astype(F32)
-        for a in range(3):
-            s_ref[128 + 4 * a : 128 + 4 * a + 3, :] = tail_refs[g][0, 0, a].astype(F32)
+        pixel_rows(pix_refs[g], s_ref)
         for shifted in range(2):
-            rows = s_ref[...]
-            if shifted:
-                rows = jnp.where(lane < 4, 0.0, pltpu.roll(rows, 4, 1))
-            rows = rows.astype(BF16)
-            stack = []
-            for start in (0, 4, 1, 5):
+            out = patch_blocks(s_ref, perm_ref[...], shifted, ((7, 0, 1, 1), (8, 1, 2, 2)))
+            for half in range(2):
                 for tile in range(TILES):
-                    stack.append(jnp.concatenate(
-                        [rows[16 * (start + k) : 16 * (start + k) + 16, 128 * tile : 128 * tile + 128] for k in range(4)], axis=1))
-            out = dot(jnp.concatenate(stack, axis=0), perm_ref[...]).astype(BF16)
-            for which, start in enumerate((0, 4, 1, 5)):
-                half, side = which // 2, which % 2
-                for tile in range(TILES):
-                    block = out[128 * which + 16 * tile : 128 * which + 16 * tile + 16]
-                    for phase in range(shifted, 4):
-                        top = 64 * half + 16 * phase if not shifted else 128 + 48 * half + 16 * (phase - 1)
-                        patch_ref[g, top : top + 16, 256 * tile + 128 * side : 256 * tile + 128 * side + 128] = block[
-                            :, 128 * phase : 128 * phase + 128]
-
-    count = pair_count(breadths)
-
-    def active(pair, carry):
-        def first_norm(k, embed, mask):
-            x0 = (embed + wide_ref[0]) * mask
-            hat, _ = normalized(x0)
-            return x0, (hat * wide_ref[1] + wide_ref[2]).astype(BF16)
-
-        x0, normed = by_lanes(first_norm, dot(wp_ref[...], load_pair(patch_ref, pair)), pair_mask(pair, breadths, row_oks))
-        store_pair(x0_ref, pair, x0)
-        store_pair(n_ref, pair, normed.astype(F32))
-        (query,) = by_lanes(lambda k, out: ((out + wide_ref[3]).astype(BF16),), dot(wqkv_ref[0:DIM, :], normed))
-        store_pair(q_ref, pair, query, 256)
-        return carry
-
-    def idle(pair, carry):
-        for g in range(GROUP):
-            n_ref[g, :, pair_lanes(pair)] = jnp.zeros((DIM, PAIR), F32)
-            q_ref[g, :, pair_lanes(pair, 256)] = jnp.zeros((DIM, PAIR), BF16)
-        return carry
-
-    lax.fori_loop(0, count, active, 0)
-    lax.fori_loop(count, PAIRS, idle, 0)
-    for g in range(GROUP):
-        q_ref[g, :, 0:256] = jnp.zeros((DIM, 256), BF16)
-        q_ref[g, :, 256 + TOKENS : 512 + TOKENS] = jnp.zeros((DIM, 256), BF16)
+                    block = out[128 * half + 16 * tile : 128 * half + 16 * tile + 16]
+                    for phase in range(4):
+                        top = 128 * shifted + 64 * half + 16 * phase
+                        p_ref[top : top + 16, 1024 * g + 128 * tile : 1024 * g + 128 * tile + 128] = block[:, 128 * phase : 128 * phase + 128]
+        col = (lane >> 7) * 32 + (lane & 31)
+        masks.append(jnp.where((col < breadths[g]) & row_oks[g], 1.0, 0.0).astype(F32))
+
+    def first_norm(k, embed, mask):
+        hat, _ = normalized((embed + wide_ref[0]) * mask)
+        return ((hat * wide_ref[1] + wide_ref[2]).astype(BF16).astype(F32),)
+
+    (normed,) = by_lanes(first_norm, dot(wp_ref[...], p_ref[...]), jnp.concatenate(masks, axis=1))
     rows = []
-    for start in (224, 0, 32):
-        rows.append(jnp.concatenate(
-            [n_ref[g, :, 256 * t + start : 256 * t + start + 32] for g in range(GROUP) for t in range(TILES)], axis=1).astype(BF16))
+    for slot in range(3):
+        rows.append(jnp.concatenate([gather_halo(normed[:, 1024 * g : 1024 * g + 1024], 32 * slot) for g in range(GROUP)], axis=1).astype(BF16))
     edge = dot(wqkv_ref[0:DIM, :], jnp.concatenate(rows[:2], axis=1))
     (edge,) = by_lanes(lambda k, out: ((out + wide_ref[3]).astype(BF16),), edge)
     nsel = dot(jnp.concatenate([row[:, CANVAS_W * g : CANVAS_W * g + CANVAS_W] for g in range(GROUP) for row in rows], axis=0), tap_ref[...])
     nsel = jnp.concatenate([nsel[DIM * k : DIM * k + DIM] for k in range(3 * GROUP)], axis=1).astype(BF16)
-    taps = (dot(wqkv_ref[DIM : 3 * DIM, :], nsel) + bkv_ref[...]).astype(BF16)
+    bias = jnp.concatenate([wide_ref[4], wide_ref[5]], axis=0)
+    (taps,) = by_lanes(lambda k, out: ((out + bias).astype(BF16),), dot(wqkv_ref[DIM : 3 * DIM, :], nsel))
     for g in range(GROUP):
         last_ref[g] = edge[:, CANVAS_W * g : CANVAS_W * g + CANVAS_W]
         first_ref[g] = edge[:, CANVAS_W * (GROUP + g) : CANVAS_W * (GROUP + g) + CANVAS_W]
@@ -343,6 +360,55 @@
         store_lanes(own_ref, sums[1] + sums[2], images[g])
 
 
+def embed_kernel(ext_ref, row_ref, order_ref, *refs, offset):
+    pix_refs, refs = refs[:GROUP], refs[GROUP:]
+    perm_ref, wp_ref, wqkv_ref, vec_ref, patch_ref, x0_ref, q_ref, s_ref, wide_ref = refs
+    images, heights, breadths, row_oks = group_extents(ext_ref, row_ref, offset)
+
+    @pl.when(pl.program_id(0) == 0)
+    def _():
+        s_ref[...] = jnp.zeros_like(s_ref)
+        fill_wide(wide_ref, vec_ref, [0, 1, 2, 42])
+
+    for g in range(GROUP):
+        pixel_rows(pix_refs[g], s_ref)
+        for shifted in range(2):
+            out = patch_blocks(s_ref, perm_ref[...], shifted, ((0, 1, 2, 3), (4, 5, 6, 7), (1, 2, 3, 4), (5, 6, 7, 8)))
+            for which in range(4):
+                half, side = which // 2, which % 2
+                for tile in range(TILES):
+                    block = out[128 * which + 16 * tile : 128 * which + 16 * tile + 16]
+                    for phase in range(4):
+                        top = 128 * shifted + 64 * half + 16 * phase
+                        patch_ref[g, top : top + 16, 256 * tile + 128 * side : 256 * tile + 128 * side + 128] = block[
+                            :, 128 * phase : 128 * phase + 128]
+
+    count = pair_count(breadths)
+
+    def active(pair, carry):
+        def first_norm(k, embed, mask):
+            x0 = (embed + wide_ref[0]) * mask
+            hat, _ = normalized(x0)
+            return x0, (hat * wide_ref[1] + wide_ref[2]).astype(BF16)
+
+        x0, normed = by_lanes(first_norm, dot(wp_ref[...], load_pair(patch_ref, pair)), pair_mask(pair, breadths, row_oks))
+        store_pair(x0_ref, pair, x0)
+        (query,) = by_lanes(lambda k, out: ((out + wide_ref[3]).astype(BF16),), dot(wqkv_ref[0:DIM, :], normed))
+        store_pair(q_ref, pair, query, 256)
+        return carry
+
+    def idle(pair, carry):
+        for g in range(GROUP):
+            q_ref[g, :, pair_lanes(pair, 256)] = jnp.zeros((DIM, PAIR), BF16)
+        return carry
+
+    lax.fori_loop(0, count, active, 0)
+    lax.fori_loop(count, PAIRS, idle, 0)
+    for g in range(GROUP):
+        q_ref[g, :, 0:256] = jnp.zeros((DIM, 256), BF16)
+        q_ref[g, :, 256 + TOKENS : 512 + TOKENS] = jnp.zeros((DIM, 256), BF16)
+
+
 def key_lanes(*lead):
     return pl.BlockSpec(lead + (128,), lambda i, *_: (0,) * len(lead) + (i * GROUP >> 2,))
 
@@ -353,28 +419,45 @@
     return whole, per
 
 
+def pixel_specs(offset):
+    return [pl.BlockSpec((1, PATCH, 3, ROWS, 1024), lambda i, ext, row, order, g=g: (order[offset + i * GROUP + g], 0, 0, 0, 0)) for g in range(GROUP)]
+
+
+def call_edge(ext, row, order, pixels, consts, wts, images, offset):
+    whole, per = specs()
+    shapes = [(DIM, CANVAS_W), (DIM, CANVAS_W), (DIM, 384), (2 * DIM, 384)]
+    return pl.pallas_call(
+        functools.partial(edge_kernel, offset=offset),
+        grid_spec=pltpu.PrefetchScalarGridSpec(
+            num_scalar_prefetch=3, grid=(images // GROUP,),
+            in_specs=pixel_specs(offset) + [
+                whole(512, 512), whole(CANVAS_W, 128), whole(DIM, PATCH_ROWS), whole(3 * DIM, DIM), whole(DIM, 64)],
+            out_specs=[per(*s) for s in shapes] + [key_lanes(2 * DIM)] * 2,
+            scratch_shapes=[pltpu.VMEM((TILES, 144, 128), F32), pltpu.VMEM((PATCH_ROWS, 1024 * GROUP), BF16), pltpu.VMEM((6, DIM, 128), F32),
+                            pltpu.VMEM((2 * DIM, 384), F32)]),
+        out_shape=[jax.ShapeDtypeStruct((images,) + s, BF16) for s in shapes]
+        + [jax.ShapeDtypeStruct((2 * DIM, 32 * images), F32)] * 2,
+        compiler_params=pltpu.CompilerParams(vmem_limit_bytes=VMEM_BYTES),
+        cost_estimate=pl.CostEstimate(flops=images * 1_000_000_000, bytes_accessed=images * 1_000_000, transcendentals=0),
+        name="edge",
+    )(ext, row, order, *[pixels] * GROUP, consts["perm"], consts["tap"], wts["wp"], wts["wqkv_t"], wts["vec"])
+
+
 def call_embed(ext, row, order, pixels, consts, wts, images, offset):
     whole, per = specs()
-    shapes = [
-        ((PATCH_ROWS, TOKENS), BF16), ((DIM, TOKENS), F32), ((DIM, PADDED), BF16), ((DIM, CANVAS_W), BF16),
-        ((DIM, CANVAS_W), BF16), ((DIM, 384), BF16), ((2 * DIM, 384), BF16)]
-    pix = [pl.BlockSpec((1, ROWS, 4, 3, 1024), lambda i, ext, row, order, g=g: (order[offset + i * GROUP + g], 0, 0, 0, 0)) for g in range(GROUP)]
-    tail = [pl.BlockSpec((1, 1, 4, 3, 1024), lambda i, ext, row, order, g=g: (order[offset + i * GROUP + g], ROWS - 1, 1, 0, 0)) for g in range(GROUP)]
+    shapes = [((PATCH_ROWS, TOKENS), BF16), ((DIM, TOKENS), F32), ((DIM, PADDED), BF16)]
     return pl.pallas_call(
         functools.partial(embed_kernel, offset=offset),
         grid_spec=pltpu.PrefetchScalarGridSpec(
             num_scalar_prefetch=3, grid=(images // GROUP,),
-            in_specs=pix + tail + [
-                whole(512, 512), whole(CANVAS_W, 128), whole(DIM, PATCH_ROWS), whole(3 * DIM, DIM), whole(DIM, 64),
-                whole(2 * DIM, 1), whole(2 * DIM, 384)],
-            out_specs=[per(*s) for s, _ in shapes] + [key_lanes(2 * DIM)] * 2,
-            scratch_shapes=[pltpu.VMEM((144, 1024), F32), pltpu.VMEM((GROUP, DIM, TOKENS), F32), pltpu.VMEM((4, DIM, 128), F32)]),
-        out_shape=[jax.ShapeDtypeStruct((images,) + s, t) for s, t in shapes]
-        + [jax.ShapeDtypeStruct((2 * DIM, 32 * images), F32)] * 2,
+            in_specs=pixel_specs(offset) + [whole(512, 512), whole(DIM, PATCH_ROWS), whole(3 * DIM, DIM), whole(DIM, 64)],
+            out_specs=[per(*s) for s, _ in shapes],
+            scratch_shapes=[pltpu.VMEM((TILES, 144, 128), F32), pltpu.VMEM((4, DIM, 128), F32)]),
+        out_shape=[jax.ShapeDtypeStruct((images,) + s, t) for s, t in shapes],
         compiler_params=pltpu.CompilerParams(vmem_limit_bytes=VMEM_BYTES),
         cost_estimate=pl.CostEstimate(flops=images * 2_000_000_000, bytes_accessed=images * 4_000_000, transcendentals=0),
         name="embed",
-    )(ext, row, order, *[pixels] * (2 * GROUP), consts["perm"], consts["tap"], wts["wp"], wts["wqkv_t"], wts["vec"], wts["b_kv"], wts["kexp"])
+    )(ext, row, order, *[pixels] * GROUP, consts["perm"], wts["wp"], wts["wqkv_t"], wts["vec"])
 
 
 def pool_norm_kernel(own_ref, got_ref, vec_ref, kv_ref):
@@ -454,8 +537,8 @@
     return (hidden * cumulative).astype(BF16), slope.astype(BF16)
 
 
-def forward_kernel(ext_ref, row_ref, q_ref, top_ref, bot_ref, x0_ref, kv_ref, vec_ref, rw_ref, wprojt_ref, w1t_ref, b1_ref, w2t_ref,
-                   hat_ref, query_ref, terms_ref, att_ref, act_ref, slope_ref, hat2_ref, hat3_ref, stat_ref, pool_ref, ka_ref, kn_ref, v_ref, ztop_ref, zbot_ref, pre_ref, wide_ref, wb1_ref,
+def forward_kernel(ext_ref, row_ref, q_ref, top_ref, bot_ref, x0_ref, kv_ref, vec_ref, rw_ref, wproj_ref, w1_ref, w2_ref,
+                   hat_ref, query_ref, terms_ref, att_ref, act_ref, slope_ref, hat2_ref, hat3_ref, stat_ref, pool_ref, ka_ref, kn_ref, v_ref, ztop_ref, zbot_ref, pre_ref, wide_ref, wb1_ref, wprojt_ref, w1t_ref, w2t_ref,
                    *, offset, key_rows):
     images, heights, breadths, row_oks = group_extents(ext_ref, row_ref, offset)
     depth = DIM + aug_rows(key_rows)
@@ -463,7 +546,10 @@
     @pl.when(pl.program_id(0) == 0)
     def _():
         fill_wide(wide_ref, vec_ref, list(range(15, 24)) + [3, 4, 9, 10, 11, 12])
-        wb1_ref[...] = jnp.broadcast_to(b1_ref[...], (MLP, 128))
+        fill_bias(wb1_ref, vec_ref)
+        fill_transpose(wprojt_ref, wproj_ref)
+        fill_transpose(w1t_ref, w1_ref)
+        fill_transpose(w2t_ref, w2_ref)
 
     lane = lane_ids(CANVAS_W, DIM)
     for g in range(GROUP):
@@ -564,18 +650,18 @@
             in_specs=[
                 per(DIM, PADDED), per(DIM, CANVAS_W), per(DIM, CANVAS_W), per(DIM, TOKENS),
                 key_lanes(key_rows, 2 * DIM),
-                whole(DIM, 64), whole(PAIRS, 8 * WIN + 8 * key_rows, DIM), whole(DIM, DIM), whole(MLP, DIM), whole(MLP, 1),
-                whole(DIM, MLP)],
+                whole(DIM, 64), whole(PAIRS, 8 * WIN + 8 * key_rows, DIM), whole(DIM, DIM), whole(DIM, MLP), whole(MLP, DIM)],
             out_specs=[per(*s) for s, _ in shapes],
             scratch_shapes=[
                 pltpu.VMEM((DIM + more, keys), BF16), pltpu.VMEM((GROUP, keys, 256), BF16), pltpu.VMEM((GROUP, DIM, keys), BF16),
                 pltpu.VMEM((GROUP, DIM, 1024), F32), pltpu.VMEM((GROUP, DIM, 1024), F32), pltpu.VMEM((DIM, GROUP * PAIR), F32),
-                pltpu.VMEM((15, DIM, 128), F32), pltpu.VMEM((MLP, 128), F32)]),
+                pltpu.VMEM((15, DIM, 128), F32), pltpu.VMEM((MLP, 128), F32),
+                pltpu.VMEM((DIM, DIM), BF16), pltpu.VMEM((MLP, DIM), BF16), pltpu.VMEM((DIM, MLP), BF16)]),
         out_shape=[jax.ShapeDtypeStruct((images,) + s, t) for s, t in shapes],
         compiler_params=pltpu.CompilerParams(vmem_limit_bytes=VMEM_BYTES),
         cost_estimate=pl.CostEstimate(flops=images * 5_000_000_000, bytes_accessed=images * 4_000_000, transcendentals=0),
         name="forward",
-    )(ext, row, q, top, bot, x0, kv, wts["vec"], wts["rw"], wts["wproj_t"], wts["w1_t"], wts["b1"], wts["w2_t"])
+    )(ext, row, q, top, bot, x0, kv, wts["vec"], wts["rw"], wts["wproj"], wts["w1"], wts["w2"])
 
 
 def backward_kernel(ext_ref, row_ref, hat_ref, query_ref, terms_ref, att_ref, act_ref, slope_ref, hat2_ref, hat3_ref, stat_ref, q_ref, top_ref, bot_ref, kv_ref,
@@ -617,7 +703,7 @@
 
         grad_x2, grad_mlp = by_lanes(third_back, load_pair(hat3_ref, pair), stat, pair_mask(pair, breadths, row_oks))
         act = load_pair(act_ref, pair)
-        a2_ref[...] += dot_nt(grad_mlp, jnp.concatenate([act, ones], axis=0))
+        a2_ref[...] += dot_nt(jnp.concatenate([act, ones], axis=0), grad_mlp)
         (grad_hidden,) = by_blocks(
             lambda part, grad, slope: ((grad * slope.astype(F32)).astype(BF16),), 64, dot(w2_ref[...], grad_mlp), load_pair(slope_ref, pair))
         hat_two = load_pair(hat2_ref, pair)
@@ -659,7 +745,7 @@
             dk_ref[g] += dot_nt(queries[g], grad_scores[g])
         back = jnp.concatenate(back, axis=1)
         (spread,) = by_lanes(lambda k, terms: (relative_spread(k, terms, key_rows),), back[DIM:])
-        ar_ref[pair] += dot_nt(query, spread)
+        ar_ref[pair] += dot_nt(spread, query)
 
         def query_back(k, grad_att, back, far, hat, stat):
             grad = grad_att + back * SCALE + far
@@ -744,7 +830,7 @@
     former = lambda *shape: pl.BlockSpec((GROUP,) + shape, lambda i, *_: (jnp.maximum(i - 1, 0),) + (0,) * len(shape))
     heads = pl.BlockSpec((key_rows, 2 * DIM, 128), lambda i, *_: (0, 0, jnp.minimum(i, steps - 1) * GROUP >> 2))
     shapes = [(DIM, TOKENS), (DIM, TOKENS), (DIM, CANVAS_W), (DIM, CANVAS_W)]
-    sums = [(DIM, MLP + 16), (DIM + 16, MLP), (DIM + 16, DIM), (4, DIM, 128), (9, DIM, 128), (PAIRS, DIM, window)]
+    sums = [(MLP + 16, DIM), (DIM + 16, MLP), (DIM + 16, DIM), (4, DIM, 128), (9, DIM, 128), (PAIRS, window, DIM)]
     return pl.pallas_call(
         functools.partial(backward_kernel, offset=offset, key_rows=key_rows),
         grid_spec=pltpu.PrefetchScalarGridSpec(
@@ -766,8 +852,8 @@
 
 
 def embed_back_kernel(ext_ref, row_ref, patch_ref, dq_ref, dx1_ref, rtop_ref, rbot_ref, nsel_ref, kvt_ref, pre_ref, under_ref,
-                      wp_ref, vec_ref, wqkv_ref, kexp_ref, tapt_ref,
-                      aq_ref, akv_ref, apatch_ref, av_ref, ak_ref, dn_ref, rim_ref, wide_ref, *, offset):
+                      wp_ref, vec_ref, wqkv_ref, tapt_ref,
+                      aq_ref, akv_ref, apatch_ref, av_ref, ak_ref, dn_ref, rim_ref, wide_ref, kexp_ref, *, offset):
     images, heights, breadths, row_oks = group_extents(ext_ref, row_ref, offset)
 
     @pl.when(pl.program_id(0) == 0)
@@ -775,6 +861,7 @@
         for ref in (aq_ref, akv_ref, apatch_ref, av_ref, ak_ref, dn_ref, rim_ref):
             ref[...] = jnp.zeros_like(ref)
         fill_wide(wide_ref, vec_ref, [0, 1, 2])
+        fill_taps(kexp_ref, vec_ref)
 
     lane = lane_ids(128, 2 * DIM)
 
@@ -844,14 +931,14 @@
             in_specs=[
                 per(PATCH_ROWS, TOKENS), per(DIM, TOKENS), per(DIM, TOKENS), per(DIM, CANVAS_W), per(DIM, CANVAS_W),
                 per(DIM, 384), per(2 * DIM, 384), key_lanes(2 * DIM), key_lanes(2 * DIM),
-                whole(DIM, PATCH_ROWS), whole(DIM, 64), whole(DIM, 3 * DIM), whole(2 * DIM, 384), whole(128, CANVAS_W)],
+                whole(DIM, PATCH_ROWS), whole(DIM, 64), whole(DIM, 3 * DIM), whole(128, CANVAS_W)],
             out_specs=[whole(*s) for s in sums],
-            scratch_shapes=[pltpu.VMEM((GROUP, DIM, TOKENS), F32)] * 2 + [pltpu.VMEM((3, DIM, 128), F32)]),
+            scratch_shapes=[pltpu.VMEM((GROUP, DIM, TOKENS), F32)] * 2 + [pltpu.VMEM((3, DIM, 128), F32), pltpu.VMEM((2 * DIM, 384), F32)]),
         out_shape=[jax.ShapeDtypeStruct(s, F32) for s in sums],
         compiler_params=pltpu.CompilerParams(vmem_limit_bytes=VMEM_BYTES),
         cost_estimate=pl.CostEstimate(flops=images * 3_000_000_000, bytes_accessed=images * 3_000_000, transcendentals=0),
         name="embed_back",
-    )(ext, row, patches, dq, dx1, rtop, rbot, nsel, kvt, pre, under, wts["wp"], wts["vec"], wts["wqkv"], wts["kexp"], consts["tap_t"])
+    )(ext, row, patches, dq, dx1, rtop, rbot, nsel, kvt, pre, under, wts["wp"], wts["vec"], wts["wqkv"], consts["tap_t"])
 
 
 def bit_count(size):
@@ -875,11 +962,13 @@
     return value
 
 
-def scatter_slots(value, axis):
-    for bit in range(bit_count(lax.axis_size(axis))):
-        half = value.shape[0] // 2
-        value = value[:half] + swap(value[half:].astype(BF16), axis, bit).astype(F32)
-    return value[0]
+def scatter_step(value, axis, bit):
+    half = value.shape[0] // 2
+    return value[:half] + swap(value[half:].astype(BF16), axis, bit).astype(F32)
+
+
+def together(*values):
+    return lax.optimization_barrier(values)
 
 
 def gather_params(value):
@@ -944,19 +1033,14 @@
 def patch_rows(weight):
     taps = jnp.pad(weight.reshape(PATCH, PATCH, 3, DIM), ((0, 1), (0, 0), (0, 1), (0, 0)))
     parts = []
-    for piece in (taps[:, 3:7], taps[:, 0:3]):
-        phases = piece.shape[1]
-        parts.append(jnp.transpose(piece.reshape(2, 4, phases, 4, DIM), (0, 2, 1, 3, 4)).reshape(32 * phases, DIM))
+    for piece in (taps[:, 3:7], jnp.pad(taps[:, 0:3], ((0, 0), (1, 0), (0, 0), (0, 0)))):
+        parts.append(jnp.transpose(piece.reshape(2, 4, 4, 4, DIM), (0, 2, 1, 3, 4)).reshape(128, DIM))
     return jnp.concatenate(parts, axis=0)
 
 
 def patch_rows_back(grad):
-    rows = grad.T
-    parts = []
-    for piece, phases in ((rows[128:], 3), (rows[:128], 4)):
-        taps = jnp.transpose(piece.reshape(2, phases, 4, 4, DIM), (0, 2, 1, 3, 4)).reshape(8, phases, 4, DIM)
-        parts.append(taps[:PATCH, :, :3])
-    return jnp.concatenate(parts, axis=1).reshape(3 * PATCH * PATCH, DIM)
+    taps = jnp.transpose(grad.T.reshape(2, 2, 4, 4, 4, DIM), (0, 1, 3, 2, 4, 5)).reshape(2, 8, 4, 4, DIM)
+    return jnp.concatenate([taps[1, :PATCH, 1:, :3], taps[0, :PATCH, :, :3]], axis=1).reshape(3 * PATCH * PATCH, DIM)
 
 
 def relative_windows(rel_rows, rel_cols, row_index, key_rows):
@@ -973,7 +1057,6 @@
 
 
 def relative_windows_back(grad, row_index, key_rows):
-    grad = jnp.transpose(grad, (0, 2, 1))
     cols = grad[:, : 8 * WIN].reshape(PAIRS, 8, WIN, DIM)
     total = 0.0
     for pair in range(PAIRS):
@@ -996,33 +1079,23 @@
 def prepare(weights, row_index, key_rows):
     small = weights["small"]
     vec = jnp.pad(small.astype(F32).T, ((0, 0), (0, 15)))
-    kernels = small[9:27].reshape(2, 3, 3, DIM).astype(F32)
-    expanded = jnp.pad(jnp.transpose(kernels, (0, 3, 1, 2)), ((0, 0), (0, 0), (0, 0), (0, 1)))
-    kexp = (expanded[..., None] * tap_keep()).reshape(2 * DIM, 384)
     windows = relative_windows(weights["rel_rows"], weights["rel_cols"], row_index, key_rows)
     return {
         "vec": vec,
-        "kexp": kexp,
         "wp": patch_rows(weights["w_patch"]).T,
         "wqkv": weights["w_qkv"],
         "wqkv_t": weights["w_qkv"].T,
-        "b_kv": small[43:45].astype(F32).reshape(2 * DIM, 1),
         "wproj": weights["w_proj"],
-        "wproj_t": weights["w_proj"].T,
         "w1": weights["w_fc1"],
-        "w1_t": weights["w_fc1"].T,
-        "b1": small[45:49].astype(F32).reshape(MLP, 1),
         "w2": weights["w_fc2"],
-        "w2_t": weights["w_fc2"].T,
         "rw": windows,
         "rw_t": jnp.transpose(windows, (0, 2, 1)),
     }
 
 
-def image_loss(pooled, head_w, head_b, teacher, labels, image_total):
+def image_loss(pooled, head_w, head_b, log_teacher, labels, image_total):
     logits = jnp.dot(pooled, head_w, precision=HIGHEST_PREC) + head_b
     log_student = jax.nn.log_softmax(logits, axis=-1)
-    log_teacher = jax.nn.log_softmax(teacher, axis=-1)
     onehot = (jnp.arange(CLASSES)[None, :] == labels[:, None]).astype(F32)
     per_image = jnp.sum(jnp.exp(log_teacher) * (log_teacher - log_student), axis=-1) - jnp.sum(onehot * log_student, axis=-1)
     return jnp.sum(per_image) / image_total
@@ -1055,13 +1128,19 @@
     order = jnp.sum(jnp.where(chosen, ids[None, :], 0), axis=1)
     ext = jnp.sum(jnp.where(chosen[:, :, None], extents[None], 0), axis=1)
 
+    log_teacher = jax.nn.log_softmax(teacher, axis=-1)
+    pixel_view = jnp.transpose(pixels, (0, 2, 3, 1, 4))
     saved = []
     for part in range(parts):
-        patches, x0, q, first, last, nsel, kvt, below, own = call_embed(ext, row, order, pixels, consts, wts, size, part * size)
+        first, last, nsel, kvt, below, own = call_edge(ext, row, order, pixel_view, consts, wts, size, part * size)
+        got = shifted(below, "row", 1)
+        kv = lax.all_gather(call_pool_norm(own, got, wts["vec"]), "row", axis=0)
         top = shifted(last, "row", 1)
         bot = shifted(first, "row", -1)
-        got = shifted(below, "row", 1)
-        kv = lax.all_gather(call_pool_norm(own, got, wts["vec"]), "row", axis=0)
+        names = sorted(wts)
+        after, log_teacher, *values = together(ext, log_teacher, *[wts[name] for name in names])
+        wts = dict(zip(names, values))
+        patches, x0, q = call_embed(after, row, order, pixel_view, consts, wts, size, part * size)
         saved.append(dict(patches=patches, x0=x0, q=q, top=top, bot=bot, nsel=nsel, kvt=kvt, own=own, got=got, kv=kv))
     for part in range(parts):
         s = saved[part]
@@ -1078,7 +1157,7 @@
     pooled = (everywhere * vectors[13] + counts * vectors[14]) / counts
 
     def loss_of(pooled_now, w, b):
-        return image_loss(pooled_now, w, b, teacher, labels, image_total)
+        return image_loss(pooled_now, w, b, log_teacher, labels, image_total)
 
     loss_value, loss_back = jax.vjp(loss_of, pooled, head_w, head_b)
     grad_pooled, total["w_head"], total["b_head"] = loss_back(jnp.ones_like(loss_value))
@@ -1095,9 +1174,14 @@
         dx1, dq, up, down, dkv, a2, a1, ap, av, ak, ar = s["bwd"]
         for name, value in (("a2", a2), ("a1", a1), ("ap", ap), ("av", av), ("ak", ak), ("ar", ar)):
             add(name, value)
-        rtop = shifted(down, "row", 1)
-        rbot = shifted(up, "row", -1)
-        grad_kv = scatter_slots(dkv, "row")
+        bits = bit_count(key_rows)
+        for bit in range(bits):
+            if bit == bits - 1:
+                dkv, up, down = together(dkv, up, down)
+                rtop = shifted(down, "row", 1)
+                rbot = shifted(up, "row", -1)
+            dkv = scatter_step(dkv, "row", bit)
+        grad_kv = dkv[0]
         pre, pool_sums = call_pool_back(s["own"], s["got"], grad_kv, wts["vec"])
         add("pool_sums", pool_sums)
         under = shifted(pre, "row", -1)
@@ -1115,13 +1199,13 @@
     kernels = jnp.concatenate([jnp.sum(t["ak"], axis=-1), jnp.transpose(taps, (0, 2, 3, 1)).reshape(18, DIM)], axis=0)
     grad_vectors = jnp.stack([
         av1[0], av1[1], av1[2], av[2], av[3], pool_sums[0], pool_sums[1], pool_sums[2], pool_sums[3],
-        t["ap"][DIM], av[0], av[1], t["a2"][:, MLP], t["g_three"], t["b_three"]])
+        t["ap"][DIM], av[0], av[1], t["a2"][MLP], t["g_three"], t["b_three"]])
     pieces = [
         patch_rows_back(t["apatch"]),
         jnp.concatenate([t["aq"][:DIM], t["akv"][:DIM]], axis=1),
         t["ap"][:DIM],
         t["a1"][:DIM],
-        t["a2"][:, :MLP].T,
+        t["a2"][:MLP],
         t["w_head"] * lead,
         rel_rows,
         rel_cols,

time: 522 us -> 497 us (0.952)
  waiting for transfers between devices: 85.6 us -> 49.1 us
  starting transfers between devices: 63 us -> 71.7 us
  local copies, waits for them, and re-layouts: 42.9 us -> 37.5 us
    all_gather x1, waiting for transfers between devices: 22.5 us -> 0.02 us  [body(): kv = lax.all_gather(call_pool_norm(own, got, wts['vec']), 'row', axis=0)]
    pallas_call x0 -> x1, Pallas kernels: none -> 20.5 us  [call_edge(): pl.pallas_call(functools.partial(edge_kernel, offset=offset), grid_spec=p...]
    ppermute x21, waiting for transfers between devices: 61.6 us -> 47 us  [swap(): return lax.ppermute(value, axis, [(i, i ^ 1 << bit) for i in range(size)])]
    ppermute x21, starting transfers between devices: 46.3 us -> 59.9 us  [swap(): return lax.ppermute(value, axis, [(i, i ^ 1 << bit) for i in range(size)])]
    unnamed x59, local copies, waits for them, and re-layouts: 11.8 us -> 2.73 us
    pallas_call x1, Pallas kernels: 37.5 us -> 29.7 us  [call_embed(): pl.pallas_call(functools.partial(embed_kernel, offset=offset), grid_spec=...]
  transfers between devices with their start and end apart: 28 -> 28, of which waited for: 21 -> 18; matrix products, arithmetic and copies ran while one was open for 6% -> 5% of each run, Pallas kernels for 0% -> 7%
where the time goes in v4:
time: 497 us; the launch traced here: 492 us
  Pallas kernels  291 us (59%)
  starting transfers between devices  71.7 us (14%)
  waiting for transfers between devices  49.1 us (10%)
  local copies, waits for them, and re-layouts  37.5 us (8%)
  other arithmetic  20.1 us (4%)
  between operations  20.1 us (4%)
    pallas_call x1, Pallas kernels, call_backward(): pl.pallas_call(functools.partial(backward_kernel, offset=offset, key_rows...  108 us
    pallas_call x1, Pallas kernels, call_forward(): pl.pallas_call(functools.partial(forward_kernel, offset=offset, key_rows=...  88.4 us
    ppermute x21, starting transfers between devices, swap(): return lax.ppermute(value, axis, [(i, i ^ 1 << bit) for i in range(size)])  59.9 us
    ppermute x21, waiting for transfers between devices, swap(): return lax.ppermute(value, axis, [(i, i ^ 1 << bit) for i in range(size)])  47 us
    pallas_call x1, Pallas kernels, call_embed_back(): pl.pallas_call(functools.partial(embed_back_kernel, offset=offset), grid_...  40 us
    pallas_call x1, Pallas kernels, call_embed(): pl.pallas_call(functools.partial(embed_kernel, offset=offset), grid_spec=...  29.7 us
    pallas_call x1, Pallas kernels, call_edge(): pl.pallas_call(functools.partial(edge_kernel, offset=offset), grid_spec=p...  20.5 us
    ppermute x6, starting transfers between devices, shifted(): return lax.ppermute(value, axis, pairs)  11.8 us
  transfers between devices with their start and end apart: 28, of which 18 were waited for; matrix products, arithmetic and copies ran while one was open for 5% of the time, Pallas kernels for 7%

profile of v4, /device:TPU:0, one launch (start us, length us, event | category | flops | bytes accessed | tf_op | source)
XLA Modules:
  0.0 492.0 jit_solution(9681960786749668910)
XLA Ops:
  8.0 4.0 collective-permute-start
  12.8 1.0 collective-permute-done
  14.6 2.0 collective-permute-start.1
  16.7 1.9 collective-permute-done.1
  18.6 2.0 collective-permute-start.2
  20.6 2.4 collective-permute-done.2
  23.1 2.0 collective-permute-start.3
  26.5 1.0 reduce_max.20
  27.5 1.0 exponential_reduce_fusion
  29.3 0.9 subtract_subtract_fusion
  34.4 20.5 %edge.1 = (bf16[16,96,256]{2,1,0:T(8,128)(2,1)}, bf16[16,96,256]{2,1,0:T(8,128)(2,1)}, bf16[16,96,384]{2,1,0:T(8,128)(2,1)}, bf16[16,192,384]{2,1,0:T(8,128)(2,1...) custom-call(s32[16,2]{1,0:T(8,128)} %copy.207.ext_ref, s32[1]{0:T(128)} %bitcast.1.row_ref, s32[16]{0:T(128)} %select_reduce_fusion.4.order_ref, ...), custom_call_target="tpu_custom_call" | custom-call | flops 16000000000 | bytes 16000000 | tf_op jit(solution)/shard_map/edge/pallas_call | solution.py:429
  54.9 2.4 collective-permute-start.7
  62.4 3.2 collective-permute-start.5
  65.6 1.5 collective-permute-start.6
  67.8 1.9 pool_norm.1
  69.8 29.7 %embed.1 = (bf16[16,256,2048]{2,1,0:T(8,128)(2,1)}, f32[16,96,2048]{2,1,0:T(8,128)}, bf16[16,96,2560]{2,1,0:T(8,128)(2,1)}) custom-call(s32[16,2]{1,0:T(8,128)} %copy.199.ext_ref, s32[1]{0:T(128)} %bitcast.1.row_ref, s32[16]{0:T(128)} %select_reduce_fusion.4.order_ref, bf16[16,7,3,8,1024]{4,3,2,1,0:T(8,128)(2,1)} %bitcast.169, ...), custom_call_target="tpu_custom_call" | custom-call | flops 32000000000 | bytes 64000000 | tf_op jit(solution)/shard_map/embed/pallas_call | solution.py:449
  99.5 0.9 copy.204.rw_ref
  100.5 0.9 copy-done.26
  101.6 88.4 %forward.1 = (bf16[16,96,2048]{2,1,0:T(8,128)(2,1)}, bf16[16,96,2048]{2,1,0:T(8,128)(2,1)}, bf16[16,96,2048]{2,1,0:T(8,128)(2,1)}, bf16[16,96,2048]{2,1,0:T(8,12...) custom-call(s32[16,2]{1,0:T(8,128)} %copy.207.ext_ref, ...), custom_call_target="tpu_custom_call" | custom-call | flops 80000000000 | bytes 64000000 | tf_op jit(solution)/shard_map/forward/pallas_call | solution.py:646
  190.1 1.5 reduce_sum.215
  191.7 1.2 collective-permute-start.8
  193.7 1.9 collective-permute-start.9
  195.6 1.8 collective-permute-done.9
  197.3 2.8 collective-permute-start.10
  200.7 1.0 collective-permute-done.10
  204.8 1.2 copy.206.gvec_ref
  206.1 107.9 %backward.1 = (bf16[16,96,2048]{2,1,0:T(8,128)(2,1)}, bf16[16,96,2048]{2,1,0:T(8,128)(2,1)}, bf16[16,96,256]{2,1,0:T(8,128)(2,1)}, bf16[16,96,256]{2,1,0:T(8,128...) custom-call(s32[16,2]{1,0:T(8,128)} %copy.207.ext_ref, ...), custom_call_target="tpu_custom_call" | custom-call | flops 192000000000 | bytes 96000000 | tf_op jit(solution)/shard_map/backward/pallas_call | solution.py:834
  314.1 1.6 slice.282
  317.2 0.9 slice.217
  319.6 0.9 slice.216
  321.9 1.3 convolution_multiply_fusion
  324.3 1.7 convert_add_fusion
  326.8 1.1 collective-permute-start.12
  328.3 10.4 %collective-permute-done.12 = bf16[2,192,512]{2,1,0:T(8,128)(2,1)} collective-permute-done((bf16[2,192,512]{2,1,0:T(8,128)(2,1)}, bf16[2,192,512]{2,1,0:T(8,128)(2,1)}, u32[]{:S(2)}, u32[]{:S(2)}) %collective-permute-start.12) | collective-permute-done | bytes 393248 | tf_op jit(solution)/shard_map/ppermute | solution.py:950
  338.6 1.1 slice_add_fusion
  339.8 2.1 collective-permute-start.15
  342.5 2.2 collective-permute-start.13
  344.7 1.3 collective-permute-start.14
  347.6 2.4 pool_back.1
  349.9 1.3 collective-permute-start.16
  351.3 1.1 reduce_sum.224
  352.3 2.0 collective-permute-done.16.under_ref
  355.1 40.0 %embed_back.1 = (f32[112,96]{1,0:T(8,128)}, f32[112,192]{1,0:T(8,128)}, f32[96,256]{1,0:T(8,128)}, f32[3,96,128]{2,1,0:T(8,128)}, f32[192,384]{1,0:T(8,128)}) custom-call(s32[16,2]{1,0:T(8,128)} %copy.207.ext_ref, s32[1]{0:T(128)} %bitcast.1.row_ref, bf16[16,256,2048]{2,1,0:T(8,128)(2,1)} %get-tuple-element.60.patch_ref, ...), custom_call_target="tpu_custom_call" | custom-call | flops 48000000000 | bytes 48000000 | tf_op jit(solution)/shard_map/embed_back/pallas_call | solution.py:927
  395.2 1.1 copy.208
  397.8 0.9 slice.214
  399.9 1.1 copy.216
  402.2 6.5 %concatenate.35 = f32[286312]{0:T(1024)S(1)} concatenate(f32[14112]{0:T(1024)S(1)} %reshape_reshape.21, f32[27648]{0:T(1024)S(1)} %reshape.187, f32[9216]{0:T(1024)S(1)} %copy-done.11, f32[36864]{0:T(1024)S(1)} %copy-done.3, f32[36864]{0:T(1024)S(1)} %copy-done.4, f32[96000]{0:T(1024)S(1)} %reshape.191, f32[11520]{0:T(1024)S(1)} %reshape_reshape.22, f32[48384]{0:T(1024)S(1)} %reshape_reshape.23, ...), dimensions={0} | concatenate | bytes 2290496 | tf_op jit(solution)/shard_map/concatenate | solution.py:1219
  409.2 13.6 %collective-permute-start.17 = (f32[2,2,2,2,70,128]{5,3,4,2,1,0:T(2,128)S(1)}, f32[2,2,2,2,70,128]{5,3,4,2,1,0:T(2,128)S(1)}, u32[]{:S(2)}, u32[]{:S(2)}) collective-permute-start(f32[2,2,2,2,70,128]{5,3,4,2,1,0:T(2,128)S(1)} %copy.218), channel_id=1, source_target_pairs={{0,1},{1,0},{2,3},{3,2},{4,5},{5,4},{6,7},{7,6},{8,9},{9,8},{10,11... | collective-permute-start | bytes 1720328 | tf_op jit(solution)/shard_map/ppermute | solution.py:950
  422.9 1.6 collective-permute-done.17
  424.6 1.2 collective-permute-start.18
  425.7 8.2 %collective-permute-done.18 = f32[2,2,2,70,128]{4,3,2,1,0:T(8,128)S(1)} collective-permute-done((f32[2,2,2,70,128]{4,3,2,1,0:T(8,128)S(1)}, f32[2,2,2,70,128]{4,3,2,1,0:T(8,128)S(1)}, u32[]{:S(2)}, u32[]{:S(2)}) %collective-permute-start.18) | collective-permute-done | bytes 286752 | tf_op jit(solution)/shard_map/ppermute | solution.py:950
  434.1 5.3 %collective-permute-done.19 = f32[2,2,70,128]{3,2,1,0:T(8,128)S(1)} collective-permute-done((f32[2,2,70,128]{3,2,1,0:T(8,128)S(1)}, f32[2,2,70,128]{3,2,1,0:T(8,128)S(1)}, u32[]{:S(2)}, u32[]{:S(2)}) %collective-permute-start.19) | collective-permute-done | bytes 143392 | tf_op jit(solution)/shard_map/ppermute | solution.py:950
  439.4 8.5 %collective-permute-start.20 = (f32[2,70,128]{2,1,0:T(8,128)S(1)}, f32[2,70,128]{2,1,0:T(8,128)S(1)}, u32[]{:S(2)}, u32[]{:S(2)}) collective-permute-start(f32[2,70,128]{2,1,0:T(8,128)S(1)} %dynamic-slice_bitcast_fusion.3), channel_id=1, source_target_pairs={{0,8},{8,0},{16,24},{24,16},{1,9},{9,1},{17,25},{25,17},{2,10},{10... | collective-permute-start | bytes 215048 | tf_op jit(solution)/shard_map/ppermute | solution.py:950
  447.9 2.3 collective-permute-done.20
  450.3 10.1 %collective-permute-start.21 = (f32[70,128]{1,0:T(8,128)S(1)}, f32[70,128]{1,0:T(8,128)S(1)}, u32[]{:S(2)}, u32[]{:S(2)}) collective-permute-start(f32[70,128]{1,0:T(8,128)S(1)} %dynamic-slice_bitcast_fusion.4), channel_id=1, source_target_pairs={{0,16},{8,24},{16,0},{24,8},{1,17},{9,25},{17,1},{25,9},{2,18},{10... | collective-permute-start | bytes 107528 | tf_op jit(solution)/shard_map/ppermute | solution.py:950
  461.0 1.3 collective-permute-done.21
  462.9 1.2 collective-permute-done.22
  465.4 2.4 collective-permute-start.23
  467.9 1.1 collective-permute-done.23
  469.6 1.9 collective-permute-start.24
  471.5 1.7 collective-permute-done.24
  473.9 3.5 collective-permute-done.25
  477.5 2.9 collective-permute-start.26
  480.4 1.5 collective-permute-done.26
  (223 shorter events, 35.6 us)
Async XLA Ops:
  7.2 93.3 %all-gather.3.cloned.1.call-start = ((), (), s32[]{:S(2)}) async-start(), calls=%async_computation | async-start | bytes 1769472 | tf_op jit(solution)/shard_map/all_gather | solution.py:1137
  8.0 5.8 %collective-permute-start = (bf16[70,128]{1,0:T(8,128)(2,1)S(1)}, bf16[70,128]{1,0:T(8,128)(2,1)S(1)}, u32[]{:S(2)}, u32[]{:S(2)}) collective-permute-start(bf16[70,128]{1,0:T(8,128)(2,1)S(1)} %convert_bitcast_fusion), channel_id=1, source_target_pairs={{0,16},{8,24},{16,0},{24,8},{1,17},{9,25},{17,1},{25,9},{2,18},{10... | collective-permute-start | bytes 53768 | tf_op jit(solution)/shard_map/ppermute | solution.py:950
  12.8 191.1 %copy-start.19 = (f32[16]{0:T(128)}, f32[16]{0:T(128)S(1)}, u32[]{:S(2)}) copy-start(f32[16]{0:T(128)S(1)} %get-tuple-element.151) | copy-start | bytes 196
  14.6 4.0 collective-permute-start.1
  18.6 4.4 collective-permute-start.2
  23.1 5.5 %collective-permute-start.3 = (bf16[2,2,2,70,128]{4,3,0,1,2:T(8,128)(2,1)S(1)}, bf16[2,2,2,70,128]{4,3,0,1,2:T(8,128)(2,1)S(1)}, u32[]{:S(2)}, u32[]{:S(2)}) collective-permute-start(bf16[2,2,2,70,128]{4,3,0,1,2:T(8,128)(2,1)S(1)} %pad_maximum_fusion.2), channel_id=1, source_target_pairs={{0,2},{1,3},{2,0},{3,1},{4,6},{5,7},{6,4},{7,5},{8,10},{9,11},{10,... | collective-permute-start | bytes 430088 | tf_op jit(solution)/shard_map/ppermute | solution.py:950
  28.6 1.6 collective-permute-start.4
  33.1 28.6 %copy-start.2 = (bf16[96,288]{1,0:T(8,128)(2,1)}, bf16[96,288]{1,0:T(8,128)(2,1)S(1)}, u32[]{:S(2)}) copy-start(bf16[96,288]{1,0:T(8,128)(2,1)S(1)} %reshape.183.wqkv_ref) | copy-start | bytes 165892
  54.9 12.2 %collective-permute-start.7 = (f32[192,512]{1,0:T(8,128)}, f32[192,512]{1,0:T(8,128)S(1)}, u32[]{:S(2)}, u32[]{:S(2)}) collective-permute-start(f32[192,512]{1,0:T(8,128)} %get-tuple-element.66), channel_id=1, source_target_pairs={{0,1},{1,2},{2,3},{3,4},{4,5},{5,6},{6,7},{8,9},{9,10},{10,11},{11... | collective-permute-start | bytes 1179656 | tf_op jit(solution)/shard_map/ppermute | solution.py:956
  62.4 38.1 %collective-permute-start.5 = (bf16[16,96,256]{2,1,0:T(8,128)(2,1)}, bf16[16,96,256]{2,1,0:T(8,128)(2,1)S(1)}, u32[]{:S(2)}, u32[]{:S(2)}) collective-permute-start(bf16[16,96,256]{2,1,0:T(8,128)(2,1)} %get-tuple-element.62), channel_id=1, source_target_pairs={{0,1},{1,2},{2,3},{3,4},{4,5},{5,6},{6,7},{8,9},{9,10},{10,11},{11... | collective-permute-start | bytes 2359304 | tf_op jit(solution)/shard_map/ppermute | solution.py:956
  65.6 34.9 %collective-permute-start.6 = (bf16[16,96,256]{2,1,0:T(8,128)(2,1)}, bf16[16,96,256]{2,1,0:T(8,128)(2,1)S(1)}, u32[]{:S(2)}, u32[]{:S(2)}) collective-permute-start(bf16[16,96,256]{2,1,0:T(8,128)(2,1)} %get-tuple-element.63), channel_id=1, source_target_pairs={{1,0},{2,1},{3,2},{4,3},{5,4},{6,5},{7,6},{9,8},{10,9},{11,10},{12... | collective-permute-start | bytes 2359304 | tf_op jit(solution)/shard_map/ppermute | solution.py:956
  67.1 0.8 copy-start
  100.5 0.9 copy-start.26
  100.5 1.1 copy-start.27
  101.6 100.7 %copy-start.23 = (s32[16]{0:T(128)S(1)}, s32[16]{0:T(128)}, u32[]{:S(2)}) copy-start(s32[16]{0:T(128)} %param.16) | copy-start | bytes 196
  191.7 2.0 collective-permute-start.8
  193.7 3.7 collective-permute-start.9
  197.3 116.7 %copy-start.13 = (f32[16,96]{1,0:T(8,128)}, f32[16,96]{1,0:T(8,128)S(1)}, u32[]{:S(2)}) copy-start(f32[16,96]{1,0:T(8,128)S(1)} %add.150) | copy-start | bytes 18436
  197.3 4.5 collective-permute-start.10
  200.2 5.9 %copy-start.21 = (f32[96]{0:T(128)}, f32[96]{0:T(128)S(1)}, u32[]{:S(2)}) copy-start(f32[96]{0:T(128)S(1)} %get-tuple-element.145) | copy-start | bytes 1156
  200.2 113.8 %copy-start.22 = (f32[96]{0:T(128)}, f32[96]{0:T(128)S(1)}, u32[]{:S(2)}) copy-start(f32[96]{0:T(128)S(1)} %get-tuple-element.146) | copy-start | bytes 1156
  201.8 112.3 %copy-start.16 = (f32[16,96]{1,0:T(8,128)}, f32[16,96]{1,0:T(8,128)S(1)}, u32[]{:S(2)}) copy-start(f32[16,96]{1,0:T(8,128)S(1)} %collective-permute-done.10) | copy-start | bytes 18436
  203.9 110.1 %copy-start.7 = (f32[16,1000]{1,0:T(8,128)}, f32[16,1000]{1,0:T(8,128)S(1)}, u32[]{:S(2)}) copy-start(f32[16,1000]{1,0:T(8,128)S(1)} %get-tuple-element.118) | copy-start | bytes 192004
  206.1 115.9 %copy-start.20 = (f32[16]{0:T(128)S(1)}, f32[16]{0:T(128)}, u32[]{:S(2)}) copy-start(f32[16]{0:T(128)} %copy-done.19) | copy-start | bytes 196
  314.0 9.6 %copy-start.1 = (f32[4,384,96]{2,1,0:T(8,128)S(1)}, f32[4,384,96]{2,1,0:T(8,128)}, u32[]{:S(2)}) copy-start(f32[4,384,96]{2,1,0:T(8,128)} %get-tuple-element.101) | copy-start | bytes 1769476
  314.0 7.9 %copy-start.8 = (f32[16,1000]{1,0:T(8,128)S(1)}, f32[16,1000]{1,0:T(8,128)}, u32[]{:S(2)}) copy-start(f32[16,1000]{1,0:T(8,128)} %copy-done.7) | copy-start | bytes 192004
  315.7 8.6 %collective-permute-start.11 = (bf16[4,192,512]{2,1,0:T(8,128)(2,1)S(1)}, bf16[4,192,512]{2,1,0:T(8,128)(2,1)S(1)}, u32[]{:S(2)}, u32[]{:S(2)}) collective-permute-start(bf16[4,192,512]{2,1,0:T(8,128)(2,1)S(1)} %slice.282), channel_id=1, source_target_pairs={{0,1},{1,0},{2,3},{3,2},{4,5},{5,4},{6,7},{7,6},{8,9},{9,8},{10,11... | collective-permute-start | bytes 2359304 | tf_op jit(solution)/shard_map/ppermute | solution.py:950
  324.3 3.6 copy-start.12
  326.8 11.8 %collective-permute-start.12 = (bf16[2,192,512]{2,1,0:T(8,128)(2,1)}, bf16[2,192,512]{2,1,0:T(8,128)(2,1)}, u32[]{:S(2)}, u32[]{:S(2)}) collective-permute-start(bf16[2,192,512]{2,1,0:T(8,128)(2,1)} %slice.283), channel_id=1, source_target_pairs={{0,2},{1,3},{2,0},{3,1},{4,6},{5,7},{6,4},{7,5},{8,10},{9,11},{10,... | collective-permute-start | bytes 1179656 | tf_op jit(solution)/shard_map/ppermute | solution.py:950
  328.0 14.1 %copy-start.5 = (f32[9,96,128]{2,1,0:T(8,128)S(1)}, f32[9,96,128]{2,1,0:T(8,128)}, u32[]{:S(2)}) copy-start(f32[9,96,128]{2,1,0:T(8,128)} %get-tuple-element.102) | copy-start | bytes 1327108
  328.1 14.3 %copy-start.9 = (f32[4,96,128]{2,1,0:T(8,128)S(1)}, f32[4,96,128]{2,1,0:T(8,128)}, u32[]{:S(2)}) copy-start(f32[4,96,128]{2,1,0:T(8,128)} %get-tuple-element.105) | copy-start | bytes 589828
  328.3 23.0 %copy-start.17 = (f32[1000]{0:T(1024)S(1)}, f32[1000]{0:T(1024)}, u32[]{:S(2)}) copy-start(f32[1000]{0:T(1024)} %get-tuple-element.117) | copy-start | bytes 12004
  339.8 7.0 %collective-permute-start.15 = (bf16[1,192,512]{2,1,0:T(8,128)(2,1)S(1)}, bf16[1,192,512]{2,1,0:T(8,128)(2,1)S(1)}, u32[]{:S(2)}, u32[]{:S(2)}) collective-permute-start(bf16[1,192,512]{2,1,0:T(8,128)(2,1)S(1)} %slice.284), channel_id=1, source_target_pairs={{0,4},{1,5},{2,6},{3,7},{4,0},{5,1},{6,2},{7,3},{8,12},{9,13},{10,... | collective-permute-start | bytes 589832 | tf_op jit(solution)/shard_map/ppermute | solution.py:950
  342.5 11.9 %collective-permute-start.13 = (bf16[16,96,256]{2,1,0:T(8,128)(2,1)}, bf16[16,96,256]{2,1,0:T(8,128)(2,1)}, u32[]{:S(2)}, u32[]{:S(2)}) collective-permute-start(bf16[16,96,256]{2,1,0:T(8,128)(2,1)} %get-tuple-element.88), channel_id=1, source_target_pairs={{0,1},{1,2},{2,3},{3,4},{4,5},{5,6},{6,7},{8,9},{9,10},{10,11},{11... | collective-permute-start | bytes 2359304 | tf_op jit(solution)/shard_map/ppermute | solution.py:956
  344.7 9.7 %collective-permute-start.14 = (bf16[16,96,256]{2,1,0:T(8,128)(2,1)}, bf16[16,96,256]{2,1,0:T(8,128)(2,1)}, u32[]{:S(2)}, u32[]{:S(2)}) collective-permute-start(bf16[16,96,256]{2,1,0:T(8,128)(2,1)} %get-tuple-element.89), channel_id=1, source_target_pairs={{1,0},{2,1},{3,2},{4,3},{5,4},{6,5},{7,6},{9,8},{10,9},{11,10},{12... | collective-permute-start | bytes 2359304 | tf_op jit(solution)/shard_map/ppermute | solution.py:956
  349.9 4.4 collective-permute-start.16
  354.4 0.8 copy-start.28
  395.1 6.1 %copy-start.18 = (f32[3,4,32]{2,1,0:T(4,128)S(1)}, f32[3,4,32]{2,1,0:T(4,128)}, u32[]{:S(2)}) copy-start(f32[3,4,32]{2,1,0:T(4,128)} %constant.112.clone) | copy-start | bytes 4612
  395.1 6.6 %copy-start.10 = (f32[3,96,128]{2,1,0:T(8,128)S(1)}, f32[3,96,128]{2,1,0:T(8,128)}, u32[]{:S(2)}) copy-start(f32[3,96,128]{2,1,0:T(8,128)} %get-tuple-element.104) | copy-start | bytes 442372
  395.2 6.8 %copy-start.24 = (f32[96]{0:T(128)S(1)}, f32[96]{0:T(128)}, u32[]{:S(2)}) copy-start(f32[96]{0:T(128)} %get-tuple-element.110) | copy-start | bytes 1156
  395.2 6.8 %copy-start.25 = (f32[96]{0:T(128)S(1)}, f32[96]{0:T(128)}, u32[]{:S(2)}) copy-start(f32[96]{0:T(128)} %get-tuple-element.111) | copy-start | bytes 1156
  395.2 7.0 %copy-start.3 = (f32[36864]{0:T(1024)S(1)}, f32[36864]{0:T(1024)}, u32[]{:S(2)}) copy-start(f32[36864]{0:T(1024)} %reshape.189) | copy-start | bytes 442372
  395.2 7.0 %copy-start.4 = (f32[36864]{0:T(1024)S(1)}, f32[36864]{0:T(1024)}, u32[]{:S(2)}) copy-start(f32[36864]{0:T(1024)} %reshape.190) | copy-start | bytes 442372
  395.2 7.0 %copy-start.11 = (f32[9216]{0:T(1024)S(1)}, f32[9216]{0:T(1024)}, u32[]{:S(2)}) copy-start(f32[9216]{0:T(1024)} %reshape.188) | copy-start | bytes 110596
  408.9 74.5 %copy-start.6 = (f32[8960]{0:T(1024)S(1)}, f32[8960]{0:T(1024)}, u32[]{:S(2)}) copy-start(f32[8960]{0:T(1024)} %param.11) | copy-start | bytes 107524
  408.9 74.5 %copy-start.14 = (f32[8960]{0:T(1024)S(1)}, f32[8960]{0:T(1024)}, u32[]{:S(2)}) copy-start(f32[8960]{0:T(1024)} %param.12) | copy-start | bytes 107524
  408.9 74.5 %copy-start.15 = (f32[8960]{0:T(1024)S(1)}, f32[8960]{0:T(1024)}, u32[]{:S(2)}) copy-start(f32[8960]{0:T(1024)} %param.13) | copy-start | bytes 107524
  409.2 15.2 %collective-permute-start.17 = (f32[2,2,2,2,70,128]{5,3,4,2,1,0:T(2,128)S(1)}, f32[2,2,2,2,70,128]{5,3,4,2,1,0:T(2,128)S(1)}, u32[]{:S(2)}, u32[]{:S(2)}) collective-permute-start(f32[2,2,2,2,70,128]{5,3,4,2,1,0:T(2,128)S(1)} %copy.218), channel_id=1, source_target_pairs={{0,1},{1,0},{2,3},{3,2},{4,5},{5,4},{6,7},{7,6},{8,9},{9,8},{10,11... | collective-permute-start | bytes 1720328 | tf_op jit(solution)/shard_map/ppermute | solution.py:950
  424.6 9.4 %collective-permute-start.18 = (f32[2,2,2,70,128]{4,3,2,1,0:T(8,128)S(1)}, f32[2,2,2,70,128]{4,3,2,1,0:T(8,128)S(1)}, u32[]{:S(2)}, u32[]{:S(2)}) collective-permute-start(f32[2,2,2,70,128]{4,3,2,1,0:T(8,128)S(1)} %dynamic-slice_bitcast_fusion.1), channel_id=1, source_target_pairs={{0,2},{1,3},{2,0},{3,1},{4,6},{5,7},{6,4},{7,5},{8,10},{9,11},{10,... | collective-permute-start | bytes 860168 | tf_op jit(solution)/shard_map/ppermute | solution.py:950
  434.0 5.4 %collective-permute-start.19 = (f32[2,2,70,128]{3,2,1,0:T(8,128)S(1)}, f32[2,2,70,128]{3,2,1,0:T(8,128)S(1)}, u32[]{:S(2)}, u32[]{:S(2)}) collective-permute-start(f32[2,2,70,128]{3,2,1,0:T(8,128)S(1)} %dynamic-slice_bitcast_fusion.2), channel_id=1, source_target_pairs={{0,4},{1,5},{2,6},{3,7},{4,0},{5,1},{6,2},{7,3},{8,12},{9,13},{10,... | collective-permute-start | bytes 430088 | tf_op jit(solution)/shard_map/ppermute | solution.py:950
  439.4 10.8 %collective-permute-start.20 = (f32[2,70,128]{2,1,0:T(8,128)S(1)}, f32[2,70,128]{2,1,0:T(8,128)S(1)}, u32[]{:S(2)}, u32[]{:S(2)}) collective-permute-start(f32[2,70,128]{2,1,0:T(8,128)S(1)} %dynamic-slice_bitcast_fusion.3), channel_id=1, source_target_pairs={{0,8},{8,0},{16,24},{24,16},{1,9},{9,1},{17,25},{25,17},{2,10},{10... | collective-permute-start | bytes 215048 | tf_op jit(solution)/shard_map/ppermute | solution.py:950
  450.3 12.0 %collective-permute-start.21 = (f32[70,128]{1,0:T(8,128)S(1)}, f32[70,128]{1,0:T(8,128)S(1)}, u32[]{:S(2)}, u32[]{:S(2)}) collective-permute-start(f32[70,128]{1,0:T(8,128)S(1)} %dynamic-slice_bitcast_fusion.4), channel_id=1, source_target_pairs={{0,16},{8,24},{16,0},{24,8},{1,17},{9,25},{17,1},{25,9},{2,18},{10... | collective-permute-start | bytes 107528 | tf_op jit(solution)/shard_map/ppermute | solution.py:950
  462.9 1.2 collective-permute-start.22
  465.4 3.6 collective-permute-start.23
  469.6 3.6 collective-permute-start.24
  473.9 3.5 collective-permute-start.25
  477.5 4.4 collective-permute-start.26
Sparse Core Ops, SparseCore 0:
  69.9 29.1 all-gather.2

commit v5 on v4

--- a/solution.py
+++ b/solution.py
@@ -334,12 +334,12 @@
 
     def first_norm(k, embed, mask):
         hat, _ = normalized((embed + wide_ref[0]) * mask)
-        return ((hat * wide_ref[1] + wide_ref[2]).astype(BF16).astype(F32),)
+        return ((hat * wide_ref[1] + wide_ref[2]).astype(BF16),)
 
     (normed,) = by_lanes(first_norm, dot(wp_ref[...], p_ref[...]), jnp.concatenate(masks, axis=1))
     rows = []
     for slot in range(3):
-        rows.append(jnp.concatenate([gather_halo(normed[:, 1024 * g : 1024 * g + 1024], 32 * slot) for g in range(GROUP)], axis=1).astype(BF16))
+        rows.append(jnp.concatenate([gather_halo(normed[:, 1024 * g : 1024 * g + 1024], 32 * slot) for g in range(GROUP)], axis=1))
     edge = dot(wqkv_ref[0:DIM, :], jnp.concatenate(rows[:2], axis=1))
     (edge,) = by_lanes(lambda k, out: ((out + wide_ref[3]).astype(BF16),), edge)
     nsel = dot(jnp.concatenate([row[:, CANVAS_W * g : CANVAS_W * g + CANVAS_W] for g in range(GROUP) for row in rows], axis=0), tap_ref[...])
@@ -873,7 +873,7 @@
     grad_taps = []
     for g in range(GROUP):
         own = thrice(pre_ref[...], images[g])
-        spread = jnp.concatenate([thrice(under_ref[...], images[g]), own, own], axis=1)
+        spread = jnp.concatenate([thrice(under_ref[...].astype(F32), images[g]), own, own], axis=1)
         ak_ref[...] += kvt_ref[g].astype(F32) * spread
         grad_taps.append((spread * kexp_ref[...]).astype(BF16))
     grad_taps = jnp.concatenate(grad_taps, axis=1)
@@ -988,21 +988,21 @@
     return value.reshape(-1)
 
 
-def scatter_grads(flat):
+def sum_grads(flat, extra):
     rows, imgs = lax.axis_size("row"), lax.axis_size("img")
-    names = [("img", b) for b in reversed(range(bit_count(imgs)))] + [("row", b) for b in reversed(range(bit_count(rows)))]
+    bits = bit_count(rows)
     leaf = flat.shape[0] // (rows * imgs)
-    value = flat.reshape((2,) * len(names) + (leaf // 128, 128))
-    for axis, bits in (("row", range(bit_count(rows))), ("img", range(bit_count(imgs)))):
-        index = lax.axis_index(axis)
-        for bit in bits:
-            place = names.index((axis, bit))
-            names.pop(place)
-            own = (index >> bit) & 1
-            keep = lax.dynamic_index_in_dim(value, own, place, False)
-            send = lax.dynamic_index_in_dim(value, 1 - own, place, False)
-            value = keep + swap(send, axis, bit)
-    return value.reshape(leaf)
+    value = flat.reshape((imgs,) + (2,) * bits + (leaf // 128, 128))
+    index = lax.axis_index("row")
+    for bit in range(bits):
+        place = value.ndim - 3
+        own = (index >> bit) & 1
+        keep = lax.dynamic_index_in_dim(value, own, place, False)
+        send = lax.dynamic_index_in_dim(value, 1 - own, place, False)
+        value = keep + swap(send, "row", bit)
+    value = jnp.concatenate([value.reshape(imgs * leaf // 128, 128), jnp.full((8, 128), extra)], axis=0)
+    value = summed(value, "img")
+    return value[:-8], value[-1, 0]
 
 
 def segment_list(canvas_rows, canvas_cols):
@@ -1171,20 +1171,21 @@
         s["bwd"] = call_backward(ext, row, s["fwd"][:-1], s["q"], s["top"], s["bot"], s["kv"], gvec[part * size : part * size + size], wts, part * size)
     for part in range(parts):
         s = saved[part]
-        dx1, dq, up, down, dkv, a2, a1, ap, av, ak, ar = s["bwd"]
-        for name, value in (("a2", a2), ("a1", a1), ("ap", ap), ("av", av), ("ak", ak), ("ar", ar)):
-            add(name, value)
-        bits = bit_count(key_rows)
-        for bit in range(bits):
-            if bit == bits - 1:
+        dx1, dq, up, down, dkv, *sums = s["bwd"]
+        for bit in range(bit_count(key_rows)):
+            if bit == 1:
                 dkv, up, down = together(dkv, up, down)
                 rtop = shifted(down, "row", 1)
                 rbot = shifted(up, "row", -1)
             dkv = scatter_step(dkv, "row", bit)
+            if bit == 1:
+                dkv, *sums = together(dkv, *sums)
+        for name, value in zip(("a2", "a1", "ap", "av", "ak", "ar"), sums):
+            add(name, value)
         grad_kv = dkv[0]
         pre, pool_sums = call_pool_back(s["own"], s["got"], grad_kv, wts["vec"])
         add("pool_sums", pool_sums)
-        under = shifted(pre, "row", -1)
+        under = shifted(pre.astype(BF16), "row", -1)
         aq, akv, apatch, av1, akt = call_embed_back(
             ext, row, s["patches"], dq, dx1, rtop, rbot, s["nsel"], s["kvt"], pre, under, consts, wts, part * size)
         for name, value in (("aq", aq), ("akv", akv), ("apatch", apatch), ("av1", av1), ("akt", akt)):
@@ -1218,10 +1219,11 @@
     ]
     joined = jnp.concatenate([piece.reshape(-1) for piece in pieces])
     grad_flat = jnp.pad(joined, (0, full_params.shape[0] - joined.shape[0]))
-    grad_shard = scatter_grads(grad_flat)
-    norm_sq = summed(jnp.sum(grad_shard * grad_shard), "row")
-    both = summed(jnp.stack([norm_sq, loss_value]), "img")
-    grad_norm = jnp.sqrt(both[0])
+    shares, loss_sum = sum_grads(grad_flat, loss_value)
+    norm_sq = summed(jnp.sum(shares * shares), "row")
+    lines = flat_params.shape[0] // 128
+    grad_shard = lax.dynamic_slice_in_dim(shares, lax.axis_index("img") * lines, lines, 0).reshape(-1)
+    grad_norm = jnp.sqrt(norm_sq)
     clip_factor = jnp.minimum(1.0, CLIP_NORM / (grad_norm + 1e-06))
     clipped = grad_shard * clip_factor
     moment_one = BETA_FIRST * first_moment + (1.0 - BETA_FIRST) * clipped
@@ -1230,7 +1232,7 @@
     fix_two = 1.0 - BETA_SECOND**STEP
     update = moment_one / fix_one / (jnp.sqrt(moment_two / fix_two) + ADAM_EPS) + WEIGHT_DECAY * flat_params
     new_params = flat_params - LEARN_RATE * update
-    return (new_params, moment_one, moment_two, grad_norm, both[1])
+    return (new_params, moment_one, moment_two, grad_norm, loss_sum)
 
 
 def solution(mesh):

time: 497 us -> 482 us (0.970); the launches traced: 492 us -> 484 us
  Pallas kernels: 291 us -> 283 us
    ppermute x21 -> x19, starting transfers between devices: 59.9 us -> 61.3 us  [swap(): return lax.ppermute(value, axis, [(i, i ^ 1 << bit) for i in range(size)])]
    ppermute x21 -> x19, waiting for transfers between devices: 47 us -> 45.8 us  [swap(): return lax.ppermute(value, axis, [(i, i ^ 1 << bit) for i in range(size)])]
  transfers between devices with their start and end apart: 28 -> 26, of which waited for: 18 -> 18; matrix products, arithmetic and copies ran while one was open for 5% -> 5% of each run, Pallas kernels for 7% -> 7%
where the time goes in v5:
time: 482 us; the launch traced here: 484 us
  Pallas kernels  283 us (59%)
  starting transfers between devices  73.7 us (15%)
  waiting for transfers between devices  46.8 us (10%)
  local copies, waits for them, and re-layouts  34 us (7%)
  other arithmetic  24.6 us (5%)
  between operations  19.7 us (4%)
    pallas_call x1, Pallas kernels, call_backward(): pl.pallas_call(functools.partial(backward_kernel, offset=offset, key_rows...  105 us
    pallas_call x1, Pallas kernels, call_forward(): pl.pallas_call(functools.partial(forward_kernel, offset=offset, key_rows=...  85.8 us
    ppermute x19, starting transfers between devices, swap(): return lax.ppermute(value, axis, [(i, i ^ 1 << bit) for i in range(size)])  61.3 us
    ppermute x19, waiting for transfers between devices, swap(): return lax.ppermute(value, axis, [(i, i ^ 1 << bit) for i in range(size)])  45.8 us
    pallas_call x1, Pallas kernels, call_embed_back(): pl.pallas_call(functools.partial(embed_back_kernel, offset=offset), grid_...  38.7 us
    pallas_call x1, Pallas kernels, call_embed(): pl.pallas_call(functools.partial(embed_kernel, offset=offset), grid_spec=...  29.3 us
    pallas_call x1, Pallas kernels, call_edge(): pl.pallas_call(functools.partial(edge_kernel, offset=offset), grid_spec=p...  20 us
    ppermute x6, starting transfers between devices, shifted(): return lax.ppermute(value, axis, pairs)  12.3 us
  transfers between devices with their start and end apart: 26, of which 18 were waited for; matrix products, arithmetic and copies ran while one was open for 5% of the time, Pallas kernels for 7%

profile of v5, /device:TPU:0, one launch (start us, length us, event | category | flops | bytes accessed | tf_op | source)
XLA Modules:
  0.0 483.8 jit_solution(6934004598107564044)
XLA Ops:
  8.0 4.0 collective-permute-start
  12.8 1.0 collective-permute-done
  14.6 2.0 collective-permute-start.1
  16.7 1.9 collective-permute-done.1
  18.6 2.0 collective-permute-start.2
  20.6 2.4 collective-permute-done.2
  23.1 2.0 collective-permute-start.3
  26.5 1.0 reduce_max.20
  27.5 1.0 exponential_reduce_fusion
  29.3 0.9 subtract_subtract_fusion
  33.9 20.0 %edge.1 = (bf16[16,96,256]{2,1,0:T(8,128)(2,1)}, bf16[16,96,256]{2,1,0:T(8,128)(2,1)}, bf16[16,96,384]{2,1,0:T(8,128)(2,1)}, bf16[16,192,384]{2,1,0:T(8,128)(2,1...) custom-call(s32[16,2]{1,0:T(8,128)} %copy.206.ext_ref, s32[1]{0:T(128)} %bitcast.1.row_ref, s32[16]{0:T(128)} %select_reduce_fusion.4.order_ref, ...), custom_call_target="tpu_custom_call" | custom-call | flops 16000000000 | bytes 16000000 | tf_op jit(solution)/shard_map/edge/pallas_call | solution.py:429
  53.9 2.4 collective-permute-start.7
  61.9 3.2 collective-permute-start.5
  65.1 1.5 collective-permute-start.6
  67.3 2.0 pool_norm.1
  69.3 29.3 %embed.1 = (bf16[16,256,2048]{2,1,0:T(8,128)(2,1)}, f32[16,96,2048]{2,1,0:T(8,128)}, bf16[16,96,2560]{2,1,0:T(8,128)(2,1)}) custom-call(s32[16,2]{1,0:T(8,128)} %copy.198.ext_ref, s32[1]{0:T(128)} %bitcast.1.row_ref, s32[16]{0:T(128)} %select_reduce_fusion.4.order_ref, bf16[16,7,3,8,1024]{4,3,2,1,0:T(8,128)(2,1)} %bitcast.157, ...), custom_call_target="tpu_custom_call" | custom-call | flops 32000000000 | bytes 64000000 | tf_op jit(solution)/shard_map/embed/pallas_call | solution.py:449
  98.6 1.0 copy.203.rw_ref
  100.7 85.8 %forward.1 = (bf16[16,96,2048]{2,1,0:T(8,128)(2,1)}, bf16[16,96,2048]{2,1,0:T(8,128)(2,1)}, bf16[16,96,2048]{2,1,0:T(8,128)(2,1)}, bf16[16,96,2048]{2,1,0:T(8,12...) custom-call(s32[16,2]{1,0:T(8,128)} %copy.206.ext_ref, ...), custom_call_target="tpu_custom_call" | custom-call | flops 80000000000 | bytes 64000000 | tf_op jit(solution)/shard_map/forward/pallas_call | solution.py:646
  186.5 1.5 reduce_sum.215
  188.1 1.1 collective-permute-start.8
  190.1 1.9 collective-permute-start.9
  192.0 1.8 collective-permute-done.9
  193.7 2.8 collective-permute-start.10
  197.1 1.0 collective-permute-done.10
  201.3 1.2 copy.205.gvec_ref
  202.5 105.0 %backward.1 = (bf16[16,96,2048]{2,1,0:T(8,128)(2,1)}, bf16[16,96,2048]{2,1,0:T(8,128)(2,1)}, bf16[16,96,256]{2,1,0:T(8,128)(2,1)}, bf16[16,96,256]{2,1,0:T(8,128...) custom-call(s32[16,2]{1,0:T(8,128)} %copy.206.ext_ref, ...), custom_call_target="tpu_custom_call" | custom-call | flops 192000000000 | bytes 96000000 | tf_op jit(solution)/shard_map/backward/pallas_call | solution.py:834
  307.6 1.5 slice.284
  309.2 2.4 collective-permute-done.11
  311.6 2.0 convert_add_fusion
  313.7 1.2 collective-permute-start.14
  315.8 2.7 collective-permute-start.12
  318.5 1.3 collective-permute-start.13
  319.8 6.0 %collective-permute-done.14 = bf16[2,192,512]{2,1,0:T(8,128)(2,1)} collective-permute-done((bf16[2,192,512]{2,1,0:T(8,128)(2,1)S(1)}, bf16[2,192,512]{2,1,0:T(8,128)(2,1)}, u32[]{:S(2)}, u32[]{:S(2)}) %collective-permute-start.14) | collective-permute-done | bytes 393248 | tf_op jit(solution)/shard_map/ppermute | solution.py:950
  325.8 1.1 convert_add_fusion.1
  327.7 0.9 slice.217
  330.2 1.3 collective-permute-start.15
  331.5 1.1 reduce_sum.223
  332.5 1.3 reduce_sum.220
  334.3 0.9 slice.216
  336.2 3.0 collective-permute-done.15
  340.0 2.4 pool_back.1
  342.4 1.0 convert_element_type.69
  343.4 1.3 collective-permute-start.16
  344.7 1.1 reduce_sum.224
  345.8 0.9 collective-permute-done.16.under_ref
  347.4 38.7 %embed_back.1 = (f32[112,96]{1,0:T(8,128)}, f32[112,192]{1,0:T(8,128)}, f32[96,256]{1,0:T(8,128)}, f32[3,96,128]{2,1,0:T(8,128)}, f32[192,384]{1,0:T(8,128)}) custom-call(s32[16,2]{1,0:T(8,128)} %copy.206.ext_ref, s32[1]{0:T(128)} %bitcast.1.row_ref, bf16[16,256,2048]{2,1,0:T(8,128)(2,1)} %get-tuple-element.67.patch_ref, ...), custom_call_target="tpu_custom_call" | custom-call | flops 48000000000 | bytes 48000000 | tf_op jit(solution)/shard_map/embed_back/pallas_call | solution.py:927
  386.1 1.0 copy.207
  390.3 1.1 reduce_sum.222
  391.5 1.1 copy.215
  393.9 6.5 %concatenate.38 = f32[286312]{0:T(1024)S(1)} concatenate(f32[14112]{0:T(1024)S(1)} %reshape_reshape.21, f32[27648]{0:T(1024)S(1)} %reshape.189, f32[9216]{0:T(1024)S(1)} %reshape.190, f32[36864]{0:T(1024)S(1)} %reshape.191, f32[36864]{0:T(1024)S(1)} %reshape.192, f32[96000]{0:T(1024)S(1)} %reshape.193, f32[11520]{0:T(1024)S(1)} %reshape_reshape.22, f32[48384]{0:T(1024)S(1)} %reshape_reshape.23, ...), dimensions={0} | concatenate | bytes 2290496 | tf_op jit(solution)/shard_map/concatenate | solution.py:1220
  401.1 3.8 collective-permute-start.17
  404.8 1.6 collective-permute-done.17
  406.6 2.5 collective-permute-start.18
  409.0 7.5 %collective-permute-done.18 = f32[4,2,70,128]{3,2,1,0:T(8,128)S(1)} collective-permute-done((f32[4,2,70,128]{3,2,1,0:T(8,128)S(1)}, f32[4,2,70,128]{3,2,1,0:T(8,128)S(1)}, u32[]{:S(2)}, u32[]{:S(2)}) %collective-permute-start.18) | collective-permute-done | bytes 286752 | tf_op jit(solution)/shard_map/ppermute | solution.py:950
  418.3 4.0 collective-permute-done.19
  422.3 22.4 %collective-permute-start.20 = (f32[288,128]{1,0:T(8,128)S(1)}, f32[288,128]{1,0:T(8,128)S(1)}, u32[]{:S(2)}, u32[]{:S(2)}) collective-permute-start(f32[288,128]{1,0:T(8,128)S(1)} %concatenate.39), channel_id=1, source_target_pairs={{0,8},{8,0},{16,24},{24,16},{1,9},{9,1},{17,25},{25,17},{2,10},{10... | collective-permute-start | bytes 442376 | tf_op jit(solution)/shard_map/ppermute | solution.py:950
  444.7 3.1 collective-permute-done.20
  447.9 9.7 %collective-permute-start.21 = (f32[288,128]{1,0:T(8,128)S(1)}, f32[288,128]{1,0:T(8,128)S(1)}, u32[]{:S(2)}, u32[]{:S(2)}) collective-permute-start(f32[288,128]{1,0:T(8,128)S(1)} %pad_add_fusion.3), channel_id=1, source_target_pairs={{0,16},{8,24},{16,0},{24,8},{1,17},{9,25},{17,1},{25,9},{2,18},{10... | collective-permute-start | bytes 442376 | tf_op jit(solution)/shard_map/ppermute | solution.py:950
  457.5 5.2 %collective-permute-done.21 = f32[288,128]{1,0:T(8,128)S(1)} collective-permute-done((f32[288,128]{1,0:T(8,128)S(1)}, f32[288,128]{1,0:T(8,128)S(1)}, u32[]{:S(2)}, u32[]{:S(2)}) %collective-permute-start.21) | collective-permute-done | bytes 147488 | tf_op jit(solution)/shard_map/ppermute | solution.py:950
  463.9 1.2 collective-permute-done.22
  466.5 2.6 collective-permute-start.23
  469.1 1.0 collective-permute-done.23
  470.8 1.6 collective-permute-start.24
  472.4 1.9 collective-permute-done.24
  (217 shorter events, 34.7 us)
Async XLA Ops:
  7.2 92.4 %all-gather.3.cloned.1.call-start = ((), (), s32[]{:S(2)}) async-start(), calls=%async_computation | async-start | bytes 1769472 | tf_op jit(solution)/shard_map/all_gather | solution.py:1137
  8.0 5.8 %collective-permute-start = (bf16[70,128]{1,0:T(8,128)(2,1)S(1)}, bf16[70,128]{1,0:T(8,128)(2,1)S(1)}, u32[]{:S(2)}, u32[]{:S(2)}) collective-permute-start(bf16[70,128]{1,0:T(8,128)(2,1)S(1)} %convert_bitcast_fusion), channel_id=1, source_target_pairs={{0,16},{8,24},{16,0},{24,8},{1,17},{9,25},{17,1},{25,9},{2,18},{10... | collective-permute-start | bytes 53768 | tf_op jit(solution)/shard_map/ppermute | solution.py:950
  12.8 187.5 %copy-start.14 = (f32[16]{0:T(128)}, f32[16]{0:T(128)S(1)}, u32[]{:S(2)}) copy-start(f32[16]{0:T(128)S(1)} %get-tuple-element.165) | copy-start | bytes 196
  14.6 4.0 collective-permute-start.1
  18.6 4.4 collective-permute-start.2
  23.1 5.5 %collective-permute-start.3 = (bf16[2,2,2,70,128]{4,3,0,1,2:T(8,128)(2,1)S(1)}, bf16[2,2,2,70,128]{4,3,0,1,2:T(8,128)(2,1)S(1)}, u32[]{:S(2)}, u32[]{:S(2)}) collective-permute-start(bf16[2,2,2,70,128]{4,3,0,1,2:T(8,128)(2,1)S(1)} %pad_maximum_fusion.2), channel_id=1, source_target_pairs={{0,2},{1,3},{2,0},{3,1},{4,6},{5,7},{6,4},{7,5},{8,10},{9,11},{10,... | collective-permute-start | bytes 430088 | tf_op jit(solution)/shard_map/ppermute | solution.py:950
  28.6 1.6 collective-permute-start.4
  31.7 28.7 %copy-start.2 = (bf16[96,288]{1,0:T(8,128)(2,1)}, bf16[96,288]{1,0:T(8,128)(2,1)S(1)}, u32[]{:S(2)}) copy-start(bf16[96,288]{1,0:T(8,128)(2,1)S(1)} %reshape.185.wqkv_ref) | copy-start | bytes 165892
  53.9 12.6 %collective-permute-start.7 = (f32[192,512]{1,0:T(8,128)}, f32[192,512]{1,0:T(8,128)S(1)}, u32[]{:S(2)}, u32[]{:S(2)}) collective-permute-start(f32[192,512]{1,0:T(8,128)} %get-tuple-element.73), channel_id=1, source_target_pairs={{0,1},{1,2},{2,3},{3,4},{4,5},{5,6},{6,7},{8,9},{9,10},{10,11},{11... | collective-permute-start | bytes 1179656 | tf_op jit(solution)/shard_map/ppermute | solution.py:956
  61.9 37.7 %collective-permute-start.5 = (bf16[16,96,256]{2,1,0:T(8,128)(2,1)}, bf16[16,96,256]{2,1,0:T(8,128)(2,1)S(1)}, u32[]{:S(2)}, u32[]{:S(2)}) collective-permute-start(bf16[16,96,256]{2,1,0:T(8,128)(2,1)} %get-tuple-element.69), channel_id=1, source_target_pairs={{0,1},{1,2},{2,3},{3,4},{4,5},{5,6},{6,7},{8,9},{9,10},{10,11},{11... | collective-permute-start | bytes 2359304 | tf_op jit(solution)/shard_map/ppermute | solution.py:956
  65.1 34.5 %collective-permute-start.6 = (bf16[16,96,256]{2,1,0:T(8,128)(2,1)}, bf16[16,96,256]{2,1,0:T(8,128)(2,1)S(1)}, u32[]{:S(2)}, u32[]{:S(2)}) collective-permute-start(bf16[16,96,256]{2,1,0:T(8,128)(2,1)} %get-tuple-element.70), channel_id=1, source_target_pairs={{1,0},{2,1},{3,2},{4,3},{5,4},{6,5},{7,6},{9,8},{10,9},{11,10},{12... | collective-permute-start | bytes 2359304 | tf_op jit(solution)/shard_map/ppermute | solution.py:956
  66.6 0.7 copy-start
  99.5 0.9 copy-start.25
  99.5 1.2 copy-start.26
  100.7 98.1 %copy-start.20 = (s32[16]{0:T(128)S(1)}, s32[16]{0:T(128)}, u32[]{:S(2)}) copy-start(s32[16]{0:T(128)} %param.16) | copy-start | bytes 196
  188.1 2.0 collective-permute-start.8
  190.1 3.7 collective-permute-start.9
  193.7 113.8 %copy-start.6 = (f32[16,96]{1,0:T(8,128)}, f32[16,96]{1,0:T(8,128)S(1)}, u32[]{:S(2)}) copy-start(f32[16,96]{1,0:T(8,128)S(1)} %add.133) | copy-start | bytes 18436
  193.7 4.5 collective-permute-start.10
  196.6 110.9 %copy-start.16 = (f32[96]{0:T(128)}, f32[96]{0:T(128)S(1)}, u32[]{:S(2)}) copy-start(f32[96]{0:T(128)S(1)} %get-tuple-element.159) | copy-start | bytes 1156
  196.6 110.9 %copy-start.18 = (f32[96]{0:T(128)}, f32[96]{0:T(128)S(1)}, u32[]{:S(2)}) copy-start(f32[96]{0:T(128)S(1)} %get-tuple-element.160) | copy-start | bytes 1156
  198.2 109.4 %copy-start.10 = (f32[16,96]{1,0:T(8,128)}, f32[16,96]{1,0:T(8,128)S(1)}, u32[]{:S(2)}) copy-start(f32[16,96]{1,0:T(8,128)S(1)} %collective-permute-done.10) | copy-start | bytes 18436
  200.2 107.3 %copy-start.4 = (f32[16,1000]{1,0:T(8,128)}, f32[16,1000]{1,0:T(8,128)S(1)}, u32[]{:S(2)}) copy-start(f32[16,1000]{1,0:T(8,128)S(1)} %get-tuple-element.130) | copy-start | bytes 192004
  307.6 7.3 %copy-start.5 = (f32[16,1000]{1,0:T(8,128)S(1)}, f32[16,1000]{1,0:T(8,128)}, u32[]{:S(2)}) copy-start(f32[16,1000]{1,0:T(8,128)} %copy-done.4) | copy-start | bytes 192004
  307.6 7.3 %copy-start.7 = (f32[16,96]{1,0:T(8,128)S(1)}, f32[16,96]{1,0:T(8,128)}, u32[]{:S(2)}) copy-start(f32[16,96]{1,0:T(8,128)} %copy-done.6) | copy-start | bytes 18436
  307.6 7.3 %copy-start.11 = (f32[16,96]{1,0:T(8,128)S(1)}, f32[16,96]{1,0:T(8,128)}, u32[]{:S(2)}) copy-start(f32[16,96]{1,0:T(8,128)} %copy-done.10) | copy-start | bytes 18436
  307.6 7.2 %copy-start.15 = (f32[16]{0:T(128)S(1)}, f32[16]{0:T(128)}, u32[]{:S(2)}) copy-start(f32[16]{0:T(128)} %copy-done.14) | copy-start | bytes 196
  307.6 7.2 %copy-start.17 = (f32[96]{0:T(128)S(1)}, f32[96]{0:T(128)}, u32[]{:S(2)}) copy-start(f32[96]{0:T(128)} %copy-done.16) | copy-start | bytes 1156
  307.6 7.2 %copy-start.19 = (f32[96]{0:T(128)S(1)}, f32[96]{0:T(128)}, u32[]{:S(2)}) copy-start(f32[96]{0:T(128)} %copy-done.18) | copy-start | bytes 1156
  309.1 6.7 %copy-start.12 = (f32[1000]{0:T(1024)S(1)}, f32[1000]{0:T(1024)}, u32[]{:S(2)}) copy-start(f32[1000]{0:T(1024)} %get-tuple-element.129) | copy-start | bytes 12004
  309.1 2.5 collective-permute-start.11
  309.2 17.7 %copy-start.1 = (f32[4,384,96]{2,1,0:T(8,128)S(1)}, f32[4,384,96]{2,1,0:T(8,128)}, u32[]{:S(2)}) copy-start(f32[4,384,96]{2,1,0:T(8,128)} %get-tuple-element.115) | copy-start | bytes 1769476
  313.7 12.1 %collective-permute-start.14 = (bf16[2,192,512]{2,1,0:T(8,128)(2,1)S(1)}, bf16[2,192,512]{2,1,0:T(8,128)(2,1)}, u32[]{:S(2)}, u32[]{:S(2)}) collective-permute-start(bf16[2,192,512]{2,1,0:T(8,128)(2,1)S(1)} %slice.285), channel_id=1, source_target_pairs={{0,2},{1,3},{2,0},{3,1},{4,6},{5,7},{6,4},{7,5},{8,10},{9,11},{10,... | collective-permute-start | bytes 1179656 | tf_op jit(solution)/shard_map/ppermute | solution.py:950
  315.8 29.9 %collective-permute-start.12 = (bf16[16,96,256]{2,1,0:T(8,128)(2,1)}, bf16[16,96,256]{2,1,0:T(8,128)(2,1)}, u32[]{:S(2)}, u32[]{:S(2)}) collective-permute-start(bf16[16,96,256]{2,1,0:T(8,128)(2,1)} %get-tuple-element.95), channel_id=1, source_target_pairs={{0,1},{1,2},{2,3},{3,4},{4,5},{5,6},{6,7},{8,9},{9,10},{10,11},{11... | collective-permute-start | bytes 2359304 | tf_op jit(solution)/shard_map/ppermute | solution.py:956
  318.5 27.3 %collective-permute-start.13 = (bf16[16,96,256]{2,1,0:T(8,128)(2,1)}, bf16[16,96,256]{2,1,0:T(8,128)(2,1)}, u32[]{:S(2)}, u32[]{:S(2)}) collective-permute-start(bf16[16,96,256]{2,1,0:T(8,128)(2,1)} %get-tuple-element.96), channel_id=1, source_target_pairs={{1,0},{2,1},{3,2},{4,3},{5,4},{6,5},{7,6},{9,8},{10,9},{11,10},{12... | collective-permute-start | bytes 2359304 | tf_op jit(solution)/shard_map/ppermute | solution.py:956
  330.2 9.0 %collective-permute-start.15 = (bf16[1,192,512]{2,1,0:T(8,128)(2,1)S(1)}, bf16[1,192,512]{2,1,0:T(8,128)(2,1)S(1)}, u32[]{:S(2)}, u32[]{:S(2)}) collective-permute-start(bf16[1,192,512]{2,1,0:T(8,128)(2,1)S(1)} %slice.286), channel_id=1, source_target_pairs={{0,4},{1,5},{2,6},{3,7},{4,0},{5,1},{6,2},{7,3},{8,12},{9,13},{10,... | collective-permute-start | bytes 589832 | tf_op jit(solution)/shard_map/ppermute | solution.py:950
  343.4 3.3 collective-permute-start.16
  346.7 0.7 copy-start.27
  347.4 43.9 %copy-start.23 = (f32[96]{0:T(128)S(1)}, f32[96]{0:T(128)}, u32[]{:S(2)}) copy-start(f32[96]{0:T(128)} %get-tuple-element.124) | copy-start | bytes 1156
  347.4 43.9 %copy-start.24 = (f32[96]{0:T(128)S(1)}, f32[96]{0:T(128)}, u32[]{:S(2)}) copy-start(f32[96]{0:T(128)} %get-tuple-element.125) | copy-start | bytes 1156
  347.4 45.5 %copy-start.13 = (f32[3,4,32]{2,1,0:T(4,128)S(1)}, f32[3,4,32]{2,1,0:T(4,128)}, u32[]{:S(2)}) copy-start(f32[3,4,32]{2,1,0:T(4,128)} %constant.102.clone) | copy-start | bytes 4612
  400.6 16.5 %copy-start.21 = (f32[16]{0:T(128)S(1)}, f32[16]{0:T(128)}, u32[]{:S(2)}) copy-start(f32[16]{0:T(128)} %get-tuple-element.121) | copy-start | bytes 196
  400.6 16.5 %copy-start.22 = (f32[16]{0:T(128)S(1)}, f32[16]{0:T(128)}, u32[]{:S(2)}) copy-start(f32[16]{0:T(128)} %get-tuple-element.122) | copy-start | bytes 196
  401.0 74.1 %copy-start.3 = (f32[8960]{0:T(1024)S(1)}, f32[8960]{0:T(1024)}, u32[]{:S(2)}) copy-start(f32[8960]{0:T(1024)} %param.11) | copy-start | bytes 107524
  401.0 74.1 %copy-start.8 = (f32[8960]{0:T(1024)S(1)}, f32[8960]{0:T(1024)}, u32[]{:S(2)}) copy-start(f32[8960]{0:T(1024)} %param.12) | copy-start | bytes 107524
  401.0 74.1 %copy-start.9 = (f32[8960]{0:T(1024)S(1)}, f32[8960]{0:T(1024)}, u32[]{:S(2)}) copy-start(f32[8960]{0:T(1024)} %param.13) | copy-start | bytes 107524
  401.1 5.4 %collective-permute-start.17 = (f32[4,2,2,70,128]{4,0,3,2,1:T(4,128)S(1)}, f32[4,2,2,70,128]{4,0,3,2,1:T(4,128)S(1)}, u32[]{:S(2)}, u32[]{:S(2)}) collective-permute-start(f32[4,2,2,70,128]{4,0,3,2,1:T(4,128)S(1)} %copy.217), channel_id=1, source_target_pairs={{0,1},{1,0},{2,3},{3,2},{4,5},{5,4},{6,7},{7,6},{8,9},{9,8},{10,11... | collective-permute-start | bytes 1720328 | tf_op jit(solution)/shard_map/ppermute | solution.py:950
  406.6 10.0 %collective-permute-start.18 = (f32[4,2,70,128]{3,2,1,0:T(8,128)S(1)}, f32[4,2,70,128]{3,2,1,0:T(8,128)S(1)}, u32[]{:S(2)}, u32[]{:S(2)}) collective-permute-start(f32[4,2,70,128]{3,2,1,0:T(8,128)S(1)} %dynamic-slice_bitcast_fusion.1), channel_id=1, source_target_pairs={{0,2},{1,3},{2,0},{3,1},{4,6},{5,7},{6,4},{7,5},{8,10},{9,11},{10,... | collective-permute-start | bytes 860168 | tf_op jit(solution)/shard_map/ppermute | solution.py:950
  416.6 5.6 %collective-permute-start.19 = (f32[4,70,128]{2,1,0:T(8,128)S(1)}, f32[4,70,128]{2,1,0:T(8,128)S(1)}, u32[]{:S(2)}, u32[]{:S(2)}) collective-permute-start(f32[4,70,128]{2,1,0:T(8,128)S(1)} %dynamic-slice_bitcast_fusion.2), channel_id=1, source_target_pairs={{0,4},{1,5},{2,6},{3,7},{4,0},{5,1},{6,2},{7,3},{8,12},{9,13},{10,... | collective-permute-start | bytes 430088 | tf_op jit(solution)/shard_map/ppermute | solution.py:950
  422.3 25.5 %collective-permute-start.20 = (f32[288,128]{1,0:T(8,128)S(1)}, f32[288,128]{1,0:T(8,128)S(1)}, u32[]{:S(2)}, u32[]{:S(2)}) collective-permute-start(f32[288,128]{1,0:T(8,128)S(1)} %concatenate.39), channel_id=1, source_target_pairs={{0,8},{8,0},{16,24},{24,16},{1,9},{9,1},{17,25},{25,17},{2,10},{10... | collective-permute-start | bytes 442376 | tf_op jit(solution)/shard_map/ppermute | solution.py:950
  447.9 14.9 %collective-permute-start.21 = (f32[288,128]{1,0:T(8,128)S(1)}, f32[288,128]{1,0:T(8,128)S(1)}, u32[]{:S(2)}, u32[]{:S(2)}) collective-permute-start(f32[288,128]{1,0:T(8,128)S(1)} %pad_add_fusion.3), channel_id=1, source_target_pairs={{0,16},{8,24},{16,0},{24,8},{1,17},{9,25},{17,1},{25,9},{2,18},{10... | collective-permute-start | bytes 442376 | tf_op jit(solution)/shard_map/ppermute | solution.py:950
  463.9 1.2 collective-permute-start.22
  466.5 3.6 collective-permute-start.23
  470.8 3.6 collective-permute-start.24
Sparse Core Ops, SparseCore 0:
  69.4 29.1 all-gather.2

commit v6 on v5

--- a/solution.py
+++ b/solution.py
@@ -36,6 +36,7 @@
 PAIRS = TOKENS // PAIR
 TILES = CANVAS_W // 32
 GROUP = 2
+WIDE = 4
 PADDED = TOKENS + 512
 WIN = 40
 PATCH_ROWS = 256
@@ -159,11 +160,11 @@
 
 def load_pair(ref, pair):
     lanes = pair_lanes(pair)
-    return jnp.concatenate([ref[g, :, lanes] for g in range(GROUP)], axis=1)
+    return jnp.concatenate([ref[g, :, lanes] for g in range(ref.shape[0])], axis=1)
 
 
 def store_pair(ref, pair, value, base=0):
-    for g in range(GROUP):
+    for g in range(value.shape[1] // PAIR):
         ref[g, :, pair_lanes(pair, base)] = value[:, PAIR * g : PAIR * g + PAIR]
 
 
@@ -178,9 +179,9 @@
     return jnp.minimum((widest >> 6) + 1, PAIRS)
 
 
-def group_extents(ext_ref, row_ref, offset, group=None):
+def group_extents(ext_ref, row_ref, offset, group=None, size=GROUP):
     group = pl.program_id(0) if group is None else group
-    images = [group * GROUP + g for g in range(GROUP)]
+    images = [group * size + g for g in range(size)]
     heights = [ext_ref[offset + image, 0] for image in images]
     breadths = [ext_ref[offset + image, 1] for image in images]
     return images, heights, breadths, [row_ref[0] * ROWS < height for height in heights]
@@ -306,10 +307,10 @@
 
 
 def edge_kernel(ext_ref, row_ref, order_ref, *refs, offset):
-    pix_refs, refs = refs[:GROUP], refs[GROUP:]
+    pix_refs, refs = refs[:WIDE], refs[WIDE:]
     (perm_ref, tap_ref, wp_ref, wqkv_ref, vec_ref,
      first_ref, last_ref, nsel_ref, kvt_ref, below_ref, own_ref, s_ref, p_ref, wide_ref, kexp_ref) = refs
-    images, heights, breadths, row_oks = group_extents(ext_ref, row_ref, offset)
+    images, heights, breadths, row_oks = group_extents(ext_ref, row_ref, offset, size=WIDE)
 
     @pl.when(pl.program_id(0) == 0)
     def _():
@@ -319,7 +320,7 @@
 
     lane = lane_ids(1024)
     masks = []
-    for g in range(GROUP):
+    for g in range(WIDE):
         pixel_rows(pix_refs[g], s_ref)
         for shifted in range(2):
             out = patch_blocks(s_ref, perm_ref[...], shifted, ((7, 0, 1, 1), (8, 1, 2, 2)))
@@ -339,16 +340,16 @@
     (normed,) = by_lanes(first_norm, dot(wp_ref[...], p_ref[...]), jnp.concatenate(masks, axis=1))
     rows = []
     for slot in range(3):
-        rows.append(jnp.concatenate([gather_halo(normed[:, 1024 * g : 1024 * g + 1024], 32 * slot) for g in range(GROUP)], axis=1))
+        rows.append(jnp.concatenate([gather_halo(normed[:, 1024 * g : 1024 * g + 1024], 32 * slot) for g in range(WIDE)], axis=1))
     edge = dot(wqkv_ref[0:DIM, :], jnp.concatenate(rows[:2], axis=1))
     (edge,) = by_lanes(lambda k, out: ((out + wide_ref[3]).astype(BF16),), edge)
-    nsel = dot(jnp.concatenate([row[:, CANVAS_W * g : CANVAS_W * g + CANVAS_W] for g in range(GROUP) for row in rows], axis=0), tap_ref[...])
-    nsel = jnp.concatenate([nsel[DIM * k : DIM * k + DIM] for k in range(3 * GROUP)], axis=1).astype(BF16)
+    nsel = dot(jnp.concatenate([row[:, CANVAS_W * g : CANVAS_W * g + CANVAS_W] for g in range(WIDE) for row in rows], axis=0), tap_ref[...])
+    nsel = jnp.concatenate([nsel[DIM * k : DIM * k + DIM] for k in range(3 * WIDE)], axis=1).astype(BF16)
     bias = jnp.concatenate([wide_ref[4], wide_ref[5]], axis=0)
     (taps,) = by_lanes(lambda k, out: ((out + bias).astype(BF16),), dot(wqkv_ref[DIM : 3 * DIM, :], nsel))
-    for g in range(GROUP):
+    for g in range(WIDE):
         last_ref[g] = edge[:, CANVAS_W * g : CANVAS_W * g + CANVAS_W]
-        first_ref[g] = edge[:, CANVAS_W * (GROUP + g) : CANVAS_W * (GROUP + g) + CANVAS_W]
+        first_ref[g] = edge[:, CANVAS_W * (WIDE + g) : CANVAS_W * (WIDE + g) + CANVAS_W]
         nsel_ref[g] = nsel[:, 384 * g : 384 * g + 384]
         kvt_ref[g] = taps[:, 384 * g : 384 * g + 384]
         product = taps[:, 384 * g : 384 * g + 384].astype(F32) * kexp_ref[...]
@@ -361,16 +362,16 @@
 
 
 def embed_kernel(ext_ref, row_ref, order_ref, *refs, offset):
-    pix_refs, refs = refs[:GROUP], refs[GROUP:]
+    pix_refs, refs = refs[:WIDE], refs[WIDE:]
     perm_ref, wp_ref, wqkv_ref, vec_ref, patch_ref, x0_ref, q_ref, s_ref, wide_ref = refs
-    images, heights, breadths, row_oks = group_extents(ext_ref, row_ref, offset)
+    images, heights, breadths, row_oks = group_extents(ext_ref, row_ref, offset, size=WIDE)
 
     @pl.when(pl.program_id(0) == 0)
     def _():
         s_ref[...] = jnp.zeros_like(s_ref)
         fill_wide(wide_ref, vec_ref, [0, 1, 2, 42])
 
-    for g in range(GROUP):
+    for g in range(WIDE):
         pixel_rows(pix_refs[g], s_ref)
         for shifted in range(2):
             out = patch_blocks(s_ref, perm_ref[...], shifted, ((0, 1, 2, 3), (4, 5, 6, 7), (1, 2, 3, 4), (5, 6, 7, 8)))
@@ -398,58 +399,58 @@
         return carry
 
     def idle(pair, carry):
-        for g in range(GROUP):
+        for g in range(WIDE):
             q_ref[g, :, pair_lanes(pair, 256)] = jnp.zeros((DIM, PAIR), BF16)
         return carry
 
     lax.fori_loop(0, count, active, 0)
     lax.fori_loop(count, PAIRS, idle, 0)
-    for g in range(GROUP):
+    for g in range(WIDE):
         q_ref[g, :, 0:256] = jnp.zeros((DIM, 256), BF16)
         q_ref[g, :, 256 + TOKENS : 512 + TOKENS] = jnp.zeros((DIM, 256), BF16)
 
 
-def key_lanes(*lead):
-    return pl.BlockSpec(lead + (128,), lambda i, *_: (0,) * len(lead) + (i * GROUP >> 2,))
-
-
-def specs():
+def key_lanes(*lead, size=GROUP):
+    return pl.BlockSpec(lead + (128,), lambda i, *_: (0,) * len(lead) + (i * size >> 2,))
+
+
+def specs(size=GROUP):
     whole = lambda *shape: pl.BlockSpec(shape, lambda i, *_: (0,) * len(shape))
-    per = lambda *shape: pl.BlockSpec((GROUP,) + shape, lambda i, *_: (i,) + (0,) * len(shape))
+    per = lambda *shape: pl.BlockSpec((size,) + shape, lambda i, *_: (i,) + (0,) * len(shape))
     return whole, per
 
 
 def pixel_specs(offset):
-    return [pl.BlockSpec((1, PATCH, 3, ROWS, 1024), lambda i, ext, row, order, g=g: (order[offset + i * GROUP + g], 0, 0, 0, 0)) for g in range(GROUP)]
+    return [pl.BlockSpec((1, PATCH, 3, ROWS, 1024), lambda i, ext, row, order, g=g: (order[offset + i * WIDE + g], 0, 0, 0, 0)) for g in range(WIDE)]
 
 
 def call_edge(ext, row, order, pixels, consts, wts, images, offset):
-    whole, per = specs()
+    whole, per = specs(WIDE)
     shapes = [(DIM, CANVAS_W), (DIM, CANVAS_W), (DIM, 384), (2 * DIM, 384)]
     return pl.pallas_call(
         functools.partial(edge_kernel, offset=offset),
         grid_spec=pltpu.PrefetchScalarGridSpec(
-            num_scalar_prefetch=3, grid=(images // GROUP,),
+            num_scalar_prefetch=3, grid=(images // WIDE,),
             in_specs=pixel_specs(offset) + [
                 whole(512, 512), whole(CANVAS_W, 128), whole(DIM, PATCH_ROWS), whole(3 * DIM, DIM), whole(DIM, 64)],
-            out_specs=[per(*s) for s in shapes] + [key_lanes(2 * DIM)] * 2,
-            scratch_shapes=[pltpu.VMEM((TILES, 144, 128), F32), pltpu.VMEM((PATCH_ROWS, 1024 * GROUP), BF16), pltpu.VMEM((6, DIM, 128), F32),
+            out_specs=[per(*s) for s in shapes] + [key_lanes(2 * DIM, size=WIDE)] * 2,
+            scratch_shapes=[pltpu.VMEM((TILES, 144, 128), F32), pltpu.VMEM((PATCH_ROWS, 1024 * WIDE), BF16), pltpu.VMEM((6, DIM, 128), F32),
                             pltpu.VMEM((2 * DIM, 384), F32)]),
         out_shape=[jax.ShapeDtypeStruct((images,) + s, BF16) for s in shapes]
         + [jax.ShapeDtypeStruct((2 * DIM, 32 * images), F32)] * 2,
         compiler_params=pltpu.CompilerParams(vmem_limit_bytes=VMEM_BYTES),
         cost_estimate=pl.CostEstimate(flops=images * 1_000_000_000, bytes_accessed=images * 1_000_000, transcendentals=0),
         name="edge",
-    )(ext, row, order, *[pixels] * GROUP, consts["perm"], consts["tap"], wts["wp"], wts["wqkv_t"], wts["vec"])
+    )(ext, row, order, *[pixels] * WIDE, consts["perm"], consts["tap"], wts["wp"], wts["wqkv_t"], wts["vec"])
 
 
 def call_embed(ext, row, order, pixels, consts, wts, images, offset):
-    whole, per = specs()
+    whole, per = specs(WIDE)
     shapes = [((PATCH_ROWS, TOKENS), BF16), ((DIM, TOKENS), F32), ((DIM, PADDED), BF16)]
     return pl.pallas_call(
         functools.partial(embed_kernel, offset=offset),
         grid_spec=pltpu.PrefetchScalarGridSpec(
-            num_scalar_prefetch=3, grid=(images // GROUP,),
+            num_scalar_prefetch=3, grid=(images // WIDE,),
             in_specs=pixel_specs(offset) + [whole(512, 512), whole(DIM, PATCH_ROWS), whole(3 * DIM, DIM), whole(DIM, 64)],
             out_specs=[per(*s) for s, _ in shapes],
             scratch_shapes=[pltpu.VMEM((TILES, 144, 128), F32), pltpu.VMEM((4, DIM, 128), F32)]),
@@ -457,7 +458,7 @@
         compiler_params=pltpu.CompilerParams(vmem_limit_bytes=VMEM_BYTES),
         cost_estimate=pl.CostEstimate(flops=images * 2_000_000_000, bytes_accessed=images * 4_000_000, transcendentals=0),
         name="embed",
-    )(ext, row, order, *[pixels] * GROUP, consts["perm"], wts["wp"], wts["wqkv_t"], wts["vec"])
+    )(ext, row, order, *[pixels] * WIDE, consts["perm"], wts["wp"], wts["wqkv_t"], wts["vec"])
 
 
 def pool_norm_kernel(own_ref, got_ref, vec_ref, kv_ref):
@@ -533,7 +534,7 @@
 
 def gelu_parts(hidden):
     cumulative = 0.5 + 0.5 * lax.erf(hidden * 0.7071067811865476)
-    slope = cumulative + hidden * (jnp.exp(hidden * hidden * -0.5) * 0.3989422804014327)
+    slope = cumulative + hidden * (jnp.exp2(hidden * hidden * (-0.5 * 1.4426950408889634)) * 0.3989422804014327)
     return (hidden * cumulative).astype(BF16), slope.astype(BF16)
 
 
@@ -787,8 +788,8 @@
                     for side in range(2):
                         lanes = pl.ds(pl.multiple_of(base + 128 * side, 128), 128)
                         dq_ref[g, part, lanes] = (sums[side][1] + up[side] + down[side]).astype(BF16)
-                    ru_ref[g, part, halo] = up[2]
-                    rd_ref[g, part, halo] = down[2]
+                    ru_ref[g, part, halo] = up[2].astype(BF16)
+                    rd_ref[g, part, halo] = down[2].astype(BF16)
             for k in range(9):
                 ak_ref[k, part] += grads[k]
         return carry
@@ -796,12 +797,18 @@
     def pool_idle(pair, carry):
         for ref in (ru_ref, rd_ref):
             for g in range(GROUP):
-                ref[g, :, pl.ds(pl.multiple_of(pair * 256, 128), 256)] = jnp.zeros((DIM, 256), F32)
+                ref[g, :, pl.ds(pl.multiple_of(pair * 256, 128), 256)] = jnp.zeros((DIM, 256), BF16)
+        store_pair(dq_ref, pair, jnp.zeros((DIM, GROUP * PAIR), BF16))
+        return carry
+
+    def idle(pair, carry):
+        store_pair(dx1_ref, pair, jnp.zeros((DIM, GROUP * PAIR), BF16))
         return carry
 
     lax.fori_loop(0, count, lambda pair, carry: step(pair, pool_step(pair, carry)), 0)
     lax.fori_loop(count, former_count, pool_step, 0)
     lax.fori_loop(former_count, PAIRS, pool_idle, 0)
+    lax.fori_loop(jnp.where(now < steps, count, PAIRS), PAIRS, idle, 0)
 
     @pl.when(now < steps)
     def _():
@@ -815,8 +822,8 @@
                 dkv_ref[slot] = jnp.where((lane >> 5) == (images[g] & 3), value, dkv_ref[slot])
 
     for g in range(GROUP):
-        up_ref[g] = gather_halo(ru_ref.at[g], 96).astype(BF16)
-        down_ref[g] = gather_halo(rd_ref.at[g], 0).astype(BF16)
+        up_ref[g] = gather_halo(ru_ref.at[g], 96)
+        down_ref[g] = gather_halo(rd_ref.at[g], 0)
 
 
 def call_backward(ext, row, saved, q, top, bot, kv, gvec, wts, offset):
@@ -841,8 +848,8 @@
             out_specs=[now(*shapes[0])] + [former(*s) for s in shapes[1:]] + [heads] + [whole(*s) for s in sums],
             scratch_shapes=[
                 pltpu.VMEM((GROUP, DIM + more, keys), BF16), pltpu.VMEM((GROUP, keys, 256), BF16), pltpu.VMEM((GROUP, keys, 128), BF16),
-                pltpu.VMEM((2, GROUP, DIM, PADDED), BF16)] + [pltpu.VMEM((GROUP, DIM, 1024), BF16)] * 2
-            + [pltpu.VMEM((GROUP, DIM, 1024), F32)] * 2 + [pltpu.VMEM((GROUP, DIM, keys), F32)] * 2 + [pltpu.VMEM((13, DIM, 128), F32)]),
+                pltpu.VMEM((2, GROUP, DIM, PADDED), BF16)] + [pltpu.VMEM((GROUP, DIM, 1024), BF16)] * 4
+            + [pltpu.VMEM((GROUP, DIM, keys), F32)] * 2 + [pltpu.VMEM((13, DIM, 128), F32)]),
         out_shape=[jax.ShapeDtypeStruct((images,) + s, BF16) for s in shapes]
         + [jax.ShapeDtypeStruct((key_rows, 2 * DIM, 32 * images), F32)] + [jax.ShapeDtypeStruct(s, F32) for s in sums],
         compiler_params=pltpu.CompilerParams(vmem_limit_bytes=VMEM_BYTES),
@@ -854,7 +861,7 @@
 def embed_back_kernel(ext_ref, row_ref, patch_ref, dq_ref, dx1_ref, rtop_ref, rbot_ref, nsel_ref, kvt_ref, pre_ref, under_ref,
                       wp_ref, vec_ref, wqkv_ref, tapt_ref,
                       aq_ref, akv_ref, apatch_ref, av_ref, ak_ref, dn_ref, rim_ref, wide_ref, kexp_ref, *, offset):
-    images, heights, breadths, row_oks = group_extents(ext_ref, row_ref, offset)
+    images, heights, breadths, row_oks = group_extents(ext_ref, row_ref, offset, size=WIDE)
 
     @pl.when(pl.program_id(0) == 0)
     def _():
@@ -871,18 +878,18 @@
         return jnp.where((lane >> 5) == 3, 0.0, block)
 
     grad_taps = []
-    for g in range(GROUP):
+    for g in range(WIDE):
         own = thrice(pre_ref[...], images[g])
         spread = jnp.concatenate([thrice(under_ref[...].astype(F32), images[g]), own, own], axis=1)
         ak_ref[...] += kvt_ref[g].astype(F32) * spread
         grad_taps.append((spread * kexp_ref[...]).astype(BF16))
     grad_taps = jnp.concatenate(grad_taps, axis=1)
-    nsel = jnp.concatenate([nsel_ref[g] for g in range(GROUP)], axis=1)
-    akv_ref[...] += dot_nt(jnp.concatenate([nsel, jnp.ones((16, 384 * GROUP), BF16)], axis=0), grad_taps)
+    nsel = jnp.concatenate([nsel_ref[g] for g in range(WIDE)], axis=1)
+    akv_ref[...] += dot_nt(jnp.concatenate([nsel, jnp.ones((16, 384 * WIDE), BF16)], axis=0), grad_taps)
     grad_sel = dot(wqkv_ref[:, DIM : 3 * DIM], grad_taps)
-    parts = [grad_sel.astype(BF16)[:, 128 * k : 128 * k + 128] for k in range(3 * GROUP)]
+    parts = [grad_sel.astype(BF16)[:, 128 * k : 128 * k + 128] for k in range(3 * WIDE)]
     lines = dot(jnp.concatenate(parts, axis=0), tapt_ref[...])
-    for g in range(GROUP):
+    for g in range(WIDE):
         for k, start in enumerate((224, 0, 32)):
             first = DIM * (3 * g + k)
             line = lines[first : first + DIM]
@@ -902,7 +909,7 @@
             return hat, rstd, (hat * wide_ref[1] + wide_ref[2]).astype(BF16), (grad.astype(F32) + rim).astype(BF16)
 
         hat, rstd, normed, grad_q = by_lanes(first_norm, dot(wp_ref[...], patches), mask, load_pair(dq_ref, pair), load_pair(rim_ref, pair))
-        aq_ref[...] += dot_nt(jnp.concatenate([normed, jnp.ones((16, GROUP * PAIR), BF16)], axis=0), grad_q)
+        aq_ref[...] += dot_nt(jnp.concatenate([normed, jnp.ones((16, WIDE * PAIR), BF16)], axis=0), grad_q)
 
         def first_back(k, out, extra, hat, rstd, mask, dx1):
             grad = out + extra
@@ -921,19 +928,19 @@
 
 
 def call_embed_back(ext, row, patches, dq, dx1, rtop, rbot, nsel, kvt, pre, under, consts, wts, offset):
-    whole, per = specs()
+    whole, per = specs(WIDE)
     images = dq.shape[0]
     sums = [(DIM + 16, DIM), (DIM + 16, 2 * DIM), (DIM, PATCH_ROWS), (3, DIM, 128), (2 * DIM, 384)]
     return pl.pallas_call(
         functools.partial(embed_back_kernel, offset=offset),
         grid_spec=pltpu.PrefetchScalarGridSpec(
-            num_scalar_prefetch=2, grid=(images // GROUP,),
+            num_scalar_prefetch=2, grid=(images // WIDE,),
             in_specs=[
                 per(PATCH_ROWS, TOKENS), per(DIM, TOKENS), per(DIM, TOKENS), per(DIM, CANVAS_W), per(DIM, CANVAS_W),
-                per(DIM, 384), per(2 * DIM, 384), key_lanes(2 * DIM), key_lanes(2 * DIM),
+                per(DIM, 384), per(2 * DIM, 384), key_lanes(2 * DIM, size=WIDE), key_lanes(2 * DIM, size=WIDE),
                 whole(DIM, PATCH_ROWS), whole(DIM, 64), whole(DIM, 3 * DIM), whole(128, CANVAS_W)],
             out_specs=[whole(*s) for s in sums],
-            scratch_shapes=[pltpu.VMEM((GROUP, DIM, TOKENS), F32)] * 2 + [pltpu.VMEM((3, DIM, 128), F32), pltpu.VMEM((2 * DIM, 384), F32)]),
+            scratch_shapes=[pltpu.VMEM((WIDE, DIM, TOKENS), F32)] * 2 + [pltpu.VMEM((3, DIM, 128), F32), pltpu.VMEM((2 * DIM, 384), F32)]),
         out_shape=[jax.ShapeDtypeStruct(s, F32) for s in sums],
         compiler_params=pltpu.CompilerParams(vmem_limit_bytes=VMEM_BYTES),
         cost_estimate=pl.CostEstimate(flops=images * 3_000_000_000, bytes_accessed=images * 3_000_000, transcendentals=0),

time: 482 us -> 468 us (0.971)
  starting transfers between devices: 73.7 us -> 45.9 us
  Pallas kernels: 283 us -> 294 us
    ppermute x19, starting transfers between devices: 61.3 us -> 33.5 us  [swap(): return lax.ppermute(value, axis, [(i, i ^ 1 << bit) for i in range(size)])]
    pallas_call x1, Pallas kernels: 105 us -> 114 us  [call_backward(): pl.pallas_call(functools.partial(backward_kernel, offset=offset, key_rows...]
    pallas_call x1, Pallas kernels: 85.8 us -> 92.4 us  [call_forward(): pl.pallas_call(functools.partial(forward_kernel, offset=offset, key_rows=...]
  transfers between devices with their start and end apart: 26 -> 26, of which waited for: 18 -> 19; matrix products, arithmetic and copies ran while one was open for 5% -> 6% of each run, Pallas kernels for 7% -> 7%
where the time goes in v6:
time: 468 us; the launch traced here: 467 us
  Pallas kernels  294 us (63%)
  waiting for transfers between devices  48.2 us (10%)
  starting transfers between devices  45.9 us (10%)
  local copies, waits for them, and re-layouts  32.9 us (7%)
  other arithmetic  24.6 us (5%)
  between operations  19.7 us (4%)
    pallas_call x1, Pallas kernels, call_backward(): pl.pallas_call(functools.partial(backward_kernel, offset=offset, key_rows...  114 us
    pallas_call x1, Pallas kernels, call_forward(): pl.pallas_call(functools.partial(forward_kernel, offset=offset, key_rows=...  92.4 us
    ppermute x19, waiting for transfers between devices, swap(): return lax.ppermute(value, axis, [(i, i ^ 1 << bit) for i in range(size)])  46.2 us
    pallas_call x1, Pallas kernels, call_embed_back(): pl.pallas_call(functools.partial(embed_back_kernel, offset=offset), grid_...  37 us
    ppermute x19, starting transfers between devices, swap(): return lax.ppermute(value, axis, [(i, i ^ 1 << bit) for i in range(size)])  33.5 us
    pallas_call x1, Pallas kernels, call_embed(): pl.pallas_call(functools.partial(embed_kernel, offset=offset), grid_spec=...  27.3 us
    pallas_call x1, Pallas kernels, call_edge(): pl.pallas_call(functools.partial(edge_kernel, offset=offset), grid_spec=p...  18.6 us
    ppermute x6, starting transfers between devices, shifted(): return lax.ppermute(value, axis, pairs)  12.3 us
  transfers between devices with their start and end apart: 26, of which 19 were waited for; matrix products, arithmetic and copies ran while one was open for 6% of the time, Pallas kernels for 7%

profile of v6, /device:TPU:0, one launch (start us, length us, event | category | flops | bytes accessed | tf_op | source)
XLA Modules:
  0.0 466.7 jit_solution(13492193415189918602)
XLA Ops:
  8.0 4.0 collective-permute-start
  12.8 1.0 collective-permute-done
  14.6 2.0 collective-permute-start.1
  16.7 1.9 collective-permute-done.1
  18.6 2.0 collective-permute-start.2
  20.6 2.4 collective-permute-done.2
  23.1 2.0 collective-permute-start.3
  26.5 1.0 reduce_max.20
  27.5 1.0 exponential_reduce_fusion
  29.3 0.9 subtract_subtract_fusion
  33.9 18.6 %edge.1 = (bf16[16,96,256]{2,1,0:T(8,128)(2,1)}, bf16[16,96,256]{2,1,0:T(8,128)(2,1)}, bf16[16,96,384]{2,1,0:T(8,128)(2,1)}, bf16[16,192,384]{2,1,0:T(8,128)(2,1...) custom-call(s32[16,2]{1,0:T(8,128)} %copy.206.ext_ref, s32[1]{0:T(128)} %bitcast.1.row_ref, s32[16]{0:T(128)} %select_reduce_fusion.4.order_ref, ...), custom_call_target="tpu_custom_call" | custom-call | flops 16000000000 | bytes 16000000 | tf_op jit(solution)/shard_map/edge/pallas_call | solution.py:430
  52.5 2.4 collective-permute-start.7
  60.5 3.2 collective-permute-start.5
  63.6 1.5 collective-permute-start.6
  65.9 2.0 pool_norm.1
  67.9 27.3 %embed.1 = (bf16[16,256,2048]{2,1,0:T(8,128)(2,1)}, f32[16,96,2048]{2,1,0:T(8,128)}, bf16[16,96,2560]{2,1,0:T(8,128)(2,1)}) custom-call(s32[16,2]{1,0:T(8,128)} %copy.198.ext_ref, s32[1]{0:T(128)} %bitcast.1.row_ref, s32[16]{0:T(128)} %select_reduce_fusion.4.order_ref, bf16[16,7,3,8,1024]{4,3,2,1,0:T(8,128)(2,1)} %bitcast.159, ...), custom_call_target="tpu_custom_call" | custom-call | flops 32000000000 | bytes 64000000 | tf_op jit(solution)/shard_map/embed/pallas_call | solution.py:450
  95.2 1.0 copy.203.rw_ref
  96.1 1.1 all-gather.3.cloned.1.call-done
  97.3 92.4 %forward.1 = (bf16[16,96,2048]{2,1,0:T(8,128)(2,1)}, bf16[16,96,2048]{2,1,0:T(8,128)(2,1)}, bf16[16,96,2048]{2,1,0:T(8,128)(2,1)}, bf16[16,96,2048]{2,1,0:T(8,12...) custom-call(s32[16,2]{1,0:T(8,128)} %copy.206.ext_ref, ...), custom_call_target="tpu_custom_call" | custom-call | flops 80000000000 | bytes 64000000 | tf_op jit(solution)/shard_map/forward/pallas_call | solution.py:647
  189.7 1.5 reduce_sum.215
  191.3 1.2 collective-permute-start.8
  193.3 1.9 collective-permute-start.9
  195.3 1.7 collective-permute-done.9
  197.0 2.8 collective-permute-start.10
  200.4 1.0 collective-permute-done.10
  204.5 1.2 copy.205.gvec_ref
  205.7 113.9 %backward.1 = (bf16[16,96,2048]{2,1,0:T(8,128)(2,1)}, bf16[16,96,2048]{2,1,0:T(8,128)(2,1)}, bf16[16,96,256]{2,1,0:T(8,128)(2,1)}, bf16[16,96,256]{2,1,0:T(8,128...) custom-call(s32[16,2]{1,0:T(8,128)} %copy.206.ext_ref, ...), custom_call_target="tpu_custom_call" | custom-call | flops 192000000000 | bytes 96000000 | tf_op jit(solution)/shard_map/backward/pallas_call | solution.py:841
  319.8 1.5 slice.284
  321.4 2.4 collective-permute-done.11
  323.8 2.0 convert_add_fusion
  325.8 1.2 collective-permute-start.14
  328.1 2.7 collective-permute-start.12
  330.7 1.3 collective-permute-start.13
  332.0 6.0 %collective-permute-done.14 = bf16[2,192,512]{2,1,0:T(8,128)(2,1)} collective-permute-done((bf16[2,192,512]{2,1,0:T(8,128)(2,1)S(1)}, bf16[2,192,512]{2,1,0:T(8,128)(2,1)}, u32[]{:S(2)}, u32[]{:S(2)}) %collective-permute-start.14) | collective-permute-done | bytes 393248 | tf_op jit(solution)/shard_map/ppermute | solution.py:957
  338.0 1.1 convert_add_fusion.1
  339.9 0.9 slice.217
  342.3 1.3 collective-permute-start.15
  343.6 1.1 reduce_sum.223
  344.7 1.3 reduce_sum.220
  346.5 0.9 slice.216
  348.4 3.0 collective-permute-done.15
  352.1 2.4 pool_back.1
  354.5 1.0 convert_element_type.69
  355.6 1.3 collective-permute-start.16
  356.9 1.1 reduce_sum.224
  358.0 0.9 collective-permute-done.16.under_ref
  359.6 37.0 %embed_back.1 = (f32[112,96]{1,0:T(8,128)}, f32[112,192]{1,0:T(8,128)}, f32[96,256]{1,0:T(8,128)}, f32[3,96,128]{2,1,0:T(8,128)}, f32[192,384]{1,0:T(8,128)}) custom-call(s32[16,2]{1,0:T(8,128)} %copy.206.ext_ref, s32[1]{0:T(128)} %bitcast.1.row_ref, bf16[16,256,2048]{2,1,0:T(8,128)(2,1)} %get-tuple-element.67.patch_ref, ...), custom_call_target="tpu_custom_call" | custom-call | flops 48000000000 | bytes 48000000 | tf_op jit(solution)/shard_map/embed_back/pallas_call | solution.py:934
  396.6 1.0 copy.207
  400.7 1.1 reduce_sum.222
  402.0 1.1 copy.215
  404.3 6.5 %concatenate.38 = f32[286312]{0:T(1024)S(1)} concatenate(f32[14112]{0:T(1024)S(1)} %reshape_reshape.21, f32[27648]{0:T(1024)S(1)} %reshape.189, f32[9216]{0:T(1024)S(1)} %reshape.190, f32[36864]{0:T(1024)S(1)} %reshape.191, f32[36864]{0:T(1024)S(1)} %reshape.192, f32[96000]{0:T(1024)S(1)} %reshape.193, f32[11520]{0:T(1024)S(1)} %reshape_reshape.22, f32[48384]{0:T(1024)S(1)} %reshape_reshape.23, ...), dimensions={0} | concatenate | bytes 2290496 | tf_op jit(solution)/shard_map/concatenate | solution.py:1227
  411.5 3.8 collective-permute-start.17
  415.3 1.6 collective-permute-done.17
  417.0 2.4 collective-permute-start.18
  419.5 7.5 %collective-permute-done.18 = f32[4,2,70,128]{3,2,1,0:T(8,128)S(1)} collective-permute-done((f32[4,2,70,128]{3,2,1,0:T(8,128)S(1)}, f32[4,2,70,128]{3,2,1,0:T(8,128)S(1)}, u32[]{:S(2)}, u32[]{:S(2)}) %collective-permute-start.18) | collective-permute-done | bytes 286752 | tf_op jit(solution)/shard_map/ppermute | solution.py:957
  428.7 4.0 collective-permute-done.19
  432.7 1.6 collective-permute-start.20
  434.3 3.6 collective-permute-done.20
  438.0 2.2 collective-permute-start.21
  440.2 5.4 %collective-permute-done.21 = f32[288,128]{1,0:T(8,128)S(1)} collective-permute-done((f32[288,128]{1,0:T(8,128)S(1)}, f32[288,128]{1,0:T(8,128)S(1)}, u32[]{:S(2)}, u32[]{:S(2)}) %collective-permute-start.21) | collective-permute-done | bytes 147488 | tf_op jit(solution)/shard_map/ppermute | solution.py:957
  446.8 1.2 collective-permute-done.22
  449.4 2.9 collective-permute-start.23
  453.7 1.6 collective-permute-start.24
  455.3 1.9 collective-permute-done.24
  (217 shorter events, 34.4 us)
Async XLA Ops:
  7.2 90.0 %all-gather.3.cloned.1.call-start = ((), (), s32[]{:S(2)}) async-start(), calls=%async_computation | async-start | bytes 1769472 | tf_op jit(solution)/shard_map/all_gather | solution.py:1144
  8.0 5.8 %collective-permute-start = (bf16[70,128]{1,0:T(8,128)(2,1)S(1)}, bf16[70,128]{1,0:T(8,128)(2,1)S(1)}, u32[]{:S(2)}, u32[]{:S(2)}) collective-permute-start(bf16[70,128]{1,0:T(8,128)(2,1)S(1)} %convert_bitcast_fusion), channel_id=1, source_target_pairs={{0,16},{8,24},{16,0},{24,8},{1,17},{9,25},{17,1},{25,9},{2,18},{10... | collective-permute-start | bytes 53768 | tf_op jit(solution)/shard_map/ppermute | solution.py:957
  12.8 190.7 %copy-start.14 = (f32[16]{0:T(128)}, f32[16]{0:T(128)S(1)}, u32[]{:S(2)}) copy-start(f32[16]{0:T(128)S(1)} %get-tuple-element.165) | copy-start | bytes 196
  14.6 4.0 collective-permute-start.1
  18.6 4.4 collective-permute-start.2
  23.1 5.5 %collective-permute-start.3 = (bf16[2,2,2,70,128]{4,3,0,1,2:T(8,128)(2,1)S(1)}, bf16[2,2,2,70,128]{4,3,0,1,2:T(8,128)(2,1)S(1)}, u32[]{:S(2)}, u32[]{:S(2)}) collective-permute-start(bf16[2,2,2,70,128]{4,3,0,1,2:T(8,128)(2,1)S(1)} %pad_maximum_fusion.2), channel_id=1, source_target_pairs={{0,2},{1,3},{2,0},{3,1},{4,6},{5,7},{6,4},{7,5},{8,10},{9,11},{10,... | collective-permute-start | bytes 430088 | tf_op jit(solution)/shard_map/ppermute | solution.py:957
  28.6 1.6 collective-permute-start.4
  31.7 27.3 %copy-start.2 = (bf16[96,288]{1,0:T(8,128)(2,1)}, bf16[96,288]{1,0:T(8,128)(2,1)S(1)}, u32[]{:S(2)}) copy-start(bf16[96,288]{1,0:T(8,128)(2,1)S(1)} %reshape.185.wqkv_ref) | copy-start | bytes 165892
  52.5 12.6 %collective-permute-start.7 = (f32[192,512]{1,0:T(8,128)}, f32[192,512]{1,0:T(8,128)S(1)}, u32[]{:S(2)}, u32[]{:S(2)}) collective-permute-start(f32[192,512]{1,0:T(8,128)} %get-tuple-element.73), channel_id=1, source_target_pairs={{0,1},{1,2},{2,3},{3,4},{4,5},{5,6},{6,7},{8,9},{9,10},{10,11},{11... | collective-permute-start | bytes 1179656 | tf_op jit(solution)/shard_map/ppermute | solution.py:963
  60.5 35.7 %collective-permute-start.5 = (bf16[16,96,256]{2,1,0:T(8,128)(2,1)}, bf16[16,96,256]{2,1,0:T(8,128)(2,1)S(1)}, u32[]{:S(2)}, u32[]{:S(2)}) collective-permute-start(bf16[16,96,256]{2,1,0:T(8,128)(2,1)} %get-tuple-element.69), channel_id=1, source_target_pairs={{0,1},{1,2},{2,3},{3,4},{4,5},{5,6},{6,7},{8,9},{9,10},{10,11},{11... | collective-permute-start | bytes 2359304 | tf_op jit(solution)/shard_map/ppermute | solution.py:963
  63.6 32.5 %collective-permute-start.6 = (bf16[16,96,256]{2,1,0:T(8,128)(2,1)}, bf16[16,96,256]{2,1,0:T(8,128)(2,1)S(1)}, u32[]{:S(2)}, u32[]{:S(2)}) collective-permute-start(bf16[16,96,256]{2,1,0:T(8,128)(2,1)} %get-tuple-element.70), channel_id=1, source_target_pairs={{1,0},{2,1},{3,2},{4,3},{5,4},{6,5},{7,6},{9,8},{10,9},{11,10},{12... | collective-permute-start | bytes 2359304 | tf_op jit(solution)/shard_map/ppermute | solution.py:963
  65.1 0.7 copy-start
  96.1 1.1 copy-start.25
  96.1 1.2 copy-start.26
  97.3 104.7 %copy-start.20 = (s32[16]{0:T(128)S(1)}, s32[16]{0:T(128)}, u32[]{:S(2)}) copy-start(s32[16]{0:T(128)} %param.16) | copy-start | bytes 196
  191.3 2.0 collective-permute-start.8
  193.3 3.7 collective-permute-start.9
  197.0 122.7 %copy-start.6 = (f32[16,96]{1,0:T(8,128)}, f32[16,96]{1,0:T(8,128)S(1)}, u32[]{:S(2)}) copy-start(f32[16,96]{1,0:T(8,128)S(1)} %add.133) | copy-start | bytes 18436
  197.0 4.4 collective-permute-start.10
  199.9 119.8 %copy-start.16 = (f32[96]{0:T(128)}, f32[96]{0:T(128)S(1)}, u32[]{:S(2)}) copy-start(f32[96]{0:T(128)S(1)} %get-tuple-element.159) | copy-start | bytes 1156
  199.9 119.8 %copy-start.18 = (f32[96]{0:T(128)}, f32[96]{0:T(128)S(1)}, u32[]{:S(2)}) copy-start(f32[96]{0:T(128)S(1)} %get-tuple-element.160) | copy-start | bytes 1156
  201.4 118.3 %copy-start.10 = (f32[16,96]{1,0:T(8,128)}, f32[16,96]{1,0:T(8,128)S(1)}, u32[]{:S(2)}) copy-start(f32[16,96]{1,0:T(8,128)S(1)} %collective-permute-done.10) | copy-start | bytes 18436
  203.5 116.2 %copy-start.4 = (f32[16,1000]{1,0:T(8,128)}, f32[16,1000]{1,0:T(8,128)S(1)}, u32[]{:S(2)}) copy-start(f32[16,1000]{1,0:T(8,128)S(1)} %get-tuple-element.130) | copy-start | bytes 192004
  319.7 7.3 %copy-start.5 = (f32[16,1000]{1,0:T(8,128)S(1)}, f32[16,1000]{1,0:T(8,128)}, u32[]{:S(2)}) copy-start(f32[16,1000]{1,0:T(8,128)} %copy-done.4) | copy-start | bytes 192004
  319.7 7.3 %copy-start.7 = (f32[16,96]{1,0:T(8,128)S(1)}, f32[16,96]{1,0:T(8,128)}, u32[]{:S(2)}) copy-start(f32[16,96]{1,0:T(8,128)} %copy-done.6) | copy-start | bytes 18436
  319.7 7.3 %copy-start.11 = (f32[16,96]{1,0:T(8,128)S(1)}, f32[16,96]{1,0:T(8,128)}, u32[]{:S(2)}) copy-start(f32[16,96]{1,0:T(8,128)} %copy-done.10) | copy-start | bytes 18436
  319.8 7.3 %copy-start.15 = (f32[16]{0:T(128)S(1)}, f32[16]{0:T(128)}, u32[]{:S(2)}) copy-start(f32[16]{0:T(128)} %copy-done.14) | copy-start | bytes 196
  319.8 7.3 %copy-start.17 = (f32[96]{0:T(128)S(1)}, f32[96]{0:T(128)}, u32[]{:S(2)}) copy-start(f32[96]{0:T(128)} %copy-done.16) | copy-start | bytes 1156
  319.8 7.3 %copy-start.19 = (f32[96]{0:T(128)S(1)}, f32[96]{0:T(128)}, u32[]{:S(2)}) copy-start(f32[96]{0:T(128)} %copy-done.18) | copy-start | bytes 1156
  321.3 6.7 %copy-start.12 = (f32[1000]{0:T(1024)S(1)}, f32[1000]{0:T(1024)}, u32[]{:S(2)}) copy-start(f32[1000]{0:T(1024)} %get-tuple-element.129) | copy-start | bytes 12004
  321.3 2.5 collective-permute-start.11
  321.4 17.7 %copy-start.1 = (f32[4,384,96]{2,1,0:T(8,128)S(1)}, f32[4,384,96]{2,1,0:T(8,128)}, u32[]{:S(2)}) copy-start(f32[4,384,96]{2,1,0:T(8,128)} %get-tuple-element.115) | copy-start | bytes 1769476
  325.8 12.1 %collective-permute-start.14 = (bf16[2,192,512]{2,1,0:T(8,128)(2,1)S(1)}, bf16[2,192,512]{2,1,0:T(8,128)(2,1)}, u32[]{:S(2)}, u32[]{:S(2)}) collective-permute-start(bf16[2,192,512]{2,1,0:T(8,128)(2,1)S(1)} %slice.285), channel_id=1, source_target_pairs={{0,2},{1,3},{2,0},{3,1},{4,6},{5,7},{6,4},{7,5},{8,10},{9,11},{10,... | collective-permute-start | bytes 1179656 | tf_op jit(solution)/shard_map/ppermute | solution.py:957
  328.1 29.9 %collective-permute-start.12 = (bf16[16,96,256]{2,1,0:T(8,128)(2,1)}, bf16[16,96,256]{2,1,0:T(8,128)(2,1)}, u32[]{:S(2)}, u32[]{:S(2)}) collective-permute-start(bf16[16,96,256]{2,1,0:T(8,128)(2,1)} %get-tuple-element.95), channel_id=1, source_target_pairs={{0,1},{1,2},{2,3},{3,4},{4,5},{5,6},{6,7},{8,9},{9,10},{10,11},{11... | collective-permute-start | bytes 2359304 | tf_op jit(solution)/shard_map/ppermute | solution.py:963
  330.7 27.2 %collective-permute-start.13 = (bf16[16,96,256]{2,1,0:T(8,128)(2,1)}, bf16[16,96,256]{2,1,0:T(8,128)(2,1)}, u32[]{:S(2)}, u32[]{:S(2)}) collective-permute-start(bf16[16,96,256]{2,1,0:T(8,128)(2,1)} %get-tuple-element.96), channel_id=1, source_target_pairs={{1,0},{2,1},{3,2},{4,3},{5,4},{6,5},{7,6},{9,8},{10,9},{11,10},{12... | collective-permute-start | bytes 2359304 | tf_op jit(solution)/shard_map/ppermute | solution.py:963
  342.3 9.0 %collective-permute-start.15 = (bf16[1,192,512]{2,1,0:T(8,128)(2,1)S(1)}, bf16[1,192,512]{2,1,0:T(8,128)(2,1)S(1)}, u32[]{:S(2)}, u32[]{:S(2)}) collective-permute-start(bf16[1,192,512]{2,1,0:T(8,128)(2,1)S(1)} %slice.286), channel_id=1, source_target_pairs={{0,4},{1,5},{2,6},{3,7},{4,0},{5,1},{6,2},{7,3},{8,12},{9,13},{10,... | collective-permute-start | bytes 589832 | tf_op jit(solution)/shard_map/ppermute | solution.py:957
  355.6 3.3 collective-permute-start.16
  358.9 0.7 copy-start.27
  359.6 42.2 %copy-start.23 = (f32[96]{0:T(128)S(1)}, f32[96]{0:T(128)}, u32[]{:S(2)}) copy-start(f32[96]{0:T(128)} %get-tuple-element.124) | copy-start | bytes 1156
  359.6 42.2 %copy-start.24 = (f32[96]{0:T(128)S(1)}, f32[96]{0:T(128)}, u32[]{:S(2)}) copy-start(f32[96]{0:T(128)} %get-tuple-element.125) | copy-start | bytes 1156
  359.6 43.8 %copy-start.13 = (f32[3,4,32]{2,1,0:T(4,128)S(1)}, f32[3,4,32]{2,1,0:T(4,128)}, u32[]{:S(2)}) copy-start(f32[3,4,32]{2,1,0:T(4,128)} %constant.102.clone) | copy-start | bytes 4612
  411.0 16.5 %copy-start.21 = (f32[16]{0:T(128)S(1)}, f32[16]{0:T(128)}, u32[]{:S(2)}) copy-start(f32[16]{0:T(128)} %get-tuple-element.121) | copy-start | bytes 196
  411.0 16.5 %copy-start.22 = (f32[16]{0:T(128)S(1)}, f32[16]{0:T(128)}, u32[]{:S(2)}) copy-start(f32[16]{0:T(128)} %get-tuple-element.122) | copy-start | bytes 196
  411.4 46.6 %copy-start.3 = (f32[8960]{0:T(1024)S(1)}, f32[8960]{0:T(1024)}, u32[]{:S(2)}) copy-start(f32[8960]{0:T(1024)} %param.11) | copy-start | bytes 107524
  411.4 46.6 %copy-start.8 = (f32[8960]{0:T(1024)S(1)}, f32[8960]{0:T(1024)}, u32[]{:S(2)}) copy-start(f32[8960]{0:T(1024)} %param.12) | copy-start | bytes 107524
  411.5 46.6 %copy-start.9 = (f32[8960]{0:T(1024)S(1)}, f32[8960]{0:T(1024)}, u32[]{:S(2)}) copy-start(f32[8960]{0:T(1024)} %param.13) | copy-start | bytes 107524
  411.5 5.4 %collective-permute-start.17 = (f32[4,2,2,70,128]{4,0,3,2,1:T(4,128)S(1)}, f32[4,2,2,70,128]{4,0,3,2,1:T(4,128)S(1)}, u32[]{:S(2)}, u32[]{:S(2)}) collective-permute-start(f32[4,2,2,70,128]{4,0,3,2,1:T(4,128)S(1)} %copy.217), channel_id=1, source_target_pairs={{0,1},{1,0},{2,3},{3,2},{4,5},{5,4},{6,7},{7,6},{8,9},{9,8},{10,11... | collective-permute-start | bytes 1720328 | tf_op jit(solution)/shard_map/ppermute | solution.py:957
  417.0 10.0 %collective-permute-start.18 = (f32[4,2,70,128]{3,2,1,0:T(8,128)S(1)}, f32[4,2,70,128]{3,2,1,0:T(8,128)S(1)}, u32[]{:S(2)}, u32[]{:S(2)}) collective-permute-start(f32[4,2,70,128]{3,2,1,0:T(8,128)S(1)} %dynamic-slice_bitcast_fusion.1), channel_id=1, source_target_pairs={{0,2},{1,3},{2,0},{3,1},{4,6},{5,7},{6,4},{7,5},{8,10},{9,11},{10,... | collective-permute-start | bytes 860168 | tf_op jit(solution)/shard_map/ppermute | solution.py:957
  427.1 5.6 %collective-permute-start.19 = (f32[4,70,128]{2,1,0:T(8,128)S(1)}, f32[4,70,128]{2,1,0:T(8,128)S(1)}, u32[]{:S(2)}, u32[]{:S(2)}) collective-permute-start(f32[4,70,128]{2,1,0:T(8,128)S(1)} %dynamic-slice_bitcast_fusion.2), channel_id=1, source_target_pairs={{0,4},{1,5},{2,6},{3,7},{4,0},{5,1},{6,2},{7,3},{8,12},{9,13},{10,... | collective-permute-start | bytes 430088 | tf_op jit(solution)/shard_map/ppermute | solution.py:957
  432.7 5.2 %collective-permute-start.20 = (f32[288,128]{1,0:T(8,128)S(1)}, f32[288,128]{1,0:T(8,128)S(1)}, u32[]{:S(2)}, u32[]{:S(2)}) collective-permute-start(f32[288,128]{1,0:T(8,128)S(1)} %concatenate.39), channel_id=1, source_target_pairs={{0,8},{8,0},{16,24},{24,16},{1,9},{9,1},{17,25},{25,17},{2,10},{10... | collective-permute-start | bytes 442376 | tf_op jit(solution)/shard_map/ppermute | solution.py:957
  438.0 7.7 %collective-permute-start.21 = (f32[288,128]{1,0:T(8,128)S(1)}, f32[288,128]{1,0:T(8,128)S(1)}, u32[]{:S(2)}, u32[]{:S(2)}) collective-permute-start(f32[288,128]{1,0:T(8,128)S(1)} %pad_add_fusion.3), channel_id=1, source_target_pairs={{0,16},{8,24},{16,0},{24,8},{1,17},{9,25},{17,1},{25,9},{2,18},{10... | collective-permute-start | bytes 442376 | tf_op jit(solution)/shard_map/ppermute | solution.py:957
  446.8 1.2 collective-permute-start.22
  449.4 3.6 collective-permute-start.23
  453.7 3.6 collective-permute-start.24
Sparse Core Ops, SparseCore 0:
  68.0 29.1 all-gather.2

commit v7 on v6

--- a/solution.py
+++ b/solution.py
@@ -601,14 +601,14 @@
             peak = jnp.max(scores, axis=0, keepdims=True)
             weights = jnp.exp2((scores - peak) * EXP2_SCALE)
             inverse = 1.0 / jnp.sum(weights, axis=0, keepdims=True)
-            return (weights * inverse).astype(BF16), peak, inverse
+            return weights.astype(BF16), peak, inverse
 
         long_query = by_image(jnp.concatenate([query, extra], axis=0))
         scores = jnp.concatenate([dot(kn_ref[g, :, :depth], long_query[g]) for g in range(GROUP)], axis=1)
         probs, peak, inverse = by_lanes(softmax, scores)
         mixed = by_image(probs)
         mixed = jnp.concatenate([dot(v_ref[g], mixed[g]) for g in range(GROUP)], axis=1)
-        attended = (mixed + query.astype(F32)).astype(BF16)
+        attended = (mixed * inverse + query.astype(F32)).astype(BF16)
         store_pair(att_ref, pair, attended)
 
         def second_norm(k, x0, out):

time: 468 us -> 470 us (level)
  no operation moved by 1% of the time
where the time goes in v7:
time: 470 us; the launch traced here: 471 us
  Pallas kernels  298 us (63%)
  waiting for transfers between devices  51.7 us (11%)
  starting transfers between devices  41.9 us (9%)
  local copies, waits for them, and re-layouts  32.9 us (7%)
  other arithmetic  24.6 us (5%)
  between operations  19.7 us (4%)
    pallas_call x1, Pallas kernels, call_backward(): pl.pallas_call(functools.partial(backward_kernel, offset=offset, key_rows...  117 us
    pallas_call x1, Pallas kernels, call_forward(): pl.pallas_call(functools.partial(forward_kernel, offset=offset, key_rows=...  94.4 us
    ppermute x19, waiting for transfers between devices, swap(): return lax.ppermute(value, axis, [(i, i ^ 1 << bit) for i in range(size)])  49.7 us
    pallas_call x1, Pallas kernels, call_embed_back(): pl.pallas_call(functools.partial(embed_back_kernel, offset=offset), grid_...  37 us
    ppermute x19, starting transfers between devices, swap(): return lax.ppermute(value, axis, [(i, i ^ 1 << bit) for i in range(size)])  29.6 us
    pallas_call x1, Pallas kernels, call_embed(): pl.pallas_call(functools.partial(embed_kernel, offset=offset), grid_spec=...  27.3 us
    pallas_call x1, Pallas kernels, call_edge(): pl.pallas_call(functools.partial(edge_kernel, offset=offset), grid_spec=p...  18.6 us
    ppermute x6, starting transfers between devices, shifted(): return lax.ppermute(value, axis, pairs)  12.3 us
  transfers between devices with their start and end apart: 26, of which 19 were waited for; matrix products, arithmetic and copies ran while one was open for 6% of the time, Pallas kernels for 7%

profile of v7, /device:TPU:0, one launch (start us, length us, event | category | flops | bytes accessed | tf_op | source)
XLA Modules:
  0.0 471.2 jit_solution(16428108660373897816)
XLA Ops:
  8.0 4.0 collective-permute-start
  12.8 1.0 collective-permute-done
  14.6 2.0 collective-permute-start.1
  16.7 1.9 collective-permute-done.1
  18.6 2.0 collective-permute-start.2
  20.6 2.4 collective-permute-done.2
  23.1 2.0 collective-permute-start.3
  26.5 1.0 reduce_max.20
  27.5 1.0 exponential_reduce_fusion
  29.3 0.9 subtract_subtract_fusion
  33.9 18.6 %edge.1 = (bf16[16,96,256]{2,1,0:T(8,128)(2,1)}, bf16[16,96,256]{2,1,0:T(8,128)(2,1)}, bf16[16,96,384]{2,1,0:T(8,128)(2,1)}, bf16[16,192,384]{2,1,0:T(8,128)(2,1...) custom-call(s32[16,2]{1,0:T(8,128)} %copy.206.ext_ref, s32[1]{0:T(128)} %bitcast.1.row_ref, s32[16]{0:T(128)} %select_reduce_fusion.4.order_ref, ...), custom_call_target="tpu_custom_call" | custom-call | flops 16000000000 | bytes 16000000 | tf_op jit(solution)/shard_map/edge/pallas_call | solution.py:430
  52.5 2.4 collective-permute-start.7
  60.5 3.2 collective-permute-start.5
  63.6 1.5 collective-permute-start.6
  65.9 2.0 pool_norm.1
  67.9 27.3 %embed.1 = (bf16[16,256,2048]{2,1,0:T(8,128)(2,1)}, f32[16,96,2048]{2,1,0:T(8,128)}, bf16[16,96,2560]{2,1,0:T(8,128)(2,1)}) custom-call(s32[16,2]{1,0:T(8,128)} %copy.198.ext_ref, s32[1]{0:T(128)} %bitcast.1.row_ref, s32[16]{0:T(128)} %select_reduce_fusion.4.order_ref, bf16[16,7,3,8,1024]{4,3,2,1,0:T(8,128)(2,1)} %bitcast.159, ...), custom_call_target="tpu_custom_call" | custom-call | flops 32000000000 | bytes 64000000 | tf_op jit(solution)/shard_map/embed/pallas_call | solution.py:450
  95.2 1.0 copy.203.rw_ref
  96.2 1.0 all-gather.3.cloned.1.call-done
  97.3 94.4 %forward.1 = (bf16[16,96,2048]{2,1,0:T(8,128)(2,1)}, bf16[16,96,2048]{2,1,0:T(8,128)(2,1)}, bf16[16,96,2048]{2,1,0:T(8,128)(2,1)}, bf16[16,96,2048]{2,1,0:T(8,12...) custom-call(s32[16,2]{1,0:T(8,128)} %copy.206.ext_ref, ...), custom_call_target="tpu_custom_call" | custom-call | flops 80000000000 | bytes 64000000 | tf_op jit(solution)/shard_map/forward/pallas_call | solution.py:647
  191.7 1.5 reduce_sum.215
  193.3 1.2 collective-permute-start.8
  195.3 1.9 collective-permute-start.9
  197.2 1.7 collective-permute-done.9
  199.0 2.8 collective-permute-start.10
  202.3 1.0 collective-permute-done.10
  206.5 1.2 copy.205.gvec_ref
  207.7 116.9 %backward.1 = (bf16[16,96,2048]{2,1,0:T(8,128)(2,1)}, bf16[16,96,2048]{2,1,0:T(8,128)(2,1)}, bf16[16,96,256]{2,1,0:T(8,128)(2,1)}, bf16[16,96,256]{2,1,0:T(8,128...) custom-call(s32[16,2]{1,0:T(8,128)} %copy.206.ext_ref, ...), custom_call_target="tpu_custom_call" | custom-call | flops 192000000000 | bytes 96000000 | tf_op jit(solution)/shard_map/backward/pallas_call | solution.py:841
  324.7 1.5 slice.284
  326.3 2.4 collective-permute-done.11
  328.7 2.0 convert_add_fusion
  330.7 1.2 collective-permute-start.14
  332.9 2.7 collective-permute-start.12
  335.6 1.3 collective-permute-start.13
  336.9 6.0 %collective-permute-done.14 = bf16[2,192,512]{2,1,0:T(8,128)(2,1)} collective-permute-done((bf16[2,192,512]{2,1,0:T(8,128)(2,1)S(1)}, bf16[2,192,512]{2,1,0:T(8,128)(2,1)}, u32[]{:S(2)}, u32[]{:S(2)}) %collective-permute-start.14) | collective-permute-done | bytes 393248 | tf_op jit(solution)/shard_map/ppermute | solution.py:957
  342.8 1.1 convert_add_fusion.1
  344.8 0.9 slice.217
  347.2 1.3 collective-permute-start.15
  348.5 1.1 reduce_sum.223
  349.6 1.3 reduce_sum.220
  351.4 0.9 slice.216
  353.3 3.0 collective-permute-done.15
  357.0 2.4 pool_back.1
  359.4 1.0 convert_element_type.69
  360.4 1.3 collective-permute-start.16
  361.7 1.1 reduce_sum.224
  362.8 0.9 collective-permute-done.16.under_ref
  364.5 37.0 %embed_back.1 = (f32[112,96]{1,0:T(8,128)}, f32[112,192]{1,0:T(8,128)}, f32[96,256]{1,0:T(8,128)}, f32[3,96,128]{2,1,0:T(8,128)}, f32[192,384]{1,0:T(8,128)}) custom-call(s32[16,2]{1,0:T(8,128)} %copy.206.ext_ref, s32[1]{0:T(128)} %bitcast.1.row_ref, bf16[16,256,2048]{2,1,0:T(8,128)(2,1)} %get-tuple-element.67.patch_ref, ...), custom_call_target="tpu_custom_call" | custom-call | flops 48000000000 | bytes 48000000 | tf_op jit(solution)/shard_map/embed_back/pallas_call | solution.py:934
  401.4 1.0 copy.207
  402.5 0.9 slice.214
  405.6 1.1 reduce_sum.222
  406.8 1.1 copy.215
  409.2 6.5 %concatenate.38 = f32[286312]{0:T(1024)S(1)} concatenate(f32[14112]{0:T(1024)S(1)} %reshape_reshape.21, f32[27648]{0:T(1024)S(1)} %reshape.189, f32[9216]{0:T(1024)S(1)} %reshape.190, f32[36864]{0:T(1024)S(1)} %reshape.191, f32[36864]{0:T(1024)S(1)} %reshape.192, f32[96000]{0:T(1024)S(1)} %reshape.193, f32[11520]{0:T(1024)S(1)} %reshape_reshape.22, f32[48384]{0:T(1024)S(1)} %reshape_reshape.23, ...), dimensions={0} | concatenate | bytes 2290496 | tf_op jit(solution)/shard_map/concatenate | solution.py:1227
  416.3 3.9 collective-permute-start.17
  420.2 1.6 collective-permute-done.17
  421.9 2.4 collective-permute-start.18
  424.3 7.5 %collective-permute-done.18 = f32[4,2,70,128]{3,2,1,0:T(8,128)S(1)} collective-permute-done((f32[4,2,70,128]{3,2,1,0:T(8,128)S(1)}, f32[4,2,70,128]{3,2,1,0:T(8,128)S(1)}, u32[]{:S(2)}, u32[]{:S(2)}) %collective-permute-start.18) | collective-permute-done | bytes 286752 | tf_op jit(solution)/shard_map/ppermute | solution.py:957
  433.6 4.0 collective-permute-done.19
  437.7 5.1 %collective-permute-done.20 = f32[288,128]{1,0:T(8,128)S(1)} collective-permute-done((f32[288,128]{1,0:T(8,128)S(1)}, f32[288,128]{1,0:T(8,128)S(1)}, u32[]{:S(2)}, u32[]{:S(2)}) %collective-permute-start.20) | collective-permute-done | bytes 147488 | tf_op jit(solution)/shard_map/ppermute | solution.py:957
  442.9 7.3 %collective-permute-done.21 = f32[288,128]{1,0:T(8,128)S(1)} collective-permute-done((f32[288,128]{1,0:T(8,128)S(1)}, f32[288,128]{1,0:T(8,128)S(1)}, u32[]{:S(2)}, u32[]{:S(2)}) %collective-permute-start.21) | collective-permute-done | bytes 147488 | tf_op jit(solution)/shard_map/ppermute | solution.py:957
  451.4 1.2 collective-permute-done.22
  454.0 2.6 collective-permute-start.23
  456.6 0.9 collective-permute-done.23
  458.2 1.6 collective-permute-start.24
  459.8 1.9 collective-permute-done.24
  (217 shorter events, 32.9 us)
Async XLA Ops:
  7.2 90.0 %all-gather.3.cloned.1.call-start = ((), (), s32[]{:S(2)}) async-start(), calls=%async_computation | async-start | bytes 1769472 | tf_op jit(solution)/shard_map/all_gather | solution.py:1144
  8.0 5.8 %collective-permute-start = (bf16[70,128]{1,0:T(8,128)(2,1)S(1)}, bf16[70,128]{1,0:T(8,128)(2,1)S(1)}, u32[]{:S(2)}, u32[]{:S(2)}) collective-permute-start(bf16[70,128]{1,0:T(8,128)(2,1)S(1)} %convert_bitcast_fusion), channel_id=1, source_target_pairs={{0,16},{8,24},{16,0},{24,8},{1,17},{9,25},{17,1},{25,9},{2,18},{10... | collective-permute-start | bytes 53768 | tf_op jit(solution)/shard_map/ppermute | solution.py:957
  12.8 192.7 %copy-start.14 = (f32[16]{0:T(128)}, f32[16]{0:T(128)S(1)}, u32[]{:S(2)}) copy-start(f32[16]{0:T(128)S(1)} %get-tuple-element.165) | copy-start | bytes 196
  14.6 4.0 collective-permute-start.1
  18.6 4.4 collective-permute-start.2
  23.1 5.5 %collective-permute-start.3 = (bf16[2,2,2,70,128]{4,3,0,1,2:T(8,128)(2,1)S(1)}, bf16[2,2,2,70,128]{4,3,0,1,2:T(8,128)(2,1)S(1)}, u32[]{:S(2)}, u32[]{:S(2)}) collective-permute-start(bf16[2,2,2,70,128]{4,3,0,1,2:T(8,128)(2,1)S(1)} %pad_maximum_fusion.2), channel_id=1, source_target_pairs={{0,2},{1,3},{2,0},{3,1},{4,6},{5,7},{6,4},{7,5},{8,10},{9,11},{10,... | collective-permute-start | bytes 430088 | tf_op jit(solution)/shard_map/ppermute | solution.py:957
  28.6 1.6 collective-permute-start.4
  31.7 27.3 %copy-start.2 = (bf16[96,288]{1,0:T(8,128)(2,1)}, bf16[96,288]{1,0:T(8,128)(2,1)S(1)}, u32[]{:S(2)}) copy-start(bf16[96,288]{1,0:T(8,128)(2,1)S(1)} %reshape.185.wqkv_ref) | copy-start | bytes 165892
  52.5 12.6 %collective-permute-start.7 = (f32[192,512]{1,0:T(8,128)}, f32[192,512]{1,0:T(8,128)S(1)}, u32[]{:S(2)}, u32[]{:S(2)}) collective-permute-start(f32[192,512]{1,0:T(8,128)} %get-tuple-element.73), channel_id=1, source_target_pairs={{0,1},{1,2},{2,3},{3,4},{4,5},{5,6},{6,7},{8,9},{9,10},{10,11},{11... | collective-permute-start | bytes 1179656 | tf_op jit(solution)/shard_map/ppermute | solution.py:963
  60.5 35.7 %collective-permute-start.5 = (bf16[16,96,256]{2,1,0:T(8,128)(2,1)}, bf16[16,96,256]{2,1,0:T(8,128)(2,1)S(1)}, u32[]{:S(2)}, u32[]{:S(2)}) collective-permute-start(bf16[16,96,256]{2,1,0:T(8,128)(2,1)} %get-tuple-element.69), channel_id=1, source_target_pairs={{0,1},{1,2},{2,3},{3,4},{4,5},{5,6},{6,7},{8,9},{9,10},{10,11},{11... | collective-permute-start | bytes 2359304 | tf_op jit(solution)/shard_map/ppermute | solution.py:963
  63.6 32.5 %collective-permute-start.6 = (bf16[16,96,256]{2,1,0:T(8,128)(2,1)}, bf16[16,96,256]{2,1,0:T(8,128)(2,1)S(1)}, u32[]{:S(2)}, u32[]{:S(2)}) collective-permute-start(bf16[16,96,256]{2,1,0:T(8,128)(2,1)} %get-tuple-element.70), channel_id=1, source_target_pairs={{1,0},{2,1},{3,2},{4,3},{5,4},{6,5},{7,6},{9,8},{10,9},{11,10},{12... | collective-permute-start | bytes 2359304 | tf_op jit(solution)/shard_map/ppermute | solution.py:963
  65.1 0.7 copy-start
  96.1 1.1 copy-start.25
  96.1 1.2 copy-start.26
  97.3 106.7 %copy-start.20 = (s32[16]{0:T(128)S(1)}, s32[16]{0:T(128)}, u32[]{:S(2)}) copy-start(s32[16]{0:T(128)} %param.16) | copy-start | bytes 196
  193.3 2.0 collective-permute-start.8
  195.3 3.7 collective-permute-start.9
  199.0 125.6 %copy-start.6 = (f32[16,96]{1,0:T(8,128)}, f32[16,96]{1,0:T(8,128)S(1)}, u32[]{:S(2)}) copy-start(f32[16,96]{1,0:T(8,128)S(1)} %add.133) | copy-start | bytes 18436
  199.0 4.4 collective-permute-start.10
  201.8 122.7 %copy-start.16 = (f32[96]{0:T(128)}, f32[96]{0:T(128)S(1)}, u32[]{:S(2)}) copy-start(f32[96]{0:T(128)S(1)} %get-tuple-element.159) | copy-start | bytes 1156
  201.8 122.7 %copy-start.18 = (f32[96]{0:T(128)}, f32[96]{0:T(128)S(1)}, u32[]{:S(2)}) copy-start(f32[96]{0:T(128)S(1)} %get-tuple-element.160) | copy-start | bytes 1156
  203.4 121.2 %copy-start.10 = (f32[16,96]{1,0:T(8,128)}, f32[16,96]{1,0:T(8,128)S(1)}, u32[]{:S(2)}) copy-start(f32[16,96]{1,0:T(8,128)S(1)} %collective-permute-done.10) | copy-start | bytes 18436
  205.5 119.1 %copy-start.4 = (f32[16,1000]{1,0:T(8,128)}, f32[16,1000]{1,0:T(8,128)S(1)}, u32[]{:S(2)}) copy-start(f32[16,1000]{1,0:T(8,128)S(1)} %get-tuple-element.130) | copy-start | bytes 192004
  324.6 7.3 %copy-start.5 = (f32[16,1000]{1,0:T(8,128)S(1)}, f32[16,1000]{1,0:T(8,128)}, u32[]{:S(2)}) copy-start(f32[16,1000]{1,0:T(8,128)} %copy-done.4) | copy-start | bytes 192004
  324.6 7.3 %copy-start.7 = (f32[16,96]{1,0:T(8,128)S(1)}, f32[16,96]{1,0:T(8,128)}, u32[]{:S(2)}) copy-start(f32[16,96]{1,0:T(8,128)} %copy-done.6) | copy-start | bytes 18436
  324.6 7.3 %copy-start.11 = (f32[16,96]{1,0:T(8,128)S(1)}, f32[16,96]{1,0:T(8,128)}, u32[]{:S(2)}) copy-start(f32[16,96]{1,0:T(8,128)} %copy-done.10) | copy-start | bytes 18436
  324.6 7.3 %copy-start.15 = (f32[16]{0:T(128)S(1)}, f32[16]{0:T(128)}, u32[]{:S(2)}) copy-start(f32[16]{0:T(128)} %copy-done.14) | copy-start | bytes 196
  324.6 7.3 %copy-start.17 = (f32[96]{0:T(128)S(1)}, f32[96]{0:T(128)}, u32[]{:S(2)}) copy-start(f32[96]{0:T(128)} %copy-done.16) | copy-start | bytes 1156
  324.7 7.3 %copy-start.19 = (f32[96]{0:T(128)S(1)}, f32[96]{0:T(128)}, u32[]{:S(2)}) copy-start(f32[96]{0:T(128)} %copy-done.18) | copy-start | bytes 1156
  326.2 6.7 %copy-start.12 = (f32[1000]{0:T(1024)S(1)}, f32[1000]{0:T(1024)}, u32[]{:S(2)}) copy-start(f32[1000]{0:T(1024)} %get-tuple-element.129) | copy-start | bytes 12004
  326.2 2.5 collective-permute-start.11
  326.3 17.7 %copy-start.1 = (f32[4,384,96]{2,1,0:T(8,128)S(1)}, f32[4,384,96]{2,1,0:T(8,128)}, u32[]{:S(2)}) copy-start(f32[4,384,96]{2,1,0:T(8,128)} %get-tuple-element.115) | copy-start | bytes 1769476
  330.7 12.1 %collective-permute-start.14 = (bf16[2,192,512]{2,1,0:T(8,128)(2,1)S(1)}, bf16[2,192,512]{2,1,0:T(8,128)(2,1)}, u32[]{:S(2)}, u32[]{:S(2)}) collective-permute-start(bf16[2,192,512]{2,1,0:T(8,128)(2,1)S(1)} %slice.285), channel_id=1, source_target_pairs={{0,2},{1,3},{2,0},{3,1},{4,6},{5,7},{6,4},{7,5},{8,10},{9,11},{10,... | collective-permute-start | bytes 1179656 | tf_op jit(solution)/shard_map/ppermute | solution.py:957
  332.9 29.9 %collective-permute-start.12 = (bf16[16,96,256]{2,1,0:T(8,128)(2,1)}, bf16[16,96,256]{2,1,0:T(8,128)(2,1)}, u32[]{:S(2)}, u32[]{:S(2)}) collective-permute-start(bf16[16,96,256]{2,1,0:T(8,128)(2,1)} %get-tuple-element.95), channel_id=1, source_target_pairs={{0,1},{1,2},{2,3},{3,4},{4,5},{5,6},{6,7},{8,9},{9,10},{10,11},{11... | collective-permute-start | bytes 2359304 | tf_op jit(solution)/shard_map/ppermute | solution.py:963
  335.6 27.2 %collective-permute-start.13 = (bf16[16,96,256]{2,1,0:T(8,128)(2,1)}, bf16[16,96,256]{2,1,0:T(8,128)(2,1)}, u32[]{:S(2)}, u32[]{:S(2)}) collective-permute-start(bf16[16,96,256]{2,1,0:T(8,128)(2,1)} %get-tuple-element.96), channel_id=1, source_target_pairs={{1,0},{2,1},{3,2},{4,3},{5,4},{6,5},{7,6},{9,8},{10,9},{11,10},{12... | collective-permute-start | bytes 2359304 | tf_op jit(solution)/shard_map/ppermute | solution.py:963
  347.2 9.0 %collective-permute-start.15 = (bf16[1,192,512]{2,1,0:T(8,128)(2,1)S(1)}, bf16[1,192,512]{2,1,0:T(8,128)(2,1)S(1)}, u32[]{:S(2)}, u32[]{:S(2)}) collective-permute-start(bf16[1,192,512]{2,1,0:T(8,128)(2,1)S(1)} %slice.286), channel_id=1, source_target_pairs={{0,4},{1,5},{2,6},{3,7},{4,0},{5,1},{6,2},{7,3},{8,12},{9,13},{10,... | collective-permute-start | bytes 589832 | tf_op jit(solution)/shard_map/ppermute | solution.py:957
  360.4 3.3 collective-permute-start.16
  363.8 0.7 copy-start.27
  364.5 42.2 %copy-start.23 = (f32[96]{0:T(128)S(1)}, f32[96]{0:T(128)}, u32[]{:S(2)}) copy-start(f32[96]{0:T(128)} %get-tuple-element.124) | copy-start | bytes 1156
  364.5 42.2 %copy-start.24 = (f32[96]{0:T(128)S(1)}, f32[96]{0:T(128)}, u32[]{:S(2)}) copy-start(f32[96]{0:T(128)} %get-tuple-element.125) | copy-start | bytes 1156
  364.5 43.8 %copy-start.13 = (f32[3,4,32]{2,1,0:T(4,128)S(1)}, f32[3,4,32]{2,1,0:T(4,128)}, u32[]{:S(2)}) copy-start(f32[3,4,32]{2,1,0:T(4,128)} %constant.102.clone) | copy-start | bytes 4612
  415.9 16.5 %copy-start.21 = (f32[16]{0:T(128)S(1)}, f32[16]{0:T(128)}, u32[]{:S(2)}) copy-start(f32[16]{0:T(128)} %get-tuple-element.121) | copy-start | bytes 196
  415.9 16.5 %copy-start.22 = (f32[16]{0:T(128)S(1)}, f32[16]{0:T(128)}, u32[]{:S(2)}) copy-start(f32[16]{0:T(128)} %get-tuple-element.122) | copy-start | bytes 196
  416.3 46.2 %copy-start.3 = (f32[8960]{0:T(1024)S(1)}, f32[8960]{0:T(1024)}, u32[]{:S(2)}) copy-start(f32[8960]{0:T(1024)} %param.11) | copy-start | bytes 107524
  416.3 46.2 %copy-start.8 = (f32[8960]{0:T(1024)S(1)}, f32[8960]{0:T(1024)}, u32[]{:S(2)}) copy-start(f32[8960]{0:T(1024)} %param.12) | copy-start | bytes 107524
  416.3 46.2 %copy-start.9 = (f32[8960]{0:T(1024)S(1)}, f32[8960]{0:T(1024)}, u32[]{:S(2)}) copy-start(f32[8960]{0:T(1024)} %param.13) | copy-start | bytes 107524
  416.3 5.5 %collective-permute-start.17 = (f32[4,2,2,70,128]{4,0,3,2,1:T(4,128)S(1)}, f32[4,2,2,70,128]{4,0,3,2,1:T(4,128)S(1)}, u32[]{:S(2)}, u32[]{:S(2)}) collective-permute-start(f32[4,2,2,70,128]{4,0,3,2,1:T(4,128)S(1)} %copy.217), channel_id=1, source_target_pairs={{0,1},{1,0},{2,3},{3,2},{4,5},{5,4},{6,7},{7,6},{8,9},{9,8},{10,11... | collective-permute-start | bytes 1720328 | tf_op jit(solution)/shard_map/ppermute | solution.py:957
  421.9 10.0 %collective-permute-start.18 = (f32[4,2,70,128]{3,2,1,0:T(8,128)S(1)}, f32[4,2,70,128]{3,2,1,0:T(8,128)S(1)}, u32[]{:S(2)}, u32[]{:S(2)}) collective-permute-start(f32[4,2,70,128]{3,2,1,0:T(8,128)S(1)} %dynamic-slice_bitcast_fusion.1), channel_id=1, source_target_pairs={{0,2},{1,3},{2,0},{3,1},{4,6},{5,7},{6,4},{7,5},{8,10},{9,11},{10,... | collective-permute-start | bytes 860168 | tf_op jit(solution)/shard_map/ppermute | solution.py:957
  431.9 5.6 %collective-permute-start.19 = (f32[4,70,128]{2,1,0:T(8,128)S(1)}, f32[4,70,128]{2,1,0:T(8,128)S(1)}, u32[]{:S(2)}, u32[]{:S(2)}) collective-permute-start(f32[4,70,128]{2,1,0:T(8,128)S(1)} %dynamic-slice_bitcast_fusion.2), channel_id=1, source_target_pairs={{0,4},{1,5},{2,6},{3,7},{4,0},{5,1},{6,2},{7,3},{8,12},{9,13},{10,... | collective-permute-start | bytes 430088 | tf_op jit(solution)/shard_map/ppermute | solution.py:957
  437.6 5.2 %collective-permute-start.20 = (f32[288,128]{1,0:T(8,128)S(1)}, f32[288,128]{1,0:T(8,128)S(1)}, u32[]{:S(2)}, u32[]{:S(2)}) collective-permute-start(f32[288,128]{1,0:T(8,128)S(1)} %concatenate.39), channel_id=1, source_target_pairs={{0,8},{8,0},{16,24},{24,16},{1,9},{9,1},{17,25},{25,17},{2,10},{10... | collective-permute-start | bytes 442376 | tf_op jit(solution)/shard_map/ppermute | solution.py:957
  442.8 7.4 %collective-permute-start.21 = (f32[288,128]{1,0:T(8,128)S(1)}, f32[288,128]{1,0:T(8,128)S(1)}, u32[]{:S(2)}, u32[]{:S(2)}) collective-permute-start(f32[288,128]{1,0:T(8,128)S(1)} %pad_add_fusion.3), channel_id=1, source_target_pairs={{0,16},{8,24},{16,0},{24,8},{1,17},{9,25},{17,1},{25,9},{2,18},{10... | collective-permute-start | bytes 442376 | tf_op jit(solution)/shard_map/ppermute | solution.py:957
  451.4 1.2 collective-permute-start.22
  454.0 3.6 collective-permute-start.23
  458.2 3.6 collective-permute-start.24
Sparse Core Ops, SparseCore 0:
  68.0 29.1 all-gather.2
